TPU v7x, 32 devices: a whole 2x2x4 slice. The times are simulated.
32 devices in a mesh: dp: 8 (over y, x, core), fsdp: 4 (over z).
Axes of the slice: x: 2, y: 2, z: 4, core: 2. Of those that a mesh axis runs over, the one named last changes fastest.
Arguments:
- queries: bfloat16 [4096, 1536], P(('dp', 'fsdp')), may hold values from -6 to 6
- grad_out: bfloat16 [4096, 1536], P(('dp', 'fsdp')), may hold values from -6 to 6
- text_cache: bfloat16 [256, 4096], P('dp', 'fsdp'), may hold values from -6 to 6
- w_kv: bfloat16 [4096, 3072], P('fsdp'), may hold values from -0.09375 to 0.09375
- image_counts: int32 [32, 2], P(('dp', 'fsdp')), may hold values from 1 to 96, 128 in all within a row
- caption_lens: int32 [8, 8], P('dp'), may hold values from 1 to 32, as said below
- caption_owner: int32 [8, 8], P('dp'), may hold values from 0 to 7
- caption_offset: int32 [8, 8], P('dp'), may hold values from 0 to 31, as said below
Outputs:
- grad_queries: bfloat16 [4096, 1536], P(('dp', 'fsdp'))
- grad_kv: bfloat16 [8, 4096, 3072], P('dp', 'fsdp')
Inputs may be any that keep to these rules, and one draw needn't show every extreme that they name: caption_offset + caption_lens <= 32 for every caption. `caption_lens`: some caption has exactly 32 tokens and some caption has exactly one.
All inputs are finite; a program needn't handle non-finite values.
Results may differ from a plain program's by a relative error of at most 0.023.
Values may be sent and summed in bfloat16 or wider, within the bound.
No kernel may reach another device: no remote copies, remote signals or barrier semaphores. Data moves between devices by JAX's collectives and lax.ppermute only.
A program may use at most 64 MiB of HBM per device.

v0:
```python
import jax
import jax.numpy as jnp
from jax import lax
from jax.sharding import PartitionSpec as P

HEADS = 12
HEAD = 128
LMAX = 32
SAMPLES = 2


def shards(
    queries, grad_out, text_cache, w_kv, image_counts, caption_lens, caption_owner, caption_offset
):
    groups = lax.axis_size("fsdp")
    member = lax.axis_index("fsdp")
    attn_scale = HEAD ** (-0.5)
    lengths = caption_lens[0]
    owners = caption_owner[0]
    offsets = caption_offset[0]
    cache_depth = text_cache.shape[0]
    slot_steps = jnp.arange(LMAX, dtype=jnp.int32)
    wanted = (owners[:, None] * cache_depth + offsets[:, None] + slot_steps[None, :]).reshape(-1)
    live_slot = (slot_steps[None, :] < lengths[:, None]).reshape(-1)
    empty = jnp.zeros((wanted.shape[0], text_cache.shape[1]), jnp.bfloat16)
    piece = lax.all_gather(text_cache, "dp", axis=0, tiled=True)
    inside = live_slot & (wanted >= 0) & (wanted < piece.shape[0])
    taken = jnp.take(piece, jnp.clip(wanted, 0, piece.shape[0] - 1), axis=0)
    fetched = jnp.where(inside[:, None], taken, empty)
    own_slots = wanted.shape[0] // groups
    partial_value = jnp.dot(fetched, w_kv, preferred_element_type=jnp.float32)
    summed = lax.psum_scatter(
        partial_value.astype(jnp.bfloat16), "fsdp", scatter_dimension=0, tiled=True
    )
    width = queries.shape[1]
    tokens = queries.shape[0]
    query_heads = queries.reshape(tokens, HEADS, HEAD)
    cotangent_heads = grad_out.reshape(tokens, HEADS, HEAD)
    key_heads = summed[:, :width].reshape(own_slots, HEADS, HEAD)
    value_heads = summed[:, width:].reshape(own_slots, HEADS, HEAD)
    positions = jnp.arange(tokens, dtype=jnp.int32)
    sample_ends = jnp.cumsum(image_counts[0])
    token_sample = jnp.sum(
        (positions[:, None] >= sample_ends[None, : SAMPLES - 1]).astype(jnp.int32), axis=1
    )
    slot_sample = jnp.arange(own_slots, dtype=jnp.int32) // LMAX
    slot_open = lax.dynamic_slice_in_dim(live_slot, member * own_slots, own_slots)
    allowed = (token_sample[:, None] == slot_sample[None, :]) & slot_open[None, :]
    scores = (
        jnp.einsum("the,she->hts", query_heads, key_heads, preferred_element_type=jnp.float32)
        * attn_scale
    )
    scores = jnp.where(allowed[None], scores, jnp.float32(-1e30))
    row_top = jnp.max(scores, axis=-1, keepdims=True)
    expon = jnp.exp(scores - row_top)
    probabilities = expon / jnp.sum(expon, axis=-1, keepdims=True)
    prob_grads = jnp.einsum(
        "the,she->hts", cotangent_heads, value_heads, preferred_element_type=jnp.float32
    )
    centre = jnp.sum(probabilities * prob_grads, axis=-1, keepdims=True)
    score_grads = (probabilities * (prob_grads - centre)).astype(jnp.bfloat16)
    probs_rounded = probabilities.astype(jnp.bfloat16)
    grad_query = (
        jnp.einsum("hts,she->the", score_grads, key_heads, preferred_element_type=jnp.float32)
        * attn_scale
    ).astype(jnp.bfloat16)
    grad_key = (
        jnp.einsum("hts,the->she", score_grads, query_heads, preferred_element_type=jnp.float32)
        * attn_scale
    )
    grad_value = jnp.einsum(
        "hts,the->she", probs_rounded, cotangent_heads, preferred_element_type=jnp.float32
    )
    grad_slots = jnp.concatenate(
        [grad_key.reshape(own_slots, width), grad_value.reshape(own_slots, width)], axis=1
    ).astype(jnp.bfloat16)
    every_slot = lax.all_gather(grad_slots, "fsdp", axis=0, tiled=True)
    grad_weight = jnp.einsum("sc,se->ce", fetched, every_slot, preferred_element_type=jnp.float32)
    return (grad_query.reshape(tokens, width), grad_weight.astype(jnp.bfloat16)[None])


def solution(mesh):
    in_specs = (
        P(("dp", "fsdp"), None),
        P(("dp", "fsdp"), None),
        P("dp", "fsdp"),
        P("fsdp", None),
        P(("dp", "fsdp"), None),
        P("dp", None),
        P("dp", None),
        P("dp", None),
    )
    out_specs = (P(("dp", "fsdp"), None), P("dp", "fsdp", None))
    return jax.shard_map(shards, mesh=mesh, in_specs=in_specs, out_specs=out_specs, check_vma=False)
```

profile of v0, /device:TPU:0, one launch (start us, length us, event | category | flops | bytes accessed | tf_op | source)
XLA Modules:
  0.0 116.6 jit_solution(5877228680347144851)
XLA Ops:
  7.2 0.0 reduce-scatter.2.cloned.1.call-start
  7.2 0.7 add_bitcast_fusion
  7.9 0.1 fusion.18
  8.0 0.1 fusion.16
  8.0 0.1 min.18
  8.1 0.1 min.16
  8.2 0.7 iota_compare_fusion
  8.9 0.1 lt.66
  9.0 0.1 ge.44
  9.1 0.1 lt.70
  9.2 11.6 %all_gather.6 = bf16[256,1024]{1,0:T(8,128)(2,1)S(1)} all-gather(bf16[32,1024]{1,0:T(8,128)(2,1)} %param.10), channel_id=1, replica_groups=mesh['dp'=8,'fsdp'=4] {'dp'}, dimensions={0}, use_global_device_ids=true | all-gather | bytes 589824 | tf_op jit(solution)/shard_map/all_gather | solution.py:26
  20.8 1.2 %gather_fusion = bf16[256,1024]{1,0:T(8,128)(2,1)S(1)} fusion(bf16[256,1024]{1,0:T(8,128)(2,1)S(1)} %all_gather.6, s32[1024]{0:T(1024)S(1)} %pad_clamp_fusion), kind=kCustom, calls=%fused_computation | custom fusion | bytes 1049600 | tf_op jit(solution)/shard_map/jit(_take)/gather | solution.py:28
  22.0 0.0 copy-start.2
  22.0 0.0 copy-start
  22.0 0.0 copy-start.1
  22.0 5.9 %convolution_convert_fusion = bf16[256,3072]{1,0:T(8,128)(2,1)} fusion(bf16[1024,3072]{1,0:T(8,128)(2,1)} %param.11, bf16[256,1024]{1,0:T(8,128)(2,1)S(1)} %gather_fusion, pred[256]{0:T(512)(128)(4,1)S(1)} %get-tuple-element.14, pred[256]{0:T(512)(128)(4,1)S(1)} %get-tuple-element.15), kind=kOutput, calls=%fused_computation.3 | convolution fusion | flops 1611923456 | bytes 8389120 | tf_op jit(solution)/shard_map/dot_general | solution.py:31
  27.9 0.0 reduce-scatter.2.cloned.1.call-update
  27.9 0.0 all-gather.2.cloned.1.call-start
  28.0 0.0 copy-done.2
  28.0 0.2 reduce-window.4
  28.1 0.1 dynamic_slice.3
  28.2 0.0 copy-done
  28.2 0.2 copy.18
  28.5 0.0 copy-done.1
  28.5 0.2 copy.21
  28.7 0.1 compare_and_fusion
  28.8 34.8 %reduce-scatter.2.cloned.1.call-done = bf16[64,3072]{1,0:T(8,128)(2,1)} async-done(((bf16[256,3072]{1,0:T(8,128)(2,1)}), bf16[64,3072]{1,0:T(8,128)(2,1)}) %reduce-scatter.2.cloned.1.call-update) | async-done | bytes 393232 | tf_op jit(solution)/shard_map/reduce_scatter | solution.py:32
  63.7 1.0 slice_bitcast_fusion.1
  64.7 0.2 fusion.5
  65.0 0.5 fusion.19
  65.5 0.4 fusion.8
  65.9 0.3 multiply_reduce_fusion
  66.1 0.1 multiply_convert_fusion
  66.2 0.4 fusion.7
  66.7 0.8 pad_maximum_fusion
  67.4 0.0 all-gather.2.cloned.1.call-update
  67.5 0.3 fusion.1
  67.8 0.9 copy.29
  68.7 35.0 %all-gather.2.cloned.1.call-done = bf16[256,3072]{1,0:T(8,128)(2,1)} async-done(((bf16[64,3072]{1,0:T(8,128)(2,1)}), bf16[256,3072]{1,0:T(8,128)(2,1)}) %all-gather.2.cloned.1.call-update) | async-done | bytes 1572880 | tf_op jit(solution)/shard_map/all_gather | solution.py:77
  103.7 6.1 %convert_bitcast_fusion = bf16[1,1024,3072]{2,1,0:T(8,128)(2,1)} fusion(bf16[256,3072]{1,0:T(8,128)(2,1)} %all-gather.2.cloned.1.call-done, bf16[256,1024]{1,0:T(8,128)(2,1)S(1)} %gather_fusion, pred[256]{0:T(512)(128)(4,1)S(1)} %get-tuple-element.14, pred[256]{0:T(512)(128)(4,1)S(1)} %get-tuple-element.15), kind=kOutput, calls=%fused_computation.2 | convolution fusion | flops 1614282752 | bytes 8389120 | tf_op jit(solution)/shard_map/sc,se->ce/dot_general | solution.py:78
  (7 shorter events, 0.1 us)
Async XLA Ops:
  7.2 56.5 %reduce-scatter.2.cloned.1.call-start = ((), (), s32[]{:S(2)}) async-start(), calls=%async_computation.1 | async-start | bytes 1966080 | tf_op jit(solution)/shard_map/reduce_scatter | solution.py:32
  22.0 6.0 %copy-start.2 = (s32[1,2]{1,0:T(1,128)S(1)}, s32[1,2]{1,0:T(1,128)}, u32[]{:S(2)}) copy-start(s32[1,2]{1,0:T(1,128)} %param.12) | copy-start | bytes 28
  22.0 6.2 %copy-start = (bf16[128,1536]{1,0:T(8,128)(2,1)S(1)}, bf16[128,1536]{1,0:T(8,128)(2,1)}, u32[]{:S(2)}) copy-start(bf16[128,1536]{1,0:T(8,128)(2,1)} %param.8) | copy-start | bytes 1179652
  22.0 6.4 %copy-start.1 = (bf16[128,1536]{1,0:T(8,128)(2,1)S(1)}, bf16[128,1536]{1,0:T(8,128)(2,1)}, u32[]{:S(2)}) copy-start(bf16[128,1536]{1,0:T(8,128)(2,1)} %param.9) | copy-start | bytes 1179652
  27.9 75.8 %all-gather.2.cloned.1.call-start = ((), (), s32[]{:S(2)}) async-start(), calls=%async_computation.2 | async-start | bytes 1966080 | tf_op jit(solution)/shard_map/all_gather | solution.py:77
Sparse Core Ops, SparseCore 0:
  28.0 35.5 reduce-scatter.1
  67.6 36.0 all-gather.1
where the time goes:
time: 117 us
  waiting for transfers between devices  69.8 us (60%)
  between operations  14.2 us (12%)
  matrix products  13.5 us (12%)
  blocking collectives  11.6 us (10%)
  local copies, waits for them, and re-layouts  4.17 us (4%)
  other arithmetic  3.24 us (3%)
    all_gather x1, waiting for transfers between devices, shards(): every_slot = lax.all_gather(grad_slots, 'fsdp', axis=0, tiled=True)  35 us
    reduce_scatter x1, waiting for transfers between devices, shards(): lax.psum_scatter(partial_value.astype(jnp.bfloat16), 'fsdp', scatter_dime...  34.8 us
    all_gather x1, blocking collectives, shards(): piece = lax.all_gather(text_cache, 'dp', axis=0, tiled=True)  11.6 us
    dot_general x1, matrix products, shards(): jnp.einsum('sc,se->ce', fetched, every_slot, preferred_element_type=jnp.f...  6.08 us
    dot_general x1, matrix products, shards(): partial_value = jnp.dot(fetched, w_kv, preferred_element_type=jnp.float32)  5.86 us
    unnamed x10, local copies, waits for them, and re-layouts  2.44 us
  transfers between devices with their start and end apart: 2, of which 2 were waited for; matrix products, arithmetic and copies ran while one was open for 2% of the time, Pallas kernels for 0%

commit v1 on v0

v1 whole, which is shorter than its diff:
```python
import functools

import jax
import jax.numpy as jnp
from jax import lax
from jax.experimental import pallas as pl
from jax.experimental.pallas import tpu as pltpu
from jax.sharding import PartitionSpec as P

HEADS = 12
HEAD = 128
LMAX = 32
SAMPLES = 2
VMEM = 48 * 1024 * 1024

F32 = jnp.float32
BF16 = jnp.bfloat16


def power_of_two(n):
    return n & (n - 1) == 0


def kernel_params(**more):
    return pltpu.CompilerParams(vmem_limit_bytes=VMEM, **more)


SMEM_SPEC = pl.BlockSpec(memory_space=pltpu.SMEM)
VMEM_SPEC = pl.BlockSpec(memory_space=pltpu.VMEM)


def scalar_table(image_counts, caption_lens, caption_owner, caption_offset):
    captions = caption_lens.shape[1]
    place = jnp.stack([lax.axis_index("dp"), lax.axis_index("fsdp"), image_counts[0, 0]]).astype(jnp.int32)
    place = jnp.pad(place, (0, captions - place.shape[0]))
    return jnp.concatenate([caption_lens, caption_owner, caption_offset, place[None]], axis=0)


def peer(index, k, paired):
    return index ^ k if paired else k


def first_of_class(offset, residue, groups):
    return lax.div(offset - residue + groups - 1, jnp.int32(groups))


def spread_rows(values, rows_each, shape):
    rows = lax.broadcasted_iota(jnp.int32, shape, 0)
    result = jnp.zeros(shape, jnp.int32)
    for g, value in enumerate(values):
        result = jnp.where((rows >= g * rows_each) & (rows < (g + 1) * rows_each), value + rows - g * rows_each, result)
    return result


def project_kernel(groups, paired, table, cache, weight, *outs):
    depth = cache.shape[0]
    each = depth // groups
    member = table[3, 1]
    rows = lax.broadcasted_iota(jnp.int32, (depth, depth), 0)
    columns = lax.broadcasted_iota(jnp.int32, (depth, depth), 1)
    wanted = jnp.zeros((depth, depth), jnp.int32)
    for k in range(groups):
        wanted = jnp.where(rows // each == k, groups * (rows - k * each) + peer(member, k, paired), wanted)
    order = (wanted == columns).astype(BF16)
    sorted_rows = jnp.dot(order, cache[...], preferred_element_type=F32).astype(BF16)
    product = jnp.dot(sorted_rows, weight[...], preferred_element_type=F32)
    for k in range(groups):
        outs[k][...] = product[k * each : (k + 1) * each].astype(BF16)


def project(groups, paired, table, text_cache, w_kv):
    depth, features = text_cache.shape
    width = w_kv.shape[1]
    block = 512
    each = depth // groups
    return pl.pallas_call(
        functools.partial(project_kernel, groups, paired),
        grid=(width // block,),
        in_specs=[
            SMEM_SPEC,
            pl.BlockSpec((depth, features), lambda n: (0, 0)),
            pl.BlockSpec((features, block), lambda n: (0, n)),
        ],
        out_specs=[pl.BlockSpec((each, block), lambda n: (0, n))] * groups,
        out_shape=[jax.ShapeDtypeStruct((each, width), BF16)] * groups,
        compiler_params=kernel_params(),
        name="project",
    )(table, text_cache, w_kv)


def select_kernel(groups, each, paired, dp_paired, table, *refs):
    pieces, outs = refs[:-groups], refs[-groups:]
    held = jnp.concatenate([piece[...] for piece in pieces], axis=0) if len(pieces) > 1 else pieces[0][...]
    total = held.shape[0]
    index, member = table[3, 0], table[3, 1]
    wanted_rows = groups * SAMPLES * each
    starts, firsts = [], []
    for k in range(groups):
        for s in range(SAMPLES):
            caption = peer(member, k, paired) * SAMPLES + s
            first = first_of_class(table[2, caption], member, groups)
            owner = table[1, caption]
            firsts.append(first)
            starts.append((owner ^ index if dp_paired else owner) * each + first)
    shape = (wanted_rows, total)
    target = spread_rows(starts, each, shape)
    inside = spread_rows(firsts, each, shape) < each
    chosen = ((target == lax.broadcasted_iota(jnp.int32, shape, 1)) & inside).astype(BF16)
    rows = jnp.dot(chosen, held, preferred_element_type=F32).astype(BF16)
    size = SAMPLES * each
    for k in range(groups):
        outs[k][...] = rows[k * size : (k + 1) * size]


def select_rows(groups, each, paired, dp_paired, table, pieces):
    width = pieces[0].shape[1]
    return pl.pallas_call(
        functools.partial(select_kernel, groups, each, paired, dp_paired),
        in_specs=[SMEM_SPEC] + [VMEM_SPEC] * len(pieces),
        out_specs=[VMEM_SPEC] * groups,
        out_shape=[jax.ShapeDtypeStruct((SAMPLES * each, width), BF16)] * groups,
        compiler_params=kernel_params(),
        name="select_rows",
    )(table, *pieces)


def attention_kernel(groups, each, paired, table, queries, cotangent, *refs):
    pieces, (grad_query, grad_slots) = refs[:groups], refs[groups:]
    tokens, width = queries.shape
    slots = groups * SAMPLES * each
    scale = HEAD ** (-0.5)
    member = table[3, 1]
    split = table[3, 2]
    shape = (slots, tokens)
    rows = lax.broadcasted_iota(jnp.int32, shape, 0)
    position = jnp.zeros(shape, jnp.int32)
    length = jnp.zeros(shape, jnp.int32)
    sample = jnp.zeros(shape, jnp.int32)
    for c in range(groups):
        residue = peer(member, c, paired)
        for s in range(SAMPLES):
            caption = member * SAMPLES + s
            run = (c * SAMPLES + s) * each
            here = (rows >= run) & (rows < run + each)
            first = first_of_class(table[2, caption], residue, groups)
            position = jnp.where(here, groups * (first + rows - run) + residue - table[2, caption], position)
            length = jnp.where(here, table[0, caption], length)
            sample = jnp.where(here, s, sample)
    token_sample = (lax.broadcasted_iota(jnp.int32, shape, 1) >= split).astype(jnp.int32)
    allowed = (position < length) & (sample == token_sample)
    last = (((1,), (1,)), ((), ()))
    first_dims = (((0,), (0,)), ((), ()))
    for h in range(width // HEAD):
        at = slice(h * HEAD, (h + 1) * HEAD)
        values_at = slice(width + h * HEAD, width + (h + 1) * HEAD)
        q, g = queries[:, at], cotangent[:, at]
        k = jnp.concatenate([piece[:, at] for piece in pieces], axis=0)
        v = jnp.concatenate([piece[:, values_at] for piece in pieces], axis=0)
        scores = lax.dot_general(k, q, last, preferred_element_type=F32) * scale
        scores = jnp.where(allowed, scores, F32(-1e30))
        expon = jnp.exp(scores - jnp.max(scores, axis=0, keepdims=True))
        probs = expon / jnp.sum(expon, axis=0, keepdims=True)
        prob_grads = lax.dot_general(v, g, last, preferred_element_type=F32)
        centre = jnp.sum(probs * prob_grads, axis=0, keepdims=True)
        score_grads = (probs * (prob_grads - centre)).astype(BF16)
        grad_query[:, at] = (lax.dot_general(score_grads, k, first_dims, preferred_element_type=F32) * scale).astype(BF16)
        grad_slots[:, at] = (jnp.dot(score_grads, q, preferred_element_type=F32) * scale).astype(BF16)
        grad_slots[:, values_at] = jnp.dot(probs.astype(BF16), g, preferred_element_type=F32).astype(BF16)


def attention(groups, each, paired, table, queries, grad_out, pieces):
    tokens, width = queries.shape
    slots = groups * SAMPLES * each
    return pl.pallas_call(
        functools.partial(attention_kernel, groups, each, paired),
        in_specs=[SMEM_SPEC] + [VMEM_SPEC] * (2 + groups),
        out_specs=[VMEM_SPEC] * 2,
        out_shape=[
            jax.ShapeDtypeStruct((tokens, width), BF16),
            jax.ShapeDtypeStruct((slots, 2 * width), BF16),
        ],
        compiler_params=kernel_params(),
        name="attention_backward",
    )(table, queries, grad_out, *pieces)


def weight_kernel(groups, each, depth, paired, dp_paired, order, n_text, n_grads, table, *refs):
    texts, grads = refs[:n_text], refs[n_text : n_text + n_grads]
    out, chosen_text = refs[n_text + n_grads :]
    index, member = table[3, 0], table[3, 1]

    @pl.when(pl.program_id(0) == 0)
    def _():
        held = jnp.concatenate([text[...] for text in texts], axis=0) if n_text > 1 else texts[0][...]
        bases, limits = [], []
        for k in range(groups):
            device = peer(member, k, paired)
            for c in range(groups):
                residue = peer(device, c, paired)
                for s in range(SAMPLES):
                    caption = device * SAMPLES + s
                    first = first_of_class(table[2, caption], residue, groups)
                    owner = table[1, caption]
                    base = (owner ^ index if dp_paired else owner) * depth
                    bases.append((base + groups * first + residue, base + table[2, caption] + table[0, caption]))
        shape = (held.shape[0], groups * groups * SAMPLES * each)
        columns = lax.broadcasted_iota(jnp.int32, shape, 1)
        runs, place = columns // each, columns % each
        target = jnp.zeros(shape, jnp.int32)
        limit = jnp.zeros(shape, jnp.int32)
        for g, (base, end) in enumerate(bases):
            target = jnp.where(runs == g, base, target)
            limit = jnp.where(runs == g, end, limit)
        target = target + groups * place
        chosen = ((target == lax.broadcasted_iota(jnp.int32, shape, 0)) & (target < limit)).astype(BF16)
        first_dims = (((0,), (0,)), ((), ()))
        chosen_text[...] = lax.dot_general(held, chosen, first_dims, preferred_element_type=F32).astype(BF16)

    if order == "chain":
        near, inner1, inner2, outer1, outer2, own = [g[...] for g in grads]
        inner = (member == 1) | (member == 2)
        pieces = [own, near, jnp.where(inner, inner2, outer1), jnp.where(inner, inner1, outer2)]
        every = jnp.concatenate(pieces, axis=0)
    else:
        every = grads[0][...]
    out[...] = jnp.dot(chosen_text[...], every, preferred_element_type=F32).astype(BF16)


def weight_grad(groups, each, depth, paired, dp_paired, order, table, texts, grads):
    features = texts[0].shape[1]
    slots, width = grads[0].shape
    total = groups * groups * SAMPLES * each
    block = 512
    return pl.pallas_call(
        functools.partial(weight_kernel, groups, each, depth, paired, dp_paired, order, len(texts), len(grads)),
        grid=(width // block,),
        in_specs=[SMEM_SPEC]
        + [pl.BlockSpec(t.shape, lambda n: (0, 0)) for t in texts]
        + [pl.BlockSpec((g.shape[0], block), lambda n: (0, n)) for g in grads],
        out_specs=pl.BlockSpec((features, block), lambda n: (0, n)),
        out_shape=jax.ShapeDtypeStruct((features, width), BF16),
        scratch_shapes=[pltpu.VMEM((features, total), BF16)],
        compiler_params=kernel_params(),
        name="weight_gradient",
    )(table, *texts, *grads)


def swap(x, axis, k):
    return lax.ppermute(x, axis, [(i, i ^ k) for i in range(lax.axis_size(axis))])


def gather_dp(x, paired):
    if not paired:
        return [lax.all_gather(x, "dp", axis=0, tiled=True)]
    near = {0: x}
    for k in range(2, lax.axis_size("dp"), 2):
        near[k] = swap(x, "dp", k)
    for k in list(near):
        near[k + 1] = swap(near[k], "dp", 1)
    return [near[k] for k in sorted(near)]


def exchange(pieces, paired):
    if paired:
        return [pieces[0]] + [swap(pieces[k], "fsdp", k) for k in range(1, len(pieces))]
    came = lax.all_to_all(jnp.stack(pieces), "fsdp", 0, 0, tiled=True)
    return [came[k] for k in range(len(pieces))]


def gather_line(x):
    near_pairs = [(0, 1), (1, 0), (2, 3), (3, 2)]
    middle_pairs = [(1, 2), (2, 1)]
    outward = [(1, 0), (2, 3)]
    near = lax.ppermute(x, "fsdp", near_pairs)
    inner1 = lax.ppermute(x, "fsdp", middle_pairs)
    inner2 = lax.ppermute(near, "fsdp", middle_pairs)
    outer1 = lax.ppermute(inner1, "fsdp", outward)
    outer2 = lax.ppermute(inner2, "fsdp", outward)
    return [near, inner1, inner2, outer1, outer2, x]


def shards(
    queries, grad_out, text_cache, w_kv, image_counts, caption_lens, caption_owner, caption_offset
):
    groups = lax.axis_size("fsdp")
    line = groups == 4
    paired = line
    dp_paired = power_of_two(lax.axis_size("dp")) and lax.axis_size("dp") <= 8
    depth = text_cache.shape[0]
    each = depth // groups
    table = scalar_table(image_counts, caption_lens, caption_owner, caption_offset)

    partials = project(groups, paired, table, text_cache, w_kv)
    came = exchange(partials, paired)
    rows = sum(piece.astype(F32) for piece in came).astype(BF16)
    class_rows = gather_dp(rows, dp_paired)
    outgoing = select_rows(groups, each, paired, dp_paired, table, class_rows)
    keys_values = exchange(outgoing, paired)
    grad_query, grad_slots = attention(groups, each, paired, table, queries, grad_out, keys_values)
    grad_slots, late_cache = lax.optimization_barrier((grad_slots, text_cache))
    texts = gather_dp(late_cache, dp_paired)
    if line:
        grads = gather_line(grad_slots)
    else:
        grads = [lax.all_gather(grad_slots, "fsdp", axis=0, tiled=True)]
    grad_weight = weight_grad(
        groups, each, depth, paired, dp_paired, "chain" if line else "whole", table, texts, grads
    )
    return grad_query, grad_weight[None]


def solution(mesh):
    in_specs = (
        P(("dp", "fsdp"), None),
        P(("dp", "fsdp"), None),
        P("dp", "fsdp"),
        P("fsdp", None),
        P(("dp", "fsdp"), None),
        P("dp", None),
        P("dp", None),
        P("dp", None),
    )
    out_specs = (P(("dp", "fsdp"), None), P("dp", "fsdp", None))
    return jax.shard_map(shards, mesh=mesh, in_specs=in_specs, out_specs=out_specs, check_vma=False)
```

time: 117 us -> 82.3 us (0.70)
  waiting for transfers between devices: 69.8 us -> 38.8 us
  starting transfers between devices: 0.08 us -> 23.5 us
  Pallas kernels: 0 us -> 16.5 us
  matrix products: 13.5 us -> 0 us
  between operations: 14.2 us -> 0.76 us
  blocking collectives: 11.6 us -> 0 us
  local copies, waits for them, and re-layouts: 4.17 us -> 0.85 us
  other arithmetic: 3.24 us -> 1.52 us
    ppermute x0 -> x25, waiting for transfers between devices: none -> 38.8 us  [the longest x20 20.9 us: swap(): lax.ppermute(x, axis, [(i, i ^ k) for i in range(lax.axis_size(axis))])]
    all_gather x1 -> x0, waiting for transfers between devices: 35 us -> none  [shards(): every_slot = lax.all_gather(grad_slots, 'fsdp', axis=0, tiled=True)]
    reduce_scatter x1 -> x0, waiting for transfers between devices: 34.8 us -> none  [shards(): lax.psum_scatter(partial_value.astype(jnp.bfloat16), 'fsdp', scatter_dime...]
    ppermute x0 -> x25, starting transfers between devices: none -> 23.5 us  [the longest x20 17.7 us: swap(): lax.ppermute(x, axis, [(i, i ^ k) for i in range(lax.axis_size(axis))])]
    pallas_call x0 -> x4, Pallas kernels: none -> 16.5 us  [the longest x1 5.9 us: weight_grad(): pl.pallas_call(functools.partial(weight_kernel, groups, each, depth, pair...]
    dot_general x7 -> x0, matrix products: 13.5 us -> none  [the longest x1 6.08 us: shards(): jnp.einsum('sc,se->ce', fetched, every_slot, preferred_element_type=jnp.f...]
    all_gather x1 -> x0, blocking collectives: 11.6 us -> none  [shards(): piece = lax.all_gather(text_cache, 'dp', axis=0, tiled=True)]
    unnamed x10 -> x8, local copies, waits for them, and re-layouts: 2.44 us -> 0.85 us
  transfers between devices with their start and end apart: 2 -> 25, of which waited for: 2 -> 18; matrix products, arithmetic and copies ran while one was open for 2% -> 0% of each run, Pallas kernels for 0% -> 0%
where the time goes in v1:
time: 82.3 us; the launch traced here: 81.9 us
  waiting for transfers between devices  38.8 us (47%)
  starting transfers between devices  23.5 us (29%)
  Pallas kernels  16.5 us (20%)
  other arithmetic  1.52 us (2%)
  local copies, waits for them, and re-layouts  0.85 us (1%)
    ppermute x20, waiting for transfers between devices, swap(): lax.ppermute(x, axis, [(i, i ^ k) for i in range(lax.axis_size(axis))])  20.9 us
    ppermute x20, starting transfers between devices, swap(): lax.ppermute(x, axis, [(i, i ^ k) for i in range(lax.axis_size(axis))])  17.7 us
    ppermute x1, waiting for transfers between devices, gather_line(): outer2 = lax.ppermute(inner2, 'fsdp', outward)  8.45 us
    ppermute x1, waiting for transfers between devices, gather_line(): near = lax.ppermute(x, 'fsdp', near_pairs)  7.92 us
    pallas_call x1, Pallas kernels, weight_grad(): pl.pallas_call(functools.partial(weight_kernel, groups, each, depth, pair...  5.9 us
    pallas_call x1, Pallas kernels, project(): pl.pallas_call(functools.partial(project_kernel, groups, paired), grid=(w...  5.41 us
    pallas_call x1, Pallas kernels, attention(): pl.pallas_call(functools.partial(attention_kernel, groups, each, paired),...  4.39 us
    ppermute x1, starting transfers between devices, gather_line(): near = lax.ppermute(x, 'fsdp', near_pairs)  1.87 us
  transfers between devices with their start and end apart: 25, of which 18 were waited for; matrix products, arithmetic and copies ran while one was open for 0% of the time, Pallas kernels for 0%

profile of v1, /device:TPU:0, one launch (start us, length us, event | category | flops | bytes accessed | tf_op | source)
XLA Modules:
  0.0 81.9 jit_solution(6165429689161019157)
XLA Ops:
  0.6 0.0 copy-start.1
  0.6 0.0 copy-start
  0.7 0.8 pad_add_fusion.1
  1.5 0.7 pad_add_fusion.table
  2.2 0.0 copy-start.2
  2.2 0.8 %copy-done.2 = bf16[32,1024]{1,0:T(8,128)(2,1)S(1)} copy-done((bf16[32,1024]{1,0:T(8,128)(2,1)S(1)}, bf16[32,1024]{1,0:T(8,128)(2,1)}, u32[]{:S(2)}) %copy-start.2) | copy-done | bytes 65560
  3.0 0.0 copy-start.3
  3.0 5.4 %project.1 = (bf16[8,3072]{1,0:T(8,128)(2,1)S(1)}, bf16[8,3072]{1,0:T(8,128)(2,1)S(1)}, bf16[8,3072]{1,0:T(8,128)(2,1)S(1)}, bf16[8,3072]{1,0:T(8,128)(2,1)S(1)}) custom-call(s32[4,8]{1,0:T(4,128)S(1)} %pad_add_fusion.table, bf16[32,1024]{1,0:T(8,128)(2,1)S(1)} %copy-done.2, bf16[1024,3072]{1,0:T(8,128)(2,1)} %weight.1), custom_call_target="tpu_custom_call" | custom-call | tf_op jit(solution)/shard_map/project/pallas_call | solution.py:76
  8.4 3.0 %collective-permute-start = (bf16[8,3072]{1,0:T(8,128)(2,1)S(1)}, bf16[8,3072]{1,0:T(8,128)(2,1)S(1)}, u32[]{:S(2)}, u32[]{:S(2)}) collective-permute-start(bf16[8,3072]{1,0:T(8,128)(2,1)S(1)} %get-tuple-element.15), channel_id=1, source_target_pairs={{0,1},{1,0},{2,3},{3,2},{4,5},{5,4},{6,7},{7,6},{8,9},{9,8},{10,11... | collective-permute-start | bytes 147464 | tf_op jit(solution)/shard_map/ppermute | solution.py:249
  11.4 2.6 %collective-permute-start.1 = (bf16[8,3072]{1,0:T(8,128)(2,1)S(1)}, bf16[8,3072]{1,0:T(8,128)(2,1)S(1)}, u32[]{:S(2)}, u32[]{:S(2)}) collective-permute-start(bf16[8,3072]{1,0:T(8,128)(2,1)S(1)} %get-tuple-element.16), channel_id=1, source_target_pairs={{0,2},{1,3},{2,0},{3,1},{4,6},{5,7},{6,4},{7,5},{8,10},{9,11},{10,... | collective-permute-start | bytes 147464 | tf_op jit(solution)/shard_map/ppermute | solution.py:249
  14.0 0.0 collective-permute-start.2
  14.0 0.0 collective-permute-done
  14.0 3.3 %collective-permute-done.1 = bf16[8,3072]{1,0:T(8,128)(2,1)S(1)} collective-permute-done((bf16[8,3072]{1,0:T(8,128)(2,1)S(1)}, bf16[8,3072]{1,0:T(8,128)(2,1)S(1)}, u32[]{:S(2)}, u32[]{:S(2)}) %collective-permute-start.1) | collective-permute-done | bytes 49184 | tf_op jit(solution)/shard_map/ppermute | solution.py:249
  17.4 2.6 %collective-permute-done.2 = bf16[8,3072]{1,0:T(8,128)(2,1)S(1)} collective-permute-done((bf16[8,3072]{1,0:T(8,128)(2,1)S(1)}, bf16[8,3072]{1,0:T(8,128)(2,1)S(1)}, u32[]{:S(2)}, u32[]{:S(2)}) %collective-permute-start.2) | collective-permute-done | bytes 49184 | tf_op jit(solution)/shard_map/ppermute | solution.py:249
  20.0 2.5 %collective-permute-start.8 = (bf16[8,3072]{1,0:T(8,128)(2,1)S(1)}, bf16[8,3072]{1,0:T(8,128)(2,1)S(1)}, u32[]{:S(2)}, u32[]{:S(2)}) collective-permute-start(bf16[8,3072]{1,0:T(8,128)(2,1)S(1)} %add_convert_fusion.refs_0_), channel_id=1, source_target_pairs={{0,24},{4,28},{8,16},{12,20},{16,8},{20,12},{24,0},{28,4},{1,25},{... | collective-permute-start | bytes 147464 | tf_op jit(solution)/shard_map/ppermute | solution.py:249
  22.5 0.5 collective-permute-start.6
  23.0 0.5 collective-permute-start.4
  23.5 0.0 collective-permute-start.3
  23.5 1.7 %collective-permute-done.8.refs_6_ = bf16[8,3072]{1,0:T(8,128)(2,1)S(1)} collective-permute-done((bf16[8,3072]{1,0:T(8,128)(2,1)S(1)}, bf16[8,3072]{1,0:T(8,128)(2,1)S(1)}, u32[]{:S(2)}, u32[]{:S(2)}) %collective-permute-start.8) | collective-permute-done | bytes 49184 | tf_op jit(solution)/shard_map/ppermute | solution.py:249
  25.2 0.0 collective-permute-start.9
  25.3 1.3 %collective-permute-done.6.refs_4_ = bf16[8,3072]{1,0:T(8,128)(2,1)S(1)} collective-permute-done((bf16[8,3072]{1,0:T(8,128)(2,1)S(1)}, bf16[8,3072]{1,0:T(8,128)(2,1)S(1)}, u32[]{:S(2)}, u32[]{:S(2)}) %collective-permute-start.6) | collective-permute-done | bytes 49184 | tf_op jit(solution)/shard_map/ppermute | solution.py:249
  26.6 0.0 collective-permute-start.7
  26.6 0.5 collective-permute-done.4.refs_2_
  27.1 0.0 collective-permute-start.5
  27.1 0.0 collective-permute-done.3.refs_1_
  27.1 0.0 collective-permute-done.9.refs_7_
  27.1 0.7 collective-permute-done.7.refs_5_
  27.8 0.5 collective-permute-done.5.refs_3_
  28.3 0.8 %select_rows.1 = (bf16[16,3072]{1,0:T(8,128)(2,1)S(1)}, bf16[16,3072]{1,0:T(8,128)(2,1)S(1)}, bf16[16,3072]{1,0:T(8,128)(2,1)S(1)}, bf16[16,3072]{1,0:T(8,128)(2,1)S(1)}) custom-call(s32[4,8]{1,0:T(4,128)S(1)} %pad_add_fusion.table, bf16[8,3072]{1,0:T(8,128)(2,1)S(1)} %add_convert_fusion.refs_0_, bf16[8,3072]{1,0:T(8,128)(2,1)S(1)} %collective-permute-done.3.refs_1_, ...), custom_call_target="tpu_custom_call" | custom-call | tf_op jit(solution)/shard_map/select_rows/pallas_call | solution.py:117
  29.1 0.1 collective-permute-start.10
  29.2 1.3 %collective-permute-start.11 = (bf16[16,3072]{1,0:T(8,128)(2,1)S(1)}, bf16[16,3072]{1,0:T(8,128)(2,1)S(1)}, u32[]{:S(2)}, u32[]{:S(2)}) collective-permute-start(bf16[16,3072]{1,0:T(8,128)(2,1)S(1)} %get-tuple-element.20), channel_id=1, source_target_pairs={{0,2},{1,3},{2,0},{3,1},{4,6},{5,7},{6,4},{7,5},{8,10},{9,11},{10,... | collective-permute-start | bytes 294920 | tf_op jit(solution)/shard_map/ppermute | solution.py:249
  30.5 3.1 %collective-permute-start.12 = (bf16[16,3072]{1,0:T(8,128)(2,1)S(1)}, bf16[16,3072]{1,0:T(8,128)(2,1)S(1)}, u32[]{:S(2)}, u32[]{:S(2)}) collective-permute-start(bf16[16,3072]{1,0:T(8,128)(2,1)S(1)} %get-tuple-element.21), channel_id=1, source_target_pairs={{0,3},{1,2},{2,1},{3,0},{4,7},{5,6},{6,5},{7,4},{8,11},{9,10},{10,... | collective-permute-start | bytes 294920 | tf_op jit(solution)/shard_map/ppermute | solution.py:249
  33.6 1.6 %collective-permute-done.10.refs_1_ = bf16[16,3072]{1,0:T(8,128)(2,1)S(1)} collective-permute-done((bf16[16,3072]{1,0:T(8,128)(2,1)S(1)}, bf16[16,3072]{1,0:T(8,128)(2,1)S(1)}, u32[]{:S(2)}, u32[]{:S(2)}) %collective-permute-start.10) | collective-permute-done | bytes 98336 | tf_op jit(solution)/shard_map/ppermute | solution.py:249
  35.2 4.9 %collective-permute-done.11.refs_2_ = bf16[16,3072]{1,0:T(8,128)(2,1)S(1)} collective-permute-done((bf16[16,3072]{1,0:T(8,128)(2,1)S(1)}, bf16[16,3072]{1,0:T(8,128)(2,1)S(1)}, u32[]{:S(2)}, u32[]{:S(2)}) %collective-permute-start.11) | collective-permute-done | bytes 98336 | tf_op jit(solution)/shard_map/ppermute | solution.py:249
  40.1 0.0 collective-permute-done.12.refs_3_
  40.1 0.0 copy-done.1
  40.1 0.0 copy-done
  40.1 4.4 %attention_backward.1 = (bf16[128,1536]{1,0:T(8,128)(2,1)}, bf16[64,3072]{1,0:T(8,128)(2,1)S(1)}) custom-call(s32[4,8]{1,0:T(4,128)S(1)} %pad_add_fusion.table, bf16[128,1536]{1,0:T(8,128)(2,1)S(1)} %copy-done, bf16[128,1536]{1,0:T(8,128)(2,1)S(1)} %copy-done.1, bf16[16,3072]{1,0:T(8,128)(2,1)S(1)} %get-tuple-element.18.refs_0_, ...), custom_call_target="tpu_custom_call" | custom-call | tf_op jit(solution)/shard_map/attention_backward/pallas_call | solution.py:174
  44.5 1.9 %collective-permute-start.20 = (bf16[64,3072]{1,0:T(8,128)(2,1)S(1)}, bf16[64,3072]{1,0:T(8,128)(2,1)S(1)}, u32[]{:S(2)}, u32[]{:S(2)}) collective-permute-start(bf16[64,3072]{1,0:T(8,128)(2,1)S(1)} %get-tuple-element.25.refs_13_), channel_id=1, source_target_pairs={{0,1},{1,0},{2,3},{3,2},{4,5},{5,4},{6,7},{7,6},{8,9},{9,8},{10,11... | collective-permute-start | bytes 1179656 | tf_op jit(solution)/shard_map/ppermute | solution.py:274
  46.4 0.7 collective-permute-start.21
  47.0 7.9 %collective-permute-done.20.refs_8_ = bf16[64,3072]{1,0:T(8,128)(2,1)S(1)} collective-permute-done((bf16[64,3072]{1,0:T(8,128)(2,1)S(1)}, bf16[64,3072]{1,0:T(8,128)(2,1)S(1)}, u32[]{:S(2)}, u32[]{:S(2)}) %collective-permute-start.20) | collective-permute-done | bytes 393248 | tf_op jit(solution)/shard_map/ppermute | solution.py:274
  55.0 0.7 collective-permute-start.22
  55.6 0.0 collective-permute-done.21.refs_9_
  55.7 1.3 %collective-permute-start.23 = (bf16[64,3072]{1,0:T(8,128)(2,1)S(1)}, bf16[64,3072]{1,0:T(8,128)(2,1)S(1)}, u32[]{:S(2)}, u32[]{:S(2)}) collective-permute-start(bf16[64,3072]{1,0:T(8,128)(2,1)S(1)} %collective-permute-done.21.refs_9_), channel_id=1, source_target_pairs={{1,0},{2,3},{5,4},{6,7},{9,8},{10,11},{13,12},{14,15},{17,16},{18,... | collective-permute-start | bytes 1179656 | tf_op jit(solution)/shard_map/ppermute | solution.py:277
  57.0 0.0 collective-permute-done.22.refs_10_
  57.0 1.3 %collective-permute-start.24 = (bf16[64,3072]{1,0:T(8,128)(2,1)S(1)}, bf16[64,3072]{1,0:T(8,128)(2,1)S(1)}, u32[]{:S(2)}, u32[]{:S(2)}) collective-permute-start(bf16[64,3072]{1,0:T(8,128)(2,1)S(1)} %collective-permute-done.22.refs_10_), channel_id=1, source_target_pairs={{1,0},{2,3},{5,4},{6,7},{9,8},{10,11},{13,12},{14,15},{17,16},{18,... | collective-permute-start | bytes 1179656 | tf_op jit(solution)/shard_map/ppermute | solution.py:278
  58.3 0.0 copy-done.3
  58.3 1.6 %collective-permute-start.18 = (bf16[32,1024]{1,0:T(8,128)(2,1)S(1)}, bf16[32,1024]{1,0:T(8,128)(2,1)S(1)}, u32[]{:S(2)}, u32[]{:S(2)}) collective-permute-start(bf16[32,1024]{1,0:T(8,128)(2,1)S(1)} %copy-done.3), channel_id=1, source_target_pairs={{0,24},{4,28},{8,16},{12,20},{16,8},{20,12},{24,0},{28,4},{1,25},{... | collective-permute-start | bytes 196616 | tf_op jit(solution)/shard_map/ppermute | solution.py:249
  59.8 0.5 collective-permute-start.16
  60.3 1.5 %collective-permute-start.14 = (bf16[32,1024]{1,0:T(8,128)(2,1)S(1)}, bf16[32,1024]{1,0:T(8,128)(2,1)S(1)}, u32[]{:S(2)}, u32[]{:S(2)}) collective-permute-start(bf16[32,1024]{1,0:T(8,128)(2,1)S(1)} %copy-done.3), channel_id=1, source_target_pairs={{0,8},{4,12},{8,0},{12,4},{16,24},{20,28},{24,16},{28,20},{1,9},{5... | collective-permute-start | bytes 196616 | tf_op jit(solution)/shard_map/ppermute | solution.py:249
  61.8 1.7 %collective-permute-done.18.refs_6_ = bf16[32,1024]{1,0:T(8,128)(2,1)S(1)} collective-permute-done((bf16[32,1024]{1,0:T(8,128)(2,1)S(1)}, bf16[32,1024]{1,0:T(8,128)(2,1)S(1)}, u32[]{:S(2)}, u32[]{:S(2)}) %collective-permute-start.18) | collective-permute-done | bytes 65568 | tf_op jit(solution)/shard_map/ppermute | solution.py:249
  63.5 0.0 collective-permute-start.13
  63.5 0.7 collective-permute-done.16.refs_4_
  64.2 0.0 collective-permute-start.19
  64.2 0.4 collective-permute-done.14.refs_2_
  64.6 0.1 collective-permute-start.17
  64.7 0.0 collective-permute-done.13.refs_1_
  64.8 0.4 collective-permute-start.15
  65.1 0.3 collective-permute-done.19.refs_7_
  65.5 0.4 collective-permute-done.17.refs_5_
  65.9 0.2 collective-permute-done.15.refs_3_
  66.0 1.6 %collective-permute-done.23.refs_11_ = bf16[64,3072]{1,0:T(8,128)(2,1)S(1)} collective-permute-done((bf16[64,3072]{1,0:T(8,128)(2,1)S(1)}, bf16[64,3072]{1,0:T(8,128)(2,1)S(1)}, u32[]{:S(2)}, u32[]{:S(2)}) %collective-permute-start.23) | collective-permute-done | bytes 393248 | tf_op jit(solution)/shard_map/ppermute | solution.py:277
  67.6 8.4 %collective-permute-done.24.refs_12_ = bf16[64,3072]{1,0:T(8,128)(2,1)S(1)} collective-permute-done((bf16[64,3072]{1,0:T(8,128)(2,1)S(1)}, bf16[64,3072]{1,0:T(8,128)(2,1)S(1)}, u32[]{:S(2)}, u32[]{:S(2)}) %collective-permute-start.24) | collective-permute-done | bytes 393248 | tf_op jit(solution)/shard_map/ppermute | solution.py:278
  76.0 5.9 %weight_gradient.1 = bf16[1024,3072]{1,0:T(8,128)(2,1)} custom-call(s32[4,8]{1,0:T(4,128)S(1)} %pad_add_fusion.table, bf16[32,1024]{1,0:T(8,128)(2,1)S(1)} %copy-done.3, bf16[32,1024]{1,0:T(8,128)(2,1)S(1)} %collective-permute-done.13.refs_1_, bf16[32,1024]{1,0:T(8,128)(2,1)S(1)} %collective-permute-done.14.refs_2_, ...), custom_call_target="tpu_custom_call" | custom-call | tf_op jit(solution)/shard_map/weight_gradient/pallas_call | solution.py:234
  (2 shorter events, 0.0 us)
Async XLA Ops:
  0.6 39.5 %copy-start.1 = (bf16[128,1536]{1,0:T(8,128)(2,1)S(1)}, bf16[128,1536]{1,0:T(8,128)(2,1)}, u32[]{:S(2)}) copy-start(bf16[128,1536]{1,0:T(8,128)(2,1)} %cotangent.1) | copy-start | bytes 1179652
  0.6 39.4 %copy-start = (bf16[128,1536]{1,0:T(8,128)(2,1)S(1)}, bf16[128,1536]{1,0:T(8,128)(2,1)}, u32[]{:S(2)}) copy-start(bf16[128,1536]{1,0:T(8,128)(2,1)} %queries.1) | copy-start | bytes 1179652
  2.2 0.8 %copy-start.2 = (bf16[32,1024]{1,0:T(8,128)(2,1)S(1)}, bf16[32,1024]{1,0:T(8,128)(2,1)}, u32[]{:S(2)}) copy-start(bf16[32,1024]{1,0:T(8,128)(2,1)} %refs_0_) | copy-start | bytes 196612
  3.0 55.3 %copy-start.3 = (bf16[32,1024]{1,0:T(8,128)(2,1)S(1)}, bf16[32,1024]{1,0:T(8,128)(2,1)}, u32[]{:S(2)}) copy-start(bf16[32,1024]{1,0:T(8,128)(2,1)} %refs_0_) | copy-start | bytes 196612
  8.4 5.6 %collective-permute-start = (bf16[8,3072]{1,0:T(8,128)(2,1)S(1)}, bf16[8,3072]{1,0:T(8,128)(2,1)S(1)}, u32[]{:S(2)}, u32[]{:S(2)}) collective-permute-start(bf16[8,3072]{1,0:T(8,128)(2,1)S(1)} %get-tuple-element.15), channel_id=1, source_target_pairs={{0,1},{1,0},{2,3},{3,2},{4,5},{5,4},{6,7},{7,6},{8,9},{9,8},{10,11... | collective-permute-start | bytes 147464 | tf_op jit(solution)/shard_map/ppermute | solution.py:249
  11.4 5.9 %collective-permute-start.1 = (bf16[8,3072]{1,0:T(8,128)(2,1)S(1)}, bf16[8,3072]{1,0:T(8,128)(2,1)S(1)}, u32[]{:S(2)}, u32[]{:S(2)}) collective-permute-start(bf16[8,3072]{1,0:T(8,128)(2,1)S(1)} %get-tuple-element.16), channel_id=1, source_target_pairs={{0,2},{1,3},{2,0},{3,1},{4,6},{5,7},{6,4},{7,5},{8,10},{9,11},{10,... | collective-permute-start | bytes 147464 | tf_op jit(solution)/shard_map/ppermute | solution.py:249
  14.0 5.9 %collective-permute-start.2 = (bf16[8,3072]{1,0:T(8,128)(2,1)S(1)}, bf16[8,3072]{1,0:T(8,128)(2,1)S(1)}, u32[]{:S(2)}, u32[]{:S(2)}) collective-permute-start(bf16[8,3072]{1,0:T(8,128)(2,1)S(1)} %get-tuple-element.17), channel_id=1, source_target_pairs={{0,3},{1,2},{2,1},{3,0},{4,7},{5,6},{6,5},{7,4},{8,11},{9,10},{10,... | collective-permute-start | bytes 147464 | tf_op jit(solution)/shard_map/ppermute | solution.py:249
  20.0 5.3 %collective-permute-start.8 = (bf16[8,3072]{1,0:T(8,128)(2,1)S(1)}, bf16[8,3072]{1,0:T(8,128)(2,1)S(1)}, u32[]{:S(2)}, u32[]{:S(2)}) collective-permute-start(bf16[8,3072]{1,0:T(8,128)(2,1)S(1)} %add_convert_fusion.refs_0_), channel_id=1, source_target_pairs={{0,24},{4,28},{8,16},{12,20},{16,8},{20,12},{24,0},{28,4},{1,25},{... | collective-permute-start | bytes 147464 | tf_op jit(solution)/shard_map/ppermute | solution.py:249
  22.5 4.1 %collective-permute-start.6 = (bf16[8,3072]{1,0:T(8,128)(2,1)S(1)}, bf16[8,3072]{1,0:T(8,128)(2,1)S(1)}, u32[]{:S(2)}, u32[]{:S(2)}) collective-permute-start(bf16[8,3072]{1,0:T(8,128)(2,1)S(1)} %add_convert_fusion.refs_0_), channel_id=1, source_target_pairs={{0,16},{4,20},{8,24},{12,28},{16,0},{20,4},{24,8},{28,12},{1,17},{... | collective-permute-start | bytes 147464 | tf_op jit(solution)/shard_map/ppermute | solution.py:249
  23.0 4.1 %collective-permute-start.4 = (bf16[8,3072]{1,0:T(8,128)(2,1)S(1)}, bf16[8,3072]{1,0:T(8,128)(2,1)S(1)}, u32[]{:S(2)}, u32[]{:S(2)}) collective-permute-start(bf16[8,3072]{1,0:T(8,128)(2,1)S(1)} %add_convert_fusion.refs_0_), channel_id=1, source_target_pairs={{0,8},{4,12},{8,0},{12,4},{16,24},{20,28},{24,16},{28,20},{1,9},{5... | collective-permute-start | bytes 147464 | tf_op jit(solution)/shard_map/ppermute | solution.py:249
  23.5 3.6 %collective-permute-start.3 = (bf16[8,3072]{1,0:T(8,128)(2,1)S(1)}, bf16[8,3072]{1,0:T(8,128)(2,1)S(1)}, u32[]{:S(2)}, u32[]{:S(2)}) collective-permute-start(bf16[8,3072]{1,0:T(8,128)(2,1)S(1)} %add_convert_fusion.refs_0_), channel_id=1, source_target_pairs={{0,4},{4,0},{8,12},{12,8},{16,20},{20,16},{24,28},{28,24},{1,5},{5... | collective-permute-start | bytes 147464 | tf_op jit(solution)/shard_map/ppermute | solution.py:249
  25.2 1.8 %collective-permute-start.9 = (bf16[8,3072]{1,0:T(8,128)(2,1)S(1)}, bf16[8,3072]{1,0:T(8,128)(2,1)S(1)}, u32[]{:S(2)}, u32[]{:S(2)}) collective-permute-start(bf16[8,3072]{1,0:T(8,128)(2,1)S(1)} %collective-permute-done.8.refs_6_), channel_id=1, source_target_pairs={{0,4},{4,0},{8,12},{12,8},{16,20},{20,16},{24,28},{28,24},{1,5},{5... | collective-permute-start | bytes 147464 | tf_op jit(solution)/shard_map/ppermute | solution.py:249
  26.6 1.2 %collective-permute-start.7 = (bf16[8,3072]{1,0:T(8,128)(2,1)S(1)}, bf16[8,3072]{1,0:T(8,128)(2,1)S(1)}, u32[]{:S(2)}, u32[]{:S(2)}) collective-permute-start(bf16[8,3072]{1,0:T(8,128)(2,1)S(1)} %collective-permute-done.6.refs_4_), channel_id=1, source_target_pairs={{0,4},{4,0},{8,12},{12,8},{16,20},{20,16},{24,28},{28,24},{1,5},{5... | collective-permute-start | bytes 147464 | tf_op jit(solution)/shard_map/ppermute | solution.py:249
  27.1 1.2 %collective-permute-start.5 = (bf16[8,3072]{1,0:T(8,128)(2,1)S(1)}, bf16[8,3072]{1,0:T(8,128)(2,1)S(1)}, u32[]{:S(2)}, u32[]{:S(2)}) collective-permute-start(bf16[8,3072]{1,0:T(8,128)(2,1)S(1)} %collective-permute-done.4.refs_2_), channel_id=1, source_target_pairs={{0,4},{4,0},{8,12},{12,8},{16,20},{20,16},{24,28},{28,24},{1,5},{5... | collective-permute-start | bytes 147464 | tf_op jit(solution)/shard_map/ppermute | solution.py:249
  29.1 6.1 %collective-permute-start.10 = (bf16[16,3072]{1,0:T(8,128)(2,1)S(1)}, bf16[16,3072]{1,0:T(8,128)(2,1)S(1)}, u32[]{:S(2)}, u32[]{:S(2)}) collective-permute-start(bf16[16,3072]{1,0:T(8,128)(2,1)S(1)} %get-tuple-element.19), channel_id=1, source_target_pairs={{0,1},{1,0},{2,3},{3,2},{4,5},{5,4},{6,7},{7,6},{8,9},{9,8},{10,11... | collective-permute-start | bytes 294920 | tf_op jit(solution)/shard_map/ppermute | solution.py:249
  29.2 10.9 %collective-permute-start.11 = (bf16[16,3072]{1,0:T(8,128)(2,1)S(1)}, bf16[16,3072]{1,0:T(8,128)(2,1)S(1)}, u32[]{:S(2)}, u32[]{:S(2)}) collective-permute-start(bf16[16,3072]{1,0:T(8,128)(2,1)S(1)} %get-tuple-element.20), channel_id=1, source_target_pairs={{0,2},{1,3},{2,0},{3,1},{4,6},{5,7},{6,4},{7,5},{8,10},{9,11},{10,... | collective-permute-start | bytes 294920 | tf_op jit(solution)/shard_map/ppermute | solution.py:249
  30.5 9.6 %collective-permute-start.12 = (bf16[16,3072]{1,0:T(8,128)(2,1)S(1)}, bf16[16,3072]{1,0:T(8,128)(2,1)S(1)}, u32[]{:S(2)}, u32[]{:S(2)}) collective-permute-start(bf16[16,3072]{1,0:T(8,128)(2,1)S(1)} %get-tuple-element.21), channel_id=1, source_target_pairs={{0,3},{1,2},{2,1},{3,0},{4,7},{5,6},{6,5},{7,4},{8,11},{9,10},{10,... | collective-permute-start | bytes 294920 | tf_op jit(solution)/shard_map/ppermute | solution.py:249
  44.5 10.5 %collective-permute-start.20 = (bf16[64,3072]{1,0:T(8,128)(2,1)S(1)}, bf16[64,3072]{1,0:T(8,128)(2,1)S(1)}, u32[]{:S(2)}, u32[]{:S(2)}) collective-permute-start(bf16[64,3072]{1,0:T(8,128)(2,1)S(1)} %get-tuple-element.25.refs_13_), channel_id=1, source_target_pairs={{0,1},{1,0},{2,3},{3,2},{4,5},{5,4},{6,7},{7,6},{8,9},{9,8},{10,11... | collective-permute-start | bytes 1179656 | tf_op jit(solution)/shard_map/ppermute | solution.py:274
  46.4 9.3 %collective-permute-start.21 = (bf16[64,3072]{1,0:T(8,128)(2,1)S(1)}, bf16[64,3072]{1,0:T(8,128)(2,1)S(1)}, u32[]{:S(2)}, u32[]{:S(2)}) collective-permute-start(bf16[64,3072]{1,0:T(8,128)(2,1)S(1)} %get-tuple-element.25.refs_13_), channel_id=1, source_target_pairs={{1,2},{2,1},{5,6},{6,5},{9,10},{10,9},{13,14},{14,13},{17,18},{18,... | collective-permute-start | bytes 1179656 | tf_op jit(solution)/shard_map/ppermute | solution.py:275
  55.0 2.0 %collective-permute-start.22 = (bf16[64,3072]{1,0:T(8,128)(2,1)S(1)}, bf16[64,3072]{1,0:T(8,128)(2,1)S(1)}, u32[]{:S(2)}, u32[]{:S(2)}) collective-permute-start(bf16[64,3072]{1,0:T(8,128)(2,1)S(1)} %collective-permute-done.20.refs_8_), channel_id=1, source_target_pairs={{1,2},{2,1},{5,6},{6,5},{9,10},{10,9},{13,14},{14,13},{17,18},{18,... | collective-permute-start | bytes 1179656 | tf_op jit(solution)/shard_map/ppermute | solution.py:276
  55.7 11.9 %collective-permute-start.23 = (bf16[64,3072]{1,0:T(8,128)(2,1)S(1)}, bf16[64,3072]{1,0:T(8,128)(2,1)S(1)}, u32[]{:S(2)}, u32[]{:S(2)}) collective-permute-start(bf16[64,3072]{1,0:T(8,128)(2,1)S(1)} %collective-permute-done.21.refs_9_), channel_id=1, source_target_pairs={{1,0},{2,3},{5,4},{6,7},{9,8},{10,11},{13,12},{14,15},{17,16},{18,... | collective-permute-start | bytes 1179656 | tf_op jit(solution)/shard_map/ppermute | solution.py:277
  57.0 19.1 %collective-permute-start.24 = (bf16[64,3072]{1,0:T(8,128)(2,1)S(1)}, bf16[64,3072]{1,0:T(8,128)(2,1)S(1)}, u32[]{:S(2)}, u32[]{:S(2)}) collective-permute-start(bf16[64,3072]{1,0:T(8,128)(2,1)S(1)} %collective-permute-done.22.refs_10_), channel_id=1, source_target_pairs={{1,0},{2,3},{5,4},{6,7},{9,8},{10,11},{13,12},{14,15},{17,16},{18,... | collective-permute-start | bytes 1179656 | tf_op jit(solution)/shard_map/ppermute | solution.py:278
  58.3 5.2 %collective-permute-start.18 = (bf16[32,1024]{1,0:T(8,128)(2,1)S(1)}, bf16[32,1024]{1,0:T(8,128)(2,1)S(1)}, u32[]{:S(2)}, u32[]{:S(2)}) collective-permute-start(bf16[32,1024]{1,0:T(8,128)(2,1)S(1)} %copy-done.3), channel_id=1, source_target_pairs={{0,24},{4,28},{8,16},{12,20},{16,8},{20,12},{24,0},{28,4},{1,25},{... | collective-permute-start | bytes 196616 | tf_op jit(solution)/shard_map/ppermute | solution.py:249
  59.8 4.4 %collective-permute-start.16 = (bf16[32,1024]{1,0:T(8,128)(2,1)S(1)}, bf16[32,1024]{1,0:T(8,128)(2,1)S(1)}, u32[]{:S(2)}, u32[]{:S(2)}) collective-permute-start(bf16[32,1024]{1,0:T(8,128)(2,1)S(1)} %copy-done.3), channel_id=1, source_target_pairs={{0,16},{4,20},{8,24},{12,28},{16,0},{20,4},{24,8},{28,12},{1,17},{... | collective-permute-start | bytes 196616 | tf_op jit(solution)/shard_map/ppermute | solution.py:249
  60.3 4.3 %collective-permute-start.14 = (bf16[32,1024]{1,0:T(8,128)(2,1)S(1)}, bf16[32,1024]{1,0:T(8,128)(2,1)S(1)}, u32[]{:S(2)}, u32[]{:S(2)}) collective-permute-start(bf16[32,1024]{1,0:T(8,128)(2,1)S(1)} %copy-done.3), channel_id=1, source_target_pairs={{0,8},{4,12},{8,0},{12,4},{16,24},{20,28},{24,16},{28,20},{1,9},{5... | collective-permute-start | bytes 196616 | tf_op jit(solution)/shard_map/ppermute | solution.py:249
  63.5 1.3 %collective-permute-start.13 = (bf16[32,1024]{1,0:T(8,128)(2,1)S(1)}, bf16[32,1024]{1,0:T(8,128)(2,1)S(1)}, u32[]{:S(2)}, u32[]{:S(2)}) collective-permute-start(bf16[32,1024]{1,0:T(8,128)(2,1)S(1)} %copy-done.3), channel_id=1, source_target_pairs={{0,4},{4,0},{8,12},{12,8},{16,20},{20,16},{24,28},{28,24},{1,5},{5... | collective-permute-start | bytes 196616 | tf_op jit(solution)/shard_map/ppermute | solution.py:249
  64.2 1.3 %collective-permute-start.19 = (bf16[32,1024]{1,0:T(8,128)(2,1)S(1)}, bf16[32,1024]{1,0:T(8,128)(2,1)S(1)}, u32[]{:S(2)}, u32[]{:S(2)}) collective-permute-start(bf16[32,1024]{1,0:T(8,128)(2,1)S(1)} %collective-permute-done.18.refs_6_), channel_id=1, source_target_pairs={{0,4},{4,0},{8,12},{12,8},{16,20},{20,16},{24,28},{28,24},{1,5},{5... | collective-permute-start | bytes 196616 | tf_op jit(solution)/shard_map/ppermute | solution.py:249
  64.6 1.3 %collective-permute-start.17 = (bf16[32,1024]{1,0:T(8,128)(2,1)S(1)}, bf16[32,1024]{1,0:T(8,128)(2,1)S(1)}, u32[]{:S(2)}, u32[]{:S(2)}) collective-permute-start(bf16[32,1024]{1,0:T(8,128)(2,1)S(1)} %collective-permute-done.16.refs_4_), channel_id=1, source_target_pairs={{0,4},{4,0},{8,12},{12,8},{16,20},{20,16},{24,28},{28,24},{1,5},{5... | collective-permute-start | bytes 196616 | tf_op jit(solution)/shard_map/ppermute | solution.py:249
  64.8 1.3 %collective-permute-start.15 = (bf16[32,1024]{1,0:T(8,128)(2,1)S(1)}, bf16[32,1024]{1,0:T(8,128)(2,1)S(1)}, u32[]{:S(2)}, u32[]{:S(2)}) collective-permute-start(bf16[32,1024]{1,0:T(8,128)(2,1)S(1)} %collective-permute-done.14.refs_2_), channel_id=1, source_target_pairs={{0,4},{4,0},{8,12},{12,8},{16,20},{20,16},{24,28},{28,24},{1,5},{5... | collective-permute-start | bytes 196616 | tf_op jit(solution)/shard_map/ppermute | solution.py:249

commit v2 on v1

v2 whole, which is shorter than its diff:
```python
import functools

import jax
import jax.numpy as jnp
from jax import lax
from jax.experimental import pallas as pl
from jax.experimental.pallas import tpu as pltpu
from jax.sharding import PartitionSpec as P

HEADS = 12
HEAD = 128
LMAX = 32
SAMPLES = 2
VMEM = 48 * 1024 * 1024

F32 = jnp.float32
BF16 = jnp.bfloat16


def power_of_two(n):
    return n & (n - 1) == 0


def kernel_params(**more):
    return pltpu.CompilerParams(vmem_limit_bytes=VMEM, **more)


SMEM_SPEC = pl.BlockSpec(memory_space=pltpu.SMEM)
VMEM_SPEC = pl.BlockSpec(memory_space=pltpu.VMEM)
ANY_SPEC = pl.BlockSpec(memory_space=pl.ANY)
HBM_SPEC = pl.BlockSpec(memory_space=pltpu.HBM)


def scalar_table(image_counts, caption_lens, caption_owner, caption_offset):
    captions = caption_lens.shape[1]
    place = jnp.stack([lax.axis_index("dp"), lax.axis_index("fsdp"), image_counts[0, 0]]).astype(jnp.int32)
    place = jnp.pad(place, (0, captions - place.shape[0]))
    return jnp.concatenate([caption_lens, caption_owner, caption_offset, place[None]], axis=0)


def peer(index, k, paired):
    return index ^ k if paired else k


def first_of_class(offset, residue, groups):
    return lax.div(offset - residue + groups - 1, jnp.int32(groups))


def spread_rows(values, rows_each, shape):
    rows = lax.broadcasted_iota(jnp.int32, shape, 0)
    result = jnp.zeros(shape, jnp.int32)
    for g, value in enumerate(values):
        result = jnp.where((rows >= g * rows_each) & (rows < (g + 1) * rows_each), value + rows - g * rows_each, result)
    return result


def project_kernel(groups, paired, chunks, cache, weight, *refs):
    outs = refs[:groups]
    held_cache, held_weight, cache_sem, weight_sem = refs[groups:]
    depth = cache.shape[0]
    each = depth // groups
    rows = weight.shape[0] // chunks
    cache_copy = pltpu.make_async_copy(cache, held_cache, cache_sem)
    cache_copy.start()
    copies = [
        pltpu.make_async_copy(weight.at[pl.ds(i * rows, rows)], held_weight.at[pl.ds(i * rows, rows)], weight_sem.at[i])
        for i in range(chunks)
    ]
    for copy in copies:
        copy.start()
    member = lax.axis_index("fsdp")
    row = lax.broadcasted_iota(jnp.int32, (depth, depth), 0)
    column = lax.broadcasted_iota(jnp.int32, (depth, depth), 1)
    wanted = jnp.zeros((depth, depth), jnp.int32)
    for k in range(groups):
        wanted = jnp.where(row // each == k, groups * (row - k * each) + peer(member, k, paired), wanted)
    order = (wanted == column).astype(BF16)
    cache_copy.wait()
    sorted_rows = jnp.dot(order, held_cache[...], preferred_element_type=F32).astype(BF16)
    product = None
    for i, copy in enumerate(copies):
        copy.wait()
        at = slice(i * rows, (i + 1) * rows)
        part = jnp.dot(sorted_rows[:, at], held_weight[at], preferred_element_type=F32)
        product = part if product is None else product + part
    for k in range(groups):
        outs[k][...] = product[k * each : (k + 1) * each].astype(BF16)


def project(groups, paired, text_cache, w_kv):
    depth, features = text_cache.shape
    width = w_kv.shape[1]
    chunks = features // 128
    each = depth // groups
    return pl.pallas_call(
        functools.partial(project_kernel, groups, paired, chunks),
        in_specs=[HBM_SPEC, HBM_SPEC],
        out_specs=[VMEM_SPEC] * groups,
        out_shape=[jax.ShapeDtypeStruct((each, width), BF16)] * groups,
        scratch_shapes=[
            pltpu.VMEM((depth, features), BF16),
            pltpu.VMEM((features, width), BF16),
            pltpu.SemaphoreType.DMA,
            pltpu.SemaphoreType.DMA((chunks,)),
        ],
        compiler_params=kernel_params(),
        name="project",
    )(text_cache, w_kv)


def select_kernel(groups, each, paired, dp_paired, table, *refs):
    pieces, outs = refs[:-groups], refs[-groups:]
    held = jnp.concatenate([piece[...] for piece in pieces], axis=0) if len(pieces) > 1 else pieces[0][...]
    total = held.shape[0]
    index, member = table[3, 0], table[3, 1]
    wanted_rows = groups * SAMPLES * each
    starts, firsts = [], []
    for k in range(groups):
        for s in range(SAMPLES):
            caption = peer(member, k, paired) * SAMPLES + s
            first = first_of_class(table[2, caption], member, groups)
            owner = table[1, caption]
            firsts.append(first)
            starts.append((owner ^ index if dp_paired else owner) * each + first)
    shape = (wanted_rows, total)
    target = spread_rows(starts, each, shape)
    inside = spread_rows(firsts, each, shape) < each
    chosen = ((target == lax.broadcasted_iota(jnp.int32, shape, 1)) & inside).astype(BF16)
    rows = jnp.dot(chosen, held, preferred_element_type=F32).astype(BF16)
    size = SAMPLES * each
    for k in range(groups):
        outs[k][...] = rows[k * size : (k + 1) * size]


def select_rows(groups, each, paired, dp_paired, table, pieces):
    width = pieces[0].shape[1]
    return pl.pallas_call(
        functools.partial(select_kernel, groups, each, paired, dp_paired),
        in_specs=[SMEM_SPEC] + [VMEM_SPEC] * len(pieces),
        out_specs=[VMEM_SPEC] * groups,
        out_shape=[jax.ShapeDtypeStruct((SAMPLES * each, width), BF16)] * groups,
        compiler_params=kernel_params(),
        name="select_rows",
    )(table, *pieces)


LAST = (((1,), (1,)), ((), ()))
FIRST = (((0,), (0,)), ((), ()))


def value_grad_kernel(groups, each, paired, table, queries, cotangent, *refs):
    pieces, (probs, probs_rounded, grad_values, scores) = refs[:groups], refs[groups:]
    tokens, width = queries.shape
    slots = groups * SAMPLES * each
    heads = width // HEAD
    member = table[3, 1]
    split = table[3, 2]
    shape = (slots, tokens)
    rows = lax.broadcasted_iota(jnp.int32, shape, 0)
    position = jnp.zeros(shape, jnp.int32)
    length = jnp.zeros(shape, jnp.int32)
    sample = jnp.zeros(shape, jnp.int32)
    for c in range(groups):
        residue = peer(member, c, paired)
        for s in range(SAMPLES):
            caption = member * SAMPLES + s
            run = (c * SAMPLES + s) * each
            here = (rows >= run) & (rows < run + each)
            first = first_of_class(table[2, caption], residue, groups)
            position = jnp.where(here, groups * (first + rows - run) + residue - table[2, caption], position)
            length = jnp.where(here, table[0, caption], length)
            sample = jnp.where(here, s, sample)
    token_sample = (lax.broadcasted_iota(jnp.int32, shape, 1) >= split).astype(jnp.int32)
    allowed = (position < length) & (sample == token_sample)
    for h in range(heads):
        at = slice(h * HEAD, (h + 1) * HEAD)
        k = jnp.concatenate([piece[:, at] for piece in pieces], axis=0)
        scores[h] = lax.dot_general(k, queries[:, at], LAST, preferred_element_type=F32)
    for h in range(heads):
        masked = jnp.where(allowed, scores[h] * HEAD ** (-0.5), F32(-1e30))
        expon = jnp.exp(masked - jnp.max(masked, axis=0, keepdims=True))
        prob = expon / jnp.sum(expon, axis=0, keepdims=True)
        probs[h] = prob
        probs_rounded[h] = prob.astype(BF16)
    for h in range(heads):
        at = slice(h * HEAD, (h + 1) * HEAD)
        grad_values[:, at] = jnp.dot(probs_rounded[h], cotangent[:, at], preferred_element_type=F32).astype(BF16)


def value_grads(groups, each, paired, table, queries, grad_out, pieces):
    tokens, width = queries.shape
    slots = groups * SAMPLES * each
    heads = width // HEAD
    return pl.pallas_call(
        functools.partial(value_grad_kernel, groups, each, paired),
        in_specs=[SMEM_SPEC] + [VMEM_SPEC] * (2 + groups),
        out_specs=[VMEM_SPEC] * 3,
        out_shape=[
            jax.ShapeDtypeStruct((heads, slots, tokens), F32),
            jax.ShapeDtypeStruct((heads, slots, tokens), BF16),
            jax.ShapeDtypeStruct((slots, width), BF16),
        ],
        scratch_shapes=[pltpu.VMEM((heads, slots, tokens), F32)],
        compiler_params=kernel_params(),
        name="value_gradients",
    )(table, queries, grad_out, *pieces)


def key_grad_kernel(groups, probs, queries, cotangent, grad_values, *refs):
    pieces, (grad_query, grad_keys, grad_both, prob_grads, score_grads) = refs[:groups], refs[groups:]
    width = queries.shape[1]
    heads = width // HEAD
    scale = HEAD ** (-0.5)
    for h in range(heads):
        values_at = slice(width + h * HEAD, width + (h + 1) * HEAD)
        v = jnp.concatenate([piece[:, values_at] for piece in pieces], axis=0)
        prob_grads[h] = lax.dot_general(v, cotangent[:, h * HEAD : (h + 1) * HEAD], LAST, preferred_element_type=F32)
    for h in range(heads):
        prob, prob_grad = probs[h], prob_grads[h]
        centre = jnp.sum(prob * prob_grad, axis=0, keepdims=True)
        score_grads[h] = (prob * (prob_grad - centre)).astype(BF16)
    for h in range(heads):
        at = slice(h * HEAD, (h + 1) * HEAD)
        k = jnp.concatenate([piece[:, at] for piece in pieces], axis=0)
        score_grad = score_grads[h]
        grad_key = (jnp.dot(score_grad, queries[:, at], preferred_element_type=F32) * scale).astype(BF16)
        grad_keys[:, at] = grad_key
        grad_both[:, at] = grad_key
        grad_query[:, at] = (lax.dot_general(score_grad, k, FIRST, preferred_element_type=F32) * scale).astype(BF16)
    grad_both[:, width:] = grad_values[...]


def key_grads(groups, probs, queries, grad_out, grad_values, pieces):
    tokens, width = queries.shape
    heads, slots, _ = probs.shape
    return pl.pallas_call(
        functools.partial(key_grad_kernel, groups),
        in_specs=[VMEM_SPEC] * (4 + groups),
        out_specs=[VMEM_SPEC] * 3,
        out_shape=[
            jax.ShapeDtypeStruct((tokens, width), BF16),
            jax.ShapeDtypeStruct((slots, width), BF16),
            jax.ShapeDtypeStruct((slots, 2 * width), BF16),
        ],
        scratch_shapes=[pltpu.VMEM((heads, slots, tokens), F32), pltpu.VMEM((heads, slots, tokens), BF16)],
        compiler_params=kernel_params(),
        name="key_gradients",
    )(probs, queries, grad_out, grad_values, *pieces)


def text_kernel(groups, each, depth, paired, dp_paired, table, *refs):
    texts, out = refs[:-1], refs[-1]
    index, member = table[3, 0], table[3, 1]
    held = jnp.concatenate([text[...] for text in texts], axis=0) if len(texts) > 1 else texts[0][...]
    shape = (held.shape[0], out.shape[1])
    columns = lax.broadcasted_iota(jnp.int32, shape, 1)
    runs, place = columns // each, columns % each
    target = jnp.zeros(shape, jnp.int32)
    limit = jnp.zeros(shape, jnp.int32)
    run = 0
    for k in range(groups):
        device = peer(member, k, paired)
        for c in range(groups):
            residue = peer(device, c, paired)
            for s in range(SAMPLES):
                caption = device * SAMPLES + s
                offset = table[2, caption]
                owner = table[1, caption]
                base = (owner ^ index if dp_paired else owner) * depth
                here = runs == run
                target = jnp.where(here, base + groups * first_of_class(offset, residue, groups) + residue, target)
                limit = jnp.where(here, base + offset + table[0, caption], limit)
                run += 1
    target = target + groups * place
    chosen = ((target == lax.broadcasted_iota(jnp.int32, shape, 0)) & (target < limit)).astype(BF16)
    out[...] = lax.dot_general(held, chosen, FIRST, preferred_element_type=F32).astype(BF16)


def slot_texts(groups, each, depth, paired, dp_paired, table, texts):
    features = texts[0].shape[1]
    return pl.pallas_call(
        functools.partial(text_kernel, groups, each, depth, paired, dp_paired),
        in_specs=[SMEM_SPEC] + [VMEM_SPEC] * len(texts),
        out_specs=VMEM_SPEC,
        out_shape=jax.ShapeDtypeStruct((features, groups * groups * SAMPLES * each), BF16),
        compiler_params=kernel_params(),
        name="slot_texts",
    )(table, *texts)


def weight_kernel(line, first, block, started, *refs):
    chosen_text, *grads = refs[: -4 if started else -3]
    out, built, sems = refs[-3:]
    part = built.shape[1]
    if line:
        member = lax.axis_index("fsdp")
        is_inner = (member == 1) | (member == 2)
    copies = []
    for i in range(part // block):
        at = slice(i * block, (i + 1) * block)
        if line:
            own, near, second, inner, outer = [g[:, at] for g in grads]
            every = jnp.concatenate([own, near, second, jnp.where(is_inner, inner, outer)], axis=0)
        else:
            every = grads[0][:, at]
        built[:, at] = jnp.dot(chosen_text[...], every, preferred_element_type=F32).astype(BF16)
        copy = pltpu.make_async_copy(
            built.at[:, pl.ds(i * block, block)], out.at[:, pl.ds(first + i * block, block)], sems.at[i]
        )
        copy.start()
        copies.append(copy)
    for copy in copies:
        copy.wait()


def weight_grad(line, chosen_text, grads, width, first, before=None):
    features, slots = chosen_text.shape
    part = grads[0].shape[1]
    block = 256
    started = before is not None
    parts = [pl.BlockSpec((g.shape[0], part), lambda n, at=first // part * (g.shape[1] > part): (0, at)) for g in grads]
    return pl.pallas_call(
        functools.partial(weight_kernel, line, first, block, started),
        grid=(1,),
        in_specs=[pl.BlockSpec((features, slots), lambda n: (0, 0))] + parts + [ANY_SPEC] * started,
        out_specs=ANY_SPEC,
        out_shape=jax.ShapeDtypeStruct((features, width), BF16),
        scratch_shapes=[pltpu.VMEM((features, part), BF16), pltpu.SemaphoreType.DMA((part // block,))],
        input_output_aliases={1 + len(grads): 0} if started else {},
        compiler_params=kernel_params(),
        name="weight_gradient",
    )(chosen_text, *grads, *([before] if started else []))


def swap(x, axis, k):
    return lax.ppermute(x, axis, [(i, i ^ k) for i in range(lax.axis_size(axis))])


def gather_dp(x, paired):
    if not paired:
        return [lax.all_gather(x, "dp", axis=0, tiled=True)]
    near = {0: x}
    for k in range(2, lax.axis_size("dp"), 2):
        near[k] = swap(x, "dp", k)
    for k in list(near):
        near[k + 1] = swap(near[k], "dp", 1)
    return [near[k] for k in sorted(near)]


def exchange(pieces, paired):
    if paired:
        return [pieces[0]] + [swap(pieces[k], "fsdp", k) for k in range(1, len(pieces))]
    came = lax.all_to_all(jnp.stack(pieces), "fsdp", 0, 0, tiled=True)
    return [came[k] for k in range(len(pieces))]


def gather_line(first_half, second_half, both, beside):
    near_pairs = [(0, 1), (1, 0), (2, 3), (3, 2)]
    middle_pairs = [(1, 2), (2, 1)]
    outward = [(1, 0), (2, 3)]
    halves = [first_half, second_half]
    second = [swap(half, "fsdp", 2) for half in halves]
    near = lax.ppermute(both, "fsdp", near_pairs)
    second[0], beside = lax.optimization_barrier((second[0], beside))
    outer = [lax.ppermute(piece, "fsdp", outward) for piece in second]
    late, _ = lax.optimization_barrier((both, second[0]))
    inner = lax.ppermute(late, "fsdp", middle_pairs)
    parts = [[halves[i], near, second[i], inner, outer[i]] for i in range(2)]
    return parts[0], parts[1], beside


def shards(
    queries, grad_out, text_cache, w_kv, image_counts, caption_lens, caption_owner, caption_offset
):
    groups = lax.axis_size("fsdp")
    line = groups == 4
    paired = line
    dp_paired = power_of_two(lax.axis_size("dp")) and lax.axis_size("dp") <= 8
    depth = text_cache.shape[0]
    each = depth // groups
    width = queries.shape[1]

    partials = project(groups, paired, text_cache, w_kv)
    came = exchange(partials, paired)
    table = scalar_table(image_counts, caption_lens, caption_owner, caption_offset)
    rows = sum(piece.astype(F32) for piece in came).astype(BF16)
    class_rows = gather_dp(rows, dp_paired)
    outgoing = select_rows(groups, each, paired, dp_paired, table, class_rows)
    keys_values = exchange(outgoing, paired)
    probs, _, grad_values = value_grads(groups, each, paired, table, queries, grad_out, keys_values)
    grad_values, probs = lax.optimization_barrier((grad_values, probs))
    grad_query, grad_keys, grad_both = key_grads(groups, probs, queries, grad_out, grad_values, keys_values)
    grad_keys, grad_both, late_cache = lax.optimization_barrier((grad_keys, grad_both, text_cache))
    texts = [lax.all_gather(late_cache, "dp", axis=0, tiled=True)]
    chosen_text = slot_texts(groups, each, depth, paired, False, table, texts)
    if line:
        value_parts, key_parts, chosen_text = gather_line(grad_values, grad_keys, grad_both, chosen_text)
    else:
        value_parts, key_parts = [
            [lax.all_gather(half, "fsdp", axis=0, tiled=True)] for half in (grad_values, grad_keys)
        ]
    value_parts, key_parts = lax.optimization_barrier((value_parts, key_parts))
    grad_weight = weight_grad(line, chosen_text, value_parts, 2 * width, width)
    grad_weight = weight_grad(line, chosen_text, key_parts, 2 * width, 0, grad_weight)
    return grad_query, grad_weight[None]


def solution(mesh):
    in_specs = (
        P(("dp", "fsdp"), None),
        P(("dp", "fsdp"), None),
        P("dp", "fsdp"),
        P("fsdp", None),
        P(("dp", "fsdp"), None),
        P("dp", None),
        P("dp", None),
        P("dp", None),
    )
    out_specs = (P(("dp", "fsdp"), None), P("dp", "fsdp", None))
    return jax.shard_map(shards, mesh=mesh, in_specs=in_specs, out_specs=out_specs, check_vma=False)
```

time: 82.3 us -> 73.8 us (0.90)
  waiting for transfers between devices: 38.8 us -> 27.7 us
  blocking collectives: 0 us -> 9.85 us
  Pallas kernels: 16.5 us -> 12.5 us
  starting transfers between devices: 23.5 us -> 21.8 us
  other arithmetic: 1.52 us -> 0.15 us
    all_gather x0 -> x1, blocking collectives: none -> 9.85 us  [shards(): texts = [lax.all_gather(late_cache, 'dp', axis=0, tiled=True)]]
    ppermute x5 -> x4, waiting for transfers between devices: 17.9 us -> 9.44 us  [the longest x2 9.44 us: gather_line(): outer = [lax.ppermute(piece, 'fsdp', outward) for piece in second]]
    pallas_call x3 -> x6, Pallas kernels: 15.7 us -> 11.7 us  [the longest x2 4.29 us: weight_grad(): pl.pallas_call(functools.partial(weight_kernel, line, first, block, start...]
    ppermute x20 -> x15, waiting for transfers between devices: 20.9 us -> 18.2 us  [swap(): lax.ppermute(x, axis, [(i, i ^ k) for i in range(lax.axis_size(axis))])]
    ppermute x20 -> x15, starting transfers between devices: 17.7 us -> 16.6 us  [swap(): lax.ppermute(x, axis, [(i, i ^ k) for i in range(lax.axis_size(axis))])]
    ppermute x5 -> x4, starting transfers between devices: 5.81 us -> 5.14 us  [the longest x2 2.57 us: gather_line(): outer = [lax.ppermute(piece, 'fsdp', outward) for piece in second]]
  transfers between devices with their start and end apart: 25 -> 19, of which waited for: 18 -> 12; matrix products, arithmetic and copies ran while one was open for 0% -> 0% of each run, Pallas kernels for 0% -> 3%
where the time goes in v2:
time: 73.8 us; the launch traced here: 73.6 us
  waiting for transfers between devices  27.7 us (38%)
  starting transfers between devices  21.8 us (30%)
  Pallas kernels  12.5 us (17%)
  blocking collectives  9.85 us (13%)
  local copies, waits for them, and re-layouts  0.91 us (1%)
  between operations  0.8 us (1%)
    ppermute x15, waiting for transfers between devices, swap(): lax.ppermute(x, axis, [(i, i ^ k) for i in range(lax.axis_size(axis))])  18.2 us
    ppermute x15, starting transfers between devices, swap(): lax.ppermute(x, axis, [(i, i ^ k) for i in range(lax.axis_size(axis))])  16.6 us
    all_gather x1, blocking collectives, shards(): texts = [lax.all_gather(late_cache, 'dp', axis=0, tiled=True)]  9.85 us
    ppermute x2, waiting for transfers between devices, gather_line(): outer = [lax.ppermute(piece, 'fsdp', outward) for piece in second]  9.44 us
    pallas_call x2, Pallas kernels, weight_grad(): pl.pallas_call(functools.partial(weight_kernel, line, first, block, start...  4.29 us
    pallas_call x1, Pallas kernels, project(): pl.pallas_call(functools.partial(project_kernel, groups, paired, chunks),...  3.28 us
    ppermute x2, starting transfers between devices, gather_line(): outer = [lax.ppermute(piece, 'fsdp', outward) for piece in second]  2.57 us
    ppermute x1, starting transfers between devices, gather_line(): near = lax.ppermute(both, 'fsdp', near_pairs)  1.88 us
  transfers between devices with their start and end apart: 19, of which 12 were waited for; matrix products, arithmetic and copies ran while one was open for 0% of the time, Pallas kernels for 3%

profile of v2, /device:TPU:0, one launch (start us, length us, event | category | flops | bytes accessed | tf_op | source)
XLA Modules:
  0.0 73.6 jit_solution(8393511381531093948)
XLA Ops:
  0.6 0.0 copy-start.1
  0.6 0.0 copy-start.2
  0.7 0.9 %copy-done.2 = bf16[32,1024]{1,0:T(8,128)(2,1)S(1)} copy-done((bf16[32,1024]{1,0:T(8,128)(2,1)S(1)}, bf16[32,1024]{1,0:T(8,128)(2,1)}, u32[]{:S(2)}) %copy-start.2) | copy-done | bytes 65560
  1.5 0.0 copy-start.4
  1.5 0.0 copy-start.5
  1.5 0.0 copy-start.6
  1.5 0.0 copy-start.7
  1.5 0.0 copy-start
  1.6 0.0 copy-start.3
  1.6 3.3 %project.1 = (bf16[8,3072]{1,0:T(8,128)(2,1)S(1)}, bf16[8,3072]{1,0:T(8,128)(2,1)S(1)}, bf16[8,3072]{1,0:T(8,128)(2,1)S(1)}, bf16[8,3072]{1,0:T(8,128)(2,1)S(1)}) custom-call(bf16[32,1024]{1,0:T(8,128)(2,1)S(1)} %copy-done.2, bf16[1024,3072]{1,0:T(8,128)(2,1)} %weight.1), custom_call_target="tpu_custom_call" | custom-call | tf_op jit(solution)/shard_map/project/pallas_call | solution.py:95
  4.8 3.1 %collective-permute-start = (bf16[8,3072]{1,0:T(8,128)(2,1)S(1)}, bf16[8,3072]{1,0:T(8,128)(2,1)S(1)}, u32[]{:S(2)}, u32[]{:S(2)}) collective-permute-start(bf16[8,3072]{1,0:T(8,128)(2,1)S(1)} %get-tuple-element.34), channel_id=1, source_target_pairs={{0,1},{1,0},{2,3},{3,2},{4,5},{5,4},{6,7},{7,6},{8,9},{9,8},{10,11... | collective-permute-start | bytes 147464 | tf_op jit(solution)/shard_map/ppermute | solution.py:336
  7.9 2.6 %collective-permute-start.1 = (bf16[8,3072]{1,0:T(8,128)(2,1)S(1)}, bf16[8,3072]{1,0:T(8,128)(2,1)S(1)}, u32[]{:S(2)}, u32[]{:S(2)}) collective-permute-start(bf16[8,3072]{1,0:T(8,128)(2,1)S(1)} %get-tuple-element.35), channel_id=1, source_target_pairs={{0,2},{1,3},{2,0},{3,1},{4,6},{5,7},{6,4},{7,5},{8,10},{9,11},{10,... | collective-permute-start | bytes 147464 | tf_op jit(solution)/shard_map/ppermute | solution.py:336
  10.5 0.0 collective-permute-start.2
  10.5 0.0 copy-done.4
  10.5 0.1 pad_add_fusion.1
  10.6 0.0 collective-permute-done
  10.6 3.2 %collective-permute-done.1 = bf16[8,3072]{1,0:T(8,128)(2,1)S(1)} collective-permute-done((bf16[8,3072]{1,0:T(8,128)(2,1)S(1)}, bf16[8,3072]{1,0:T(8,128)(2,1)S(1)}, u32[]{:S(2)}, u32[]{:S(2)}) %collective-permute-start.1) | collective-permute-done | bytes 49184 | tf_op jit(solution)/shard_map/ppermute | solution.py:336
  13.9 2.6 %collective-permute-done.2 = bf16[8,3072]{1,0:T(8,128)(2,1)S(1)} collective-permute-done((bf16[8,3072]{1,0:T(8,128)(2,1)S(1)}, bf16[8,3072]{1,0:T(8,128)(2,1)S(1)}, u32[]{:S(2)}, u32[]{:S(2)}) %collective-permute-start.2) | collective-permute-done | bytes 49184 | tf_op jit(solution)/shard_map/ppermute | solution.py:336
  16.4 2.5 %collective-permute-start.8 = (bf16[8,3072]{1,0:T(8,128)(2,1)S(1)}, bf16[8,3072]{1,0:T(8,128)(2,1)S(1)}, u32[]{:S(2)}, u32[]{:S(2)}) collective-permute-start(bf16[8,3072]{1,0:T(8,128)(2,1)S(1)} %add_convert_fusion.refs_0_), channel_id=1, source_target_pairs={{0,24},{4,28},{8,16},{12,20},{16,8},{20,12},{24,0},{28,4},{1,25},{... | collective-permute-start | bytes 147464 | tf_op jit(solution)/shard_map/ppermute | solution.py:336
  19.0 0.5 collective-permute-start.6
  19.5 0.5 collective-permute-start.4
  20.0 0.0 collective-permute-start.3
  20.0 1.7 %collective-permute-done.8.refs_6_ = bf16[8,3072]{1,0:T(8,128)(2,1)S(1)} collective-permute-done((bf16[8,3072]{1,0:T(8,128)(2,1)S(1)}, bf16[8,3072]{1,0:T(8,128)(2,1)S(1)}, u32[]{:S(2)}, u32[]{:S(2)}) %collective-permute-start.8) | collective-permute-done | bytes 49184 | tf_op jit(solution)/shard_map/ppermute | solution.py:336
  21.7 0.0 collective-permute-start.9
  21.7 1.3 %collective-permute-done.6.refs_4_ = bf16[8,3072]{1,0:T(8,128)(2,1)S(1)} collective-permute-done((bf16[8,3072]{1,0:T(8,128)(2,1)S(1)}, bf16[8,3072]{1,0:T(8,128)(2,1)S(1)}, u32[]{:S(2)}, u32[]{:S(2)}) %collective-permute-start.6) | collective-permute-done | bytes 49184 | tf_op jit(solution)/shard_map/ppermute | solution.py:336
  23.0 0.0 collective-permute-start.7
  23.1 0.5 collective-permute-done.4.refs_2_
  23.6 0.0 collective-permute-start.5
  23.6 0.0 copy-done.5
  23.6 0.0 copy-done.6
  23.6 0.0 copy-done.7
  23.6 0.0 collective-permute-done.3.refs_1_
  23.6 0.0 collective-permute-done.9.refs_7_
  23.6 0.7 collective-permute-done.7.refs_5_
  24.3 0.5 collective-permute-done.5.refs_3_
  24.8 0.8 %select_rows.1 = (bf16[16,3072]{1,0:T(8,128)(2,1)S(1)}, bf16[16,3072]{1,0:T(8,128)(2,1)S(1)}, bf16[16,3072]{1,0:T(8,128)(2,1)S(1)}, bf16[16,3072]{1,0:T(8,128)(2,1)S(1)}) custom-call(s32[4,8]{1,0:T(4,128)S(1)} %pad_add_fusion.table, bf16[8,3072]{1,0:T(8,128)(2,1)S(1)} %add_convert_fusion.refs_0_, bf16[8,3072]{1,0:T(8,128)(2,1)S(1)} %collective-permute-done.3.refs_1_, ...), custom_call_target="tpu_custom_call" | custom-call | tf_op jit(solution)/shard_map/select_rows/pallas_call | solution.py:137
  25.6 0.1 collective-permute-start.10
  25.7 1.3 %collective-permute-start.11 = (bf16[16,3072]{1,0:T(8,128)(2,1)S(1)}, bf16[16,3072]{1,0:T(8,128)(2,1)S(1)}, u32[]{:S(2)}, u32[]{:S(2)}) collective-permute-start(bf16[16,3072]{1,0:T(8,128)(2,1)S(1)} %get-tuple-element.39), channel_id=1, source_target_pairs={{0,2},{1,3},{2,0},{3,1},{4,6},{5,7},{6,4},{7,5},{8,10},{9,11},{10,... | collective-permute-start | bytes 294920 | tf_op jit(solution)/shard_map/ppermute | solution.py:336
  27.0 3.1 %collective-permute-start.12 = (bf16[16,3072]{1,0:T(8,128)(2,1)S(1)}, bf16[16,3072]{1,0:T(8,128)(2,1)S(1)}, u32[]{:S(2)}, u32[]{:S(2)}) collective-permute-start(bf16[16,3072]{1,0:T(8,128)(2,1)S(1)} %get-tuple-element.40), channel_id=1, source_target_pairs={{0,3},{1,2},{2,1},{3,0},{4,7},{5,6},{6,5},{7,4},{8,11},{9,10},{10,... | collective-permute-start | bytes 294920 | tf_op jit(solution)/shard_map/ppermute | solution.py:336
  30.1 1.7 %collective-permute-done.10.refs_1_ = bf16[16,3072]{1,0:T(8,128)(2,1)S(1)} collective-permute-done((bf16[16,3072]{1,0:T(8,128)(2,1)S(1)}, bf16[16,3072]{1,0:T(8,128)(2,1)S(1)}, u32[]{:S(2)}, u32[]{:S(2)}) %collective-permute-start.10) | collective-permute-done | bytes 98336 | tf_op jit(solution)/shard_map/ppermute | solution.py:336
  31.7 4.8 %collective-permute-done.11.refs_2_ = bf16[16,3072]{1,0:T(8,128)(2,1)S(1)} collective-permute-done((bf16[16,3072]{1,0:T(8,128)(2,1)S(1)}, bf16[16,3072]{1,0:T(8,128)(2,1)S(1)}, u32[]{:S(2)}, u32[]{:S(2)}) %collective-permute-start.11) | collective-permute-done | bytes 98336 | tf_op jit(solution)/shard_map/ppermute | solution.py:336
  36.6 0.0 collective-permute-done.12.refs_3_
  36.6 0.0 copy-done.1
  36.6 0.0 copy-done
  36.6 1.7 %value_gradients.1 = (f32[12,64,128]{2,1,0:T(8,128)S(1)}, bf16[12,64,128]{2,1,0:T(8,128)(2,1)}, bf16[64,1536]{1,0:T(8,128)(2,1)S(1)}) custom-call(s32[4,8]{1,0:T(4,128)S(1)} %pad_add_fusion.table, bf16[128,1536]{1,0:T(8,128)(2,1)S(1)} %copy-done, bf16[128,1536]{1,0:T(8,128)(2,1)S(1)} %copy-done.1, bf16[16,3072]{1,0:T(8,128)(2,1)S(1)} %get-tuple-element.37.refs_0_, ...), custom_call_target="tpu_custom_call" | custom-call | tf_op jit(solution)/shard_map/value_gradients/pallas_call | solution.py:194
  38.3 1.9 %collective-permute-start.13 = (bf16[64,1536]{1,0:T(8,128)(2,1)S(1)}, bf16[64,1536]{1,0:T(8,128)(2,1)S(1)}, u32[]{:S(2)}, u32[]{:S(2)}) collective-permute-start(bf16[64,1536]{1,0:T(8,128)(2,1)S(1)} %get-tuple-element.59.grad_values.refs_1_), channel_id=1, source_target_pairs={{0,2},{1,3},{2,0},{3,1},{4,6},{5,7},{6,4},{7,5},{8,10},{9,11},{10,... | collective-permute-start | bytes 589832 | tf_op jit(solution)/shard_map/ppermute | solution.py:336
  40.2 1.4 %key_gradients.1 = (bf16[128,1536]{1,0:T(8,128)(2,1)}, bf16[64,1536]{1,0:T(8,128)(2,1)S(1)}, bf16[64,3072]{1,0:T(8,128)(2,1)S(1)}) custom-call(f32[12,64,128]{2,1,0:T(8,128)S(1)} %get-tuple-element.43.probs, bf16[128,1536]{1,0:T(8,128)(2,1)S(1)} %copy-done, bf16[128,1536]{1,0:T(8,128)(2,1)S(1)} %copy-done.1, ...), custom_call_target="tpu_custom_call" | custom-call | tf_op jit(solution)/shard_map/key_gradients/pallas_call | solution.py:236
  41.6 1.0 %collective-permute-start.17 = (bf16[64,1536]{1,0:T(8,128)(2,1)S(1)}, bf16[64,1536]{1,0:T(8,128)(2,1)S(1)}, u32[]{:S(2)}, u32[]{:S(2)}) collective-permute-start(bf16[64,1536]{1,0:T(8,128)(2,1)S(1)} %get-tuple-element.54.refs_1_), channel_id=1, source_target_pairs={{0,2},{1,3},{2,0},{3,1},{4,6},{5,7},{6,4},{7,5},{8,10},{9,11},{10,... | collective-permute-start | bytes 589832 | tf_op jit(solution)/shard_map/ppermute | solution.py:336
  42.6 1.9 %collective-permute-start.14 = (bf16[64,3072]{1,0:T(8,128)(2,1)S(1)}, bf16[64,3072]{1,0:T(8,128)(2,1)S(1)}, u32[]{:S(2)}, u32[]{:S(2)}) collective-permute-start(bf16[64,3072]{1,0:T(8,128)(2,1)S(1)} %get-tuple-element.52), channel_id=1, source_target_pairs={{0,1},{1,0},{2,3},{3,2},{4,5},{5,4},{6,7},{7,6},{8,9},{9,8},{10,11... | collective-permute-start | bytes 1179656 | tf_op jit(solution)/shard_map/ppermute | solution.py:363
  44.5 0.0 copy-done.3
  44.5 9.8 %all_gather.3.refs_0_ = bf16[256,1024]{1,0:T(8,128)(2,1)S(1)} all-gather(bf16[32,1024]{1,0:T(8,128)(2,1)S(1)} %copy-done.3), channel_id=1, replica_groups=mesh['dp'=8,'fsdp'=4] {'dp'}, dimensions={0}, use_global_device_ids=true | all-gather | bytes 589824 | tf_op jit(solution)/shard_map/all_gather | solution.py:394
  54.3 1.0 %slot_texts.1.refs_0_ = bf16[1024,256]{1,0:T(8,128)(2,1)S(1)} custom-call(s32[4,8]{1,0:T(4,128)S(1)} %pad_add_fusion.table, bf16[256,1024]{1,0:T(8,128)(2,1)S(1)} %all_gather.3.refs_0_), custom_call_target="tpu_custom_call" | custom-call | tf_op jit(solution)/shard_map/slot_texts/pallas_call | solution.py:281
  55.4 0.0 collective-permute-done.13.refs_3_
  55.4 0.7 collective-permute-start.15
  56.1 1.2 %collective-permute-done.17.refs_3_ = bf16[64,1536]{1,0:T(8,128)(2,1)S(1)} collective-permute-done((bf16[64,1536]{1,0:T(8,128)(2,1)S(1)}, bf16[64,1536]{1,0:T(8,128)(2,1)S(1)}, u32[]{:S(2)}, u32[]{:S(2)}) %collective-permute-start.17) | collective-permute-done | bytes 196640 | tf_op jit(solution)/shard_map/ppermute | solution.py:336
  57.3 1.3 %collective-permute-start.18 = (bf16[64,1536]{1,0:T(8,128)(2,1)S(1)}, bf16[64,1536]{1,0:T(8,128)(2,1)S(1)}, u32[]{:S(2)}, u32[]{:S(2)}) collective-permute-start(bf16[64,1536]{1,0:T(8,128)(2,1)S(1)} %collective-permute-done.17.refs_3_), channel_id=1, source_target_pairs={{1,0},{2,3},{5,4},{6,7},{9,8},{10,11},{13,12},{14,15},{17,16},{18,... | collective-permute-start | bytes 589832 | tf_op jit(solution)/shard_map/ppermute | solution.py:365
  58.6 1.3 %collective-permute-start.16 = (bf16[64,1536]{1,0:T(8,128)(2,1)S(1)}, bf16[64,1536]{1,0:T(8,128)(2,1)S(1)}, u32[]{:S(2)}, u32[]{:S(2)}) collective-permute-start(bf16[64,1536]{1,0:T(8,128)(2,1)S(1)} %collective-permute-done.13.refs_3_), channel_id=1, source_target_pairs={{1,0},{2,3},{5,4},{6,7},{9,8},{10,11},{13,12},{14,15},{17,16},{18,... | collective-permute-start | bytes 589832 | tf_op jit(solution)/shard_map/ppermute | solution.py:365
  59.9 7.1 %collective-permute-done.18.refs_5_ = bf16[64,1536]{1,0:T(8,128)(2,1)S(1)} collective-permute-done((bf16[64,1536]{1,0:T(8,128)(2,1)S(1)}, bf16[64,1536]{1,0:T(8,128)(2,1)S(1)}, u32[]{:S(2)}, u32[]{:S(2)}) %collective-permute-start.18) | collective-permute-done | bytes 196640 | tf_op jit(solution)/shard_map/ppermute | solution.py:365
  67.0 0.0 collective-permute-done.14.refs_2_
  67.0 2.3 %collective-permute-done.16.refs_5_ = bf16[64,1536]{1,0:T(8,128)(2,1)S(1)} collective-permute-done((bf16[64,1536]{1,0:T(8,128)(2,1)S(1)}, bf16[64,1536]{1,0:T(8,128)(2,1)S(1)}, u32[]{:S(2)}, u32[]{:S(2)}) %collective-permute-start.16) | collective-permute-done | bytes 196640 | tf_op jit(solution)/shard_map/ppermute | solution.py:365
  69.3 0.0 collective-permute-done.15.refs_4_
  69.3 2.1 %weight_gradient.2.refs_6_ = bf16[1024,3072]{1,0:T(8,128)(2,1)} custom-call(bf16[1024,256]{1,0:T(8,128)(2,1)S(1)} %slot_texts.1.refs_0_, bf16[64,1536]{1,0:T(8,128)(2,1)S(1)} %get-tuple-element.59.grad_values.refs_1_, bf16[64,3072]{1,0:T(8,128)(2,1)S(1)} %collective-permute-done.14.refs_2_, bf16[64,1536]{1,0:T(8,128)(2,1)S(1)} %collective-permute-done.13.refs_3_, ...), custom_call_target="tpu_custom_call" | custom-call | tf_op jit(solution)/shard_map/weight_gradient/pallas_call | solution.py:322
  71.5 2.1 %weight_gradient.3 = bf16[1024,3072]{1,0:T(8,128)(2,1)} custom-call(bf16[1024,256]{1,0:T(8,128)(2,1)S(1)} %slot_texts.1.refs_0_, bf16[64,1536]{1,0:T(8,128)(2,1)S(1)} %get-tuple-element.54.refs_1_, bf16[64,3072]{1,0:T(8,128)(2,1)S(1)} %collective-permute-done.14.refs_2_, ...), custom_call_target="tpu_custom_call", output_to_operand_aliasing={{}: (6, {})} | custom-call | tf_op jit(solution)/shard_map/weight_gradient/pallas_call | solution.py:322
  (3 shorter events, 0.0 us)
Async XLA Ops:
  0.6 35.9 %copy-start.1 = (bf16[128,1536]{1,0:T(8,128)(2,1)S(1)}, bf16[128,1536]{1,0:T(8,128)(2,1)}, u32[]{:S(2)}) copy-start(bf16[128,1536]{1,0:T(8,128)(2,1)} %cotangent.3) | copy-start | bytes 1179652
  0.6 0.9 %copy-start.2 = (bf16[32,1024]{1,0:T(8,128)(2,1)S(1)}, bf16[32,1024]{1,0:T(8,128)(2,1)}, u32[]{:S(2)}) copy-start(bf16[32,1024]{1,0:T(8,128)(2,1)} %cache.1) | copy-start | bytes 196612
  1.5 9.0 %copy-start.4 = (s32[1,2]{1,0:T(1,128)S(1)}, s32[1,2]{1,0:T(1,128)}, u32[]{:S(2)}) copy-start(s32[1,2]{1,0:T(1,128)} %param.12) | copy-start | bytes 28
  1.5 22.0 %copy-start.5 = (s32[1,8]{1,0:T(1,128)S(1)}, s32[1,8]{1,0:T(1,128)}, u32[]{:S(2)}) copy-start(s32[1,8]{1,0:T(1,128)} %param.15) | copy-start | bytes 100
  1.5 22.0 %copy-start.6 = (s32[1,8]{1,0:T(1,128)S(1)}, s32[1,8]{1,0:T(1,128)}, u32[]{:S(2)}) copy-start(s32[1,8]{1,0:T(1,128)} %param.14) | copy-start | bytes 100
  1.5 22.0 %copy-start.7 = (s32[1,8]{1,0:T(1,128)S(1)}, s32[1,8]{1,0:T(1,128)}, u32[]{:S(2)}) copy-start(s32[1,8]{1,0:T(1,128)} %param.13) | copy-start | bytes 100
  1.5 35.0 %copy-start = (bf16[128,1536]{1,0:T(8,128)(2,1)S(1)}, bf16[128,1536]{1,0:T(8,128)(2,1)}, u32[]{:S(2)}) copy-start(bf16[128,1536]{1,0:T(8,128)(2,1)} %queries.3) | copy-start | bytes 1179652
  1.6 42.9 %copy-start.3 = (bf16[32,1024]{1,0:T(8,128)(2,1)S(1)}, bf16[32,1024]{1,0:T(8,128)(2,1)}, u32[]{:S(2)}) copy-start(bf16[32,1024]{1,0:T(8,128)(2,1)} %cache.1) | copy-start | bytes 196612
  4.8 5.8 %collective-permute-start = (bf16[8,3072]{1,0:T(8,128)(2,1)S(1)}, bf16[8,3072]{1,0:T(8,128)(2,1)S(1)}, u32[]{:S(2)}, u32[]{:S(2)}) collective-permute-start(bf16[8,3072]{1,0:T(8,128)(2,1)S(1)} %get-tuple-element.34), channel_id=1, source_target_pairs={{0,1},{1,0},{2,3},{3,2},{4,5},{5,4},{6,7},{7,6},{8,9},{9,8},{10,11... | collective-permute-start | bytes 147464 | tf_op jit(solution)/shard_map/ppermute | solution.py:336
  7.9 5.9 %collective-permute-start.1 = (bf16[8,3072]{1,0:T(8,128)(2,1)S(1)}, bf16[8,3072]{1,0:T(8,128)(2,1)S(1)}, u32[]{:S(2)}, u32[]{:S(2)}) collective-permute-start(bf16[8,3072]{1,0:T(8,128)(2,1)S(1)} %get-tuple-element.35), channel_id=1, source_target_pairs={{0,2},{1,3},{2,0},{3,1},{4,6},{5,7},{6,4},{7,5},{8,10},{9,11},{10,... | collective-permute-start | bytes 147464 | tf_op jit(solution)/shard_map/ppermute | solution.py:336
  10.5 5.9 %collective-permute-start.2 = (bf16[8,3072]{1,0:T(8,128)(2,1)S(1)}, bf16[8,3072]{1,0:T(8,128)(2,1)S(1)}, u32[]{:S(2)}, u32[]{:S(2)}) collective-permute-start(bf16[8,3072]{1,0:T(8,128)(2,1)S(1)} %get-tuple-element.36), channel_id=1, source_target_pairs={{0,3},{1,2},{2,1},{3,0},{4,7},{5,6},{6,5},{7,4},{8,11},{9,10},{10,... | collective-permute-start | bytes 147464 | tf_op jit(solution)/shard_map/ppermute | solution.py:336
  16.4 5.3 %collective-permute-start.8 = (bf16[8,3072]{1,0:T(8,128)(2,1)S(1)}, bf16[8,3072]{1,0:T(8,128)(2,1)S(1)}, u32[]{:S(2)}, u32[]{:S(2)}) collective-permute-start(bf16[8,3072]{1,0:T(8,128)(2,1)S(1)} %add_convert_fusion.refs_0_), channel_id=1, source_target_pairs={{0,24},{4,28},{8,16},{12,20},{16,8},{20,12},{24,0},{28,4},{1,25},{... | collective-permute-start | bytes 147464 | tf_op jit(solution)/shard_map/ppermute | solution.py:336
  19.0 4.1 %collective-permute-start.6 = (bf16[8,3072]{1,0:T(8,128)(2,1)S(1)}, bf16[8,3072]{1,0:T(8,128)(2,1)S(1)}, u32[]{:S(2)}, u32[]{:S(2)}) collective-permute-start(bf16[8,3072]{1,0:T(8,128)(2,1)S(1)} %add_convert_fusion.refs_0_), channel_id=1, source_target_pairs={{0,16},{4,20},{8,24},{12,28},{16,0},{20,4},{24,8},{28,12},{1,17},{... | collective-permute-start | bytes 147464 | tf_op jit(solution)/shard_map/ppermute | solution.py:336
  19.5 4.1 %collective-permute-start.4 = (bf16[8,3072]{1,0:T(8,128)(2,1)S(1)}, bf16[8,3072]{1,0:T(8,128)(2,1)S(1)}, u32[]{:S(2)}, u32[]{:S(2)}) collective-permute-start(bf16[8,3072]{1,0:T(8,128)(2,1)S(1)} %add_convert_fusion.refs_0_), channel_id=1, source_target_pairs={{0,8},{4,12},{8,0},{12,4},{16,24},{20,28},{24,16},{28,20},{1,9},{5... | collective-permute-start | bytes 147464 | tf_op jit(solution)/shard_map/ppermute | solution.py:336
  20.0 3.6 %collective-permute-start.3 = (bf16[8,3072]{1,0:T(8,128)(2,1)S(1)}, bf16[8,3072]{1,0:T(8,128)(2,1)S(1)}, u32[]{:S(2)}, u32[]{:S(2)}) collective-permute-start(bf16[8,3072]{1,0:T(8,128)(2,1)S(1)} %add_convert_fusion.refs_0_), channel_id=1, source_target_pairs={{0,4},{4,0},{8,12},{12,8},{16,20},{20,16},{24,28},{28,24},{1,5},{5... | collective-permute-start | bytes 147464 | tf_op jit(solution)/shard_map/ppermute | solution.py:336
  21.7 1.9 %collective-permute-start.9 = (bf16[8,3072]{1,0:T(8,128)(2,1)S(1)}, bf16[8,3072]{1,0:T(8,128)(2,1)S(1)}, u32[]{:S(2)}, u32[]{:S(2)}) collective-permute-start(bf16[8,3072]{1,0:T(8,128)(2,1)S(1)} %collective-permute-done.8.refs_6_), channel_id=1, source_target_pairs={{0,4},{4,0},{8,12},{12,8},{16,20},{20,16},{24,28},{28,24},{1,5},{5... | collective-permute-start | bytes 147464 | tf_op jit(solution)/shard_map/ppermute | solution.py:336
  23.0 1.2 %collective-permute-start.7 = (bf16[8,3072]{1,0:T(8,128)(2,1)S(1)}, bf16[8,3072]{1,0:T(8,128)(2,1)S(1)}, u32[]{:S(2)}, u32[]{:S(2)}) collective-permute-start(bf16[8,3072]{1,0:T(8,128)(2,1)S(1)} %collective-permute-done.6.refs_4_), channel_id=1, source_target_pairs={{0,4},{4,0},{8,12},{12,8},{16,20},{20,16},{24,28},{28,24},{1,5},{5... | collective-permute-start | bytes 147464 | tf_op jit(solution)/shard_map/ppermute | solution.py:336
  23.6 1.2 %collective-permute-start.5 = (bf16[8,3072]{1,0:T(8,128)(2,1)S(1)}, bf16[8,3072]{1,0:T(8,128)(2,1)S(1)}, u32[]{:S(2)}, u32[]{:S(2)}) collective-permute-start(bf16[8,3072]{1,0:T(8,128)(2,1)S(1)} %collective-permute-done.4.refs_2_), channel_id=1, source_target_pairs={{0,4},{4,0},{8,12},{12,8},{16,20},{20,16},{24,28},{28,24},{1,5},{5... | collective-permute-start | bytes 147464 | tf_op jit(solution)/shard_map/ppermute | solution.py:336
  25.6 6.1 %collective-permute-start.10 = (bf16[16,3072]{1,0:T(8,128)(2,1)S(1)}, bf16[16,3072]{1,0:T(8,128)(2,1)S(1)}, u32[]{:S(2)}, u32[]{:S(2)}) collective-permute-start(bf16[16,3072]{1,0:T(8,128)(2,1)S(1)} %get-tuple-element.38), channel_id=1, source_target_pairs={{0,1},{1,0},{2,3},{3,2},{4,5},{5,4},{6,7},{7,6},{8,9},{9,8},{10,11... | collective-permute-start | bytes 294920 | tf_op jit(solution)/shard_map/ppermute | solution.py:336
  25.7 10.9 %collective-permute-start.11 = (bf16[16,3072]{1,0:T(8,128)(2,1)S(1)}, bf16[16,3072]{1,0:T(8,128)(2,1)S(1)}, u32[]{:S(2)}, u32[]{:S(2)}) collective-permute-start(bf16[16,3072]{1,0:T(8,128)(2,1)S(1)} %get-tuple-element.39), channel_id=1, source_target_pairs={{0,2},{1,3},{2,0},{3,1},{4,6},{5,7},{6,4},{7,5},{8,10},{9,11},{10,... | collective-permute-start | bytes 294920 | tf_op jit(solution)/shard_map/ppermute | solution.py:336
  27.0 9.6 %collective-permute-start.12 = (bf16[16,3072]{1,0:T(8,128)(2,1)S(1)}, bf16[16,3072]{1,0:T(8,128)(2,1)S(1)}, u32[]{:S(2)}, u32[]{:S(2)}) collective-permute-start(bf16[16,3072]{1,0:T(8,128)(2,1)S(1)} %get-tuple-element.40), channel_id=1, source_target_pairs={{0,3},{1,2},{2,1},{3,0},{4,7},{5,6},{6,5},{7,4},{8,11},{9,10},{10,... | collective-permute-start | bytes 294920 | tf_op jit(solution)/shard_map/ppermute | solution.py:336
  38.3 17.1 %collective-permute-start.13 = (bf16[64,1536]{1,0:T(8,128)(2,1)S(1)}, bf16[64,1536]{1,0:T(8,128)(2,1)S(1)}, u32[]{:S(2)}, u32[]{:S(2)}) collective-permute-start(bf16[64,1536]{1,0:T(8,128)(2,1)S(1)} %get-tuple-element.59.grad_values.refs_1_), channel_id=1, source_target_pairs={{0,2},{1,3},{2,0},{3,1},{4,6},{5,7},{6,4},{7,5},{8,10},{9,11},{10,... | collective-permute-start | bytes 589832 | tf_op jit(solution)/shard_map/ppermute | solution.py:336
  41.6 15.7 %collective-permute-start.17 = (bf16[64,1536]{1,0:T(8,128)(2,1)S(1)}, bf16[64,1536]{1,0:T(8,128)(2,1)S(1)}, u32[]{:S(2)}, u32[]{:S(2)}) collective-permute-start(bf16[64,1536]{1,0:T(8,128)(2,1)S(1)} %get-tuple-element.54.refs_1_), channel_id=1, source_target_pairs={{0,2},{1,3},{2,0},{3,1},{4,6},{5,7},{6,4},{7,5},{8,10},{9,11},{10,... | collective-permute-start | bytes 589832 | tf_op jit(solution)/shard_map/ppermute | solution.py:336
  42.6 24.4 %collective-permute-start.14 = (bf16[64,3072]{1,0:T(8,128)(2,1)S(1)}, bf16[64,3072]{1,0:T(8,128)(2,1)S(1)}, u32[]{:S(2)}, u32[]{:S(2)}) collective-permute-start(bf16[64,3072]{1,0:T(8,128)(2,1)S(1)} %get-tuple-element.52), channel_id=1, source_target_pairs={{0,1},{1,0},{2,3},{3,2},{4,5},{5,4},{6,7},{7,6},{8,9},{9,8},{10,11... | collective-permute-start | bytes 1179656 | tf_op jit(solution)/shard_map/ppermute | solution.py:363
  55.4 14.0 %collective-permute-start.15 = (bf16[64,3072]{1,0:T(8,128)(2,1)S(1)}, bf16[64,3072]{1,0:T(8,128)(2,1)S(1)}, u32[]{:S(2)}, u32[]{:S(2)}) collective-permute-start(bf16[64,3072]{1,0:T(8,128)(2,1)S(1)} %get-tuple-element.52), channel_id=1, source_target_pairs={{1,2},{2,1},{5,6},{6,5},{9,10},{10,9},{13,14},{14,13},{17,18},{18,... | collective-permute-start | bytes 1179656 | tf_op jit(solution)/shard_map/ppermute | solution.py:367
  57.3 9.7 %collective-permute-start.18 = (bf16[64,1536]{1,0:T(8,128)(2,1)S(1)}, bf16[64,1536]{1,0:T(8,128)(2,1)S(1)}, u32[]{:S(2)}, u32[]{:S(2)}) collective-permute-start(bf16[64,1536]{1,0:T(8,128)(2,1)S(1)} %collective-permute-done.17.refs_3_), channel_id=1, source_target_pairs={{1,0},{2,3},{5,4},{6,7},{9,8},{10,11},{13,12},{14,15},{17,16},{18,... | collective-permute-start | bytes 589832 | tf_op jit(solution)/shard_map/ppermute | solution.py:365
  58.6 10.7 %collective-permute-start.16 = (bf16[64,1536]{1,0:T(8,128)(2,1)S(1)}, bf16[64,1536]{1,0:T(8,128)(2,1)S(1)}, u32[]{:S(2)}, u32[]{:S(2)}) collective-permute-start(bf16[64,1536]{1,0:T(8,128)(2,1)S(1)} %collective-permute-done.13.refs_3_), channel_id=1, source_target_pairs={{1,0},{2,3},{5,4},{6,7},{9,8},{10,11},{13,12},{14,15},{17,16},{18,... | collective-permute-start | bytes 589832 | tf_op jit(solution)/shard_map/ppermute | solution.py:365

commit v3 on v2

--- a/solution.py
+++ b/solution.py
@@ -105,11 +105,14 @@
         ],
         compiler_params=kernel_params(),
         name="project",
-    )(text_cache, w_kv)
-
-
-def select_kernel(groups, each, paired, dp_paired, table, *refs):
-    pieces, outs = refs[:-groups], refs[-groups:]
+    )(pltpu.with_memory_space_constraint(text_cache, pltpu.HBM), w_kv)
+
+
+def select_kernel(groups, each, paired, dp_paired, n_texts, table, *refs):
+    texts, pieces, outs, chip_text = refs[:n_texts], refs[n_texts : -groups - 1], refs[-groups - 1 : -1], refs[-1]
+    depth = texts[0].shape[0]
+    for i, text in enumerate(texts):
+        chip_text[i * depth : (i + 1) * depth] = text[...]
     held = jnp.concatenate([piece[...] for piece in pieces], axis=0) if len(pieces) > 1 else pieces[0][...]
     total = held.shape[0]
     index, member = table[3, 0], table[3, 1]
@@ -132,16 +135,18 @@
         outs[k][...] = rows[k * size : (k + 1) * size]
 
 
-def select_rows(groups, each, paired, dp_paired, table, pieces):
+def select_rows(groups, each, paired, dp_paired, table, texts, pieces):
     width = pieces[0].shape[1]
-    return pl.pallas_call(
-        functools.partial(select_kernel, groups, each, paired, dp_paired),
-        in_specs=[SMEM_SPEC] + [VMEM_SPEC] * len(pieces),
-        out_specs=[VMEM_SPEC] * groups,
-        out_shape=[jax.ShapeDtypeStruct((SAMPLES * each, width), BF16)] * groups,
+    depth, features = texts[0].shape
+    return pl.pallas_call(
+        functools.partial(select_kernel, groups, each, paired, dp_paired, len(texts)),
+        in_specs=[SMEM_SPEC] + [VMEM_SPEC] * (len(texts) + len(pieces)),
+        out_specs=[VMEM_SPEC] * (groups + 1),
+        out_shape=[jax.ShapeDtypeStruct((SAMPLES * each, width), BF16)] * groups
+        + [jax.ShapeDtypeStruct((len(texts) * depth, features), BF16)],
         compiler_params=kernel_params(),
         name="select_rows",
-    )(table, *pieces)
+    )(table, *texts, *pieces)
 
 
 LAST = (((1,), (1,)), ((), ()))
@@ -248,11 +253,9 @@
     )(probs, queries, grad_out, grad_values, *pieces)
 
 
-def text_kernel(groups, each, depth, paired, dp_paired, table, *refs):
-    texts, out = refs[:-1], refs[-1]
+def text_kernel(groups, each, depth, paired, dp_paired, table, text, out):
     index, member = table[3, 0], table[3, 1]
-    held = jnp.concatenate([text[...] for text in texts], axis=0) if len(texts) > 1 else texts[0][...]
-    shape = (held.shape[0], out.shape[1])
+    shape = (text.shape[0], out.shape[1])
     columns = lax.broadcasted_iota(jnp.int32, shape, 1)
     runs, place = columns // each, columns % each
     target = jnp.zeros(shape, jnp.int32)
@@ -266,70 +269,79 @@
                 caption = device * SAMPLES + s
                 offset = table[2, caption]
                 owner = table[1, caption]
-                base = (owner ^ index if dp_paired else owner) * depth
+                if dp_paired:
+                    owner = owner - (owner & 1) + ((owner ^ index) & 1)
+                base = owner * depth
                 here = runs == run
                 target = jnp.where(here, base + groups * first_of_class(offset, residue, groups) + residue, target)
                 limit = jnp.where(here, base + offset + table[0, caption], limit)
                 run += 1
     target = target + groups * place
     chosen = ((target == lax.broadcasted_iota(jnp.int32, shape, 0)) & (target < limit)).astype(BF16)
-    out[...] = lax.dot_general(held, chosen, FIRST, preferred_element_type=F32).astype(BF16)
-
-
-def slot_texts(groups, each, depth, paired, dp_paired, table, texts):
-    features = texts[0].shape[1]
+    out[...] = lax.dot_general(text[...], chosen, FIRST, preferred_element_type=F32).astype(BF16)
+
+
+def slot_texts(groups, each, depth, paired, dp_paired, table, text):
+    features = text.shape[1]
     return pl.pallas_call(
         functools.partial(text_kernel, groups, each, depth, paired, dp_paired),
-        in_specs=[SMEM_SPEC] + [VMEM_SPEC] * len(texts),
+        in_specs=[SMEM_SPEC, VMEM_SPEC],
         out_specs=VMEM_SPEC,
         out_shape=jax.ShapeDtypeStruct((features, groups * groups * SAMPLES * each), BF16),
         compiler_params=kernel_params(),
         name="slot_texts",
-    )(table, *texts)
-
-
-def weight_kernel(line, first, block, started, *refs):
-    chosen_text, *grads = refs[: -4 if started else -3]
-    out, built, sems = refs[-3:]
-    part = built.shape[1]
+    )(table, text)
+
+
+def weight_kernel(line, blocks, *refs):
+    chosen_text, *grads = refs[:-4]
+    out, every, built, sems = refs[-4:]
+    halves = [grads[: len(grads) // 2], grads[len(grads) // 2 :]]
+    width = every.shape[1] // 2
     if line:
         member = lax.axis_index("fsdp")
         is_inner = (member == 1) | (member == 2)
+        each = every.shape[0] // 4
+    for i, half in enumerate(halves):
+        at = slice(i * width, (i + 1) * width)
+        if line:
+            own, near, second, inner, outer = half
+            every[0:each, at] = own[...]
+            every[each : 2 * each, at] = near[:, at]
+            every[2 * each : 3 * each, at] = second[...]
+            every[3 * each :, at] = jnp.where(is_inner, inner[:, at], outer[...])
+        else:
+            every[:, at] = half[0][...]
+    rows = built.shape[0] // blocks
     copies = []
-    for i in range(part // block):
-        at = slice(i * block, (i + 1) * block)
-        if line:
-            own, near, second, inner, outer = [g[:, at] for g in grads]
-            every = jnp.concatenate([own, near, second, jnp.where(is_inner, inner, outer)], axis=0)
-        else:
-            every = grads[0][:, at]
-        built[:, at] = jnp.dot(chosen_text[...], every, preferred_element_type=F32).astype(BF16)
-        copy = pltpu.make_async_copy(
-            built.at[:, pl.ds(i * block, block)], out.at[:, pl.ds(first + i * block, block)], sems.at[i]
-        )
+    for i in range(blocks):
+        at = slice(i * rows, (i + 1) * rows)
+        built[at] = jnp.dot(chosen_text[at], every[...], preferred_element_type=F32).astype(BF16)
+        copy = pltpu.make_async_copy(built.at[pl.ds(i * rows, rows)], out.at[pl.ds(i * rows, rows)], sems.at[i])
         copy.start()
         copies.append(copy)
     for copy in copies:
         copy.wait()
 
 
-def weight_grad(line, chosen_text, grads, width, first, before=None):
+def weight_grad(line, chosen_text, first_parts, second_parts):
     features, slots = chosen_text.shape
-    part = grads[0].shape[1]
-    block = 256
-    started = before is not None
-    parts = [pl.BlockSpec((g.shape[0], part), lambda n, at=first // part * (g.shape[1] > part): (0, at)) for g in grads]
-    return pl.pallas_call(
-        functools.partial(weight_kernel, line, first, block, started),
-        grid=(1,),
-        in_specs=[pl.BlockSpec((features, slots), lambda n: (0, 0))] + parts + [ANY_SPEC] * started,
+    width = first_parts[0].shape[1] * 2
+    grads = [*first_parts, *second_parts]
+    blocks = 8
+    return pl.pallas_call(
+        functools.partial(weight_kernel, line, blocks),
+        in_specs=[VMEM_SPEC] * (1 + len(grads)),
         out_specs=ANY_SPEC,
         out_shape=jax.ShapeDtypeStruct((features, width), BF16),
-        scratch_shapes=[pltpu.VMEM((features, part), BF16), pltpu.SemaphoreType.DMA((part // block,))],
-        input_output_aliases={1 + len(grads): 0} if started else {},
+        scratch_shapes=[
+            pltpu.VMEM((slots, width), BF16),
+            pltpu.VMEM((features, width), BF16),
+            pltpu.SemaphoreType.DMA((blocks,)),
+        ],
         compiler_params=kernel_params(),
         name="weight_gradient",
-    )(chosen_text, *grads, *([before] if started else []))
+    )(chosen_text, *grads)
 
 
 def swap(x, axis, k):
@@ -347,9 +359,16 @@
     return [near[k] for k in sorted(near)]
 
 
+def gather_chips(x):
+    size = lax.axis_size("dp")
+    cores = [list(range(core, size, 2)) for core in range(2)]
+    return lax.all_gather(x, "dp", axis=0, tiled=True, axis_index_groups=cores)
+
+
 def exchange(pieces, paired):
     if paired:
-        return [pieces[0]] + [swap(pieces[k], "fsdp", k) for k in range(1, len(pieces))]
+        far_first = {k: swap(pieces[k], "fsdp", k) for k in (*range(2, len(pieces)), 1)}
+        return [pieces[0]] + [far_first[k] for k in range(1, len(pieces))]
     came = lax.all_to_all(jnp.stack(pieces), "fsdp", 0, 0, tiled=True)
     return [came[k] for k in range(len(pieces))]
 
@@ -381,27 +400,30 @@
     width = queries.shape[1]
 
     partials = project(groups, paired, text_cache, w_kv)
+    partials, late_cache = lax.optimization_barrier((partials, text_cache))
+    texts = [late_cache, swap(late_cache, "dp", 1)] if dp_paired else [late_cache]
     came = exchange(partials, paired)
     table = scalar_table(image_counts, caption_lens, caption_owner, caption_offset)
     rows = sum(piece.astype(F32) for piece in came).astype(BF16)
     class_rows = gather_dp(rows, dp_paired)
-    outgoing = select_rows(groups, each, paired, dp_paired, table, class_rows)
+    *outgoing, chip_text = select_rows(groups, each, paired, dp_paired, table, texts, class_rows)
     keys_values = exchange(outgoing, paired)
     probs, _, grad_values = value_grads(groups, each, paired, table, queries, grad_out, keys_values)
     grad_values, probs = lax.optimization_barrier((grad_values, probs))
     grad_query, grad_keys, grad_both = key_grads(groups, probs, queries, grad_out, grad_values, keys_values)
-    grad_keys, grad_both, late_cache = lax.optimization_barrier((grad_keys, grad_both, text_cache))
-    texts = [lax.all_gather(late_cache, "dp", axis=0, tiled=True)]
-    chosen_text = slot_texts(groups, each, depth, paired, False, table, texts)
+    grad_keys, grad_both, chip_text = lax.optimization_barrier((grad_keys, grad_both, chip_text))
+    if dp_paired:
+        text = gather_chips(chip_text)
+    else:
+        text = lax.all_gather(chip_text, "dp", axis=0, tiled=True)
     if line:
-        value_parts, key_parts, chosen_text = gather_line(grad_values, grad_keys, grad_both, chosen_text)
+        value_parts, key_parts, text = gather_line(grad_values, grad_keys, grad_both, text)
     else:
         value_parts, key_parts = [
             [lax.all_gather(half, "fsdp", axis=0, tiled=True)] for half in (grad_values, grad_keys)
         ]
-    value_parts, key_parts = lax.optimization_barrier((value_parts, key_parts))
-    grad_weight = weight_grad(line, chosen_text, value_parts, 2 * width, width)
-    grad_weight = weight_grad(line, chosen_text, key_parts, 2 * width, 0, grad_weight)
+    chosen_text = slot_texts(groups, each, depth, paired, dp_paired, table, text)
+    grad_weight = weight_grad(line, chosen_text, key_parts, value_parts)
     return grad_query, grad_weight[None]
 
 

time: 73.8 us -> 71.4 us (0.967)
  waiting for transfers between devices: 27.7 us -> 25.7 us
  local copies, waits for them, and re-layouts: 0.91 us -> 0.03 us
  blocking collectives: 9.85 us -> 10.7 us
    ppermute x2, waiting for transfers between devices: 9.44 us -> 6.05 us  [gather_line(): outer = [lax.ppermute(piece, 'fsdp', outward) for piece in second]]
    ppermute x15 -> x16, waiting for transfers between devices: 18.2 us -> 19.6 us  [swap(): lax.ppermute(x, axis, [(i, i ^ k) for i in range(lax.axis_size(axis))])]
    pallas_call x2 -> x1, Pallas kernels: 4.29 us -> 3.13 us  [weight_grad(): pl.pallas_call(functools.partial(weight_kernel, line, blocks), in_specs=[...]
    all_gather x1, blocking collectives: 9.85 us -> 10.7 us  [gather_chips(): return lax.all_gather(x, 'dp', axis=0, tiled=True, axis_index_groups=cores)]
    unnamed x16 -> x14, local copies, waits for them, and re-layouts: 0.91 us -> 0.03 us
    ppermute x15 -> x16, starting transfers between devices: 16.6 us -> 16.6 us  [swap(): lax.ppermute(x, axis, [(i, i ^ k) for i in range(lax.axis_size(axis))])]
  transfers between devices with their start and end apart: 19 -> 20, of which waited for: 12 -> 12; matrix products, arithmetic and copies ran while one was open for 0% -> 0% of each run, Pallas kernels for 3% -> 3%
where the time goes in v3:
time: 71.4 us; the launch traced here: 71.2 us
  waiting for transfers between devices  25.7 us (36%)
  starting transfers between devices  21.8 us (31%)
  Pallas kernels  12 us (17%)
  blocking collectives  10.7 us (15%)
  between operations  0.82 us (1%)
    ppermute x16, waiting for transfers between devices, swap(): lax.ppermute(x, axis, [(i, i ^ k) for i in range(lax.axis_size(axis))])  19.6 us
    ppermute x16, starting transfers between devices, swap(): lax.ppermute(x, axis, [(i, i ^ k) for i in range(lax.axis_size(axis))])  16.6 us
    all_gather x1, blocking collectives, gather_chips(): return lax.all_gather(x, 'dp', axis=0, tiled=True, axis_index_groups=cores)  10.7 us
    ppermute x2, waiting for transfers between devices, gather_line(): outer = [lax.ppermute(piece, 'fsdp', outward) for piece in second]  6.05 us
    pallas_call x1, Pallas kernels, project(): pl.pallas_call(functools.partial(project_kernel, groups, paired, chunks),...  3.92 us
    pallas_call x1, Pallas kernels, weight_grad(): pl.pallas_call(functools.partial(weight_kernel, line, blocks), in_specs=[...  3.13 us
    ppermute x2, starting transfers between devices, gather_line(): outer = [lax.ppermute(piece, 'fsdp', outward) for piece in second]  2.57 us
    ppermute x1, starting transfers between devices, gather_line(): near = lax.ppermute(both, 'fsdp', near_pairs)  1.89 us
  transfers between devices with their start and end apart: 20, of which 12 were waited for; matrix products, arithmetic and copies ran while one was open for 0% of the time, Pallas kernels for 3%

profile of v3, /device:TPU:0, one launch (start us, length us, event | category | flops | bytes accessed | tf_op | source)
XLA Modules:
  0.0 71.2 jit_solution(10414314508722568529)
XLA Ops:
  0.6 0.0 copy-start.2
  0.6 0.0 copy-start.3
  0.7 0.0 copy-start.4
  0.7 0.0 copy-start.5
  0.7 0.0 copy-start.6
  0.7 0.0 copy-start.1
  0.7 0.0 copy-start
  0.7 3.9 %project.1 = (bf16[8,3072]{1,0:T(8,128)(2,1)S(1)}, bf16[8,3072]{1,0:T(8,128)(2,1)S(1)}, bf16[8,3072]{1,0:T(8,128)(2,1)S(1)}, bf16[8,3072]{1,0:T(8,128)(2,1)S(1)}) custom-call(bf16[32,1024]{1,0:T(8,128)(2,1)} %refs_0_, bf16[1024,3072]{1,0:T(8,128)(2,1)} %weight.1), custom_call_target="tpu_custom_call" | custom-call | tf_op jit(solution)/shard_map/project/pallas_call | solution.py:95
  4.6 3.1 %collective-permute-start.1 = (bf16[8,3072]{1,0:T(8,128)(2,1)S(1)}, bf16[8,3072]{1,0:T(8,128)(2,1)S(1)}, u32[]{:S(2)}, u32[]{:S(2)}) collective-permute-start(bf16[8,3072]{1,0:T(8,128)(2,1)S(1)} %get-tuple-element.35), channel_id=1, source_target_pairs={{0,1},{1,0},{2,3},{3,2},{4,5},{5,4},{6,7},{7,6},{8,9},{9,8},{10,11... | collective-permute-start | bytes 147464 | tf_op jit(solution)/shard_map/ppermute | solution.py:348
  7.7 2.6 %collective-permute-start.2 = (bf16[8,3072]{1,0:T(8,128)(2,1)S(1)}, bf16[8,3072]{1,0:T(8,128)(2,1)S(1)}, u32[]{:S(2)}, u32[]{:S(2)}) collective-permute-start(bf16[8,3072]{1,0:T(8,128)(2,1)S(1)} %get-tuple-element.36), channel_id=1, source_target_pairs={{0,2},{1,3},{2,0},{3,1},{4,6},{5,7},{6,4},{7,5},{8,10},{9,11},{10,... | collective-permute-start | bytes 147464 | tf_op jit(solution)/shard_map/ppermute | solution.py:348
  10.3 0.0 collective-permute-start.3
  10.3 0.0 copy-done.2
  10.3 0.0 collective-permute-start
  10.3 0.0 copy-done.3
  10.3 0.1 pad_add_fusion.1
  10.4 0.0 collective-permute-done.1
  10.4 3.2 %collective-permute-done.2 = bf16[8,3072]{1,0:T(8,128)(2,1)S(1)} collective-permute-done((bf16[8,3072]{1,0:T(8,128)(2,1)S(1)}, bf16[8,3072]{1,0:T(8,128)(2,1)S(1)}, u32[]{:S(2)}, u32[]{:S(2)}) %collective-permute-start.2) | collective-permute-done | bytes 49184 | tf_op jit(solution)/shard_map/ppermute | solution.py:348
  13.6 2.6 %collective-permute-done.3 = bf16[8,3072]{1,0:T(8,128)(2,1)S(1)} collective-permute-done((bf16[8,3072]{1,0:T(8,128)(2,1)S(1)}, bf16[8,3072]{1,0:T(8,128)(2,1)S(1)}, u32[]{:S(2)}, u32[]{:S(2)}) %collective-permute-start.3) | collective-permute-done | bytes 49184 | tf_op jit(solution)/shard_map/ppermute | solution.py:348
  16.2 2.5 %collective-permute-start.9 = (bf16[8,3072]{1,0:T(8,128)(2,1)S(1)}, bf16[8,3072]{1,0:T(8,128)(2,1)S(1)}, u32[]{:S(2)}, u32[]{:S(2)}) collective-permute-start(bf16[8,3072]{1,0:T(8,128)(2,1)S(1)} %add_convert_fusion.refs_2_), channel_id=1, source_target_pairs={{0,24},{4,28},{8,16},{12,20},{16,8},{20,12},{24,0},{28,4},{1,25},{... | collective-permute-start | bytes 147464 | tf_op jit(solution)/shard_map/ppermute | solution.py:348
  18.7 0.5 collective-permute-start.7
  19.2 0.5 collective-permute-start.5
  19.8 0.0 collective-permute-start.4
  19.8 1.7 %collective-permute-done.9.refs_8_ = bf16[8,3072]{1,0:T(8,128)(2,1)S(1)} collective-permute-done((bf16[8,3072]{1,0:T(8,128)(2,1)S(1)}, bf16[8,3072]{1,0:T(8,128)(2,1)S(1)}, u32[]{:S(2)}, u32[]{:S(2)}) %collective-permute-start.9) | collective-permute-done | bytes 49184 | tf_op jit(solution)/shard_map/ppermute | solution.py:348
  21.5 0.0 collective-permute-start.10
  21.5 1.3 %collective-permute-done.7.refs_6_ = bf16[8,3072]{1,0:T(8,128)(2,1)S(1)} collective-permute-done((bf16[8,3072]{1,0:T(8,128)(2,1)S(1)}, bf16[8,3072]{1,0:T(8,128)(2,1)S(1)}, u32[]{:S(2)}, u32[]{:S(2)}) %collective-permute-start.7) | collective-permute-done | bytes 49184 | tf_op jit(solution)/shard_map/ppermute | solution.py:348
  22.8 0.0 collective-permute-start.8
  22.8 0.5 collective-permute-done.5.refs_4_
  23.3 0.0 collective-permute-start.6
  23.3 0.0 copy-done.4
  23.3 0.0 copy-done.5
  23.4 0.0 copy-done.6
  23.4 0.0 collective-permute-done.refs_1_
  23.4 0.0 collective-permute-done.4.refs_3_
  23.4 0.0 collective-permute-done.10.refs_9_
  23.4 0.7 collective-permute-done.8.refs_7_
  24.1 0.5 collective-permute-done.6.refs_5_
  24.6 0.8 %select_rows.1 = (bf16[16,3072]{1,0:T(8,128)(2,1)S(1)}, bf16[16,3072]{1,0:T(8,128)(2,1)S(1)}, bf16[16,3072]{1,0:T(8,128)(2,1)S(1)}, bf16[16,3072]{1,0:T(8,128)(2,1)S(1)}, bf16[64,1024]{1,0:T(8,128)(2,1)S(1)}) custom-call(s32[4,8]{1,0:T(4,128)S(1)} %pad_add_fusion.table, bf16[32,1024]{1,0:T(8,128)(2,1)S(1)} %copy-done.2, ...), custom_call_target="tpu_custom_call" | custom-call | tf_op jit(solution)/shard_map/select_rows/pallas_call | solution.py:141
  25.4 0.1 collective-permute-start.11
  25.5 1.3 %collective-permute-start.12 = (bf16[16,3072]{1,0:T(8,128)(2,1)S(1)}, bf16[16,3072]{1,0:T(8,128)(2,1)S(1)}, u32[]{:S(2)}, u32[]{:S(2)}) collective-permute-start(bf16[16,3072]{1,0:T(8,128)(2,1)S(1)} %get-tuple-element.40), channel_id=1, source_target_pairs={{0,2},{1,3},{2,0},{3,1},{4,6},{5,7},{6,4},{7,5},{8,10},{9,11},{10,... | collective-permute-start | bytes 294920 | tf_op jit(solution)/shard_map/ppermute | solution.py:348
  26.8 3.1 %collective-permute-start.13 = (bf16[16,3072]{1,0:T(8,128)(2,1)S(1)}, bf16[16,3072]{1,0:T(8,128)(2,1)S(1)}, u32[]{:S(2)}, u32[]{:S(2)}) collective-permute-start(bf16[16,3072]{1,0:T(8,128)(2,1)S(1)} %get-tuple-element.41), channel_id=1, source_target_pairs={{0,3},{1,2},{2,1},{3,0},{4,7},{5,6},{6,5},{7,4},{8,11},{9,10},{10,... | collective-permute-start | bytes 294920 | tf_op jit(solution)/shard_map/ppermute | solution.py:348
  29.9 1.7 %collective-permute-done.11.refs_1_ = bf16[16,3072]{1,0:T(8,128)(2,1)S(1)} collective-permute-done((bf16[16,3072]{1,0:T(8,128)(2,1)S(1)}, bf16[16,3072]{1,0:T(8,128)(2,1)S(1)}, u32[]{:S(2)}, u32[]{:S(2)}) %collective-permute-start.11) | collective-permute-done | bytes 98336 | tf_op jit(solution)/shard_map/ppermute | solution.py:348
  31.5 4.8 %collective-permute-done.12.refs_2_ = bf16[16,3072]{1,0:T(8,128)(2,1)S(1)} collective-permute-done((bf16[16,3072]{1,0:T(8,128)(2,1)S(1)}, bf16[16,3072]{1,0:T(8,128)(2,1)S(1)}, u32[]{:S(2)}, u32[]{:S(2)}) %collective-permute-start.12) | collective-permute-done | bytes 98336 | tf_op jit(solution)/shard_map/ppermute | solution.py:348
  36.4 0.0 collective-permute-done.13.refs_3_
  36.4 0.0 copy-done.1
  36.4 0.0 copy-done
  36.4 1.7 %value_gradients.1 = (f32[12,64,128]{2,1,0:T(8,128)S(1)}, bf16[12,64,128]{2,1,0:T(8,128)(2,1)}, bf16[64,1536]{1,0:T(8,128)(2,1)S(1)}) custom-call(s32[4,8]{1,0:T(4,128)S(1)} %pad_add_fusion.table, bf16[128,1536]{1,0:T(8,128)(2,1)S(1)} %copy-done, bf16[128,1536]{1,0:T(8,128)(2,1)S(1)} %copy-done.1, bf16[16,3072]{1,0:T(8,128)(2,1)S(1)} %get-tuple-element.38.refs_0_, ...), custom_call_target="tpu_custom_call" | custom-call | tf_op jit(solution)/shard_map/value_gradients/pallas_call | solution.py:199
  38.1 1.9 %collective-permute-start.14 = (bf16[64,1536]{1,0:T(8,128)(2,1)S(1)}, bf16[64,1536]{1,0:T(8,128)(2,1)S(1)}, u32[]{:S(2)}, u32[]{:S(2)}) collective-permute-start(bf16[64,1536]{1,0:T(8,128)(2,1)S(1)} %get-tuple-element.45.grad_values.refs_6_), channel_id=1, source_target_pairs={{0,2},{1,3},{2,0},{3,1},{4,6},{5,7},{6,4},{7,5},{8,10},{9,11},{10,... | collective-permute-start | bytes 589832 | tf_op jit(solution)/shard_map/ppermute | solution.py:348
  40.0 1.4 %key_gradients.1 = (bf16[128,1536]{1,0:T(8,128)(2,1)}, bf16[64,1536]{1,0:T(8,128)(2,1)S(1)}, bf16[64,3072]{1,0:T(8,128)(2,1)S(1)}) custom-call(f32[12,64,128]{2,1,0:T(8,128)S(1)} %get-tuple-element.44.probs, bf16[128,1536]{1,0:T(8,128)(2,1)S(1)} %copy-done, bf16[128,1536]{1,0:T(8,128)(2,1)S(1)} %copy-done.1, ...), custom_call_target="tpu_custom_call" | custom-call | tf_op jit(solution)/shard_map/key_gradients/pallas_call | solution.py:241
  41.4 1.1 %collective-permute-start.16 = (bf16[64,1536]{1,0:T(8,128)(2,1)S(1)}, bf16[64,1536]{1,0:T(8,128)(2,1)S(1)}, u32[]{:S(2)}, u32[]{:S(2)}) collective-permute-start(bf16[64,1536]{1,0:T(8,128)(2,1)S(1)} %get-tuple-element.52.refs_1_), channel_id=1, source_target_pairs={{0,2},{1,3},{2,0},{3,1},{4,6},{5,7},{6,4},{7,5},{8,10},{9,11},{10,... | collective-permute-start | bytes 589832 | tf_op jit(solution)/shard_map/ppermute | solution.py:348
  42.4 1.9 %collective-permute-start.15 = (bf16[64,3072]{1,0:T(8,128)(2,1)S(1)}, bf16[64,3072]{1,0:T(8,128)(2,1)S(1)}, u32[]{:S(2)}, u32[]{:S(2)}) collective-permute-start(bf16[64,3072]{1,0:T(8,128)(2,1)S(1)} %get-tuple-element.55), channel_id=1, source_target_pairs={{0,1},{1,0},{2,3},{3,2},{4,5},{5,4},{6,7},{7,6},{8,9},{9,8},{10,11... | collective-permute-start | bytes 1179656 | tf_op jit(solution)/shard_map/ppermute | solution.py:382
  44.3 10.7 %all_gather.3.text = bf16[256,1024]{1,0:T(8,128)(2,1)S(1)} all-gather(bf16[64,1024]{1,0:T(8,128)(2,1)S(1)} %get-tuple-element.50), channel_id=1, replica_groups={{0,8,16,24},{4,12,20,28},{1,9,17,25},{5,13,21,29},{2,10,18,26},{6,14,22..., dimensions={0}, use_global_device_ids=true | all-gather | bytes 655360 | tf_op jit(solution)/shard_map/all_gather | solution.py:365
  55.0 0.0 collective-permute-done.14.refs_8_
  55.0 0.7 collective-permute-start.17
  55.7 2.7 %collective-permute-done.16.refs_3_ = bf16[64,1536]{1,0:T(8,128)(2,1)S(1)} collective-permute-done((bf16[64,1536]{1,0:T(8,128)(2,1)S(1)}, bf16[64,1536]{1,0:T(8,128)(2,1)S(1)}, u32[]{:S(2)}, u32[]{:S(2)}) %collective-permute-start.16) | collective-permute-done | bytes 196640 | tf_op jit(solution)/shard_map/ppermute | solution.py:348
  58.4 1.3 %collective-permute-start.18 = (bf16[64,1536]{1,0:T(8,128)(2,1)S(1)}, bf16[64,1536]{1,0:T(8,128)(2,1)S(1)}, u32[]{:S(2)}, u32[]{:S(2)}) collective-permute-start(bf16[64,1536]{1,0:T(8,128)(2,1)S(1)} %collective-permute-done.16.refs_3_), channel_id=1, source_target_pairs={{1,0},{2,3},{5,4},{6,7},{9,8},{10,11},{13,12},{14,15},{17,16},{18,... | collective-permute-start | bytes 589832 | tf_op jit(solution)/shard_map/ppermute | solution.py:384
  59.7 1.3 %collective-permute-start.19 = (bf16[64,1536]{1,0:T(8,128)(2,1)S(1)}, bf16[64,1536]{1,0:T(8,128)(2,1)S(1)}, u32[]{:S(2)}, u32[]{:S(2)}) collective-permute-start(bf16[64,1536]{1,0:T(8,128)(2,1)S(1)} %collective-permute-done.14.refs_8_), channel_id=1, source_target_pairs={{1,0},{2,3},{5,4},{6,7},{9,8},{10,11},{13,12},{14,15},{17,16},{18,... | collective-permute-start | bytes 589832 | tf_op jit(solution)/shard_map/ppermute | solution.py:384
  61.0 1.0 %slot_texts.1.refs_0_ = bf16[1024,256]{1,0:T(8,128)(2,1)S(1)} custom-call(s32[4,8]{1,0:T(4,128)S(1)} %pad_add_fusion.table, bf16[256,1024]{1,0:T(8,128)(2,1)S(1)} %all_gather.3.text), custom_call_target="tpu_custom_call" | custom-call | tf_op jit(solution)/shard_map/slot_texts/pallas_call | solution.py:286
  62.0 3.9 %collective-permute-done.18.refs_5_ = bf16[64,1536]{1,0:T(8,128)(2,1)S(1)} collective-permute-done((bf16[64,1536]{1,0:T(8,128)(2,1)S(1)}, bf16[64,1536]{1,0:T(8,128)(2,1)S(1)}, u32[]{:S(2)}, u32[]{:S(2)}) %collective-permute-start.18) | collective-permute-done | bytes 196640 | tf_op jit(solution)/shard_map/ppermute | solution.py:384
  65.9 2.1 %collective-permute-done.19.refs_10_ = bf16[64,1536]{1,0:T(8,128)(2,1)S(1)} collective-permute-done((bf16[64,1536]{1,0:T(8,128)(2,1)S(1)}, bf16[64,1536]{1,0:T(8,128)(2,1)S(1)}, u32[]{:S(2)}, u32[]{:S(2)}) %collective-permute-start.19) | collective-permute-done | bytes 196640 | tf_op jit(solution)/shard_map/ppermute | solution.py:384
  68.1 0.0 collective-permute-done.15.refs_2_.refs_7_
  68.1 0.0 collective-permute-done.17.refs_4_.refs_9_
  68.1 3.1 %weight_gradient.1 = bf16[1024,3072]{1,0:T(8,128)(2,1)} custom-call(bf16[1024,256]{1,0:T(8,128)(2,1)S(1)} %slot_texts.1.refs_0_, bf16[64,1536]{1,0:T(8,128)(2,1)S(1)} %get-tuple-element.52.refs_1_, bf16[64,3072]{1,0:T(8,128)(2,1)S(1)} %collective-permute-done.15.refs_2_.refs_7_, bf16[64,1536]{1,0:T(8,128)(2,1)S(1)} %collective-permute-done.16.refs_3_, ...), custom_call_target="tpu_custom_call" | custom-call | tf_op jit(solution)/shard_map/weight_gradient/pallas_call | solution.py:332
  (3 shorter events, 0.0 us)
Async XLA Ops:
  0.6 9.7 %copy-start.2 = (bf16[32,1024]{1,0:T(8,128)(2,1)S(1)}, bf16[32,1024]{1,0:T(8,128)(2,1)}, u32[]{:S(2)}) copy-start(bf16[32,1024]{1,0:T(8,128)(2,1)} %refs_0_) | copy-start | bytes 196612
  0.6 9.7 %copy-start.3 = (s32[1,2]{1,0:T(1,128)S(1)}, s32[1,2]{1,0:T(1,128)}, u32[]{:S(2)}) copy-start(s32[1,2]{1,0:T(1,128)} %param.12) | copy-start | bytes 28
  0.7 22.7 %copy-start.4 = (s32[1,8]{1,0:T(1,128)S(1)}, s32[1,8]{1,0:T(1,128)}, u32[]{:S(2)}) copy-start(s32[1,8]{1,0:T(1,128)} %param.15) | copy-start | bytes 100
  0.7 22.7 %copy-start.5 = (s32[1,8]{1,0:T(1,128)S(1)}, s32[1,8]{1,0:T(1,128)}, u32[]{:S(2)}) copy-start(s32[1,8]{1,0:T(1,128)} %param.14) | copy-start | bytes 100
  0.7 22.7 %copy-start.6 = (s32[1,8]{1,0:T(1,128)S(1)}, s32[1,8]{1,0:T(1,128)}, u32[]{:S(2)}) copy-start(s32[1,8]{1,0:T(1,128)} %param.13) | copy-start | bytes 100
  0.7 35.7 %copy-start.1 = (bf16[128,1536]{1,0:T(8,128)(2,1)S(1)}, bf16[128,1536]{1,0:T(8,128)(2,1)}, u32[]{:S(2)}) copy-start(bf16[128,1536]{1,0:T(8,128)(2,1)} %cotangent.3) | copy-start | bytes 1179652
  0.7 35.7 %copy-start = (bf16[128,1536]{1,0:T(8,128)(2,1)S(1)}, bf16[128,1536]{1,0:T(8,128)(2,1)}, u32[]{:S(2)}) copy-start(bf16[128,1536]{1,0:T(8,128)(2,1)} %queries.3) | copy-start | bytes 1179652
  4.6 5.8 %collective-permute-start.1 = (bf16[8,3072]{1,0:T(8,128)(2,1)S(1)}, bf16[8,3072]{1,0:T(8,128)(2,1)S(1)}, u32[]{:S(2)}, u32[]{:S(2)}) collective-permute-start(bf16[8,3072]{1,0:T(8,128)(2,1)S(1)} %get-tuple-element.35), channel_id=1, source_target_pairs={{0,1},{1,0},{2,3},{3,2},{4,5},{5,4},{6,7},{7,6},{8,9},{9,8},{10,11... | collective-permute-start | bytes 147464 | tf_op jit(solution)/shard_map/ppermute | solution.py:348
  7.7 5.9 %collective-permute-start.2 = (bf16[8,3072]{1,0:T(8,128)(2,1)S(1)}, bf16[8,3072]{1,0:T(8,128)(2,1)S(1)}, u32[]{:S(2)}, u32[]{:S(2)}) collective-permute-start(bf16[8,3072]{1,0:T(8,128)(2,1)S(1)} %get-tuple-element.36), channel_id=1, source_target_pairs={{0,2},{1,3},{2,0},{3,1},{4,6},{5,7},{6,4},{7,5},{8,10},{9,11},{10,... | collective-permute-start | bytes 147464 | tf_op jit(solution)/shard_map/ppermute | solution.py:348
  10.3 5.9 %collective-permute-start.3 = (bf16[8,3072]{1,0:T(8,128)(2,1)S(1)}, bf16[8,3072]{1,0:T(8,128)(2,1)S(1)}, u32[]{:S(2)}, u32[]{:S(2)}) collective-permute-start(bf16[8,3072]{1,0:T(8,128)(2,1)S(1)} %get-tuple-element.37), channel_id=1, source_target_pairs={{0,3},{1,2},{2,1},{3,0},{4,7},{5,6},{6,5},{7,4},{8,11},{9,10},{10,... | collective-permute-start | bytes 147464 | tf_op jit(solution)/shard_map/ppermute | solution.py:348
  10.3 13.1 %collective-permute-start = (bf16[32,1024]{1,0:T(8,128)(2,1)S(1)}, bf16[32,1024]{1,0:T(8,128)(2,1)S(1)}, u32[]{:S(2)}, u32[]{:S(2)}) collective-permute-start(bf16[32,1024]{1,0:T(8,128)(2,1)S(1)} %copy-done.2), channel_id=1, source_target_pairs={{0,4},{4,0},{8,12},{12,8},{16,20},{20,16},{24,28},{28,24},{1,5},{5... | collective-permute-start | bytes 196616 | tf_op jit(solution)/shard_map/ppermute | solution.py:348
  16.2 5.3 %collective-permute-start.9 = (bf16[8,3072]{1,0:T(8,128)(2,1)S(1)}, bf16[8,3072]{1,0:T(8,128)(2,1)S(1)}, u32[]{:S(2)}, u32[]{:S(2)}) collective-permute-start(bf16[8,3072]{1,0:T(8,128)(2,1)S(1)} %add_convert_fusion.refs_2_), channel_id=1, source_target_pairs={{0,24},{4,28},{8,16},{12,20},{16,8},{20,12},{24,0},{28,4},{1,25},{... | collective-permute-start | bytes 147464 | tf_op jit(solution)/shard_map/ppermute | solution.py:348
  18.7 4.1 %collective-permute-start.7 = (bf16[8,3072]{1,0:T(8,128)(2,1)S(1)}, bf16[8,3072]{1,0:T(8,128)(2,1)S(1)}, u32[]{:S(2)}, u32[]{:S(2)}) collective-permute-start(bf16[8,3072]{1,0:T(8,128)(2,1)S(1)} %add_convert_fusion.refs_2_), channel_id=1, source_target_pairs={{0,16},{4,20},{8,24},{12,28},{16,0},{20,4},{24,8},{28,12},{1,17},{... | collective-permute-start | bytes 147464 | tf_op jit(solution)/shard_map/ppermute | solution.py:348
  19.2 4.1 %collective-permute-start.5 = (bf16[8,3072]{1,0:T(8,128)(2,1)S(1)}, bf16[8,3072]{1,0:T(8,128)(2,1)S(1)}, u32[]{:S(2)}, u32[]{:S(2)}) collective-permute-start(bf16[8,3072]{1,0:T(8,128)(2,1)S(1)} %add_convert_fusion.refs_2_), channel_id=1, source_target_pairs={{0,8},{4,12},{8,0},{12,4},{16,24},{20,28},{24,16},{28,20},{1,9},{5... | collective-permute-start | bytes 147464 | tf_op jit(solution)/shard_map/ppermute | solution.py:348
  19.8 3.6 %collective-permute-start.4 = (bf16[8,3072]{1,0:T(8,128)(2,1)S(1)}, bf16[8,3072]{1,0:T(8,128)(2,1)S(1)}, u32[]{:S(2)}, u32[]{:S(2)}) collective-permute-start(bf16[8,3072]{1,0:T(8,128)(2,1)S(1)} %add_convert_fusion.refs_2_), channel_id=1, source_target_pairs={{0,4},{4,0},{8,12},{12,8},{16,20},{20,16},{24,28},{28,24},{1,5},{5... | collective-permute-start | bytes 147464 | tf_op jit(solution)/shard_map/ppermute | solution.py:348
  21.5 1.9 %collective-permute-start.10 = (bf16[8,3072]{1,0:T(8,128)(2,1)S(1)}, bf16[8,3072]{1,0:T(8,128)(2,1)S(1)}, u32[]{:S(2)}, u32[]{:S(2)}) collective-permute-start(bf16[8,3072]{1,0:T(8,128)(2,1)S(1)} %collective-permute-done.9.refs_8_), channel_id=1, source_target_pairs={{0,4},{4,0},{8,12},{12,8},{16,20},{20,16},{24,28},{28,24},{1,5},{5... | collective-permute-start | bytes 147464 | tf_op jit(solution)/shard_map/ppermute | solution.py:348
  22.8 1.2 %collective-permute-start.8 = (bf16[8,3072]{1,0:T(8,128)(2,1)S(1)}, bf16[8,3072]{1,0:T(8,128)(2,1)S(1)}, u32[]{:S(2)}, u32[]{:S(2)}) collective-permute-start(bf16[8,3072]{1,0:T(8,128)(2,1)S(1)} %collective-permute-done.7.refs_6_), channel_id=1, source_target_pairs={{0,4},{4,0},{8,12},{12,8},{16,20},{20,16},{24,28},{28,24},{1,5},{5... | collective-permute-start | bytes 147464 | tf_op jit(solution)/shard_map/ppermute | solution.py:348
  23.3 1.2 %collective-permute-start.6 = (bf16[8,3072]{1,0:T(8,128)(2,1)S(1)}, bf16[8,3072]{1,0:T(8,128)(2,1)S(1)}, u32[]{:S(2)}, u32[]{:S(2)}) collective-permute-start(bf16[8,3072]{1,0:T(8,128)(2,1)S(1)} %collective-permute-done.5.refs_4_), channel_id=1, source_target_pairs={{0,4},{4,0},{8,12},{12,8},{16,20},{20,16},{24,28},{28,24},{1,5},{5... | collective-permute-start | bytes 147464 | tf_op jit(solution)/shard_map/ppermute | solution.py:348
  25.4 6.1 %collective-permute-start.11 = (bf16[16,3072]{1,0:T(8,128)(2,1)S(1)}, bf16[16,3072]{1,0:T(8,128)(2,1)S(1)}, u32[]{:S(2)}, u32[]{:S(2)}) collective-permute-start(bf16[16,3072]{1,0:T(8,128)(2,1)S(1)} %get-tuple-element.39), channel_id=1, source_target_pairs={{0,1},{1,0},{2,3},{3,2},{4,5},{5,4},{6,7},{7,6},{8,9},{9,8},{10,11... | collective-permute-start | bytes 294920 | tf_op jit(solution)/shard_map/ppermute | solution.py:348
  25.5 10.9 %collective-permute-start.12 = (bf16[16,3072]{1,0:T(8,128)(2,1)S(1)}, bf16[16,3072]{1,0:T(8,128)(2,1)S(1)}, u32[]{:S(2)}, u32[]{:S(2)}) collective-permute-start(bf16[16,3072]{1,0:T(8,128)(2,1)S(1)} %get-tuple-element.40), channel_id=1, source_target_pairs={{0,2},{1,3},{2,0},{3,1},{4,6},{5,7},{6,4},{7,5},{8,10},{9,11},{10,... | collective-permute-start | bytes 294920 | tf_op jit(solution)/shard_map/ppermute | solution.py:348
  26.8 9.6 %collective-permute-start.13 = (bf16[16,3072]{1,0:T(8,128)(2,1)S(1)}, bf16[16,3072]{1,0:T(8,128)(2,1)S(1)}, u32[]{:S(2)}, u32[]{:S(2)}) collective-permute-start(bf16[16,3072]{1,0:T(8,128)(2,1)S(1)} %get-tuple-element.41), channel_id=1, source_target_pairs={{0,3},{1,2},{2,1},{3,0},{4,7},{5,6},{6,5},{7,4},{8,11},{9,10},{10,... | collective-permute-start | bytes 294920 | tf_op jit(solution)/shard_map/ppermute | solution.py:348
  38.1 17.0 %collective-permute-start.14 = (bf16[64,1536]{1,0:T(8,128)(2,1)S(1)}, bf16[64,1536]{1,0:T(8,128)(2,1)S(1)}, u32[]{:S(2)}, u32[]{:S(2)}) collective-permute-start(bf16[64,1536]{1,0:T(8,128)(2,1)S(1)} %get-tuple-element.45.grad_values.refs_6_), channel_id=1, source_target_pairs={{0,2},{1,3},{2,0},{3,1},{4,6},{5,7},{6,4},{7,5},{8,10},{9,11},{10,... | collective-permute-start | bytes 589832 | tf_op jit(solution)/shard_map/ppermute | solution.py:348
  41.4 17.0 %collective-permute-start.16 = (bf16[64,1536]{1,0:T(8,128)(2,1)S(1)}, bf16[64,1536]{1,0:T(8,128)(2,1)S(1)}, u32[]{:S(2)}, u32[]{:S(2)}) collective-permute-start(bf16[64,1536]{1,0:T(8,128)(2,1)S(1)} %get-tuple-element.52.refs_1_), channel_id=1, source_target_pairs={{0,2},{1,3},{2,0},{3,1},{4,6},{5,7},{6,4},{7,5},{8,10},{9,11},{10,... | collective-permute-start | bytes 589832 | tf_op jit(solution)/shard_map/ppermute | solution.py:348
  42.4 25.6 %collective-permute-start.15 = (bf16[64,3072]{1,0:T(8,128)(2,1)S(1)}, bf16[64,3072]{1,0:T(8,128)(2,1)S(1)}, u32[]{:S(2)}, u32[]{:S(2)}) collective-permute-start(bf16[64,3072]{1,0:T(8,128)(2,1)S(1)} %get-tuple-element.55), channel_id=1, source_target_pairs={{0,1},{1,0},{2,3},{3,2},{4,5},{5,4},{6,7},{7,6},{8,9},{9,8},{10,11... | collective-permute-start | bytes 1179656 | tf_op jit(solution)/shard_map/ppermute | solution.py:382
  55.0 13.0 %collective-permute-start.17 = (bf16[64,3072]{1,0:T(8,128)(2,1)S(1)}, bf16[64,3072]{1,0:T(8,128)(2,1)S(1)}, u32[]{:S(2)}, u32[]{:S(2)}) collective-permute-start(bf16[64,3072]{1,0:T(8,128)(2,1)S(1)} %get-tuple-element.55), channel_id=1, source_target_pairs={{1,2},{2,1},{5,6},{6,5},{9,10},{10,9},{13,14},{14,13},{17,18},{18,... | collective-permute-start | bytes 1179656 | tf_op jit(solution)/shard_map/ppermute | solution.py:386
  58.4 7.6 %collective-permute-start.18 = (bf16[64,1536]{1,0:T(8,128)(2,1)S(1)}, bf16[64,1536]{1,0:T(8,128)(2,1)S(1)}, u32[]{:S(2)}, u32[]{:S(2)}) collective-permute-start(bf16[64,1536]{1,0:T(8,128)(2,1)S(1)} %collective-permute-done.16.refs_3_), channel_id=1, source_target_pairs={{1,0},{2,3},{5,4},{6,7},{9,8},{10,11},{13,12},{14,15},{17,16},{18,... | collective-permute-start | bytes 589832 | tf_op jit(solution)/shard_map/ppermute | solution.py:384
  59.7 8.4 %collective-permute-start.19 = (bf16[64,1536]{1,0:T(8,128)(2,1)S(1)}, bf16[64,1536]{1,0:T(8,128)(2,1)S(1)}, u32[]{:S(2)}, u32[]{:S(2)}) collective-permute-start(bf16[64,1536]{1,0:T(8,128)(2,1)S(1)} %collective-permute-done.14.refs_8_), channel_id=1, source_target_pairs={{1,0},{2,3},{5,4},{6,7},{9,8},{10,11},{13,12},{14,15},{17,16},{18,... | collective-permute-start | bytes 589832 | tf_op jit(solution)/shard_map/ppermute | solution.py:384

commit v4 on v3

--- a/solution.py
+++ b/solution.py
@@ -109,7 +109,7 @@
 
 
 def select_kernel(groups, each, paired, dp_paired, n_texts, table, *refs):
-    texts, pieces, outs, chip_text = refs[:n_texts], refs[n_texts : -groups - 1], refs[-groups - 1 : -1], refs[-1]
+    texts, pieces, outs, chip_text = refs[:n_texts], refs[n_texts : -2 * groups - 1], refs[-2 * groups - 1 : -1], refs[-1]
     depth = texts[0].shape[0]
     for i, text in enumerate(texts):
         chip_text[i * depth : (i + 1) * depth] = text[...]
@@ -130,9 +130,10 @@
     inside = spread_rows(firsts, each, shape) < each
     chosen = ((target == lax.broadcasted_iota(jnp.int32, shape, 1)) & inside).astype(BF16)
     rows = jnp.dot(chosen, held, preferred_element_type=F32).astype(BF16)
-    size = SAMPLES * each
+    size, width = SAMPLES * each, rows.shape[1] // 2
     for k in range(groups):
-        outs[k][...] = rows[k * size : (k + 1) * size]
+        outs[k][...] = rows[k * size : (k + 1) * size, :width]
+        outs[groups + k][...] = rows[k * size : (k + 1) * size, width:]
 
 
 def select_rows(groups, each, paired, dp_paired, table, texts, pieces):
@@ -141,8 +142,8 @@
     return pl.pallas_call(
         functools.partial(select_kernel, groups, each, paired, dp_paired, len(texts)),
         in_specs=[SMEM_SPEC] + [VMEM_SPEC] * (len(texts) + len(pieces)),
-        out_specs=[VMEM_SPEC] * (groups + 1),
-        out_shape=[jax.ShapeDtypeStruct((SAMPLES * each, width), BF16)] * groups
+        out_specs=[VMEM_SPEC] * (2 * groups + 1),
+        out_shape=[jax.ShapeDtypeStruct((SAMPLES * each, width // 2), BF16)] * (2 * groups)
         + [jax.ShapeDtypeStruct((len(texts) * depth, features), BF16)],
         compiler_params=kernel_params(),
         name="select_rows",
@@ -154,7 +155,7 @@
 
 
 def value_grad_kernel(groups, each, paired, table, queries, cotangent, *refs):
-    pieces, (probs, probs_rounded, grad_values, scores) = refs[:groups], refs[groups:]
+    pieces, (probs, grad_values, scores, probs_rounded) = refs[:groups], refs[groups:]
     tokens, width = queries.shape
     slots = groups * SAMPLES * each
     heads = width // HEAD
@@ -199,43 +200,39 @@
     return pl.pallas_call(
         functools.partial(value_grad_kernel, groups, each, paired),
         in_specs=[SMEM_SPEC] + [VMEM_SPEC] * (2 + groups),
-        out_specs=[VMEM_SPEC] * 3,
+        out_specs=[VMEM_SPEC] * 2,
         out_shape=[
             jax.ShapeDtypeStruct((heads, slots, tokens), F32),
-            jax.ShapeDtypeStruct((heads, slots, tokens), BF16),
             jax.ShapeDtypeStruct((slots, width), BF16),
         ],
-        scratch_shapes=[pltpu.VMEM((heads, slots, tokens), F32)],
+        scratch_shapes=[pltpu.VMEM((heads, slots, tokens), F32), pltpu.VMEM((heads, slots, tokens), BF16)],
         compiler_params=kernel_params(),
         name="value_gradients",
     )(table, queries, grad_out, *pieces)
 
 
 def key_grad_kernel(groups, probs, queries, cotangent, grad_values, *refs):
-    pieces, (grad_query, grad_keys, grad_both, prob_grads, score_grads) = refs[:groups], refs[groups:]
+    values, (score_grads, grad_keys, grad_both, prob_grads) = refs[:groups], refs[groups:]
     width = queries.shape[1]
     heads = width // HEAD
     scale = HEAD ** (-0.5)
     for h in range(heads):
-        values_at = slice(width + h * HEAD, width + (h + 1) * HEAD)
-        v = jnp.concatenate([piece[:, values_at] for piece in pieces], axis=0)
-        prob_grads[h] = lax.dot_general(v, cotangent[:, h * HEAD : (h + 1) * HEAD], LAST, preferred_element_type=F32)
+        at = slice(h * HEAD, (h + 1) * HEAD)
+        v = jnp.concatenate([piece[:, at] for piece in values], axis=0)
+        prob_grads[h] = lax.dot_general(v, cotangent[:, at], LAST, preferred_element_type=F32)
     for h in range(heads):
         prob, prob_grad = probs[h], prob_grads[h]
         centre = jnp.sum(prob * prob_grad, axis=0, keepdims=True)
         score_grads[h] = (prob * (prob_grad - centre)).astype(BF16)
     for h in range(heads):
         at = slice(h * HEAD, (h + 1) * HEAD)
-        k = jnp.concatenate([piece[:, at] for piece in pieces], axis=0)
-        score_grad = score_grads[h]
-        grad_key = (jnp.dot(score_grad, queries[:, at], preferred_element_type=F32) * scale).astype(BF16)
+        grad_key = (jnp.dot(score_grads[h], queries[:, at], preferred_element_type=F32) * scale).astype(BF16)
         grad_keys[:, at] = grad_key
         grad_both[:, at] = grad_key
-        grad_query[:, at] = (lax.dot_general(score_grad, k, FIRST, preferred_element_type=F32) * scale).astype(BF16)
     grad_both[:, width:] = grad_values[...]
 
 
-def key_grads(groups, probs, queries, grad_out, grad_values, pieces):
+def key_grads(groups, probs, queries, grad_out, grad_values, values):
     tokens, width = queries.shape
     heads, slots, _ = probs.shape
     return pl.pallas_call(
@@ -243,17 +240,23 @@
         in_specs=[VMEM_SPEC] * (4 + groups),
         out_specs=[VMEM_SPEC] * 3,
         out_shape=[
-            jax.ShapeDtypeStruct((tokens, width), BF16),
+            jax.ShapeDtypeStruct((heads, slots, tokens), BF16),
             jax.ShapeDtypeStruct((slots, width), BF16),
             jax.ShapeDtypeStruct((slots, 2 * width), BF16),
         ],
-        scratch_shapes=[pltpu.VMEM((heads, slots, tokens), F32), pltpu.VMEM((heads, slots, tokens), BF16)],
+        scratch_shapes=[pltpu.VMEM((heads, slots, tokens), F32)],
         compiler_params=kernel_params(),
         name="key_gradients",
-    )(probs, queries, grad_out, grad_values, *pieces)
-
-
-def text_kernel(groups, each, depth, paired, dp_paired, table, text, out):
+    )(probs, queries, grad_out, grad_values, *values)
+
+
+def text_kernel(groups, each, depth, paired, dp_paired, table, text, score_grads, *refs):
+    keys, (out, grad_query) = refs[:groups], refs[groups:]
+    for h in range(score_grads.shape[0]):
+        at = slice(h * HEAD, (h + 1) * HEAD)
+        k = jnp.concatenate([piece[:, at] for piece in keys], axis=0)
+        product = lax.dot_general(score_grads[h], k, FIRST, preferred_element_type=F32)
+        grad_query[:, at] = (product * HEAD ** (-0.5)).astype(BF16)
     index, member = table[3, 0], table[3, 1]
     shape = (text.shape[0], out.shape[1])
     columns = lax.broadcasted_iota(jnp.int32, shape, 1)
@@ -281,16 +284,19 @@
     out[...] = lax.dot_general(text[...], chosen, FIRST, preferred_element_type=F32).astype(BF16)
 
 
-def slot_texts(groups, each, depth, paired, dp_paired, table, text):
+def slot_texts(groups, each, depth, paired, dp_paired, table, text, score_grads, keys):
     features = text.shape[1]
     return pl.pallas_call(
         functools.partial(text_kernel, groups, each, depth, paired, dp_paired),
-        in_specs=[SMEM_SPEC, VMEM_SPEC],
-        out_specs=VMEM_SPEC,
-        out_shape=jax.ShapeDtypeStruct((features, groups * groups * SAMPLES * each), BF16),
+        in_specs=[SMEM_SPEC] + [VMEM_SPEC] * (2 + groups),
+        out_specs=[VMEM_SPEC] * 2,
+        out_shape=[
+            jax.ShapeDtypeStruct((features, groups * groups * SAMPLES * each), BF16),
+            jax.ShapeDtypeStruct((score_grads.shape[2], keys[0].shape[1]), BF16),
+        ],
         compiler_params=kernel_params(),
         name="slot_texts",
-    )(table, text)
+    )(table, text, score_grads, *keys)
 
 
 def weight_kernel(line, blocks, *refs):
@@ -407,11 +413,14 @@
     rows = sum(piece.astype(F32) for piece in came).astype(BF16)
     class_rows = gather_dp(rows, dp_paired)
     *outgoing, chip_text = select_rows(groups, each, paired, dp_paired, table, texts, class_rows)
-    keys_values = exchange(outgoing, paired)
-    probs, _, grad_values = value_grads(groups, each, paired, table, queries, grad_out, keys_values)
+    keys = exchange(outgoing[:groups], paired)
+    values = exchange(outgoing[groups:], paired)
+    probs, grad_values = value_grads(groups, each, paired, table, queries, grad_out, keys)
     grad_values, probs = lax.optimization_barrier((grad_values, probs))
-    grad_query, grad_keys, grad_both = key_grads(groups, probs, queries, grad_out, grad_values, keys_values)
-    grad_keys, grad_both, chip_text = lax.optimization_barrier((grad_keys, grad_both, chip_text))
+    score_grads, grad_keys, grad_both = key_grads(groups, probs, queries, grad_out, grad_values, values)
+    grad_values, grad_keys, grad_both, chip_text = lax.optimization_barrier(
+        (grad_values, grad_keys, grad_both, chip_text)
+    )
     if dp_paired:
         text = gather_chips(chip_text)
     else:
@@ -422,7 +431,7 @@
         value_parts, key_parts = [
             [lax.all_gather(half, "fsdp", axis=0, tiled=True)] for half in (grad_values, grad_keys)
         ]
-    chosen_text = slot_texts(groups, each, depth, paired, dp_paired, table, text)
+    chosen_text, grad_query = slot_texts(groups, each, depth, paired, dp_paired, table, text, score_grads, keys)
     grad_weight = weight_grad(line, chosen_text, key_parts, value_parts)
     return grad_query, grad_weight[None]
 

time: 71.4 us -> 70.6 us (0.989)
  waiting for transfers between devices: 25.7 us -> 22 us
  starting transfers between devices: 21.8 us -> 25.4 us
    ppermute x16 -> x19, starting transfers between devices: 16.6 us -> 21.1 us  [swap(): lax.ppermute(x, axis, [(i, i ^ k) for i in range(lax.axis_size(axis))])]
    ppermute x16 -> x19, waiting for transfers between devices: 19.6 us -> 15.9 us  [swap(): lax.ppermute(x, axis, [(i, i ^ k) for i in range(lax.axis_size(axis))])]
    pallas_call x1, Pallas kernels: 1.4 us -> 0.57 us  [key_grads(): pl.pallas_call(functools.partial(key_grad_kernel, groups), in_specs=[VMEM...]
    ppermute x1, starting transfers between devices: 1.89 us -> 1.09 us  [gather_line(): near = lax.ppermute(both, 'fsdp', near_pairs)]
  transfers between devices with their start and end apart: 20 -> 23, of which waited for: 12 -> 12; matrix products, arithmetic and copies ran while one was open for 0% -> 0% of each run, Pallas kernels for 3% -> 4%
where the time goes in v4:
time: 70.6 us; the launch traced here: 70.4 us
  starting transfers between devices  25.4 us (36%)
  waiting for transfers between devices  22 us (31%)
  Pallas kernels  11.3 us (16%)
  blocking collectives  10.6 us (15%)
  between operations  0.85 us (1%)
    ppermute x19, starting transfers between devices, swap(): lax.ppermute(x, axis, [(i, i ^ k) for i in range(lax.axis_size(axis))])  21.1 us
    ppermute x19, waiting for transfers between devices, swap(): lax.ppermute(x, axis, [(i, i ^ k) for i in range(lax.axis_size(axis))])  15.9 us
    all_gather x1, blocking collectives, gather_chips(): return lax.all_gather(x, 'dp', axis=0, tiled=True, axis_index_groups=cores)  10.6 us
    ppermute x2, waiting for transfers between devices, gather_line(): outer = [lax.ppermute(piece, 'fsdp', outward) for piece in second]  6.17 us
    pallas_call x1, Pallas kernels, project(): pl.pallas_call(functools.partial(project_kernel, groups, paired, chunks),...  3.92 us
    pallas_call x1, Pallas kernels, weight_grad(): pl.pallas_call(functools.partial(weight_kernel, line, blocks), in_specs=[...  3.13 us
    ppermute x2, starting transfers between devices, gather_line(): outer = [lax.ppermute(piece, 'fsdp', outward) for piece in second]  2.57 us
    pallas_call x1, Pallas kernels, slot_texts(): pl.pallas_call(functools.partial(text_kernel, groups, each, depth, paired...  1.64 us
  transfers between devices with their start and end apart: 23, of which 12 were waited for; matrix products, arithmetic and copies ran while one was open for 0% of the time, Pallas kernels for 4%

profile of v4, /device:TPU:0, one launch (start us, length us, event | category | flops | bytes accessed | tf_op | source)
XLA Modules:
  0.0 70.4 jit_solution(6490884062701803508)
XLA Ops:
  0.6 0.0 copy-start.2
  0.6 0.0 copy-start.3
  0.7 0.0 copy-start.4
  0.7 0.0 copy-start.5
  0.7 0.0 copy-start.6
  0.7 0.0 copy-start.1
  0.7 0.0 copy-start
  0.7 3.9 %project.1 = (bf16[8,3072]{1,0:T(8,128)(2,1)S(1)}, bf16[8,3072]{1,0:T(8,128)(2,1)S(1)}, bf16[8,3072]{1,0:T(8,128)(2,1)S(1)}, bf16[8,3072]{1,0:T(8,128)(2,1)S(1)}) custom-call(bf16[32,1024]{1,0:T(8,128)(2,1)} %refs_0_, bf16[1024,3072]{1,0:T(8,128)(2,1)} %weight.1), custom_call_target="tpu_custom_call" | custom-call | tf_op jit(solution)/shard_map/project/pallas_call | solution.py:95
  4.6 3.1 %collective-permute-start.1 = (bf16[8,3072]{1,0:T(8,128)(2,1)S(1)}, bf16[8,3072]{1,0:T(8,128)(2,1)S(1)}, u32[]{:S(2)}, u32[]{:S(2)}) collective-permute-start(bf16[8,3072]{1,0:T(8,128)(2,1)S(1)} %get-tuple-element.42), channel_id=1, source_target_pairs={{0,1},{1,0},{2,3},{3,2},{4,5},{5,4},{6,7},{7,6},{8,9},{9,8},{10,11... | collective-permute-start | bytes 147464 | tf_op jit(solution)/shard_map/ppermute | solution.py:354
  7.7 2.6 %collective-permute-start.2 = (bf16[8,3072]{1,0:T(8,128)(2,1)S(1)}, bf16[8,3072]{1,0:T(8,128)(2,1)S(1)}, u32[]{:S(2)}, u32[]{:S(2)}) collective-permute-start(bf16[8,3072]{1,0:T(8,128)(2,1)S(1)} %get-tuple-element.43), channel_id=1, source_target_pairs={{0,2},{1,3},{2,0},{3,1},{4,6},{5,7},{6,4},{7,5},{8,10},{9,11},{10,... | collective-permute-start | bytes 147464 | tf_op jit(solution)/shard_map/ppermute | solution.py:354
  10.3 0.0 collective-permute-start.3
  10.3 0.0 copy-done.2
  10.3 0.0 collective-permute-start
  10.3 0.0 copy-done.3
  10.3 0.1 pad_add_fusion.1
  10.4 0.0 collective-permute-done.1
  10.4 3.2 %collective-permute-done.2 = bf16[8,3072]{1,0:T(8,128)(2,1)S(1)} collective-permute-done((bf16[8,3072]{1,0:T(8,128)(2,1)S(1)}, bf16[8,3072]{1,0:T(8,128)(2,1)S(1)}, u32[]{:S(2)}, u32[]{:S(2)}) %collective-permute-start.2) | collective-permute-done | bytes 49184 | tf_op jit(solution)/shard_map/ppermute | solution.py:354
  13.6 2.6 %collective-permute-done.3 = bf16[8,3072]{1,0:T(8,128)(2,1)S(1)} collective-permute-done((bf16[8,3072]{1,0:T(8,128)(2,1)S(1)}, bf16[8,3072]{1,0:T(8,128)(2,1)S(1)}, u32[]{:S(2)}, u32[]{:S(2)}) %collective-permute-start.3) | collective-permute-done | bytes 49184 | tf_op jit(solution)/shard_map/ppermute | solution.py:354
  16.2 2.5 %collective-permute-start.9 = (bf16[8,3072]{1,0:T(8,128)(2,1)S(1)}, bf16[8,3072]{1,0:T(8,128)(2,1)S(1)}, u32[]{:S(2)}, u32[]{:S(2)}) collective-permute-start(bf16[8,3072]{1,0:T(8,128)(2,1)S(1)} %add_convert_fusion.refs_2_), channel_id=1, source_target_pairs={{0,24},{4,28},{8,16},{12,20},{16,8},{20,12},{24,0},{28,4},{1,25},{... | collective-permute-start | bytes 147464 | tf_op jit(solution)/shard_map/ppermute | solution.py:354
  18.7 0.5 collective-permute-start.7
  19.2 0.5 collective-permute-start.5
  19.8 0.0 collective-permute-start.4
  19.8 1.7 %collective-permute-done.9.refs_8_ = bf16[8,3072]{1,0:T(8,128)(2,1)S(1)} collective-permute-done((bf16[8,3072]{1,0:T(8,128)(2,1)S(1)}, bf16[8,3072]{1,0:T(8,128)(2,1)S(1)}, u32[]{:S(2)}, u32[]{:S(2)}) %collective-permute-start.9) | collective-permute-done | bytes 49184 | tf_op jit(solution)/shard_map/ppermute | solution.py:354
  21.5 0.0 collective-permute-start.10
  21.5 1.3 %collective-permute-done.7.refs_6_ = bf16[8,3072]{1,0:T(8,128)(2,1)S(1)} collective-permute-done((bf16[8,3072]{1,0:T(8,128)(2,1)S(1)}, bf16[8,3072]{1,0:T(8,128)(2,1)S(1)}, u32[]{:S(2)}, u32[]{:S(2)}) %collective-permute-start.7) | collective-permute-done | bytes 49184 | tf_op jit(solution)/shard_map/ppermute | solution.py:354
  22.8 0.0 collective-permute-start.8
  22.8 0.5 collective-permute-done.5.refs_4_
  23.3 0.0 collective-permute-start.6
  23.3 0.0 copy-done.5
  23.4 0.0 collective-permute-done.refs_1_
  23.4 0.0 collective-permute-done.4.refs_3_
  23.4 0.0 collective-permute-done.10.refs_9_
  23.4 0.7 collective-permute-done.8.refs_7_
  24.1 0.5 collective-permute-done.6.refs_5_
  24.6 0.8 %select_rows.1 = (bf16[16,1536]{1,0:T(8,128)(2,1)S(1)}, bf16[16,1536]{1,0:T(8,128)(2,1)S(1)}, bf16[16,1536]{1,0:T(8,128)(2,1)S(1)}, bf16[16,1536]{1,0:T(8,128)(2...) custom-call(s32[4,8]{1,0:T(4,128)S(1)} %pad_add_fusion.table, ...), custom_call_target="tpu_custom_call" | custom-call | tf_op jit(solution)/shard_map/select_rows/pallas_call | solution.py:142
  25.4 0.1 collective-permute-start.11
  25.5 1.3 %collective-permute-start.12 = (bf16[16,1536]{1,0:T(8,128)(2,1)S(1)}, bf16[16,1536]{1,0:T(8,128)(2,1)S(1)}, u32[]{:S(2)}, u32[]{:S(2)}) collective-permute-start(bf16[16,1536]{1,0:T(8,128)(2,1)S(1)} %get-tuple-element.47), channel_id=1, source_target_pairs={{0,2},{1,3},{2,0},{3,1},{4,6},{5,7},{6,4},{7,5},{8,10},{9,11},{10,... | collective-permute-start | bytes 147464 | tf_op jit(solution)/shard_map/ppermute | solution.py:354
  26.8 3.1 %collective-permute-start.13 = (bf16[16,1536]{1,0:T(8,128)(2,1)S(1)}, bf16[16,1536]{1,0:T(8,128)(2,1)S(1)}, u32[]{:S(2)}, u32[]{:S(2)}) collective-permute-start(bf16[16,1536]{1,0:T(8,128)(2,1)S(1)} %get-tuple-element.48), channel_id=1, source_target_pairs={{0,3},{1,2},{2,1},{3,0},{4,7},{5,6},{6,5},{7,4},{8,11},{9,10},{10,... | collective-permute-start | bytes 147464 | tf_op jit(solution)/shard_map/ppermute | solution.py:354
  29.9 0.0 collective-permute-start.14
  29.9 1.3 %collective-permute-start.15 = (bf16[16,1536]{1,0:T(8,128)(2,1)S(1)}, bf16[16,1536]{1,0:T(8,128)(2,1)S(1)}, u32[]{:S(2)}, u32[]{:S(2)}) collective-permute-start(bf16[16,1536]{1,0:T(8,128)(2,1)S(1)} %get-tuple-element.55), channel_id=1, source_target_pairs={{0,2},{1,3},{2,0},{3,1},{4,6},{5,7},{6,4},{7,5},{8,10},{9,11},{10,... | collective-permute-start | bytes 147464 | tf_op jit(solution)/shard_map/ppermute | solution.py:354
  31.2 0.0 collective-permute-done.11.refs_1_
  31.2 3.1 %collective-permute-start.16 = (bf16[16,1536]{1,0:T(8,128)(2,1)S(1)}, bf16[16,1536]{1,0:T(8,128)(2,1)S(1)}, u32[]{:S(2)}, u32[]{:S(2)}) collective-permute-start(bf16[16,1536]{1,0:T(8,128)(2,1)S(1)} %get-tuple-element.56), channel_id=1, source_target_pairs={{0,3},{1,2},{2,1},{3,0},{4,7},{5,6},{6,5},{7,4},{8,11},{9,10},{10,... | collective-permute-start | bytes 147464 | tf_op jit(solution)/shard_map/ppermute | solution.py:354
  34.3 0.0 collective-permute-done.12.refs_2_
  34.3 0.0 collective-permute-done.13.refs_3_
  34.3 1.2 %value_gradients.1 = (f32[12,64,128]{2,1,0:T(8,128)S(1)}, bf16[64,1536]{1,0:T(8,128)(2,1)S(1)}) custom-call(s32[4,8]{1,0:T(4,128)S(1)} %pad_add_fusion.table, bf16[128,1536]{1,0:T(8,128)(2,1)S(1)} %copy-done, bf16[128,1536]{1,0:T(8,128)(2,1)S(1)} %copy-done.1, bf16[16,1536]{1,0:T(8,128)(2,1)S(1)} %get-tuple-element.45.refs_0_, ...), custom_call_target="tpu_custom_call" | custom-call | tf_op jit(solution)/shard_map/value_gradients/pallas_call | solution.py:200
  35.4 0.0 collective-permute-done.14.refs_1_
  35.5 1.7 %collective-permute-done.15.refs_2_ = bf16[16,1536]{1,0:T(8,128)(2,1)S(1)} collective-permute-done((bf16[16,1536]{1,0:T(8,128)(2,1)S(1)}, bf16[16,1536]{1,0:T(8,128)(2,1)S(1)}, u32[]{:S(2)}, u32[]{:S(2)}) %collective-permute-start.15) | collective-permute-done | bytes 49184 | tf_op jit(solution)/shard_map/ppermute | solution.py:354
  37.1 0.0 collective-permute-done.16.refs_3_
  37.1 0.6 key_gradients.1
  37.7 0.8 %collective-permute-start.17 = (bf16[64,1536]{1,0:T(8,128)(2,1)S(1)}, bf16[64,1536]{1,0:T(8,128)(2,1)S(1)}, u32[]{:S(2)}, u32[]{:S(2)}) collective-permute-start(bf16[64,1536]{1,0:T(8,128)(2,1)S(1)} %get-tuple-element.60.grad_values.refs_6_), channel_id=1, source_target_pairs={{0,2},{1,3},{2,0},{3,1},{4,6},{5,7},{6,4},{7,5},{8,10},{9,11},{10,... | collective-permute-start | bytes 589832 | tf_op jit(solution)/shard_map/ppermute | solution.py:354
  38.5 2.2 %collective-permute-start.19 = (bf16[64,1536]{1,0:T(8,128)(2,1)S(1)}, bf16[64,1536]{1,0:T(8,128)(2,1)S(1)}, u32[]{:S(2)}, u32[]{:S(2)}) collective-permute-start(bf16[64,1536]{1,0:T(8,128)(2,1)S(1)} %get-tuple-element.66.refs_1_), channel_id=1, source_target_pairs={{0,2},{1,3},{2,0},{3,1},{4,6},{5,7},{6,4},{7,5},{8,10},{9,11},{10,... | collective-permute-start | bytes 589832 | tf_op jit(solution)/shard_map/ppermute | solution.py:354
  40.7 1.1 %collective-permute-start.18 = (bf16[64,3072]{1,0:T(8,128)(2,1)S(1)}, bf16[64,3072]{1,0:T(8,128)(2,1)S(1)}, u32[]{:S(2)}, u32[]{:S(2)}) collective-permute-start(bf16[64,3072]{1,0:T(8,128)(2,1)S(1)} %get-tuple-element.69), channel_id=1, source_target_pairs={{0,1},{1,0},{2,3},{3,2},{4,5},{5,4},{6,7},{7,6},{8,9},{9,8},{10,11... | collective-permute-start | bytes 1179656 | tf_op jit(solution)/shard_map/ppermute | solution.py:388
  41.8 10.6 %all_gather.3.text = bf16[256,1024]{1,0:T(8,128)(2,1)S(1)} all-gather(bf16[64,1024]{1,0:T(8,128)(2,1)S(1)} %get-tuple-element.61), channel_id=1, replica_groups={{0,8,16,24},{4,12,20,28},{1,9,17,25},{5,13,21,29},{2,10,18,26},{6,14,22..., dimensions={0}, use_global_device_ids=true | all-gather | bytes 655360 | tf_op jit(solution)/shard_map/all_gather | solution.py:371
  52.4 1.1 %collective-permute-done.17.refs_8_ = bf16[64,1536]{1,0:T(8,128)(2,1)S(1)} collective-permute-done((bf16[64,1536]{1,0:T(8,128)(2,1)S(1)}, bf16[64,1536]{1,0:T(8,128)(2,1)S(1)}, u32[]{:S(2)}, u32[]{:S(2)}) %collective-permute-start.17) | collective-permute-done | bytes 196640 | tf_op jit(solution)/shard_map/ppermute | solution.py:354
  53.5 0.7 collective-permute-start.20
  54.2 2.7 %collective-permute-done.19.refs_3_ = bf16[64,1536]{1,0:T(8,128)(2,1)S(1)} collective-permute-done((bf16[64,1536]{1,0:T(8,128)(2,1)S(1)}, bf16[64,1536]{1,0:T(8,128)(2,1)S(1)}, u32[]{:S(2)}, u32[]{:S(2)}) %collective-permute-start.19) | collective-permute-done | bytes 196640 | tf_op jit(solution)/shard_map/ppermute | solution.py:354
  56.8 1.3 %collective-permute-start.21 = (bf16[64,1536]{1,0:T(8,128)(2,1)S(1)}, bf16[64,1536]{1,0:T(8,128)(2,1)S(1)}, u32[]{:S(2)}, u32[]{:S(2)}) collective-permute-start(bf16[64,1536]{1,0:T(8,128)(2,1)S(1)} %collective-permute-done.19.refs_3_), channel_id=1, source_target_pairs={{1,0},{2,3},{5,4},{6,7},{9,8},{10,11},{13,12},{14,15},{17,16},{18,... | collective-permute-start | bytes 589832 | tf_op jit(solution)/shard_map/ppermute | solution.py:390
  58.1 1.3 %collective-permute-start.22 = (bf16[64,1536]{1,0:T(8,128)(2,1)S(1)}, bf16[64,1536]{1,0:T(8,128)(2,1)S(1)}, u32[]{:S(2)}, u32[]{:S(2)}) collective-permute-start(bf16[64,1536]{1,0:T(8,128)(2,1)S(1)} %collective-permute-done.17.refs_8_), channel_id=1, source_target_pairs={{1,0},{2,3},{5,4},{6,7},{9,8},{10,11},{13,12},{14,15},{17,16},{18,... | collective-permute-start | bytes 589832 | tf_op jit(solution)/shard_map/ppermute | solution.py:390
  59.4 1.6 %slot_texts.1 = (bf16[1024,256]{1,0:T(8,128)(2,1)S(1)}, bf16[128,1536]{1,0:T(8,128)(2,1)}) custom-call(s32[4,8]{1,0:T(4,128)S(1)} %pad_add_fusion.table, bf16[256,1024]{1,0:T(8,128)(2,1)S(1)} %all_gather.3.text, bf16[12,64,128]{2,1,0:T(8,128)(2,1)S(1)} %get-tuple-element.63.score_grads, bf16[16,1536]{1,0:T(8,128)(2,1)S(1)} %get-tuple-element.45.refs_0_, ...), custom_call_target="tpu_custom_call" | custom-call | tf_op jit(solution)/shard_map/slot_texts/pallas_call | solution.py:289
  61.1 4.1 %collective-permute-done.21.refs_5_ = bf16[64,1536]{1,0:T(8,128)(2,1)S(1)} collective-permute-done((bf16[64,1536]{1,0:T(8,128)(2,1)S(1)}, bf16[64,1536]{1,0:T(8,128)(2,1)S(1)}, u32[]{:S(2)}, u32[]{:S(2)}) %collective-permute-start.21) | collective-permute-done | bytes 196640 | tf_op jit(solution)/shard_map/ppermute | solution.py:390
  65.1 2.1 %collective-permute-done.22.refs_10_ = bf16[64,1536]{1,0:T(8,128)(2,1)S(1)} collective-permute-done((bf16[64,1536]{1,0:T(8,128)(2,1)S(1)}, bf16[64,1536]{1,0:T(8,128)(2,1)S(1)}, u32[]{:S(2)}, u32[]{:S(2)}) %collective-permute-start.22) | collective-permute-done | bytes 196640 | tf_op jit(solution)/shard_map/ppermute | solution.py:390
  67.2 0.0 collective-permute-done.18.refs_2_.refs_7_
  67.2 0.0 collective-permute-done.20.refs_4_.refs_9_
  67.2 3.1 %weight_gradient.1 = bf16[1024,3072]{1,0:T(8,128)(2,1)} custom-call(bf16[1024,256]{1,0:T(8,128)(2,1)S(1)} %get-tuple-element.65.refs_0_, bf16[64,1536]{1,0:T(8,128)(2,1)S(1)} %get-tuple-element.66.refs_1_, bf16[64,3072]{1,0:T(8,128)(2,1)S(1)} %collective-permute-done.18.refs_2_.refs_7_, bf16[64,1536]{1,0:T(8,128)(2,1)S(1)} %collective-permute-done.19.refs_3_, ...), custom_call_target="tpu_custom_call" | custom-call | tf_op jit(solution)/shard_map/weight_gradient/pallas_call | solution.py:338
  (7 shorter events, 0.1 us)
Async XLA Ops:
  0.6 9.7 %copy-start.2 = (bf16[32,1024]{1,0:T(8,128)(2,1)S(1)}, bf16[32,1024]{1,0:T(8,128)(2,1)}, u32[]{:S(2)}) copy-start(bf16[32,1024]{1,0:T(8,128)(2,1)} %refs_0_) | copy-start | bytes 196612
  0.6 9.7 %copy-start.3 = (s32[1,2]{1,0:T(1,128)S(1)}, s32[1,2]{1,0:T(1,128)}, u32[]{:S(2)}) copy-start(s32[1,2]{1,0:T(1,128)} %param.12) | copy-start | bytes 28
  0.7 22.7 %copy-start.4 = (s32[1,8]{1,0:T(1,128)S(1)}, s32[1,8]{1,0:T(1,128)}, u32[]{:S(2)}) copy-start(s32[1,8]{1,0:T(1,128)} %param.15) | copy-start | bytes 100
  0.7 22.7 %copy-start.5 = (s32[1,8]{1,0:T(1,128)S(1)}, s32[1,8]{1,0:T(1,128)}, u32[]{:S(2)}) copy-start(s32[1,8]{1,0:T(1,128)} %param.14) | copy-start | bytes 100
  0.7 22.7 %copy-start.6 = (s32[1,8]{1,0:T(1,128)S(1)}, s32[1,8]{1,0:T(1,128)}, u32[]{:S(2)}) copy-start(s32[1,8]{1,0:T(1,128)} %param.13) | copy-start | bytes 100
  0.7 33.6 %copy-start.1 = (bf16[128,1536]{1,0:T(8,128)(2,1)S(1)}, bf16[128,1536]{1,0:T(8,128)(2,1)}, u32[]{:S(2)}) copy-start(bf16[128,1536]{1,0:T(8,128)(2,1)} %cotangent.3) | copy-start | bytes 1179652
  0.7 33.6 %copy-start = (bf16[128,1536]{1,0:T(8,128)(2,1)S(1)}, bf16[128,1536]{1,0:T(8,128)(2,1)}, u32[]{:S(2)}) copy-start(bf16[128,1536]{1,0:T(8,128)(2,1)} %queries.3) | copy-start | bytes 1179652
  4.6 5.8 %collective-permute-start.1 = (bf16[8,3072]{1,0:T(8,128)(2,1)S(1)}, bf16[8,3072]{1,0:T(8,128)(2,1)S(1)}, u32[]{:S(2)}, u32[]{:S(2)}) collective-permute-start(bf16[8,3072]{1,0:T(8,128)(2,1)S(1)} %get-tuple-element.42), channel_id=1, source_target_pairs={{0,1},{1,0},{2,3},{3,2},{4,5},{5,4},{6,7},{7,6},{8,9},{9,8},{10,11... | collective-permute-start | bytes 147464 | tf_op jit(solution)/shard_map/ppermute | solution.py:354
  7.7 5.9 %collective-permute-start.2 = (bf16[8,3072]{1,0:T(8,128)(2,1)S(1)}, bf16[8,3072]{1,0:T(8,128)(2,1)S(1)}, u32[]{:S(2)}, u32[]{:S(2)}) collective-permute-start(bf16[8,3072]{1,0:T(8,128)(2,1)S(1)} %get-tuple-element.43), channel_id=1, source_target_pairs={{0,2},{1,3},{2,0},{3,1},{4,6},{5,7},{6,4},{7,5},{8,10},{9,11},{10,... | collective-permute-start | bytes 147464 | tf_op jit(solution)/shard_map/ppermute | solution.py:354
  10.3 5.9 %collective-permute-start.3 = (bf16[8,3072]{1,0:T(8,128)(2,1)S(1)}, bf16[8,3072]{1,0:T(8,128)(2,1)S(1)}, u32[]{:S(2)}, u32[]{:S(2)}) collective-permute-start(bf16[8,3072]{1,0:T(8,128)(2,1)S(1)} %get-tuple-element.44), channel_id=1, source_target_pairs={{0,3},{1,2},{2,1},{3,0},{4,7},{5,6},{6,5},{7,4},{8,11},{9,10},{10,... | collective-permute-start | bytes 147464 | tf_op jit(solution)/shard_map/ppermute | solution.py:354
  10.3 13.1 %collective-permute-start = (bf16[32,1024]{1,0:T(8,128)(2,1)S(1)}, bf16[32,1024]{1,0:T(8,128)(2,1)S(1)}, u32[]{:S(2)}, u32[]{:S(2)}) collective-permute-start(bf16[32,1024]{1,0:T(8,128)(2,1)S(1)} %copy-done.2), channel_id=1, source_target_pairs={{0,4},{4,0},{8,12},{12,8},{16,20},{20,16},{24,28},{28,24},{1,5},{5... | collective-permute-start | bytes 196616 | tf_op jit(solution)/shard_map/ppermute | solution.py:354
  16.2 5.3 %collective-permute-start.9 = (bf16[8,3072]{1,0:T(8,128)(2,1)S(1)}, bf16[8,3072]{1,0:T(8,128)(2,1)S(1)}, u32[]{:S(2)}, u32[]{:S(2)}) collective-permute-start(bf16[8,3072]{1,0:T(8,128)(2,1)S(1)} %add_convert_fusion.refs_2_), channel_id=1, source_target_pairs={{0,24},{4,28},{8,16},{12,20},{16,8},{20,12},{24,0},{28,4},{1,25},{... | collective-permute-start | bytes 147464 | tf_op jit(solution)/shard_map/ppermute | solution.py:354
  18.7 4.1 %collective-permute-start.7 = (bf16[8,3072]{1,0:T(8,128)(2,1)S(1)}, bf16[8,3072]{1,0:T(8,128)(2,1)S(1)}, u32[]{:S(2)}, u32[]{:S(2)}) collective-permute-start(bf16[8,3072]{1,0:T(8,128)(2,1)S(1)} %add_convert_fusion.refs_2_), channel_id=1, source_target_pairs={{0,16},{4,20},{8,24},{12,28},{16,0},{20,4},{24,8},{28,12},{1,17},{... | collective-permute-start | bytes 147464 | tf_op jit(solution)/shard_map/ppermute | solution.py:354
  19.2 4.1 %collective-permute-start.5 = (bf16[8,3072]{1,0:T(8,128)(2,1)S(1)}, bf16[8,3072]{1,0:T(8,128)(2,1)S(1)}, u32[]{:S(2)}, u32[]{:S(2)}) collective-permute-start(bf16[8,3072]{1,0:T(8,128)(2,1)S(1)} %add_convert_fusion.refs_2_), channel_id=1, source_target_pairs={{0,8},{4,12},{8,0},{12,4},{16,24},{20,28},{24,16},{28,20},{1,9},{5... | collective-permute-start | bytes 147464 | tf_op jit(solution)/shard_map/ppermute | solution.py:354
  19.8 3.6 %collective-permute-start.4 = (bf16[8,3072]{1,0:T(8,128)(2,1)S(1)}, bf16[8,3072]{1,0:T(8,128)(2,1)S(1)}, u32[]{:S(2)}, u32[]{:S(2)}) collective-permute-start(bf16[8,3072]{1,0:T(8,128)(2,1)S(1)} %add_convert_fusion.refs_2_), channel_id=1, source_target_pairs={{0,4},{4,0},{8,12},{12,8},{16,20},{20,16},{24,28},{28,24},{1,5},{5... | collective-permute-start | bytes 147464 | tf_op jit(solution)/shard_map/ppermute | solution.py:354
  21.5 1.9 %collective-permute-start.10 = (bf16[8,3072]{1,0:T(8,128)(2,1)S(1)}, bf16[8,3072]{1,0:T(8,128)(2,1)S(1)}, u32[]{:S(2)}, u32[]{:S(2)}) collective-permute-start(bf16[8,3072]{1,0:T(8,128)(2,1)S(1)} %collective-permute-done.9.refs_8_), channel_id=1, source_target_pairs={{0,4},{4,0},{8,12},{12,8},{16,20},{20,16},{24,28},{28,24},{1,5},{5... | collective-permute-start | bytes 147464 | tf_op jit(solution)/shard_map/ppermute | solution.py:354
  22.8 1.2 %collective-permute-start.8 = (bf16[8,3072]{1,0:T(8,128)(2,1)S(1)}, bf16[8,3072]{1,0:T(8,128)(2,1)S(1)}, u32[]{:S(2)}, u32[]{:S(2)}) collective-permute-start(bf16[8,3072]{1,0:T(8,128)(2,1)S(1)} %collective-permute-done.7.refs_6_), channel_id=1, source_target_pairs={{0,4},{4,0},{8,12},{12,8},{16,20},{20,16},{24,28},{28,24},{1,5},{5... | collective-permute-start | bytes 147464 | tf_op jit(solution)/shard_map/ppermute | solution.py:354
  23.3 1.2 %collective-permute-start.6 = (bf16[8,3072]{1,0:T(8,128)(2,1)S(1)}, bf16[8,3072]{1,0:T(8,128)(2,1)S(1)}, u32[]{:S(2)}, u32[]{:S(2)}) collective-permute-start(bf16[8,3072]{1,0:T(8,128)(2,1)S(1)} %collective-permute-done.5.refs_4_), channel_id=1, source_target_pairs={{0,4},{4,0},{8,12},{12,8},{16,20},{20,16},{24,28},{28,24},{1,5},{5... | collective-permute-start | bytes 147464 | tf_op jit(solution)/shard_map/ppermute | solution.py:354
  25.4 5.7 %collective-permute-start.11 = (bf16[16,1536]{1,0:T(8,128)(2,1)S(1)}, bf16[16,1536]{1,0:T(8,128)(2,1)S(1)}, u32[]{:S(2)}, u32[]{:S(2)}) collective-permute-start(bf16[16,1536]{1,0:T(8,128)(2,1)S(1)} %get-tuple-element.46), channel_id=1, source_target_pairs={{0,1},{1,0},{2,3},{3,2},{4,5},{5,4},{6,7},{7,6},{8,9},{9,8},{10,11... | collective-permute-start | bytes 147464 | tf_op jit(solution)/shard_map/ppermute | solution.py:354
  25.5 8.8 %collective-permute-start.12 = (bf16[16,1536]{1,0:T(8,128)(2,1)S(1)}, bf16[16,1536]{1,0:T(8,128)(2,1)S(1)}, u32[]{:S(2)}, u32[]{:S(2)}) collective-permute-start(bf16[16,1536]{1,0:T(8,128)(2,1)S(1)} %get-tuple-element.47), channel_id=1, source_target_pairs={{0,2},{1,3},{2,0},{3,1},{4,6},{5,7},{6,4},{7,5},{8,10},{9,11},{10,... | collective-permute-start | bytes 147464 | tf_op jit(solution)/shard_map/ppermute | solution.py:354
  26.8 7.5 %collective-permute-start.13 = (bf16[16,1536]{1,0:T(8,128)(2,1)S(1)}, bf16[16,1536]{1,0:T(8,128)(2,1)S(1)}, u32[]{:S(2)}, u32[]{:S(2)}) collective-permute-start(bf16[16,1536]{1,0:T(8,128)(2,1)S(1)} %get-tuple-element.48), channel_id=1, source_target_pairs={{0,3},{1,2},{2,1},{3,0},{4,7},{5,6},{6,5},{7,4},{8,11},{9,10},{10,... | collective-permute-start | bytes 147464 | tf_op jit(solution)/shard_map/ppermute | solution.py:354
  29.9 5.6 %collective-permute-start.14 = (bf16[16,1536]{1,0:T(8,128)(2,1)S(1)}, bf16[16,1536]{1,0:T(8,128)(2,1)S(1)}, u32[]{:S(2)}, u32[]{:S(2)}) collective-permute-start(bf16[16,1536]{1,0:T(8,128)(2,1)S(1)} %get-tuple-element.54), channel_id=1, source_target_pairs={{0,1},{1,0},{2,3},{3,2},{4,5},{5,4},{6,7},{7,6},{8,9},{9,8},{10,11... | collective-permute-start | bytes 147464 | tf_op jit(solution)/shard_map/ppermute | solution.py:354
  29.9 7.2 %collective-permute-start.15 = (bf16[16,1536]{1,0:T(8,128)(2,1)S(1)}, bf16[16,1536]{1,0:T(8,128)(2,1)S(1)}, u32[]{:S(2)}, u32[]{:S(2)}) collective-permute-start(bf16[16,1536]{1,0:T(8,128)(2,1)S(1)} %get-tuple-element.55), channel_id=1, source_target_pairs={{0,2},{1,3},{2,0},{3,1},{4,6},{5,7},{6,4},{7,5},{8,10},{9,11},{10,... | collective-permute-start | bytes 147464 | tf_op jit(solution)/shard_map/ppermute | solution.py:354
  31.2 5.9 %collective-permute-start.16 = (bf16[16,1536]{1,0:T(8,128)(2,1)S(1)}, bf16[16,1536]{1,0:T(8,128)(2,1)S(1)}, u32[]{:S(2)}, u32[]{:S(2)}) collective-permute-start(bf16[16,1536]{1,0:T(8,128)(2,1)S(1)} %get-tuple-element.56), channel_id=1, source_target_pairs={{0,3},{1,2},{2,1},{3,0},{4,7},{5,6},{6,5},{7,4},{8,11},{9,10},{10,... | collective-permute-start | bytes 147464 | tf_op jit(solution)/shard_map/ppermute | solution.py:354
  37.7 15.8 %collective-permute-start.17 = (bf16[64,1536]{1,0:T(8,128)(2,1)S(1)}, bf16[64,1536]{1,0:T(8,128)(2,1)S(1)}, u32[]{:S(2)}, u32[]{:S(2)}) collective-permute-start(bf16[64,1536]{1,0:T(8,128)(2,1)S(1)} %get-tuple-element.60.grad_values.refs_6_), channel_id=1, source_target_pairs={{0,2},{1,3},{2,0},{3,1},{4,6},{5,7},{6,4},{7,5},{8,10},{9,11},{10,... | collective-permute-start | bytes 589832 | tf_op jit(solution)/shard_map/ppermute | solution.py:354
  38.5 18.3 %collective-permute-start.19 = (bf16[64,1536]{1,0:T(8,128)(2,1)S(1)}, bf16[64,1536]{1,0:T(8,128)(2,1)S(1)}, u32[]{:S(2)}, u32[]{:S(2)}) collective-permute-start(bf16[64,1536]{1,0:T(8,128)(2,1)S(1)} %get-tuple-element.66.refs_1_), channel_id=1, source_target_pairs={{0,2},{1,3},{2,0},{3,1},{4,6},{5,7},{6,4},{7,5},{8,10},{9,11},{10,... | collective-permute-start | bytes 589832 | tf_op jit(solution)/shard_map/ppermute | solution.py:354
  40.7 26.5 %collective-permute-start.18 = (bf16[64,3072]{1,0:T(8,128)(2,1)S(1)}, bf16[64,3072]{1,0:T(8,128)(2,1)S(1)}, u32[]{:S(2)}, u32[]{:S(2)}) collective-permute-start(bf16[64,3072]{1,0:T(8,128)(2,1)S(1)} %get-tuple-element.69), channel_id=1, source_target_pairs={{0,1},{1,0},{2,3},{3,2},{4,5},{5,4},{6,7},{7,6},{8,9},{9,8},{10,11... | collective-permute-start | bytes 1179656 | tf_op jit(solution)/shard_map/ppermute | solution.py:388
  53.5 13.8 %collective-permute-start.20 = (bf16[64,3072]{1,0:T(8,128)(2,1)S(1)}, bf16[64,3072]{1,0:T(8,128)(2,1)S(1)}, u32[]{:S(2)}, u32[]{:S(2)}) collective-permute-start(bf16[64,3072]{1,0:T(8,128)(2,1)S(1)} %get-tuple-element.69), channel_id=1, source_target_pairs={{1,2},{2,1},{5,6},{6,5},{9,10},{10,9},{13,14},{14,13},{17,18},{18,... | collective-permute-start | bytes 1179656 | tf_op jit(solution)/shard_map/ppermute | solution.py:392
  56.8 8.3 %collective-permute-start.21 = (bf16[64,1536]{1,0:T(8,128)(2,1)S(1)}, bf16[64,1536]{1,0:T(8,128)(2,1)S(1)}, u32[]{:S(2)}, u32[]{:S(2)}) collective-permute-start(bf16[64,1536]{1,0:T(8,128)(2,1)S(1)} %collective-permute-done.19.refs_3_), channel_id=1, source_target_pairs={{1,0},{2,3},{5,4},{6,7},{9,8},{10,11},{13,12},{14,15},{17,16},{18,... | collective-permute-start | bytes 589832 | tf_op jit(solution)/shard_map/ppermute | solution.py:390
  58.1 9.1 %collective-permute-start.22 = (bf16[64,1536]{1,0:T(8,128)(2,1)S(1)}, bf16[64,1536]{1,0:T(8,128)(2,1)S(1)}, u32[]{:S(2)}, u32[]{:S(2)}) collective-permute-start(bf16[64,1536]{1,0:T(8,128)(2,1)S(1)} %collective-permute-done.17.refs_8_), channel_id=1, source_target_pairs={{1,0},{2,3},{5,4},{6,7},{9,8},{10,11},{13,12},{14,15},{17,16},{18,... | collective-permute-start | bytes 589832 | tf_op jit(solution)/shard_map/ppermute | solution.py:390

commit v5 on v4

--- a/solution.py
+++ b/solution.py
@@ -67,7 +67,7 @@
         for i in range(chunks)
     ]
     for copy in copies:
-        copy.start()
+        copy.start(priority=1)
     member = lax.axis_index("fsdp")
     row = lax.broadcasted_iota(jnp.int32, (depth, depth), 0)
     column = lax.broadcasted_iota(jnp.int32, (depth, depth), 1)

time: 70.6 us -> 69.9 us (0.990)
    pallas_call x1, Pallas kernels: 3.92 us -> 3.21 us  [project(): pl.pallas_call(functools.partial(project_kernel, groups, paired, chunks),...]
where the time goes in v5:
time: 69.9 us; the launch traced here: 69.7 us
  starting transfers between devices  25.4 us (36%)
  waiting for transfers between devices  22 us (31%)
  Pallas kernels  10.6 us (15%)
  blocking collectives  10.6 us (15%)
  between operations  0.85 us (1%)
    ppermute x19, starting transfers between devices, swap(): lax.ppermute(x, axis, [(i, i ^ k) for i in range(lax.axis_size(axis))])  21.1 us
    ppermute x19, waiting for transfers between devices, swap(): lax.ppermute(x, axis, [(i, i ^ k) for i in range(lax.axis_size(axis))])  15.9 us
    all_gather x1, blocking collectives, gather_chips(): return lax.all_gather(x, 'dp', axis=0, tiled=True, axis_index_groups=cores)  10.6 us
    ppermute x2, waiting for transfers between devices, gather_line(): outer = [lax.ppermute(piece, 'fsdp', outward) for piece in second]  6.16 us
    pallas_call x1, Pallas kernels, project(): pl.pallas_call(functools.partial(project_kernel, groups, paired, chunks),...  3.21 us
    pallas_call x1, Pallas kernels, weight_grad(): pl.pallas_call(functools.partial(weight_kernel, line, blocks), in_specs=[...  3.14 us
    ppermute x2, starting transfers between devices, gather_line(): outer = [lax.ppermute(piece, 'fsdp', outward) for piece in second]  2.57 us
    pallas_call x1, Pallas kernels, slot_texts(): pl.pallas_call(functools.partial(text_kernel, groups, each, depth, paired...  1.64 us
  transfers between devices with their start and end apart: 23, of which 12 were waited for; matrix products, arithmetic and copies ran while one was open for 0% of the time, Pallas kernels for 4%

profile of v5, /device:TPU:0, one launch (start us, length us, event | category | flops | bytes accessed | tf_op | source)
XLA Modules:
  0.0 69.7 jit_solution(16844909677783428741)
XLA Ops:
  0.6 0.0 copy-start.2
  0.6 0.0 copy-start.3
  0.7 0.0 copy-start.4
  0.7 0.0 copy-start.5
  0.7 0.0 copy-start.6
  0.7 0.0 copy-start.1
  0.7 0.0 copy-start
  0.7 3.2 %project.1 = (bf16[8,3072]{1,0:T(8,128)(2,1)S(1)}, bf16[8,3072]{1,0:T(8,128)(2,1)S(1)}, bf16[8,3072]{1,0:T(8,128)(2,1)S(1)}, bf16[8,3072]{1,0:T(8,128)(2,1)S(1)}) custom-call(bf16[32,1024]{1,0:T(8,128)(2,1)} %refs_0_, bf16[1024,3072]{1,0:T(8,128)(2,1)} %weight.1), custom_call_target="tpu_custom_call" | custom-call | tf_op jit(solution)/shard_map/project/pallas_call | solution.py:95
  3.9 3.1 %collective-permute-start.1 = (bf16[8,3072]{1,0:T(8,128)(2,1)S(1)}, bf16[8,3072]{1,0:T(8,128)(2,1)S(1)}, u32[]{:S(2)}, u32[]{:S(2)}) collective-permute-start(bf16[8,3072]{1,0:T(8,128)(2,1)S(1)} %get-tuple-element.42), channel_id=1, source_target_pairs={{0,1},{1,0},{2,3},{3,2},{4,5},{5,4},{6,7},{7,6},{8,9},{9,8},{10,11... | collective-permute-start | bytes 147464 | tf_op jit(solution)/shard_map/ppermute | solution.py:354
  7.0 2.6 %collective-permute-start.2 = (bf16[8,3072]{1,0:T(8,128)(2,1)S(1)}, bf16[8,3072]{1,0:T(8,128)(2,1)S(1)}, u32[]{:S(2)}, u32[]{:S(2)}) collective-permute-start(bf16[8,3072]{1,0:T(8,128)(2,1)S(1)} %get-tuple-element.43), channel_id=1, source_target_pairs={{0,2},{1,3},{2,0},{3,1},{4,6},{5,7},{6,4},{7,5},{8,10},{9,11},{10,... | collective-permute-start | bytes 147464 | tf_op jit(solution)/shard_map/ppermute | solution.py:354
  9.6 0.0 collective-permute-start.3
  9.6 0.0 copy-done.2
  9.6 0.0 collective-permute-start
  9.6 0.1 pad_add_fusion.1
  9.7 0.0 collective-permute-done.1
  9.7 3.2 %collective-permute-done.2 = bf16[8,3072]{1,0:T(8,128)(2,1)S(1)} collective-permute-done((bf16[8,3072]{1,0:T(8,128)(2,1)S(1)}, bf16[8,3072]{1,0:T(8,128)(2,1)S(1)}, u32[]{:S(2)}, u32[]{:S(2)}) %collective-permute-start.2) | collective-permute-done | bytes 49184 | tf_op jit(solution)/shard_map/ppermute | solution.py:354
  12.9 2.6 %collective-permute-done.3 = bf16[8,3072]{1,0:T(8,128)(2,1)S(1)} collective-permute-done((bf16[8,3072]{1,0:T(8,128)(2,1)S(1)}, bf16[8,3072]{1,0:T(8,128)(2,1)S(1)}, u32[]{:S(2)}, u32[]{:S(2)}) %collective-permute-start.3) | collective-permute-done | bytes 49184 | tf_op jit(solution)/shard_map/ppermute | solution.py:354
  15.5 2.5 %collective-permute-start.9 = (bf16[8,3072]{1,0:T(8,128)(2,1)S(1)}, bf16[8,3072]{1,0:T(8,128)(2,1)S(1)}, u32[]{:S(2)}, u32[]{:S(2)}) collective-permute-start(bf16[8,3072]{1,0:T(8,128)(2,1)S(1)} %add_convert_fusion.refs_2_), channel_id=1, source_target_pairs={{0,24},{4,28},{8,16},{12,20},{16,8},{20,12},{24,0},{28,4},{1,25},{... | collective-permute-start | bytes 147464 | tf_op jit(solution)/shard_map/ppermute | solution.py:354
  18.0 0.5 collective-permute-start.7
  18.5 0.5 collective-permute-start.5
  19.1 0.0 collective-permute-start.4
  19.1 1.7 %collective-permute-done.9.refs_8_ = bf16[8,3072]{1,0:T(8,128)(2,1)S(1)} collective-permute-done((bf16[8,3072]{1,0:T(8,128)(2,1)S(1)}, bf16[8,3072]{1,0:T(8,128)(2,1)S(1)}, u32[]{:S(2)}, u32[]{:S(2)}) %collective-permute-start.9) | collective-permute-done | bytes 49184 | tf_op jit(solution)/shard_map/ppermute | solution.py:354
  20.8 0.0 collective-permute-start.10
  20.8 1.3 %collective-permute-done.7.refs_6_ = bf16[8,3072]{1,0:T(8,128)(2,1)S(1)} collective-permute-done((bf16[8,3072]{1,0:T(8,128)(2,1)S(1)}, bf16[8,3072]{1,0:T(8,128)(2,1)S(1)}, u32[]{:S(2)}, u32[]{:S(2)}) %collective-permute-start.7) | collective-permute-done | bytes 49184 | tf_op jit(solution)/shard_map/ppermute | solution.py:354
  22.1 0.0 collective-permute-start.8
  22.1 0.5 collective-permute-done.5.refs_4_
  22.6 0.0 collective-permute-start.6
  22.6 0.0 copy-done.4
  22.7 0.0 collective-permute-done.refs_1_
  22.7 0.0 collective-permute-done.4.refs_3_
  22.7 0.0 collective-permute-done.10.refs_9_
  22.7 0.7 collective-permute-done.8.refs_7_
  23.4 0.5 collective-permute-done.6.refs_5_
  23.9 0.8 %select_rows.1 = (bf16[16,1536]{1,0:T(8,128)(2,1)S(1)}, bf16[16,1536]{1,0:T(8,128)(2,1)S(1)}, bf16[16,1536]{1,0:T(8,128)(2,1)S(1)}, bf16[16,1536]{1,0:T(8,128)(2...) custom-call(s32[4,8]{1,0:T(4,128)S(1)} %pad_add_fusion.table, ...), custom_call_target="tpu_custom_call" | custom-call | tf_op jit(solution)/shard_map/select_rows/pallas_call | solution.py:142
  24.7 0.1 collective-permute-start.11
  24.8 1.3 %collective-permute-start.12 = (bf16[16,1536]{1,0:T(8,128)(2,1)S(1)}, bf16[16,1536]{1,0:T(8,128)(2,1)S(1)}, u32[]{:S(2)}, u32[]{:S(2)}) collective-permute-start(bf16[16,1536]{1,0:T(8,128)(2,1)S(1)} %get-tuple-element.47), channel_id=1, source_target_pairs={{0,2},{1,3},{2,0},{3,1},{4,6},{5,7},{6,4},{7,5},{8,10},{9,11},{10,... | collective-permute-start | bytes 147464 | tf_op jit(solution)/shard_map/ppermute | solution.py:354
  26.1 3.1 %collective-permute-start.13 = (bf16[16,1536]{1,0:T(8,128)(2,1)S(1)}, bf16[16,1536]{1,0:T(8,128)(2,1)S(1)}, u32[]{:S(2)}, u32[]{:S(2)}) collective-permute-start(bf16[16,1536]{1,0:T(8,128)(2,1)S(1)} %get-tuple-element.48), channel_id=1, source_target_pairs={{0,3},{1,2},{2,1},{3,0},{4,7},{5,6},{6,5},{7,4},{8,11},{9,10},{10,... | collective-permute-start | bytes 147464 | tf_op jit(solution)/shard_map/ppermute | solution.py:354
  29.2 0.0 collective-permute-start.14
  29.2 1.3 %collective-permute-start.15 = (bf16[16,1536]{1,0:T(8,128)(2,1)S(1)}, bf16[16,1536]{1,0:T(8,128)(2,1)S(1)}, u32[]{:S(2)}, u32[]{:S(2)}) collective-permute-start(bf16[16,1536]{1,0:T(8,128)(2,1)S(1)} %get-tuple-element.55), channel_id=1, source_target_pairs={{0,2},{1,3},{2,0},{3,1},{4,6},{5,7},{6,4},{7,5},{8,10},{9,11},{10,... | collective-permute-start | bytes 147464 | tf_op jit(solution)/shard_map/ppermute | solution.py:354
  30.5 0.0 collective-permute-done.11.refs_1_
  30.5 3.1 %collective-permute-start.16 = (bf16[16,1536]{1,0:T(8,128)(2,1)S(1)}, bf16[16,1536]{1,0:T(8,128)(2,1)S(1)}, u32[]{:S(2)}, u32[]{:S(2)}) collective-permute-start(bf16[16,1536]{1,0:T(8,128)(2,1)S(1)} %get-tuple-element.56), channel_id=1, source_target_pairs={{0,3},{1,2},{2,1},{3,0},{4,7},{5,6},{6,5},{7,4},{8,11},{9,10},{10,... | collective-permute-start | bytes 147464 | tf_op jit(solution)/shard_map/ppermute | solution.py:354
  33.6 0.0 collective-permute-done.12.refs_2_
  33.6 0.0 collective-permute-done.13.refs_3_
  33.6 0.0 copy-done
  33.6 1.1 %value_gradients.1 = (f32[12,64,128]{2,1,0:T(8,128)S(1)}, bf16[64,1536]{1,0:T(8,128)(2,1)S(1)}) custom-call(s32[4,8]{1,0:T(4,128)S(1)} %pad_add_fusion.table, bf16[128,1536]{1,0:T(8,128)(2,1)S(1)} %copy-done, bf16[128,1536]{1,0:T(8,128)(2,1)S(1)} %copy-done.1, bf16[16,1536]{1,0:T(8,128)(2,1)S(1)} %get-tuple-element.45.refs_0_, ...), custom_call_target="tpu_custom_call" | custom-call | tf_op jit(solution)/shard_map/value_gradients/pallas_call | solution.py:200
  34.7 0.0 collective-permute-done.14.refs_1_
  34.8 1.7 %collective-permute-done.15.refs_2_ = bf16[16,1536]{1,0:T(8,128)(2,1)S(1)} collective-permute-done((bf16[16,1536]{1,0:T(8,128)(2,1)S(1)}, bf16[16,1536]{1,0:T(8,128)(2,1)S(1)}, u32[]{:S(2)}, u32[]{:S(2)}) %collective-permute-start.15) | collective-permute-done | bytes 49184 | tf_op jit(solution)/shard_map/ppermute | solution.py:354
  36.4 0.0 collective-permute-done.16.refs_3_
  36.4 0.6 key_gradients.1
  37.0 0.8 %collective-permute-start.17 = (bf16[64,1536]{1,0:T(8,128)(2,1)S(1)}, bf16[64,1536]{1,0:T(8,128)(2,1)S(1)}, u32[]{:S(2)}, u32[]{:S(2)}) collective-permute-start(bf16[64,1536]{1,0:T(8,128)(2,1)S(1)} %get-tuple-element.60.grad_values.refs_6_), channel_id=1, source_target_pairs={{0,2},{1,3},{2,0},{3,1},{4,6},{5,7},{6,4},{7,5},{8,10},{9,11},{10,... | collective-permute-start | bytes 589832 | tf_op jit(solution)/shard_map/ppermute | solution.py:354
  37.8 2.2 %collective-permute-start.19 = (bf16[64,1536]{1,0:T(8,128)(2,1)S(1)}, bf16[64,1536]{1,0:T(8,128)(2,1)S(1)}, u32[]{:S(2)}, u32[]{:S(2)}) collective-permute-start(bf16[64,1536]{1,0:T(8,128)(2,1)S(1)} %get-tuple-element.66.refs_1_), channel_id=1, source_target_pairs={{0,2},{1,3},{2,0},{3,1},{4,6},{5,7},{6,4},{7,5},{8,10},{9,11},{10,... | collective-permute-start | bytes 589832 | tf_op jit(solution)/shard_map/ppermute | solution.py:354
  40.0 1.1 %collective-permute-start.18 = (bf16[64,3072]{1,0:T(8,128)(2,1)S(1)}, bf16[64,3072]{1,0:T(8,128)(2,1)S(1)}, u32[]{:S(2)}, u32[]{:S(2)}) collective-permute-start(bf16[64,3072]{1,0:T(8,128)(2,1)S(1)} %get-tuple-element.69), channel_id=1, source_target_pairs={{0,1},{1,0},{2,3},{3,2},{4,5},{5,4},{6,7},{7,6},{8,9},{9,8},{10,11... | collective-permute-start | bytes 1179656 | tf_op jit(solution)/shard_map/ppermute | solution.py:388
  41.1 10.6 %all_gather.3.text = bf16[256,1024]{1,0:T(8,128)(2,1)S(1)} all-gather(bf16[64,1024]{1,0:T(8,128)(2,1)S(1)} %get-tuple-element.61), channel_id=1, replica_groups={{0,8,16,24},{4,12,20,28},{1,9,17,25},{5,13,21,29},{2,10,18,26},{6,14,22..., dimensions={0}, use_global_device_ids=true | all-gather | bytes 655360 | tf_op jit(solution)/shard_map/all_gather | solution.py:371
  51.7 1.1 %collective-permute-done.17.refs_8_ = bf16[64,1536]{1,0:T(8,128)(2,1)S(1)} collective-permute-done((bf16[64,1536]{1,0:T(8,128)(2,1)S(1)}, bf16[64,1536]{1,0:T(8,128)(2,1)S(1)}, u32[]{:S(2)}, u32[]{:S(2)}) %collective-permute-start.17) | collective-permute-done | bytes 196640 | tf_op jit(solution)/shard_map/ppermute | solution.py:354
  52.8 0.7 collective-permute-start.20
  53.5 2.7 %collective-permute-done.19.refs_3_ = bf16[64,1536]{1,0:T(8,128)(2,1)S(1)} collective-permute-done((bf16[64,1536]{1,0:T(8,128)(2,1)S(1)}, bf16[64,1536]{1,0:T(8,128)(2,1)S(1)}, u32[]{:S(2)}, u32[]{:S(2)}) %collective-permute-start.19) | collective-permute-done | bytes 196640 | tf_op jit(solution)/shard_map/ppermute | solution.py:354
  56.1 1.3 %collective-permute-start.21 = (bf16[64,1536]{1,0:T(8,128)(2,1)S(1)}, bf16[64,1536]{1,0:T(8,128)(2,1)S(1)}, u32[]{:S(2)}, u32[]{:S(2)}) collective-permute-start(bf16[64,1536]{1,0:T(8,128)(2,1)S(1)} %collective-permute-done.19.refs_3_), channel_id=1, source_target_pairs={{1,0},{2,3},{5,4},{6,7},{9,8},{10,11},{13,12},{14,15},{17,16},{18,... | collective-permute-start | bytes 589832 | tf_op jit(solution)/shard_map/ppermute | solution.py:390
  57.4 1.3 %collective-permute-start.22 = (bf16[64,1536]{1,0:T(8,128)(2,1)S(1)}, bf16[64,1536]{1,0:T(8,128)(2,1)S(1)}, u32[]{:S(2)}, u32[]{:S(2)}) collective-permute-start(bf16[64,1536]{1,0:T(8,128)(2,1)S(1)} %collective-permute-done.17.refs_8_), channel_id=1, source_target_pairs={{1,0},{2,3},{5,4},{6,7},{9,8},{10,11},{13,12},{14,15},{17,16},{18,... | collective-permute-start | bytes 589832 | tf_op jit(solution)/shard_map/ppermute | solution.py:390
  58.7 1.6 %slot_texts.1 = (bf16[1024,256]{1,0:T(8,128)(2,1)S(1)}, bf16[128,1536]{1,0:T(8,128)(2,1)}) custom-call(s32[4,8]{1,0:T(4,128)S(1)} %pad_add_fusion.table, bf16[256,1024]{1,0:T(8,128)(2,1)S(1)} %all_gather.3.text, bf16[12,64,128]{2,1,0:T(8,128)(2,1)S(1)} %get-tuple-element.63.score_grads, bf16[16,1536]{1,0:T(8,128)(2,1)S(1)} %get-tuple-element.45.refs_0_, ...), custom_call_target="tpu_custom_call" | custom-call | tf_op jit(solution)/shard_map/slot_texts/pallas_call | solution.py:289
  60.4 4.1 %collective-permute-done.21.refs_5_ = bf16[64,1536]{1,0:T(8,128)(2,1)S(1)} collective-permute-done((bf16[64,1536]{1,0:T(8,128)(2,1)S(1)}, bf16[64,1536]{1,0:T(8,128)(2,1)S(1)}, u32[]{:S(2)}, u32[]{:S(2)}) %collective-permute-start.21) | collective-permute-done | bytes 196640 | tf_op jit(solution)/shard_map/ppermute | solution.py:390
  64.4 2.1 %collective-permute-done.22.refs_10_ = bf16[64,1536]{1,0:T(8,128)(2,1)S(1)} collective-permute-done((bf16[64,1536]{1,0:T(8,128)(2,1)S(1)}, bf16[64,1536]{1,0:T(8,128)(2,1)S(1)}, u32[]{:S(2)}, u32[]{:S(2)}) %collective-permute-start.22) | collective-permute-done | bytes 196640 | tf_op jit(solution)/shard_map/ppermute | solution.py:390
  66.5 0.0 collective-permute-done.18.refs_2_.refs_7_
  66.5 0.0 collective-permute-done.20.refs_4_.refs_9_
  66.5 3.1 %weight_gradient.1 = bf16[1024,3072]{1,0:T(8,128)(2,1)} custom-call(bf16[1024,256]{1,0:T(8,128)(2,1)S(1)} %get-tuple-element.65.refs_0_, bf16[64,1536]{1,0:T(8,128)(2,1)S(1)} %get-tuple-element.66.refs_1_, bf16[64,3072]{1,0:T(8,128)(2,1)S(1)} %collective-permute-done.18.refs_2_.refs_7_, bf16[64,1536]{1,0:T(8,128)(2,1)S(1)} %collective-permute-done.19.refs_3_, ...), custom_call_target="tpu_custom_call" | custom-call | tf_op jit(solution)/shard_map/weight_gradient/pallas_call | solution.py:338
  (7 shorter events, 0.1 us)
Async XLA Ops:
  0.6 9.0 %copy-start.2 = (bf16[32,1024]{1,0:T(8,128)(2,1)S(1)}, bf16[32,1024]{1,0:T(8,128)(2,1)}, u32[]{:S(2)}) copy-start(bf16[32,1024]{1,0:T(8,128)(2,1)} %refs_0_) | copy-start | bytes 196612
  0.6 9.0 %copy-start.3 = (s32[1,2]{1,0:T(1,128)S(1)}, s32[1,2]{1,0:T(1,128)}, u32[]{:S(2)}) copy-start(s32[1,2]{1,0:T(1,128)} %param.12) | copy-start | bytes 28
  0.7 22.0 %copy-start.4 = (s32[1,8]{1,0:T(1,128)S(1)}, s32[1,8]{1,0:T(1,128)}, u32[]{:S(2)}) copy-start(s32[1,8]{1,0:T(1,128)} %param.15) | copy-start | bytes 100
  0.7 22.0 %copy-start.5 = (s32[1,8]{1,0:T(1,128)S(1)}, s32[1,8]{1,0:T(1,128)}, u32[]{:S(2)}) copy-start(s32[1,8]{1,0:T(1,128)} %param.14) | copy-start | bytes 100
  0.7 22.0 %copy-start.6 = (s32[1,8]{1,0:T(1,128)S(1)}, s32[1,8]{1,0:T(1,128)}, u32[]{:S(2)}) copy-start(s32[1,8]{1,0:T(1,128)} %param.13) | copy-start | bytes 100
  0.7 32.9 %copy-start.1 = (bf16[128,1536]{1,0:T(8,128)(2,1)S(1)}, bf16[128,1536]{1,0:T(8,128)(2,1)}, u32[]{:S(2)}) copy-start(bf16[128,1536]{1,0:T(8,128)(2,1)} %cotangent.3) | copy-start | bytes 1179652
  0.7 32.9 %copy-start = (bf16[128,1536]{1,0:T(8,128)(2,1)S(1)}, bf16[128,1536]{1,0:T(8,128)(2,1)}, u32[]{:S(2)}) copy-start(bf16[128,1536]{1,0:T(8,128)(2,1)} %queries.3) | copy-start | bytes 1179652
  3.9 5.8 %collective-permute-start.1 = (bf16[8,3072]{1,0:T(8,128)(2,1)S(1)}, bf16[8,3072]{1,0:T(8,128)(2,1)S(1)}, u32[]{:S(2)}, u32[]{:S(2)}) collective-permute-start(bf16[8,3072]{1,0:T(8,128)(2,1)S(1)} %get-tuple-element.42), channel_id=1, source_target_pairs={{0,1},{1,0},{2,3},{3,2},{4,5},{5,4},{6,7},{7,6},{8,9},{9,8},{10,11... | collective-permute-start | bytes 147464 | tf_op jit(solution)/shard_map/ppermute | solution.py:354
  7.0 5.9 %collective-permute-start.2 = (bf16[8,3072]{1,0:T(8,128)(2,1)S(1)}, bf16[8,3072]{1,0:T(8,128)(2,1)S(1)}, u32[]{:S(2)}, u32[]{:S(2)}) collective-permute-start(bf16[8,3072]{1,0:T(8,128)(2,1)S(1)} %get-tuple-element.43), channel_id=1, source_target_pairs={{0,2},{1,3},{2,0},{3,1},{4,6},{5,7},{6,4},{7,5},{8,10},{9,11},{10,... | collective-permute-start | bytes 147464 | tf_op jit(solution)/shard_map/ppermute | solution.py:354
  9.6 5.9 %collective-permute-start.3 = (bf16[8,3072]{1,0:T(8,128)(2,1)S(1)}, bf16[8,3072]{1,0:T(8,128)(2,1)S(1)}, u32[]{:S(2)}, u32[]{:S(2)}) collective-permute-start(bf16[8,3072]{1,0:T(8,128)(2,1)S(1)} %get-tuple-element.44), channel_id=1, source_target_pairs={{0,3},{1,2},{2,1},{3,0},{4,7},{5,6},{6,5},{7,4},{8,11},{9,10},{10,... | collective-permute-start | bytes 147464 | tf_op jit(solution)/shard_map/ppermute | solution.py:354
  9.6 13.1 %collective-permute-start = (bf16[32,1024]{1,0:T(8,128)(2,1)S(1)}, bf16[32,1024]{1,0:T(8,128)(2,1)S(1)}, u32[]{:S(2)}, u32[]{:S(2)}) collective-permute-start(bf16[32,1024]{1,0:T(8,128)(2,1)S(1)} %copy-done.2), channel_id=1, source_target_pairs={{0,4},{4,0},{8,12},{12,8},{16,20},{20,16},{24,28},{28,24},{1,5},{5... | collective-permute-start | bytes 196616 | tf_op jit(solution)/shard_map/ppermute | solution.py:354
  15.5 5.3 %collective-permute-start.9 = (bf16[8,3072]{1,0:T(8,128)(2,1)S(1)}, bf16[8,3072]{1,0:T(8,128)(2,1)S(1)}, u32[]{:S(2)}, u32[]{:S(2)}) collective-permute-start(bf16[8,3072]{1,0:T(8,128)(2,1)S(1)} %add_convert_fusion.refs_2_), channel_id=1, source_target_pairs={{0,24},{4,28},{8,16},{12,20},{16,8},{20,12},{24,0},{28,4},{1,25},{... | collective-permute-start | bytes 147464 | tf_op jit(solution)/shard_map/ppermute | solution.py:354
  18.0 4.1 %collective-permute-start.7 = (bf16[8,3072]{1,0:T(8,128)(2,1)S(1)}, bf16[8,3072]{1,0:T(8,128)(2,1)S(1)}, u32[]{:S(2)}, u32[]{:S(2)}) collective-permute-start(bf16[8,3072]{1,0:T(8,128)(2,1)S(1)} %add_convert_fusion.refs_2_), channel_id=1, source_target_pairs={{0,16},{4,20},{8,24},{12,28},{16,0},{20,4},{24,8},{28,12},{1,17},{... | collective-permute-start | bytes 147464 | tf_op jit(solution)/shard_map/ppermute | solution.py:354
  18.5 4.1 %collective-permute-start.5 = (bf16[8,3072]{1,0:T(8,128)(2,1)S(1)}, bf16[8,3072]{1,0:T(8,128)(2,1)S(1)}, u32[]{:S(2)}, u32[]{:S(2)}) collective-permute-start(bf16[8,3072]{1,0:T(8,128)(2,1)S(1)} %add_convert_fusion.refs_2_), channel_id=1, source_target_pairs={{0,8},{4,12},{8,0},{12,4},{16,24},{20,28},{24,16},{28,20},{1,9},{5... | collective-permute-start | bytes 147464 | tf_op jit(solution)/shard_map/ppermute | solution.py:354
  19.1 3.6 %collective-permute-start.4 = (bf16[8,3072]{1,0:T(8,128)(2,1)S(1)}, bf16[8,3072]{1,0:T(8,128)(2,1)S(1)}, u32[]{:S(2)}, u32[]{:S(2)}) collective-permute-start(bf16[8,3072]{1,0:T(8,128)(2,1)S(1)} %add_convert_fusion.refs_2_), channel_id=1, source_target_pairs={{0,4},{4,0},{8,12},{12,8},{16,20},{20,16},{24,28},{28,24},{1,5},{5... | collective-permute-start | bytes 147464 | tf_op jit(solution)/shard_map/ppermute | solution.py:354
  20.8 1.9 %collective-permute-start.10 = (bf16[8,3072]{1,0:T(8,128)(2,1)S(1)}, bf16[8,3072]{1,0:T(8,128)(2,1)S(1)}, u32[]{:S(2)}, u32[]{:S(2)}) collective-permute-start(bf16[8,3072]{1,0:T(8,128)(2,1)S(1)} %collective-permute-done.9.refs_8_), channel_id=1, source_target_pairs={{0,4},{4,0},{8,12},{12,8},{16,20},{20,16},{24,28},{28,24},{1,5},{5... | collective-permute-start | bytes 147464 | tf_op jit(solution)/shard_map/ppermute | solution.py:354
  22.1 1.2 %collective-permute-start.8 = (bf16[8,3072]{1,0:T(8,128)(2,1)S(1)}, bf16[8,3072]{1,0:T(8,128)(2,1)S(1)}, u32[]{:S(2)}, u32[]{:S(2)}) collective-permute-start(bf16[8,3072]{1,0:T(8,128)(2,1)S(1)} %collective-permute-done.7.refs_6_), channel_id=1, source_target_pairs={{0,4},{4,0},{8,12},{12,8},{16,20},{20,16},{24,28},{28,24},{1,5},{5... | collective-permute-start | bytes 147464 | tf_op jit(solution)/shard_map/ppermute | solution.py:354
  22.6 1.2 %collective-permute-start.6 = (bf16[8,3072]{1,0:T(8,128)(2,1)S(1)}, bf16[8,3072]{1,0:T(8,128)(2,1)S(1)}, u32[]{:S(2)}, u32[]{:S(2)}) collective-permute-start(bf16[8,3072]{1,0:T(8,128)(2,1)S(1)} %collective-permute-done.5.refs_4_), channel_id=1, source_target_pairs={{0,4},{4,0},{8,12},{12,8},{16,20},{20,16},{24,28},{28,24},{1,5},{5... | collective-permute-start | bytes 147464 | tf_op jit(solution)/shard_map/ppermute | solution.py:354
  24.7 5.8 %collective-permute-start.11 = (bf16[16,1536]{1,0:T(8,128)(2,1)S(1)}, bf16[16,1536]{1,0:T(8,128)(2,1)S(1)}, u32[]{:S(2)}, u32[]{:S(2)}) collective-permute-start(bf16[16,1536]{1,0:T(8,128)(2,1)S(1)} %get-tuple-element.46), channel_id=1, source_target_pairs={{0,1},{1,0},{2,3},{3,2},{4,5},{5,4},{6,7},{7,6},{8,9},{9,8},{10,11... | collective-permute-start | bytes 147464 | tf_op jit(solution)/shard_map/ppermute | solution.py:354
  24.8 8.8 %collective-permute-start.12 = (bf16[16,1536]{1,0:T(8,128)(2,1)S(1)}, bf16[16,1536]{1,0:T(8,128)(2,1)S(1)}, u32[]{:S(2)}, u32[]{:S(2)}) collective-permute-start(bf16[16,1536]{1,0:T(8,128)(2,1)S(1)} %get-tuple-element.47), channel_id=1, source_target_pairs={{0,2},{1,3},{2,0},{3,1},{4,6},{5,7},{6,4},{7,5},{8,10},{9,11},{10,... | collective-permute-start | bytes 147464 | tf_op jit(solution)/shard_map/ppermute | solution.py:354
  26.1 7.5 %collective-permute-start.13 = (bf16[16,1536]{1,0:T(8,128)(2,1)S(1)}, bf16[16,1536]{1,0:T(8,128)(2,1)S(1)}, u32[]{:S(2)}, u32[]{:S(2)}) collective-permute-start(bf16[16,1536]{1,0:T(8,128)(2,1)S(1)} %get-tuple-element.48), channel_id=1, source_target_pairs={{0,3},{1,2},{2,1},{3,0},{4,7},{5,6},{6,5},{7,4},{8,11},{9,10},{10,... | collective-permute-start | bytes 147464 | tf_op jit(solution)/shard_map/ppermute | solution.py:354
  29.2 5.6 %collective-permute-start.14 = (bf16[16,1536]{1,0:T(8,128)(2,1)S(1)}, bf16[16,1536]{1,0:T(8,128)(2,1)S(1)}, u32[]{:S(2)}, u32[]{:S(2)}) collective-permute-start(bf16[16,1536]{1,0:T(8,128)(2,1)S(1)} %get-tuple-element.54), channel_id=1, source_target_pairs={{0,1},{1,0},{2,3},{3,2},{4,5},{5,4},{6,7},{7,6},{8,9},{9,8},{10,11... | collective-permute-start | bytes 147464 | tf_op jit(solution)/shard_map/ppermute | solution.py:354
  29.2 7.2 %collective-permute-start.15 = (bf16[16,1536]{1,0:T(8,128)(2,1)S(1)}, bf16[16,1536]{1,0:T(8,128)(2,1)S(1)}, u32[]{:S(2)}, u32[]{:S(2)}) collective-permute-start(bf16[16,1536]{1,0:T(8,128)(2,1)S(1)} %get-tuple-element.55), channel_id=1, source_target_pairs={{0,2},{1,3},{2,0},{3,1},{4,6},{5,7},{6,4},{7,5},{8,10},{9,11},{10,... | collective-permute-start | bytes 147464 | tf_op jit(solution)/shard_map/ppermute | solution.py:354
  30.5 5.9 %collective-permute-start.16 = (bf16[16,1536]{1,0:T(8,128)(2,1)S(1)}, bf16[16,1536]{1,0:T(8,128)(2,1)S(1)}, u32[]{:S(2)}, u32[]{:S(2)}) collective-permute-start(bf16[16,1536]{1,0:T(8,128)(2,1)S(1)} %get-tuple-element.56), channel_id=1, source_target_pairs={{0,3},{1,2},{2,1},{3,0},{4,7},{5,6},{6,5},{7,4},{8,11},{9,10},{10,... | collective-permute-start | bytes 147464 | tf_op jit(solution)/shard_map/ppermute | solution.py:354
  37.0 15.8 %collective-permute-start.17 = (bf16[64,1536]{1,0:T(8,128)(2,1)S(1)}, bf16[64,1536]{1,0:T(8,128)(2,1)S(1)}, u32[]{:S(2)}, u32[]{:S(2)}) collective-permute-start(bf16[64,1536]{1,0:T(8,128)(2,1)S(1)} %get-tuple-element.60.grad_values.refs_6_), channel_id=1, source_target_pairs={{0,2},{1,3},{2,0},{3,1},{4,6},{5,7},{6,4},{7,5},{8,10},{9,11},{10,... | collective-permute-start | bytes 589832 | tf_op jit(solution)/shard_map/ppermute | solution.py:354
  37.8 18.3 %collective-permute-start.19 = (bf16[64,1536]{1,0:T(8,128)(2,1)S(1)}, bf16[64,1536]{1,0:T(8,128)(2,1)S(1)}, u32[]{:S(2)}, u32[]{:S(2)}) collective-permute-start(bf16[64,1536]{1,0:T(8,128)(2,1)S(1)} %get-tuple-element.66.refs_1_), channel_id=1, source_target_pairs={{0,2},{1,3},{2,0},{3,1},{4,6},{5,7},{6,4},{7,5},{8,10},{9,11},{10,... | collective-permute-start | bytes 589832 | tf_op jit(solution)/shard_map/ppermute | solution.py:354
  40.0 26.5 %collective-permute-start.18 = (bf16[64,3072]{1,0:T(8,128)(2,1)S(1)}, bf16[64,3072]{1,0:T(8,128)(2,1)S(1)}, u32[]{:S(2)}, u32[]{:S(2)}) collective-permute-start(bf16[64,3072]{1,0:T(8,128)(2,1)S(1)} %get-tuple-element.69), channel_id=1, source_target_pairs={{0,1},{1,0},{2,3},{3,2},{4,5},{5,4},{6,7},{7,6},{8,9},{9,8},{10,11... | collective-permute-start | bytes 1179656 | tf_op jit(solution)/shard_map/ppermute | solution.py:388
  52.8 13.8 %collective-permute-start.20 = (bf16[64,3072]{1,0:T(8,128)(2,1)S(1)}, bf16[64,3072]{1,0:T(8,128)(2,1)S(1)}, u32[]{:S(2)}, u32[]{:S(2)}) collective-permute-start(bf16[64,3072]{1,0:T(8,128)(2,1)S(1)} %get-tuple-element.69), channel_id=1, source_target_pairs={{1,2},{2,1},{5,6},{6,5},{9,10},{10,9},{13,14},{14,13},{17,18},{18,... | collective-permute-start | bytes 1179656 | tf_op jit(solution)/shard_map/ppermute | solution.py:392
  56.1 8.3 %collective-permute-start.21 = (bf16[64,1536]{1,0:T(8,128)(2,1)S(1)}, bf16[64,1536]{1,0:T(8,128)(2,1)S(1)}, u32[]{:S(2)}, u32[]{:S(2)}) collective-permute-start(bf16[64,1536]{1,0:T(8,128)(2,1)S(1)} %collective-permute-done.19.refs_3_), channel_id=1, source_target_pairs={{1,0},{2,3},{5,4},{6,7},{9,8},{10,11},{13,12},{14,15},{17,16},{18,... | collective-permute-start | bytes 589832 | tf_op jit(solution)/shard_map/ppermute | solution.py:390
  57.4 9.1 %collective-permute-start.22 = (bf16[64,1536]{1,0:T(8,128)(2,1)S(1)}, bf16[64,1536]{1,0:T(8,128)(2,1)S(1)}, u32[]{:S(2)}, u32[]{:S(2)}) collective-permute-start(bf16[64,1536]{1,0:T(8,128)(2,1)S(1)} %collective-permute-done.17.refs_8_), channel_id=1, source_target_pairs={{1,0},{2,3},{5,4},{6,7},{9,8},{10,11},{13,12},{14,15},{17,16},{18,... | collective-permute-start | bytes 589832 | tf_op jit(solution)/shard_map/ppermute | solution.py:390

commit v6 on v5

--- a/solution.py
+++ b/solution.py
@@ -11,6 +11,8 @@
 HEAD = 128
 LMAX = 32
 SAMPLES = 2
+FIRST_HEADS = 12
+CLASSES = 4
 VMEM = 48 * 1024 * 1024
 
 F32 = jnp.float32
@@ -40,6 +42,14 @@
 
 def peer(index, k, paired):
     return index ^ k if paired else k
+
+
+def residue_of(member, k, classes, paired):
+    return (member ^ k) & (classes - 1) if paired else k
+
+
+def own_residue(member, classes, paired):
+    return member & (classes - 1) if paired else member
 
 
 def first_of_class(offset, residue, groups):
@@ -73,7 +83,8 @@
     column = lax.broadcasted_iota(jnp.int32, (depth, depth), 1)
     wanted = jnp.zeros((depth, depth), jnp.int32)
     for k in range(groups):
-        wanted = jnp.where(row // each == k, groups * (row - k * each) + peer(member, k, paired), wanted)
+        residue = residue_of(member, k, groups, paired)
+        wanted = jnp.where(row // each == k, groups * (row - k * each) + residue, wanted)
     order = (wanted == column).astype(BF16)
     cache_copy.wait()
     sorted_rows = jnp.dot(order, held_cache[...], preferred_element_type=F32).astype(BF16)
@@ -121,7 +132,7 @@
     for k in range(groups):
         for s in range(SAMPLES):
             caption = peer(member, k, paired) * SAMPLES + s
-            first = first_of_class(table[2, caption], member, groups)
+            first = first_of_class(table[2, caption], own_residue(member, groups, paired), groups)
             owner = table[1, caption]
             firsts.append(first)
             starts.append((owner ^ index if dp_paired else owner) * each + first)
@@ -167,7 +178,7 @@
     length = jnp.zeros(shape, jnp.int32)
     sample = jnp.zeros(shape, jnp.int32)
     for c in range(groups):
-        residue = peer(member, c, paired)
+        residue = residue_of(member, c, groups, paired)
         for s in range(SAMPLES):
             caption = member * SAMPLES + s
             run = (c * SAMPLES + s) * each
@@ -212,7 +223,7 @@
 
 
 def key_grad_kernel(groups, probs, queries, cotangent, grad_values, *refs):
-    values, (score_grads, grad_keys, grad_both, prob_grads) = refs[:groups], refs[groups:]
+    values, (score_grads, first_part, last_part, grad_both, prob_grads) = refs[:groups], refs[groups:]
     width = queries.shape[1]
     heads = width // HEAD
     scale = HEAD ** (-0.5)
@@ -226,10 +237,12 @@
         score_grads[h] = (prob * (prob_grad - centre)).astype(BF16)
     for h in range(heads):
         at = slice(h * HEAD, (h + 1) * HEAD)
-        grad_key = (jnp.dot(score_grads[h], queries[:, at], preferred_element_type=F32) * scale).astype(BF16)
-        grad_keys[:, at] = grad_key
-        grad_both[:, at] = grad_key
+        grad_key = jnp.dot(score_grads[h], queries[:, at], preferred_element_type=F32) * scale
+        grad_both[:, at] = grad_key.astype(BF16)
     grad_both[:, width:] = grad_values[...]
+    cut = first_part.shape[1]
+    first_part[...] = grad_both[:, :cut]
+    last_part[...] = grad_both[:, cut:]
 
 
 def key_grads(groups, probs, queries, grad_out, grad_values, values):
@@ -238,10 +251,11 @@
     return pl.pallas_call(
         functools.partial(key_grad_kernel, groups),
         in_specs=[VMEM_SPEC] * (4 + groups),
-        out_specs=[VMEM_SPEC] * 3,
+        out_specs=[VMEM_SPEC] * 4,
         out_shape=[
             jax.ShapeDtypeStruct((heads, slots, tokens), BF16),
-            jax.ShapeDtypeStruct((slots, width), BF16),
+            jax.ShapeDtypeStruct((slots, FIRST_HEADS * HEAD), BF16),
+            jax.ShapeDtypeStruct((slots, 2 * width - FIRST_HEADS * HEAD), BF16),
             jax.ShapeDtypeStruct((slots, 2 * width), BF16),
         ],
         scratch_shapes=[pltpu.VMEM((heads, slots, tokens), F32)],
@@ -250,7 +264,7 @@
     )(probs, queries, grad_out, grad_values, *values)
 
 
-def text_kernel(groups, each, depth, paired, dp_paired, table, text, score_grads, *refs):
+def text_kernel(members, groups, each, depth, paired, dp_paired, table, text, score_grads, *refs):
     keys, (out, grad_query) = refs[:groups], refs[groups:]
     for h in range(score_grads.shape[0]):
         at = slice(h * HEAD, (h + 1) * HEAD)
@@ -264,10 +278,10 @@
     target = jnp.zeros(shape, jnp.int32)
     limit = jnp.zeros(shape, jnp.int32)
     run = 0
-    for k in range(groups):
+    for k in range(members):
         device = peer(member, k, paired)
         for c in range(groups):
-            residue = peer(device, c, paired)
+            residue = residue_of(device, c, groups, paired)
             for s in range(SAMPLES):
                 caption = device * SAMPLES + s
                 offset = table[2, caption]
@@ -284,14 +298,14 @@
     out[...] = lax.dot_general(text[...], chosen, FIRST, preferred_element_type=F32).astype(BF16)
 
 
-def slot_texts(groups, each, depth, paired, dp_paired, table, text, score_grads, keys):
+def slot_texts(members, groups, each, depth, paired, dp_paired, table, text, score_grads, keys):
     features = text.shape[1]
     return pl.pallas_call(
-        functools.partial(text_kernel, groups, each, depth, paired, dp_paired),
+        functools.partial(text_kernel, members, groups, each, depth, paired, dp_paired),
         in_specs=[SMEM_SPEC] + [VMEM_SPEC] * (2 + groups),
         out_specs=[VMEM_SPEC] * 2,
         out_shape=[
-            jax.ShapeDtypeStruct((features, groups * groups * SAMPLES * each), BF16),
+            jax.ShapeDtypeStruct((features, members * groups * SAMPLES * each), BF16),
             jax.ShapeDtypeStruct((score_grads.shape[2], keys[0].shape[1]), BF16),
         ],
         compiler_params=kernel_params(),
@@ -299,55 +313,56 @@
     )(table, text, score_grads, *keys)
 
 
-def weight_kernel(line, blocks, *refs):
-    chosen_text, *grads = refs[:-4]
+def weight_kernel(line, start, blocks, *refs):
+    chosen_text, *grads = refs[:6] if line else refs[:2]
     out, every, built, sems = refs[-4:]
-    halves = [grads[: len(grads) // 2], grads[len(grads) // 2 :]]
-    width = every.shape[1] // 2
+    at = slice(start, start + every.shape[1])
     if line:
+        own, near, inner, second, outer = grads
         member = lax.axis_index("fsdp")
         is_inner = (member == 1) | (member == 2)
-        each = every.shape[0] // 4
-    for i, half in enumerate(halves):
-        at = slice(i * width, (i + 1) * width)
-        if line:
-            own, near, second, inner, outer = half
-            every[0:each, at] = own[...]
-            every[each : 2 * each, at] = near[:, at]
-            every[2 * each : 3 * each, at] = second[...]
-            every[3 * each :, at] = jnp.where(is_inner, inner[:, at], outer[...])
-        else:
-            every[:, at] = half[0][...]
+        each = own.shape[0]
+        every[0:each] = own[:, at]
+        every[each : 2 * each] = near[:, at]
+        every[2 * each : 3 * each] = second[...]
+        every[3 * each :] = jnp.where(is_inner, inner[:, at], outer[...])
+    else:
+        every[...] = grads[0][:, at]
     rows = built.shape[0] // blocks
     copies = []
     for i in range(blocks):
-        at = slice(i * rows, (i + 1) * rows)
-        built[at] = jnp.dot(chosen_text[at], every[...], preferred_element_type=F32).astype(BF16)
-        copy = pltpu.make_async_copy(built.at[pl.ds(i * rows, rows)], out.at[pl.ds(i * rows, rows)], sems.at[i])
+        block = slice(i * rows, (i + 1) * rows)
+        built[block] = jnp.dot(chosen_text[block], every[...], preferred_element_type=F32).astype(BF16)
+        copy = pltpu.make_async_copy(
+            built.at[pl.ds(i * rows, rows)],
+            out.at[pl.ds(i * rows, rows), pl.ds(start, every.shape[1])],
+            sems.at[i],
+        )
         copy.start()
         copies.append(copy)
     for copy in copies:
         copy.wait()
 
 
-def weight_grad(line, chosen_text, first_parts, second_parts):
+def weight_grad(line, chosen_text, grads, start, size, before=None):
     features, slots = chosen_text.shape
-    width = first_parts[0].shape[1] * 2
-    grads = [*first_parts, *second_parts]
+    width = grads[0].shape[1]
     blocks = 8
-    return pl.pallas_call(
-        functools.partial(weight_kernel, line, blocks),
-        in_specs=[VMEM_SPEC] * (1 + len(grads)),
+    earlier = [] if before is None else [before]
+    return pl.pallas_call(
+        functools.partial(weight_kernel, line, start, blocks),
+        in_specs=[VMEM_SPEC] * (1 + len(grads)) + [ANY_SPEC] * len(earlier),
         out_specs=ANY_SPEC,
         out_shape=jax.ShapeDtypeStruct((features, width), BF16),
         scratch_shapes=[
-            pltpu.VMEM((slots, width), BF16),
-            pltpu.VMEM((features, width), BF16),
+            pltpu.VMEM((slots, size), BF16),
+            pltpu.VMEM((features, size), BF16),
             pltpu.SemaphoreType.DMA((blocks,)),
         ],
+        input_output_aliases={1 + len(grads): 0} if earlier else {},
         compiler_params=kernel_params(),
         name="weight_gradient",
-    )(chosen_text, *grads)
+    )(chosen_text, *grads, *earlier)
 
 
 def swap(x, axis, k):
@@ -371,34 +386,38 @@
     return lax.all_gather(x, "dp", axis=0, tiled=True, axis_index_groups=cores)
 
 
+def reduce_line(pieces, members, paired):
+    if paired:
+        return [pieces[0]] + [swap(pieces[k % len(pieces)], "fsdp", k) for k in range(1, members)]
+    return exchange(pieces, paired)
+
+
 def exchange(pieces, paired):
     if paired:
-        far_first = {k: swap(pieces[k], "fsdp", k) for k in (*range(2, len(pieces)), 1)}
-        return [pieces[0]] + [far_first[k] for k in range(1, len(pieces))]
+        return [pieces[0]] + [swap(pieces[k], "fsdp", k) for k in range(1, len(pieces))]
     came = lax.all_to_all(jnp.stack(pieces), "fsdp", 0, 0, tiled=True)
     return [came[k] for k in range(len(pieces))]
 
 
-def gather_line(first_half, second_half, both, beside):
+def gather_line(parts, both, beside):
     near_pairs = [(0, 1), (1, 0), (2, 3), (3, 2)]
     middle_pairs = [(1, 2), (2, 1)]
     outward = [(1, 0), (2, 3)]
-    halves = [first_half, second_half]
-    second = [swap(half, "fsdp", 2) for half in halves]
+    second = [swap(part, "fsdp", 2) for part in parts]
     near = lax.ppermute(both, "fsdp", near_pairs)
-    second[0], beside = lax.optimization_barrier((second[0], beside))
+    second[1], beside = lax.optimization_barrier((second[1], beside))
     outer = [lax.ppermute(piece, "fsdp", outward) for piece in second]
-    late, _ = lax.optimization_barrier((both, second[0]))
+    late, _ = lax.optimization_barrier((both, second[1]))
     inner = lax.ppermute(late, "fsdp", middle_pairs)
-    parts = [[halves[i], near, second[i], inner, outer[i]] for i in range(2)]
-    return parts[0], parts[1], beside
+    return near, inner, second, outer, beside
 
 
 def shards(
     queries, grad_out, text_cache, w_kv, image_counts, caption_lens, caption_owner, caption_offset
 ):
-    groups = lax.axis_size("fsdp")
-    line = groups == 4
+    members = lax.axis_size("fsdp")
+    line = members == 4
+    groups = CLASSES if line else members
     paired = line
     dp_paired = power_of_two(lax.axis_size("dp")) and lax.axis_size("dp") <= 8
     depth = text_cache.shape[0]
@@ -408,7 +427,7 @@
     partials = project(groups, paired, text_cache, w_kv)
     partials, late_cache = lax.optimization_barrier((partials, text_cache))
     texts = [late_cache, swap(late_cache, "dp", 1)] if dp_paired else [late_cache]
-    came = exchange(partials, paired)
+    came = reduce_line(partials, members, paired)
     table = scalar_table(image_counts, caption_lens, caption_owner, caption_offset)
     rows = sum(piece.astype(F32) for piece in came).astype(BF16)
     class_rows = gather_dp(rows, dp_paired)
@@ -417,22 +436,21 @@
     values = exchange(outgoing[groups:], paired)
     probs, grad_values = value_grads(groups, each, paired, table, queries, grad_out, keys)
     grad_values, probs = lax.optimization_barrier((grad_values, probs))
-    score_grads, grad_keys, grad_both = key_grads(groups, probs, queries, grad_out, grad_values, values)
-    grad_values, grad_keys, grad_both, chip_text = lax.optimization_barrier(
-        (grad_values, grad_keys, grad_both, chip_text)
-    )
+    score_grads, *parts, grad_both = key_grads(groups, probs, queries, grad_out, grad_values, values)
+    parts, grad_both, chip_text = lax.optimization_barrier((parts, grad_both, chip_text))
     if dp_paired:
         text = gather_chips(chip_text)
     else:
         text = lax.all_gather(chip_text, "dp", axis=0, tiled=True)
     if line:
-        value_parts, key_parts, text = gather_line(grad_values, grad_keys, grad_both, text)
+        near, inner, second, outer, text = gather_line(parts, grad_both, text)
+        operands = [[grad_both, near, inner, second[i], outer[i]] for i in range(2)]
     else:
-        value_parts, key_parts = [
-            [lax.all_gather(half, "fsdp", axis=0, tiled=True)] for half in (grad_values, grad_keys)
-        ]
-    chosen_text, grad_query = slot_texts(groups, each, depth, paired, dp_paired, table, text, score_grads, keys)
-    grad_weight = weight_grad(line, chosen_text, key_parts, value_parts)
+        operands = [[lax.all_gather(grad_both, "fsdp", axis=0, tiled=True)]] * 2
+    chosen_text, grad_query = slot_texts(members, groups, each, depth, paired, dp_paired, table, text, score_grads, keys)
+    cut = parts[0].shape[1]
+    grad_weight = weight_grad(line, chosen_text, operands[0], 0, cut)
+    grad_weight = weight_grad(line, chosen_text, operands[1], cut, 2 * width - cut, grad_weight)
     return grad_query, grad_weight[None]
 
 

time: 69.9 us -> 68.7 us (0.983)
  waiting for transfers between devices: 22 us -> 20 us
  Pallas kernels: 10.6 us -> 11.5 us
    ppermute x2, waiting for transfers between devices: 6.16 us -> 4.14 us  [gather_line(): outer = [lax.ppermute(piece, 'fsdp', outward) for piece in second]]
    pallas_call x2 -> x3, Pallas kernels: 4.78 us -> 5.69 us  [the longest x2 4.05 us: weight_grad(): pl.pallas_call(functools.partial(weight_kernel, line, start, blocks), in_...]
  transfers between devices with their start and end apart: 23 -> 23, of which waited for: 12 -> 12; matrix products, arithmetic and copies ran while one was open for 0% -> 0% of each run, Pallas kernels for 4% -> 7%
where the time goes in v6:
time: 68.7 us; the launch traced here: 68.5 us
  starting transfers between devices  25.4 us (37%)
  waiting for transfers between devices  20 us (29%)
  Pallas kernels  11.5 us (17%)
  blocking collectives  10.6 us (15%)
  between operations  0.85 us (1%)
    ppermute x19, starting transfers between devices, swap(): lax.ppermute(x, axis, [(i, i ^ k) for i in range(lax.axis_size(axis))])  21.1 us
    ppermute x19, waiting for transfers between devices, swap(): lax.ppermute(x, axis, [(i, i ^ k) for i in range(lax.axis_size(axis))])  15.8 us
    all_gather x1, blocking collectives, gather_chips(): return lax.all_gather(x, 'dp', axis=0, tiled=True, axis_index_groups=cores)  10.6 us
    ppermute x2, waiting for transfers between devices, gather_line(): outer = [lax.ppermute(piece, 'fsdp', outward) for piece in second]  4.14 us
    pallas_call x2, Pallas kernels, weight_grad(): pl.pallas_call(functools.partial(weight_kernel, line, start, blocks), in_...  4.05 us
    pallas_call x1, Pallas kernels, project(): pl.pallas_call(functools.partial(project_kernel, groups, paired, chunks),...  3.21 us
    ppermute x2, starting transfers between devices, gather_line(): outer = [lax.ppermute(piece, 'fsdp', outward) for piece in second]  2.57 us
    pallas_call x1, Pallas kernels, slot_texts(): pl.pallas_call(functools.partial(text_kernel, members, groups, each, dept...  1.64 us
  transfers between devices with their start and end apart: 23, of which 12 were waited for; matrix products, arithmetic and copies ran while one was open for 0% of the time, Pallas kernels for 7%

profile of v6, /device:TPU:0, one launch (start us, length us, event | category | flops | bytes accessed | tf_op | source)
XLA Modules:
  0.0 68.5 jit_solution(9051440129336792024)
XLA Ops:
  0.6 0.0 copy-start.2
  0.6 0.0 copy-start.3
  0.7 0.0 copy-start.4
  0.7 0.0 copy-start.5
  0.7 0.0 copy-start.6
  0.7 0.0 copy-start.1
  0.7 0.0 copy-start
  0.7 3.2 %project.1 = (bf16[8,3072]{1,0:T(8,128)(2,1)S(1)}, bf16[8,3072]{1,0:T(8,128)(2,1)S(1)}, bf16[8,3072]{1,0:T(8,128)(2,1)S(1)}, bf16[8,3072]{1,0:T(8,128)(2,1)S(1)}) custom-call(bf16[32,1024]{1,0:T(8,128)(2,1)} %refs_0_, bf16[1024,3072]{1,0:T(8,128)(2,1)} %weight.1), custom_call_target="tpu_custom_call" | custom-call | tf_op jit(solution)/shard_map/project/pallas_call | solution.py:106
  3.9 3.1 %collective-permute-start.1 = (bf16[8,3072]{1,0:T(8,128)(2,1)S(1)}, bf16[8,3072]{1,0:T(8,128)(2,1)S(1)}, u32[]{:S(2)}, u32[]{:S(2)}) collective-permute-start(bf16[8,3072]{1,0:T(8,128)(2,1)S(1)} %get-tuple-element.43), channel_id=1, source_target_pairs={{0,1},{1,0},{2,3},{3,2},{4,5},{5,4},{6,7},{7,6},{8,9},{9,8},{10,11... | collective-permute-start | bytes 147464 | tf_op jit(solution)/shard_map/ppermute | solution.py:369
  7.0 2.6 %collective-permute-start.2 = (bf16[8,3072]{1,0:T(8,128)(2,1)S(1)}, bf16[8,3072]{1,0:T(8,128)(2,1)S(1)}, u32[]{:S(2)}, u32[]{:S(2)}) collective-permute-start(bf16[8,3072]{1,0:T(8,128)(2,1)S(1)} %get-tuple-element.44), channel_id=1, source_target_pairs={{0,2},{1,3},{2,0},{3,1},{4,6},{5,7},{6,4},{7,5},{8,10},{9,11},{10,... | collective-permute-start | bytes 147464 | tf_op jit(solution)/shard_map/ppermute | solution.py:369
  9.6 0.0 collective-permute-start.3
  9.6 0.0 copy-done.2
  9.6 0.0 collective-permute-start
  9.6 0.1 pad_add_fusion.1
  9.7 0.0 collective-permute-done.1
  9.7 3.2 %collective-permute-done.2 = bf16[8,3072]{1,0:T(8,128)(2,1)S(1)} collective-permute-done((bf16[8,3072]{1,0:T(8,128)(2,1)S(1)}, bf16[8,3072]{1,0:T(8,128)(2,1)S(1)}, u32[]{:S(2)}, u32[]{:S(2)}) %collective-permute-start.2) | collective-permute-done | bytes 49184 | tf_op jit(solution)/shard_map/ppermute | solution.py:369
  12.9 2.6 %collective-permute-done.3 = bf16[8,3072]{1,0:T(8,128)(2,1)S(1)} collective-permute-done((bf16[8,3072]{1,0:T(8,128)(2,1)S(1)}, bf16[8,3072]{1,0:T(8,128)(2,1)S(1)}, u32[]{:S(2)}, u32[]{:S(2)}) %collective-permute-start.3) | collective-permute-done | bytes 49184 | tf_op jit(solution)/shard_map/ppermute | solution.py:369
  15.5 2.5 %collective-permute-start.9 = (bf16[8,3072]{1,0:T(8,128)(2,1)S(1)}, bf16[8,3072]{1,0:T(8,128)(2,1)S(1)}, u32[]{:S(2)}, u32[]{:S(2)}) collective-permute-start(bf16[8,3072]{1,0:T(8,128)(2,1)S(1)} %add_convert_fusion.refs_2_), channel_id=1, source_target_pairs={{0,24},{4,28},{8,16},{12,20},{16,8},{20,12},{24,0},{28,4},{1,25},{... | collective-permute-start | bytes 147464 | tf_op jit(solution)/shard_map/ppermute | solution.py:369
  18.0 0.5 collective-permute-start.7
  18.5 0.5 collective-permute-start.5
  19.1 0.0 collective-permute-start.4
  19.1 1.7 %collective-permute-done.9.refs_8_ = bf16[8,3072]{1,0:T(8,128)(2,1)S(1)} collective-permute-done((bf16[8,3072]{1,0:T(8,128)(2,1)S(1)}, bf16[8,3072]{1,0:T(8,128)(2,1)S(1)}, u32[]{:S(2)}, u32[]{:S(2)}) %collective-permute-start.9) | collective-permute-done | bytes 49184 | tf_op jit(solution)/shard_map/ppermute | solution.py:369
  20.8 0.0 collective-permute-start.10
  20.8 1.3 %collective-permute-done.7.refs_6_ = bf16[8,3072]{1,0:T(8,128)(2,1)S(1)} collective-permute-done((bf16[8,3072]{1,0:T(8,128)(2,1)S(1)}, bf16[8,3072]{1,0:T(8,128)(2,1)S(1)}, u32[]{:S(2)}, u32[]{:S(2)}) %collective-permute-start.7) | collective-permute-done | bytes 49184 | tf_op jit(solution)/shard_map/ppermute | solution.py:369
  22.1 0.0 collective-permute-start.8
  22.1 0.5 collective-permute-done.5.refs_4_
  22.6 0.0 collective-permute-start.6
  22.6 0.0 copy-done.6
  22.7 0.0 collective-permute-done.refs_1_
  22.7 0.0 collective-permute-done.4.refs_3_
  22.7 0.0 collective-permute-done.10.refs_9_
  22.7 0.7 collective-permute-done.8.refs_7_
  23.4 0.5 collective-permute-done.6.refs_5_
  23.9 0.8 %select_rows.1 = (bf16[16,1536]{1,0:T(8,128)(2,1)S(1)}, bf16[16,1536]{1,0:T(8,128)(2,1)S(1)}, bf16[16,1536]{1,0:T(8,128)(2,1)S(1)}, bf16[16,1536]{1,0:T(8,128)(2...) custom-call(s32[4,8]{1,0:T(4,128)S(1)} %pad_add_fusion.table, ...), custom_call_target="tpu_custom_call" | custom-call | tf_op jit(solution)/shard_map/select_rows/pallas_call | solution.py:153
  24.7 0.1 collective-permute-start.11
  24.8 1.3 %collective-permute-start.12 = (bf16[16,1536]{1,0:T(8,128)(2,1)S(1)}, bf16[16,1536]{1,0:T(8,128)(2,1)S(1)}, u32[]{:S(2)}, u32[]{:S(2)}) collective-permute-start(bf16[16,1536]{1,0:T(8,128)(2,1)S(1)} %get-tuple-element.48), channel_id=1, source_target_pairs={{0,2},{1,3},{2,0},{3,1},{4,6},{5,7},{6,4},{7,5},{8,10},{9,11},{10,... | collective-permute-start | bytes 147464 | tf_op jit(solution)/shard_map/ppermute | solution.py:369
  26.1 3.1 %collective-permute-start.13 = (bf16[16,1536]{1,0:T(8,128)(2,1)S(1)}, bf16[16,1536]{1,0:T(8,128)(2,1)S(1)}, u32[]{:S(2)}, u32[]{:S(2)}) collective-permute-start(bf16[16,1536]{1,0:T(8,128)(2,1)S(1)} %get-tuple-element.49), channel_id=1, source_target_pairs={{0,3},{1,2},{2,1},{3,0},{4,7},{5,6},{6,5},{7,4},{8,11},{9,10},{10,... | collective-permute-start | bytes 147464 | tf_op jit(solution)/shard_map/ppermute | solution.py:369
  29.2 0.0 collective-permute-start.14
  29.2 1.3 %collective-permute-start.15 = (bf16[16,1536]{1,0:T(8,128)(2,1)S(1)}, bf16[16,1536]{1,0:T(8,128)(2,1)S(1)}, u32[]{:S(2)}, u32[]{:S(2)}) collective-permute-start(bf16[16,1536]{1,0:T(8,128)(2,1)S(1)} %get-tuple-element.56), channel_id=1, source_target_pairs={{0,2},{1,3},{2,0},{3,1},{4,6},{5,7},{6,4},{7,5},{8,10},{9,11},{10,... | collective-permute-start | bytes 147464 | tf_op jit(solution)/shard_map/ppermute | solution.py:369
  30.5 0.0 collective-permute-done.11.refs_1_
  30.5 3.1 %collective-permute-start.16 = (bf16[16,1536]{1,0:T(8,128)(2,1)S(1)}, bf16[16,1536]{1,0:T(8,128)(2,1)S(1)}, u32[]{:S(2)}, u32[]{:S(2)}) collective-permute-start(bf16[16,1536]{1,0:T(8,128)(2,1)S(1)} %get-tuple-element.57), channel_id=1, source_target_pairs={{0,3},{1,2},{2,1},{3,0},{4,7},{5,6},{6,5},{7,4},{8,11},{9,10},{10,... | collective-permute-start | bytes 147464 | tf_op jit(solution)/shard_map/ppermute | solution.py:369
  33.6 0.0 collective-permute-done.12.refs_2_
  33.6 0.0 collective-permute-done.13.refs_3_
  33.6 1.2 %value_gradients.1 = (f32[12,64,128]{2,1,0:T(8,128)S(1)}, bf16[64,1536]{1,0:T(8,128)(2,1)S(1)}) custom-call(s32[4,8]{1,0:T(4,128)S(1)} %pad_add_fusion.table, bf16[128,1536]{1,0:T(8,128)(2,1)S(1)} %copy-done, bf16[128,1536]{1,0:T(8,128)(2,1)S(1)} %copy-done.1, bf16[16,1536]{1,0:T(8,128)(2,1)S(1)} %get-tuple-element.46.refs_0_, ...), custom_call_target="tpu_custom_call" | custom-call | tf_op jit(solution)/shard_map/value_gradients/pallas_call | solution.py:211
  34.7 0.0 collective-permute-done.14.refs_1_
  34.7 1.7 %collective-permute-done.15.refs_2_ = bf16[16,1536]{1,0:T(8,128)(2,1)S(1)} collective-permute-done((bf16[16,1536]{1,0:T(8,128)(2,1)S(1)}, bf16[16,1536]{1,0:T(8,128)(2,1)S(1)}, u32[]{:S(2)}, u32[]{:S(2)}) %collective-permute-start.15) | collective-permute-done | bytes 49184 | tf_op jit(solution)/shard_map/ppermute | solution.py:369
  36.4 0.0 collective-permute-done.16.refs_3_
  36.4 0.6 key_gradients.1
  37.0 0.8 %collective-permute-start.17 = (bf16[64,1536]{1,0:T(8,128)(2,1)S(1)}, bf16[64,1536]{1,0:T(8,128)(2,1)S(1)}, u32[]{:S(2)}, u32[]{:S(2)}) collective-permute-start(bf16[64,1536]{1,0:T(8,128)(2,1)S(1)} %get-tuple-element.62), channel_id=1, source_target_pairs={{0,2},{1,3},{2,0},{3,1},{4,6},{5,7},{6,4},{7,5},{8,10},{9,11},{10,... | collective-permute-start | bytes 589832 | tf_op jit(solution)/shard_map/ppermute | solution.py:369
  37.8 2.2 %collective-permute-start.21 = (bf16[64,1536]{1,0:T(8,128)(2,1)S(1)}, bf16[64,1536]{1,0:T(8,128)(2,1)S(1)}, u32[]{:S(2)}, u32[]{:S(2)}) collective-permute-start(bf16[64,1536]{1,0:T(8,128)(2,1)S(1)} %get-tuple-element.71), channel_id=1, source_target_pairs={{0,2},{1,3},{2,0},{3,1},{4,6},{5,7},{6,4},{7,5},{8,10},{9,11},{10,... | collective-permute-start | bytes 589832 | tf_op jit(solution)/shard_map/ppermute | solution.py:369
  40.0 1.1 %collective-permute-start.18 = (bf16[64,3072]{1,0:T(8,128)(2,1)S(1)}, bf16[64,3072]{1,0:T(8,128)(2,1)S(1)}, u32[]{:S(2)}, u32[]{:S(2)}) collective-permute-start(bf16[64,3072]{1,0:T(8,128)(2,1)S(1)} %get-tuple-element.70.refs_1_), channel_id=1, source_target_pairs={{0,1},{1,0},{2,3},{3,2},{4,5},{5,4},{6,7},{7,6},{8,9},{9,8},{10,11... | collective-permute-start | bytes 1179656 | tf_op jit(solution)/shard_map/ppermute | solution.py:407
  41.1 10.6 %all_gather.3.text = bf16[256,1024]{1,0:T(8,128)(2,1)S(1)} all-gather(bf16[64,1024]{1,0:T(8,128)(2,1)S(1)} %get-tuple-element.63), channel_id=1, replica_groups={{0,8,16,24},{4,12,20,28},{1,9,17,25},{5,13,21,29},{2,10,18,26},{6,14,22..., dimensions={0}, use_global_device_ids=true | all-gather | bytes 655360 | tf_op jit(solution)/shard_map/all_gather | solution.py:386
  51.7 1.1 %collective-permute-done.17.refs_4_ = bf16[64,1536]{1,0:T(8,128)(2,1)S(1)} collective-permute-done((bf16[64,1536]{1,0:T(8,128)(2,1)S(1)}, bf16[64,1536]{1,0:T(8,128)(2,1)S(1)}, u32[]{:S(2)}, u32[]{:S(2)}) %collective-permute-start.17) | collective-permute-done | bytes 196640 | tf_op jit(solution)/shard_map/ppermute | solution.py:369
  52.8 0.7 collective-permute-start.19
  53.4 2.6 %collective-permute-done.21.refs_4_ = bf16[64,1536]{1,0:T(8,128)(2,1)S(1)} collective-permute-done((bf16[64,1536]{1,0:T(8,128)(2,1)S(1)}, bf16[64,1536]{1,0:T(8,128)(2,1)S(1)}, u32[]{:S(2)}, u32[]{:S(2)}) %collective-permute-start.21) | collective-permute-done | bytes 196640 | tf_op jit(solution)/shard_map/ppermute | solution.py:369
  56.1 1.3 %collective-permute-start.22 = (bf16[64,1536]{1,0:T(8,128)(2,1)S(1)}, bf16[64,1536]{1,0:T(8,128)(2,1)S(1)}, u32[]{:S(2)}, u32[]{:S(2)}) collective-permute-start(bf16[64,1536]{1,0:T(8,128)(2,1)S(1)} %collective-permute-done.21.refs_4_), channel_id=1, source_target_pairs={{1,0},{2,3},{5,4},{6,7},{9,8},{10,11},{13,12},{14,15},{17,16},{18,... | collective-permute-start | bytes 589832 | tf_op jit(solution)/shard_map/ppermute | solution.py:409
  57.4 1.3 %collective-permute-start.20 = (bf16[64,1536]{1,0:T(8,128)(2,1)S(1)}, bf16[64,1536]{1,0:T(8,128)(2,1)S(1)}, u32[]{:S(2)}, u32[]{:S(2)}) collective-permute-start(bf16[64,1536]{1,0:T(8,128)(2,1)S(1)} %collective-permute-done.17.refs_4_), channel_id=1, source_target_pairs={{1,0},{2,3},{5,4},{6,7},{9,8},{10,11},{13,12},{14,15},{17,16},{18,... | collective-permute-start | bytes 589832 | tf_op jit(solution)/shard_map/ppermute | solution.py:409
  58.7 1.6 %slot_texts.1 = (bf16[1024,256]{1,0:T(8,128)(2,1)S(1)}, bf16[128,1536]{1,0:T(8,128)(2,1)}) custom-call(s32[4,8]{1,0:T(4,128)S(1)} %pad_add_fusion.table, bf16[256,1024]{1,0:T(8,128)(2,1)S(1)} %all_gather.3.text, bf16[12,64,128]{2,1,0:T(8,128)(2,1)S(1)} %get-tuple-element.65.score_grads, bf16[16,1536]{1,0:T(8,128)(2,1)S(1)} %get-tuple-element.46.refs_0_, ...), custom_call_target="tpu_custom_call" | custom-call | tf_op jit(solution)/shard_map/slot_texts/pallas_call | solution.py:303
  60.3 4.1 %collective-permute-done.22.refs_5_ = bf16[64,1536]{1,0:T(8,128)(2,1)S(1)} collective-permute-done((bf16[64,1536]{1,0:T(8,128)(2,1)S(1)}, bf16[64,1536]{1,0:T(8,128)(2,1)S(1)}, u32[]{:S(2)}, u32[]{:S(2)}) %collective-permute-start.22) | collective-permute-done | bytes 196640 | tf_op jit(solution)/shard_map/ppermute | solution.py:409
  64.4 0.0 collective-permute-done.18.refs_2_
  64.4 0.0 collective-permute-done.19.refs_3_
  64.4 2.0 %weight_gradient.2.refs_6_ = bf16[1024,3072]{1,0:T(8,128)(2,1)} custom-call(bf16[1024,256]{1,0:T(8,128)(2,1)S(1)} %get-tuple-element.67.refs_0_, bf16[64,3072]{1,0:T(8,128)(2,1)S(1)} %get-tuple-element.70.refs_1_, bf16[64,3072]{1,0:T(8,128)(2,1)S(1)} %collective-permute-done.18.refs_2_, bf16[64,3072]{1,0:T(8,128)(2,1)S(1)} %collective-permute-done.19.refs_3_, ...), custom_call_target="tpu_custom_call" | custom-call | tf_op jit(solution)/shard_map/weight_gradient/pallas_call | solution.py:352
  66.4 0.1 collective-permute-done.20.refs_5_
  66.5 2.0 %weight_gradient.3 = bf16[1024,3072]{1,0:T(8,128)(2,1)} custom-call(bf16[1024,256]{1,0:T(8,128)(2,1)S(1)} %get-tuple-element.67.refs_0_, bf16[64,3072]{1,0:T(8,128)(2,1)S(1)} %get-tuple-element.70.refs_1_, bf16[64,3072]{1,0:T(8,128)(2,1)S(1)} %collective-permute-done.18.refs_2_, ...), custom_call_target="tpu_custom_call", output_to_operand_aliasing={{}: (6, {})} | custom-call | tf_op jit(solution)/shard_map/weight_gradient/pallas_call | solution.py:352
  (8 shorter events, 0.1 us)
Async XLA Ops:
  0.6 9.0 %copy-start.2 = (bf16[32,1024]{1,0:T(8,128)(2,1)S(1)}, bf16[32,1024]{1,0:T(8,128)(2,1)}, u32[]{:S(2)}) copy-start(bf16[32,1024]{1,0:T(8,128)(2,1)} %refs_0_) | copy-start | bytes 196612
  0.6 9.0 %copy-start.3 = (s32[1,2]{1,0:T(1,128)S(1)}, s32[1,2]{1,0:T(1,128)}, u32[]{:S(2)}) copy-start(s32[1,2]{1,0:T(1,128)} %param.12) | copy-start | bytes 28
  0.7 22.0 %copy-start.4 = (s32[1,8]{1,0:T(1,128)S(1)}, s32[1,8]{1,0:T(1,128)}, u32[]{:S(2)}) copy-start(s32[1,8]{1,0:T(1,128)} %param.15) | copy-start | bytes 100
  0.7 22.0 %copy-start.5 = (s32[1,8]{1,0:T(1,128)S(1)}, s32[1,8]{1,0:T(1,128)}, u32[]{:S(2)}) copy-start(s32[1,8]{1,0:T(1,128)} %param.14) | copy-start | bytes 100
  0.7 22.0 %copy-start.6 = (s32[1,8]{1,0:T(1,128)S(1)}, s32[1,8]{1,0:T(1,128)}, u32[]{:S(2)}) copy-start(s32[1,8]{1,0:T(1,128)} %param.13) | copy-start | bytes 100
  0.7 32.9 %copy-start.1 = (bf16[128,1536]{1,0:T(8,128)(2,1)S(1)}, bf16[128,1536]{1,0:T(8,128)(2,1)}, u32[]{:S(2)}) copy-start(bf16[128,1536]{1,0:T(8,128)(2,1)} %cotangent.3) | copy-start | bytes 1179652
  0.7 32.9 %copy-start = (bf16[128,1536]{1,0:T(8,128)(2,1)S(1)}, bf16[128,1536]{1,0:T(8,128)(2,1)}, u32[]{:S(2)}) copy-start(bf16[128,1536]{1,0:T(8,128)(2,1)} %queries.3) | copy-start | bytes 1179652
  3.9 5.8 %collective-permute-start.1 = (bf16[8,3072]{1,0:T(8,128)(2,1)S(1)}, bf16[8,3072]{1,0:T(8,128)(2,1)S(1)}, u32[]{:S(2)}, u32[]{:S(2)}) collective-permute-start(bf16[8,3072]{1,0:T(8,128)(2,1)S(1)} %get-tuple-element.43), channel_id=1, source_target_pairs={{0,1},{1,0},{2,3},{3,2},{4,5},{5,4},{6,7},{7,6},{8,9},{9,8},{10,11... | collective-permute-start | bytes 147464 | tf_op jit(solution)/shard_map/ppermute | solution.py:369
  7.0 5.9 %collective-permute-start.2 = (bf16[8,3072]{1,0:T(8,128)(2,1)S(1)}, bf16[8,3072]{1,0:T(8,128)(2,1)S(1)}, u32[]{:S(2)}, u32[]{:S(2)}) collective-permute-start(bf16[8,3072]{1,0:T(8,128)(2,1)S(1)} %get-tuple-element.44), channel_id=1, source_target_pairs={{0,2},{1,3},{2,0},{3,1},{4,6},{5,7},{6,4},{7,5},{8,10},{9,11},{10,... | collective-permute-start | bytes 147464 | tf_op jit(solution)/shard_map/ppermute | solution.py:369
  9.6 5.9 %collective-permute-start.3 = (bf16[8,3072]{1,0:T(8,128)(2,1)S(1)}, bf16[8,3072]{1,0:T(8,128)(2,1)S(1)}, u32[]{:S(2)}, u32[]{:S(2)}) collective-permute-start(bf16[8,3072]{1,0:T(8,128)(2,1)S(1)} %get-tuple-element.45), channel_id=1, source_target_pairs={{0,3},{1,2},{2,1},{3,0},{4,7},{5,6},{6,5},{7,4},{8,11},{9,10},{10,... | collective-permute-start | bytes 147464 | tf_op jit(solution)/shard_map/ppermute | solution.py:369
  9.6 13.1 %collective-permute-start = (bf16[32,1024]{1,0:T(8,128)(2,1)S(1)}, bf16[32,1024]{1,0:T(8,128)(2,1)S(1)}, u32[]{:S(2)}, u32[]{:S(2)}) collective-permute-start(bf16[32,1024]{1,0:T(8,128)(2,1)S(1)} %copy-done.2), channel_id=1, source_target_pairs={{0,4},{4,0},{8,12},{12,8},{16,20},{20,16},{24,28},{28,24},{1,5},{5... | collective-permute-start | bytes 196616 | tf_op jit(solution)/shard_map/ppermute | solution.py:369
  15.5 5.3 %collective-permute-start.9 = (bf16[8,3072]{1,0:T(8,128)(2,1)S(1)}, bf16[8,3072]{1,0:T(8,128)(2,1)S(1)}, u32[]{:S(2)}, u32[]{:S(2)}) collective-permute-start(bf16[8,3072]{1,0:T(8,128)(2,1)S(1)} %add_convert_fusion.refs_2_), channel_id=1, source_target_pairs={{0,24},{4,28},{8,16},{12,20},{16,8},{20,12},{24,0},{28,4},{1,25},{... | collective-permute-start | bytes 147464 | tf_op jit(solution)/shard_map/ppermute | solution.py:369
  18.0 4.1 %collective-permute-start.7 = (bf16[8,3072]{1,0:T(8,128)(2,1)S(1)}, bf16[8,3072]{1,0:T(8,128)(2,1)S(1)}, u32[]{:S(2)}, u32[]{:S(2)}) collective-permute-start(bf16[8,3072]{1,0:T(8,128)(2,1)S(1)} %add_convert_fusion.refs_2_), channel_id=1, source_target_pairs={{0,16},{4,20},{8,24},{12,28},{16,0},{20,4},{24,8},{28,12},{1,17},{... | collective-permute-start | bytes 147464 | tf_op jit(solution)/shard_map/ppermute | solution.py:369
  18.5 4.1 %collective-permute-start.5 = (bf16[8,3072]{1,0:T(8,128)(2,1)S(1)}, bf16[8,3072]{1,0:T(8,128)(2,1)S(1)}, u32[]{:S(2)}, u32[]{:S(2)}) collective-permute-start(bf16[8,3072]{1,0:T(8,128)(2,1)S(1)} %add_convert_fusion.refs_2_), channel_id=1, source_target_pairs={{0,8},{4,12},{8,0},{12,4},{16,24},{20,28},{24,16},{28,20},{1,9},{5... | collective-permute-start | bytes 147464 | tf_op jit(solution)/shard_map/ppermute | solution.py:369
  19.1 3.6 %collective-permute-start.4 = (bf16[8,3072]{1,0:T(8,128)(2,1)S(1)}, bf16[8,3072]{1,0:T(8,128)(2,1)S(1)}, u32[]{:S(2)}, u32[]{:S(2)}) collective-permute-start(bf16[8,3072]{1,0:T(8,128)(2,1)S(1)} %add_convert_fusion.refs_2_), channel_id=1, source_target_pairs={{0,4},{4,0},{8,12},{12,8},{16,20},{20,16},{24,28},{28,24},{1,5},{5... | collective-permute-start | bytes 147464 | tf_op jit(solution)/shard_map/ppermute | solution.py:369
  20.8 1.9 %collective-permute-start.10 = (bf16[8,3072]{1,0:T(8,128)(2,1)S(1)}, bf16[8,3072]{1,0:T(8,128)(2,1)S(1)}, u32[]{:S(2)}, u32[]{:S(2)}) collective-permute-start(bf16[8,3072]{1,0:T(8,128)(2,1)S(1)} %collective-permute-done.9.refs_8_), channel_id=1, source_target_pairs={{0,4},{4,0},{8,12},{12,8},{16,20},{20,16},{24,28},{28,24},{1,5},{5... | collective-permute-start | bytes 147464 | tf_op jit(solution)/shard_map/ppermute | solution.py:369
  22.1 1.2 %collective-permute-start.8 = (bf16[8,3072]{1,0:T(8,128)(2,1)S(1)}, bf16[8,3072]{1,0:T(8,128)(2,1)S(1)}, u32[]{:S(2)}, u32[]{:S(2)}) collective-permute-start(bf16[8,3072]{1,0:T(8,128)(2,1)S(1)} %collective-permute-done.7.refs_6_), channel_id=1, source_target_pairs={{0,4},{4,0},{8,12},{12,8},{16,20},{20,16},{24,28},{28,24},{1,5},{5... | collective-permute-start | bytes 147464 | tf_op jit(solution)/shard_map/ppermute | solution.py:369
  22.6 1.2 %collective-permute-start.6 = (bf16[8,3072]{1,0:T(8,128)(2,1)S(1)}, bf16[8,3072]{1,0:T(8,128)(2,1)S(1)}, u32[]{:S(2)}, u32[]{:S(2)}) collective-permute-start(bf16[8,3072]{1,0:T(8,128)(2,1)S(1)} %collective-permute-done.5.refs_4_), channel_id=1, source_target_pairs={{0,4},{4,0},{8,12},{12,8},{16,20},{20,16},{24,28},{28,24},{1,5},{5... | collective-permute-start | bytes 147464 | tf_op jit(solution)/shard_map/ppermute | solution.py:369
  24.7 5.8 %collective-permute-start.11 = (bf16[16,1536]{1,0:T(8,128)(2,1)S(1)}, bf16[16,1536]{1,0:T(8,128)(2,1)S(1)}, u32[]{:S(2)}, u32[]{:S(2)}) collective-permute-start(bf16[16,1536]{1,0:T(8,128)(2,1)S(1)} %get-tuple-element.47), channel_id=1, source_target_pairs={{0,1},{1,0},{2,3},{3,2},{4,5},{5,4},{6,7},{7,6},{8,9},{9,8},{10,11... | collective-permute-start | bytes 147464 | tf_op jit(solution)/shard_map/ppermute | solution.py:369
  24.8 8.8 %collective-permute-start.12 = (bf16[16,1536]{1,0:T(8,128)(2,1)S(1)}, bf16[16,1536]{1,0:T(8,128)(2,1)S(1)}, u32[]{:S(2)}, u32[]{:S(2)}) collective-permute-start(bf16[16,1536]{1,0:T(8,128)(2,1)S(1)} %get-tuple-element.48), channel_id=1, source_target_pairs={{0,2},{1,3},{2,0},{3,1},{4,6},{5,7},{6,4},{7,5},{8,10},{9,11},{10,... | collective-permute-start | bytes 147464 | tf_op jit(solution)/shard_map/ppermute | solution.py:369
  26.1 7.5 %collective-permute-start.13 = (bf16[16,1536]{1,0:T(8,128)(2,1)S(1)}, bf16[16,1536]{1,0:T(8,128)(2,1)S(1)}, u32[]{:S(2)}, u32[]{:S(2)}) collective-permute-start(bf16[16,1536]{1,0:T(8,128)(2,1)S(1)} %get-tuple-element.49), channel_id=1, source_target_pairs={{0,3},{1,2},{2,1},{3,0},{4,7},{5,6},{6,5},{7,4},{8,11},{9,10},{10,... | collective-permute-start | bytes 147464 | tf_op jit(solution)/shard_map/ppermute | solution.py:369
  29.2 5.6 %collective-permute-start.14 = (bf16[16,1536]{1,0:T(8,128)(2,1)S(1)}, bf16[16,1536]{1,0:T(8,128)(2,1)S(1)}, u32[]{:S(2)}, u32[]{:S(2)}) collective-permute-start(bf16[16,1536]{1,0:T(8,128)(2,1)S(1)} %get-tuple-element.55), channel_id=1, source_target_pairs={{0,1},{1,0},{2,3},{3,2},{4,5},{5,4},{6,7},{7,6},{8,9},{9,8},{10,11... | collective-permute-start | bytes 147464 | tf_op jit(solution)/shard_map/ppermute | solution.py:369
  29.2 7.2 %collective-permute-start.15 = (bf16[16,1536]{1,0:T(8,128)(2,1)S(1)}, bf16[16,1536]{1,0:T(8,128)(2,1)S(1)}, u32[]{:S(2)}, u32[]{:S(2)}) collective-permute-start(bf16[16,1536]{1,0:T(8,128)(2,1)S(1)} %get-tuple-element.56), channel_id=1, source_target_pairs={{0,2},{1,3},{2,0},{3,1},{4,6},{5,7},{6,4},{7,5},{8,10},{9,11},{10,... | collective-permute-start | bytes 147464 | tf_op jit(solution)/shard_map/ppermute | solution.py:369
  30.5 5.9 %collective-permute-start.16 = (bf16[16,1536]{1,0:T(8,128)(2,1)S(1)}, bf16[16,1536]{1,0:T(8,128)(2,1)S(1)}, u32[]{:S(2)}, u32[]{:S(2)}) collective-permute-start(bf16[16,1536]{1,0:T(8,128)(2,1)S(1)} %get-tuple-element.57), channel_id=1, source_target_pairs={{0,3},{1,2},{2,1},{3,0},{4,7},{5,6},{6,5},{7,4},{8,11},{9,10},{10,... | collective-permute-start | bytes 147464 | tf_op jit(solution)/shard_map/ppermute | solution.py:369
  37.0 15.8 %collective-permute-start.17 = (bf16[64,1536]{1,0:T(8,128)(2,1)S(1)}, bf16[64,1536]{1,0:T(8,128)(2,1)S(1)}, u32[]{:S(2)}, u32[]{:S(2)}) collective-permute-start(bf16[64,1536]{1,0:T(8,128)(2,1)S(1)} %get-tuple-element.62), channel_id=1, source_target_pairs={{0,2},{1,3},{2,0},{3,1},{4,6},{5,7},{6,4},{7,5},{8,10},{9,11},{10,... | collective-permute-start | bytes 589832 | tf_op jit(solution)/shard_map/ppermute | solution.py:369
  37.8 18.3 %collective-permute-start.21 = (bf16[64,1536]{1,0:T(8,128)(2,1)S(1)}, bf16[64,1536]{1,0:T(8,128)(2,1)S(1)}, u32[]{:S(2)}, u32[]{:S(2)}) collective-permute-start(bf16[64,1536]{1,0:T(8,128)(2,1)S(1)} %get-tuple-element.71), channel_id=1, source_target_pairs={{0,2},{1,3},{2,0},{3,1},{4,6},{5,7},{6,4},{7,5},{8,10},{9,11},{10,... | collective-permute-start | bytes 589832 | tf_op jit(solution)/shard_map/ppermute | solution.py:369
  40.0 24.4 %collective-permute-start.18 = (bf16[64,3072]{1,0:T(8,128)(2,1)S(1)}, bf16[64,3072]{1,0:T(8,128)(2,1)S(1)}, u32[]{:S(2)}, u32[]{:S(2)}) collective-permute-start(bf16[64,3072]{1,0:T(8,128)(2,1)S(1)} %get-tuple-element.70.refs_1_), channel_id=1, source_target_pairs={{0,1},{1,0},{2,3},{3,2},{4,5},{5,4},{6,7},{7,6},{8,9},{9,8},{10,11... | collective-permute-start | bytes 1179656 | tf_op jit(solution)/shard_map/ppermute | solution.py:407
  52.8 11.6 %collective-permute-start.19 = (bf16[64,3072]{1,0:T(8,128)(2,1)S(1)}, bf16[64,3072]{1,0:T(8,128)(2,1)S(1)}, u32[]{:S(2)}, u32[]{:S(2)}) collective-permute-start(bf16[64,3072]{1,0:T(8,128)(2,1)S(1)} %get-tuple-element.70.refs_1_), channel_id=1, source_target_pairs={{1,2},{2,1},{5,6},{6,5},{9,10},{10,9},{13,14},{14,13},{17,18},{18,... | collective-permute-start | bytes 1179656 | tf_op jit(solution)/shard_map/ppermute | solution.py:411
  56.1 8.3 %collective-permute-start.22 = (bf16[64,1536]{1,0:T(8,128)(2,1)S(1)}, bf16[64,1536]{1,0:T(8,128)(2,1)S(1)}, u32[]{:S(2)}, u32[]{:S(2)}) collective-permute-start(bf16[64,1536]{1,0:T(8,128)(2,1)S(1)} %collective-permute-done.21.refs_4_), channel_id=1, source_target_pairs={{1,0},{2,3},{5,4},{6,7},{9,8},{10,11},{13,12},{14,15},{17,16},{18,... | collective-permute-start | bytes 589832 | tf_op jit(solution)/shard_map/ppermute | solution.py:409
  57.4 9.1 %collective-permute-start.20 = (bf16[64,1536]{1,0:T(8,128)(2,1)S(1)}, bf16[64,1536]{1,0:T(8,128)(2,1)S(1)}, u32[]{:S(2)}, u32[]{:S(2)}) collective-permute-start(bf16[64,1536]{1,0:T(8,128)(2,1)S(1)} %collective-permute-done.17.refs_4_), channel_id=1, source_target_pairs={{1,0},{2,3},{5,4},{6,7},{9,8},{10,11},{13,12},{14,15},{17,16},{18,... | collective-permute-start | bytes 589832 | tf_op jit(solution)/shard_map/ppermute | solution.py:409

commit v7 on v6

--- a/solution.py
+++ b/solution.py
@@ -12,7 +12,6 @@
 LMAX = 32
 SAMPLES = 2
 FIRST_HEADS = 12
-CLASSES = 4
 VMEM = 48 * 1024 * 1024
 
 F32 = jnp.float32
@@ -42,14 +41,6 @@
 
 def peer(index, k, paired):
     return index ^ k if paired else k
-
-
-def residue_of(member, k, classes, paired):
-    return (member ^ k) & (classes - 1) if paired else k
-
-
-def own_residue(member, classes, paired):
-    return member & (classes - 1) if paired else member
 
 
 def first_of_class(offset, residue, groups):
@@ -83,7 +74,7 @@
     column = lax.broadcasted_iota(jnp.int32, (depth, depth), 1)
     wanted = jnp.zeros((depth, depth), jnp.int32)
     for k in range(groups):
-        residue = residue_of(member, k, groups, paired)
+        residue = peer(member, k, paired)
         wanted = jnp.where(row // each == k, groups * (row - k * each) + residue, wanted)
     order = (wanted == column).astype(BF16)
     cache_copy.wait()
@@ -132,7 +123,7 @@
     for k in range(groups):
         for s in range(SAMPLES):
             caption = peer(member, k, paired) * SAMPLES + s
-            first = first_of_class(table[2, caption], own_residue(member, groups, paired), groups)
+            first = first_of_class(table[2, caption], member, groups)
             owner = table[1, caption]
             firsts.append(first)
             starts.append((owner ^ index if dp_paired else owner) * each + first)
@@ -178,7 +169,7 @@
     length = jnp.zeros(shape, jnp.int32)
     sample = jnp.zeros(shape, jnp.int32)
     for c in range(groups):
-        residue = residue_of(member, c, groups, paired)
+        residue = peer(member, c, paired)
         for s in range(SAMPLES):
             caption = member * SAMPLES + s
             run = (c * SAMPLES + s) * each
@@ -281,7 +272,7 @@
     for k in range(members):
         device = peer(member, k, paired)
         for c in range(groups):
-            residue = residue_of(device, c, groups, paired)
+            residue = peer(device, c, paired)
             for s in range(SAMPLES):
                 caption = device * SAMPLES + s
                 offset = table[2, caption]
@@ -388,7 +379,8 @@
 
 def reduce_line(pieces, members, paired):
     if paired:
-        return [pieces[0]] + [swap(pieces[k % len(pieces)], "fsdp", k) for k in range(1, members)]
+        distances = sorted(range(1, members), key=lambda k: (k != 2, k))
+        return [pieces[0]] + [swap(pieces[k], "fsdp", k) for k in distances]
     return exchange(pieces, paired)
 
 
@@ -417,7 +409,7 @@
 ):
     members = lax.axis_size("fsdp")
     line = members == 4
-    groups = CLASSES if line else members
+    groups = members
     paired = line
     dp_paired = power_of_two(lax.axis_size("dp")) and lax.axis_size("dp") <= 8
     depth = text_cache.shape[0]

time: 68.7 us -> 68.2 us (level)
    ppermute x19, waiting for transfers between devices: 15.8 us -> 15.1 us  [swap(): lax.ppermute(x, axis, [(i, i ^ k) for i in range(lax.axis_size(axis))])]
  transfers between devices with their start and end apart: 23 -> 23, of which waited for: 12 -> 13; matrix products, arithmetic and copies ran while one was open for 0% -> 0% of each run, Pallas kernels for 7% -> 7%
where the time goes in v7:
time: 68.2 us; the launch traced here: 68 us
  starting transfers between devices  25.4 us (37%)
  waiting for transfers between devices  19.5 us (29%)
  Pallas kernels  11.4 us (17%)
  blocking collectives  10.7 us (16%)
  between operations  0.85 us (1%)
    ppermute x19, starting transfers between devices, swap(): lax.ppermute(x, axis, [(i, i ^ k) for i in range(lax.axis_size(axis))])  21.1 us
    ppermute x19, waiting for transfers between devices, swap(): lax.ppermute(x, axis, [(i, i ^ k) for i in range(lax.axis_size(axis))])  15.1 us
    all_gather x1, blocking collectives, gather_chips(): return lax.all_gather(x, 'dp', axis=0, tiled=True, axis_index_groups=cores)  10.7 us
    ppermute x2, waiting for transfers between devices, gather_line(): outer = [lax.ppermute(piece, 'fsdp', outward) for piece in second]  4.39 us
    pallas_call x2, Pallas kernels, weight_grad(): pl.pallas_call(functools.partial(weight_kernel, line, start, blocks), in_...  4.01 us
    pallas_call x1, Pallas kernels, project(): pl.pallas_call(functools.partial(project_kernel, groups, paired, chunks),...  3.21 us
    ppermute x2, starting transfers between devices, gather_line(): outer = [lax.ppermute(piece, 'fsdp', outward) for piece in second]  2.57 us
    pallas_call x1, Pallas kernels, slot_texts(): pl.pallas_call(functools.partial(text_kernel, members, groups, each, dept...  1.64 us
  transfers between devices with their start and end apart: 23, of which 13 were waited for; matrix products, arithmetic and copies ran while one was open for 0% of the time, Pallas kernels for 7%

profile of v7, /device:TPU:0, one launch (start us, length us, event | category | flops | bytes accessed | tf_op | source)
XLA Modules:
  0.0 68.0 jit_solution(11161950845302282461)
XLA Ops:
  0.6 0.0 copy-start.2
  0.6 0.0 copy-start.3
  0.7 0.0 copy-start.4
  0.7 0.0 copy-start.5
  0.7 0.0 copy-start.6
  0.7 3.2 %project.1 = (bf16[8,3072]{1,0:T(8,128)(2,1)S(1)}, bf16[8,3072]{1,0:T(8,128)(2,1)S(1)}, bf16[8,3072]{1,0:T(8,128)(2,1)S(1)}, bf16[8,3072]{1,0:T(8,128)(2,1)S(1)}) custom-call(bf16[32,1024]{1,0:T(8,128)(2,1)} %refs_0_, bf16[1024,3072]{1,0:T(8,128)(2,1)} %weight.1), custom_call_target="tpu_custom_call" | custom-call | tf_op jit(solution)/shard_map/project/pallas_call | solution.py:97
  3.9 4.1 %collective-permute-start.1 = (bf16[8,3072]{1,0:T(8,128)(2,1)S(1)}, bf16[8,3072]{1,0:T(8,128)(2,1)S(1)}, u32[]{:S(2)}, u32[]{:S(2)}) collective-permute-start(bf16[8,3072]{1,0:T(8,128)(2,1)S(1)} %get-tuple-element.43), channel_id=1, source_target_pairs={{0,2},{1,3},{2,0},{3,1},{4,6},{5,7},{6,4},{7,5},{8,10},{9,11},{10,... | collective-permute-start | bytes 147464 | tf_op jit(solution)/shard_map/ppermute | solution.py:360
  8.0 1.6 %collective-permute-start.2 = (bf16[8,3072]{1,0:T(8,128)(2,1)S(1)}, bf16[8,3072]{1,0:T(8,128)(2,1)S(1)}, u32[]{:S(2)}, u32[]{:S(2)}) collective-permute-start(bf16[8,3072]{1,0:T(8,128)(2,1)S(1)} %get-tuple-element.44), channel_id=1, source_target_pairs={{0,1},{1,0},{2,3},{3,2},{4,5},{5,4},{6,7},{7,6},{8,9},{9,8},{10,11... | collective-permute-start | bytes 147464 | tf_op jit(solution)/shard_map/ppermute | solution.py:360
  9.6 0.0 collective-permute-start.3
  9.6 0.0 copy-done.2
  9.6 0.0 collective-permute-start
  9.6 0.1 pad_add_fusion.1
  9.7 1.0 %collective-permute-done.1 = bf16[8,3072]{1,0:T(8,128)(2,1)S(1)} collective-permute-done((bf16[8,3072]{1,0:T(8,128)(2,1)S(1)}, bf16[8,3072]{1,0:T(8,128)(2,1)S(1)}, u32[]{:S(2)}, u32[]{:S(2)}) %collective-permute-start.1) | collective-permute-done | bytes 49184 | tf_op jit(solution)/shard_map/ppermute | solution.py:360
  10.7 1.4 %collective-permute-done.2 = bf16[8,3072]{1,0:T(8,128)(2,1)S(1)} collective-permute-done((bf16[8,3072]{1,0:T(8,128)(2,1)S(1)}, bf16[8,3072]{1,0:T(8,128)(2,1)S(1)}, u32[]{:S(2)}, u32[]{:S(2)}) %collective-permute-start.2) | collective-permute-done | bytes 49184 | tf_op jit(solution)/shard_map/ppermute | solution.py:360
  12.1 3.4 %collective-permute-done.3 = bf16[8,3072]{1,0:T(8,128)(2,1)S(1)} collective-permute-done((bf16[8,3072]{1,0:T(8,128)(2,1)S(1)}, bf16[8,3072]{1,0:T(8,128)(2,1)S(1)}, u32[]{:S(2)}, u32[]{:S(2)}) %collective-permute-start.3) | collective-permute-done | bytes 49184 | tf_op jit(solution)/shard_map/ppermute | solution.py:360
  15.5 2.5 %collective-permute-start.9 = (bf16[8,3072]{1,0:T(8,128)(2,1)S(1)}, bf16[8,3072]{1,0:T(8,128)(2,1)S(1)}, u32[]{:S(2)}, u32[]{:S(2)}) collective-permute-start(bf16[8,3072]{1,0:T(8,128)(2,1)S(1)} %add_convert_fusion.refs_2_), channel_id=1, source_target_pairs={{0,24},{4,28},{8,16},{12,20},{16,8},{20,12},{24,0},{28,4},{1,25},{... | collective-permute-start | bytes 147464 | tf_op jit(solution)/shard_map/ppermute | solution.py:360
  18.0 0.5 collective-permute-start.7
  18.5 0.5 collective-permute-start.5
  19.1 0.0 collective-permute-start.4
  19.1 1.7 %collective-permute-done.9.refs_8_ = bf16[8,3072]{1,0:T(8,128)(2,1)S(1)} collective-permute-done((bf16[8,3072]{1,0:T(8,128)(2,1)S(1)}, bf16[8,3072]{1,0:T(8,128)(2,1)S(1)}, u32[]{:S(2)}, u32[]{:S(2)}) %collective-permute-start.9) | collective-permute-done | bytes 49184 | tf_op jit(solution)/shard_map/ppermute | solution.py:360
  20.8 0.0 collective-permute-start.10
  20.8 1.3 %collective-permute-done.7.refs_6_ = bf16[8,3072]{1,0:T(8,128)(2,1)S(1)} collective-permute-done((bf16[8,3072]{1,0:T(8,128)(2,1)S(1)}, bf16[8,3072]{1,0:T(8,128)(2,1)S(1)}, u32[]{:S(2)}, u32[]{:S(2)}) %collective-permute-start.7) | collective-permute-done | bytes 49184 | tf_op jit(solution)/shard_map/ppermute | solution.py:360
  22.1 0.0 collective-permute-start.8
  22.1 0.5 collective-permute-done.5.refs_4_
  22.6 0.0 collective-permute-start.6
  22.6 0.0 copy-done.6
  22.7 0.0 collective-permute-done.refs_1_
  22.7 0.0 collective-permute-done.4.refs_3_
  22.7 0.0 collective-permute-done.10.refs_9_
  22.7 0.7 collective-permute-done.8.refs_7_
  23.4 0.5 collective-permute-done.6.refs_5_
  23.9 0.8 %select_rows.1 = (bf16[16,1536]{1,0:T(8,128)(2,1)S(1)}, bf16[16,1536]{1,0:T(8,128)(2,1)S(1)}, bf16[16,1536]{1,0:T(8,128)(2,1)S(1)}, bf16[16,1536]{1,0:T(8,128)(2...) custom-call(s32[4,8]{1,0:T(4,128)S(1)} %pad_add_fusion.table, ...), custom_call_target="tpu_custom_call" | custom-call | tf_op jit(solution)/shard_map/select_rows/pallas_call | solution.py:144
  24.7 0.1 collective-permute-start.11
  24.8 1.2 %collective-permute-start.12 = (bf16[16,1536]{1,0:T(8,128)(2,1)S(1)}, bf16[16,1536]{1,0:T(8,128)(2,1)S(1)}, u32[]{:S(2)}, u32[]{:S(2)}) collective-permute-start(bf16[16,1536]{1,0:T(8,128)(2,1)S(1)} %get-tuple-element.48), channel_id=1, source_target_pairs={{0,2},{1,3},{2,0},{3,1},{4,6},{5,7},{6,4},{7,5},{8,10},{9,11},{10,... | collective-permute-start | bytes 147464 | tf_op jit(solution)/shard_map/ppermute | solution.py:360
  26.0 3.2 %collective-permute-start.13 = (bf16[16,1536]{1,0:T(8,128)(2,1)S(1)}, bf16[16,1536]{1,0:T(8,128)(2,1)S(1)}, u32[]{:S(2)}, u32[]{:S(2)}) collective-permute-start(bf16[16,1536]{1,0:T(8,128)(2,1)S(1)} %get-tuple-element.49), channel_id=1, source_target_pairs={{0,3},{1,2},{2,1},{3,0},{4,7},{5,6},{6,5},{7,4},{8,11},{9,10},{10,... | collective-permute-start | bytes 147464 | tf_op jit(solution)/shard_map/ppermute | solution.py:360
  29.2 0.0 collective-permute-start.14
  29.2 1.2 %collective-permute-start.15 = (bf16[16,1536]{1,0:T(8,128)(2,1)S(1)}, bf16[16,1536]{1,0:T(8,128)(2,1)S(1)}, u32[]{:S(2)}, u32[]{:S(2)}) collective-permute-start(bf16[16,1536]{1,0:T(8,128)(2,1)S(1)} %get-tuple-element.56), channel_id=1, source_target_pairs={{0,2},{1,3},{2,0},{3,1},{4,6},{5,7},{6,4},{7,5},{8,10},{9,11},{10,... | collective-permute-start | bytes 147464 | tf_op jit(solution)/shard_map/ppermute | solution.py:360
  30.4 0.0 collective-permute-done.11.refs_1_
  30.4 3.2 %collective-permute-start.16 = (bf16[16,1536]{1,0:T(8,128)(2,1)S(1)}, bf16[16,1536]{1,0:T(8,128)(2,1)S(1)}, u32[]{:S(2)}, u32[]{:S(2)}) collective-permute-start(bf16[16,1536]{1,0:T(8,128)(2,1)S(1)} %get-tuple-element.57), channel_id=1, source_target_pairs={{0,3},{1,2},{2,1},{3,0},{4,7},{5,6},{6,5},{7,4},{8,11},{9,10},{10,... | collective-permute-start | bytes 147464 | tf_op jit(solution)/shard_map/ppermute | solution.py:360
  33.6 0.0 collective-permute-done.12.refs_2_
  33.6 0.0 collective-permute-done.13.refs_3_
  33.6 0.0 copy-done.1
  33.6 0.0 copy-done
  33.6 1.2 %value_gradients.1 = (f32[12,64,128]{2,1,0:T(8,128)S(1)}, bf16[64,1536]{1,0:T(8,128)(2,1)S(1)}) custom-call(s32[4,8]{1,0:T(4,128)S(1)} %pad_add_fusion.table, bf16[128,1536]{1,0:T(8,128)(2,1)S(1)} %copy-done, bf16[128,1536]{1,0:T(8,128)(2,1)S(1)} %copy-done.1, bf16[16,1536]{1,0:T(8,128)(2,1)S(1)} %get-tuple-element.46.refs_0_, ...), custom_call_target="tpu_custom_call" | custom-call | tf_op jit(solution)/shard_map/value_gradients/pallas_call | solution.py:202
  34.7 0.0 collective-permute-done.14.refs_1_
  34.8 1.6 %collective-permute-done.15.refs_2_ = bf16[16,1536]{1,0:T(8,128)(2,1)S(1)} collective-permute-done((bf16[16,1536]{1,0:T(8,128)(2,1)S(1)}, bf16[16,1536]{1,0:T(8,128)(2,1)S(1)}, u32[]{:S(2)}, u32[]{:S(2)}) %collective-permute-start.15) | collective-permute-done | bytes 49184 | tf_op jit(solution)/shard_map/ppermute | solution.py:360
  36.4 0.0 collective-permute-done.16.refs_3_
  36.4 0.6 key_gradients.1
  37.0 0.7 collective-permute-start.17
  37.6 2.3 %collective-permute-start.21 = (bf16[64,1536]{1,0:T(8,128)(2,1)S(1)}, bf16[64,1536]{1,0:T(8,128)(2,1)S(1)}, u32[]{:S(2)}, u32[]{:S(2)}) collective-permute-start(bf16[64,1536]{1,0:T(8,128)(2,1)S(1)} %get-tuple-element.71), channel_id=1, source_target_pairs={{0,2},{1,3},{2,0},{3,1},{4,6},{5,7},{6,4},{7,5},{8,10},{9,11},{10,... | collective-permute-start | bytes 589832 | tf_op jit(solution)/shard_map/ppermute | solution.py:360
  40.0 1.1 %collective-permute-start.18 = (bf16[64,3072]{1,0:T(8,128)(2,1)S(1)}, bf16[64,3072]{1,0:T(8,128)(2,1)S(1)}, u32[]{:S(2)}, u32[]{:S(2)}) collective-permute-start(bf16[64,3072]{1,0:T(8,128)(2,1)S(1)} %get-tuple-element.70.refs_1_), channel_id=1, source_target_pairs={{0,1},{1,0},{2,3},{3,2},{4,5},{5,4},{6,7},{7,6},{8,9},{9,8},{10,11... | collective-permute-start | bytes 1179656 | tf_op jit(solution)/shard_map/ppermute | solution.py:399
  41.1 10.7 %all_gather.3.text = bf16[256,1024]{1,0:T(8,128)(2,1)S(1)} all-gather(bf16[64,1024]{1,0:T(8,128)(2,1)S(1)} %get-tuple-element.63), channel_id=1, replica_groups={{0,8,16,24},{4,12,20,28},{1,9,17,25},{5,13,21,29},{2,10,18,26},{6,14,22..., dimensions={0}, use_global_device_ids=true | all-gather | bytes 655360 | tf_op jit(solution)/shard_map/all_gather | solution.py:377
  51.7 1.4 %collective-permute-done.17.refs_4_ = bf16[64,1536]{1,0:T(8,128)(2,1)S(1)} collective-permute-done((bf16[64,1536]{1,0:T(8,128)(2,1)S(1)}, bf16[64,1536]{1,0:T(8,128)(2,1)S(1)}, u32[]{:S(2)}, u32[]{:S(2)}) %collective-permute-start.17) | collective-permute-done | bytes 196640 | tf_op jit(solution)/shard_map/ppermute | solution.py:360
  53.1 0.7 collective-permute-start.19
  53.8 1.6 %collective-permute-done.21.refs_4_ = bf16[64,1536]{1,0:T(8,128)(2,1)S(1)} collective-permute-done((bf16[64,1536]{1,0:T(8,128)(2,1)S(1)}, bf16[64,1536]{1,0:T(8,128)(2,1)S(1)}, u32[]{:S(2)}, u32[]{:S(2)}) %collective-permute-start.21) | collective-permute-done | bytes 196640 | tf_op jit(solution)/shard_map/ppermute | solution.py:360
  55.3 1.3 %collective-permute-start.22 = (bf16[64,1536]{1,0:T(8,128)(2,1)S(1)}, bf16[64,1536]{1,0:T(8,128)(2,1)S(1)}, u32[]{:S(2)}, u32[]{:S(2)}) collective-permute-start(bf16[64,1536]{1,0:T(8,128)(2,1)S(1)} %collective-permute-done.21.refs_4_), channel_id=1, source_target_pairs={{1,0},{2,3},{5,4},{6,7},{9,8},{10,11},{13,12},{14,15},{17,16},{18,... | collective-permute-start | bytes 589832 | tf_op jit(solution)/shard_map/ppermute | solution.py:401
  56.6 1.3 %collective-permute-start.20 = (bf16[64,1536]{1,0:T(8,128)(2,1)S(1)}, bf16[64,1536]{1,0:T(8,128)(2,1)S(1)}, u32[]{:S(2)}, u32[]{:S(2)}) collective-permute-start(bf16[64,1536]{1,0:T(8,128)(2,1)S(1)} %collective-permute-done.17.refs_4_), channel_id=1, source_target_pairs={{1,0},{2,3},{5,4},{6,7},{9,8},{10,11},{13,12},{14,15},{17,16},{18,... | collective-permute-start | bytes 589832 | tf_op jit(solution)/shard_map/ppermute | solution.py:401
  57.9 1.6 %slot_texts.1 = (bf16[1024,256]{1,0:T(8,128)(2,1)S(1)}, bf16[128,1536]{1,0:T(8,128)(2,1)}) custom-call(s32[4,8]{1,0:T(4,128)S(1)} %pad_add_fusion.table, bf16[256,1024]{1,0:T(8,128)(2,1)S(1)} %all_gather.3.text, bf16[12,64,128]{2,1,0:T(8,128)(2,1)S(1)} %get-tuple-element.65.score_grads, bf16[16,1536]{1,0:T(8,128)(2,1)S(1)} %get-tuple-element.46.refs_0_, ...), custom_call_target="tpu_custom_call" | custom-call | tf_op jit(solution)/shard_map/slot_texts/pallas_call | solution.py:294
  59.6 4.3 %collective-permute-done.22.refs_5_ = bf16[64,1536]{1,0:T(8,128)(2,1)S(1)} collective-permute-done((bf16[64,1536]{1,0:T(8,128)(2,1)S(1)}, bf16[64,1536]{1,0:T(8,128)(2,1)S(1)}, u32[]{:S(2)}, u32[]{:S(2)}) %collective-permute-start.22) | collective-permute-done | bytes 196640 | tf_op jit(solution)/shard_map/ppermute | solution.py:401
  63.9 0.0 collective-permute-done.18.refs_2_
  63.9 0.0 collective-permute-done.19.refs_3_
  63.9 2.0 %weight_gradient.2.refs_6_ = bf16[1024,3072]{1,0:T(8,128)(2,1)} custom-call(bf16[1024,256]{1,0:T(8,128)(2,1)S(1)} %get-tuple-element.67.refs_0_, bf16[64,3072]{1,0:T(8,128)(2,1)S(1)} %get-tuple-element.70.refs_1_, bf16[64,3072]{1,0:T(8,128)(2,1)S(1)} %collective-permute-done.18.refs_2_, bf16[64,3072]{1,0:T(8,128)(2,1)S(1)} %collective-permute-done.19.refs_3_, ...), custom_call_target="tpu_custom_call" | custom-call | tf_op jit(solution)/shard_map/weight_gradient/pallas_call | solution.py:343
  65.9 0.1 collective-permute-done.20.refs_5_
  66.0 2.0 %weight_gradient.3 = bf16[1024,3072]{1,0:T(8,128)(2,1)} custom-call(bf16[1024,256]{1,0:T(8,128)(2,1)S(1)} %get-tuple-element.67.refs_0_, bf16[64,3072]{1,0:T(8,128)(2,1)S(1)} %get-tuple-element.70.refs_1_, bf16[64,3072]{1,0:T(8,128)(2,1)S(1)} %collective-permute-done.18.refs_2_, ...), custom_call_target="tpu_custom_call", output_to_operand_aliasing={{}: (6, {})} | custom-call | tf_op jit(solution)/shard_map/weight_gradient/pallas_call | solution.py:343
  (8 shorter events, 0.1 us)
Async XLA Ops:
  0.6 9.0 %copy-start.2 = (bf16[32,1024]{1,0:T(8,128)(2,1)S(1)}, bf16[32,1024]{1,0:T(8,128)(2,1)}, u32[]{:S(2)}) copy-start(bf16[32,1024]{1,0:T(8,128)(2,1)} %refs_0_) | copy-start | bytes 196612
  0.6 9.0 %copy-start.3 = (s32[1,2]{1,0:T(1,128)S(1)}, s32[1,2]{1,0:T(1,128)}, u32[]{:S(2)}) copy-start(s32[1,2]{1,0:T(1,128)} %param.12) | copy-start | bytes 28
  0.7 22.0 %copy-start.4 = (s32[1,8]{1,0:T(1,128)S(1)}, s32[1,8]{1,0:T(1,128)}, u32[]{:S(2)}) copy-start(s32[1,8]{1,0:T(1,128)} %param.15) | copy-start | bytes 100
  0.7 22.0 %copy-start.5 = (s32[1,8]{1,0:T(1,128)S(1)}, s32[1,8]{1,0:T(1,128)}, u32[]{:S(2)}) copy-start(s32[1,8]{1,0:T(1,128)} %param.14) | copy-start | bytes 100
  0.7 22.0 %copy-start.6 = (s32[1,8]{1,0:T(1,128)S(1)}, s32[1,8]{1,0:T(1,128)}, u32[]{:S(2)}) copy-start(s32[1,8]{1,0:T(1,128)} %param.13) | copy-start | bytes 100
  0.7 32.9 %copy-start.1 = (bf16[128,1536]{1,0:T(8,128)(2,1)S(1)}, bf16[128,1536]{1,0:T(8,128)(2,1)}, u32[]{:S(2)}) copy-start(bf16[128,1536]{1,0:T(8,128)(2,1)} %cotangent.3) | copy-start | bytes 1179652
  0.7 32.9 %copy-start = (bf16[128,1536]{1,0:T(8,128)(2,1)S(1)}, bf16[128,1536]{1,0:T(8,128)(2,1)}, u32[]{:S(2)}) copy-start(bf16[128,1536]{1,0:T(8,128)(2,1)} %queries.3) | copy-start | bytes 1179652
  3.9 6.8 %collective-permute-start.1 = (bf16[8,3072]{1,0:T(8,128)(2,1)S(1)}, bf16[8,3072]{1,0:T(8,128)(2,1)S(1)}, u32[]{:S(2)}, u32[]{:S(2)}) collective-permute-start(bf16[8,3072]{1,0:T(8,128)(2,1)S(1)} %get-tuple-element.43), channel_id=1, source_target_pairs={{0,2},{1,3},{2,0},{3,1},{4,6},{5,7},{6,4},{7,5},{8,10},{9,11},{10,... | collective-permute-start | bytes 147464 | tf_op jit(solution)/shard_map/ppermute | solution.py:360
  8.0 4.1 %collective-permute-start.2 = (bf16[8,3072]{1,0:T(8,128)(2,1)S(1)}, bf16[8,3072]{1,0:T(8,128)(2,1)S(1)}, u32[]{:S(2)}, u32[]{:S(2)}) collective-permute-start(bf16[8,3072]{1,0:T(8,128)(2,1)S(1)} %get-tuple-element.44), channel_id=1, source_target_pairs={{0,1},{1,0},{2,3},{3,2},{4,5},{5,4},{6,7},{7,6},{8,9},{9,8},{10,11... | collective-permute-start | bytes 147464 | tf_op jit(solution)/shard_map/ppermute | solution.py:360
  9.6 5.9 %collective-permute-start.3 = (bf16[8,3072]{1,0:T(8,128)(2,1)S(1)}, bf16[8,3072]{1,0:T(8,128)(2,1)S(1)}, u32[]{:S(2)}, u32[]{:S(2)}) collective-permute-start(bf16[8,3072]{1,0:T(8,128)(2,1)S(1)} %get-tuple-element.45), channel_id=1, source_target_pairs={{0,3},{1,2},{2,1},{3,0},{4,7},{5,6},{6,5},{7,4},{8,11},{9,10},{10,... | collective-permute-start | bytes 147464 | tf_op jit(solution)/shard_map/ppermute | solution.py:360
  9.6 13.1 %collective-permute-start = (bf16[32,1024]{1,0:T(8,128)(2,1)S(1)}, bf16[32,1024]{1,0:T(8,128)(2,1)S(1)}, u32[]{:S(2)}, u32[]{:S(2)}) collective-permute-start(bf16[32,1024]{1,0:T(8,128)(2,1)S(1)} %copy-done.2), channel_id=1, source_target_pairs={{0,4},{4,0},{8,12},{12,8},{16,20},{20,16},{24,28},{28,24},{1,5},{5... | collective-permute-start | bytes 196616 | tf_op jit(solution)/shard_map/ppermute | solution.py:360
  15.5 5.3 %collective-permute-start.9 = (bf16[8,3072]{1,0:T(8,128)(2,1)S(1)}, bf16[8,3072]{1,0:T(8,128)(2,1)S(1)}, u32[]{:S(2)}, u32[]{:S(2)}) collective-permute-start(bf16[8,3072]{1,0:T(8,128)(2,1)S(1)} %add_convert_fusion.refs_2_), channel_id=1, source_target_pairs={{0,24},{4,28},{8,16},{12,20},{16,8},{20,12},{24,0},{28,4},{1,25},{... | collective-permute-start | bytes 147464 | tf_op jit(solution)/shard_map/ppermute | solution.py:360
  18.0 4.1 %collective-permute-start.7 = (bf16[8,3072]{1,0:T(8,128)(2,1)S(1)}, bf16[8,3072]{1,0:T(8,128)(2,1)S(1)}, u32[]{:S(2)}, u32[]{:S(2)}) collective-permute-start(bf16[8,3072]{1,0:T(8,128)(2,1)S(1)} %add_convert_fusion.refs_2_), channel_id=1, source_target_pairs={{0,16},{4,20},{8,24},{12,28},{16,0},{20,4},{24,8},{28,12},{1,17},{... | collective-permute-start | bytes 147464 | tf_op jit(solution)/shard_map/ppermute | solution.py:360
  18.5 4.1 %collective-permute-start.5 = (bf16[8,3072]{1,0:T(8,128)(2,1)S(1)}, bf16[8,3072]{1,0:T(8,128)(2,1)S(1)}, u32[]{:S(2)}, u32[]{:S(2)}) collective-permute-start(bf16[8,3072]{1,0:T(8,128)(2,1)S(1)} %add_convert_fusion.refs_2_), channel_id=1, source_target_pairs={{0,8},{4,12},{8,0},{12,4},{16,24},{20,28},{24,16},{28,20},{1,9},{5... | collective-permute-start | bytes 147464 | tf_op jit(solution)/shard_map/ppermute | solution.py:360
  19.1 3.6 %collective-permute-start.4 = (bf16[8,3072]{1,0:T(8,128)(2,1)S(1)}, bf16[8,3072]{1,0:T(8,128)(2,1)S(1)}, u32[]{:S(2)}, u32[]{:S(2)}) collective-permute-start(bf16[8,3072]{1,0:T(8,128)(2,1)S(1)} %add_convert_fusion.refs_2_), channel_id=1, source_target_pairs={{0,4},{4,0},{8,12},{12,8},{16,20},{20,16},{24,28},{28,24},{1,5},{5... | collective-permute-start | bytes 147464 | tf_op jit(solution)/shard_map/ppermute | solution.py:360
  20.8 1.9 %collective-permute-start.10 = (bf16[8,3072]{1,0:T(8,128)(2,1)S(1)}, bf16[8,3072]{1,0:T(8,128)(2,1)S(1)}, u32[]{:S(2)}, u32[]{:S(2)}) collective-permute-start(bf16[8,3072]{1,0:T(8,128)(2,1)S(1)} %collective-permute-done.9.refs_8_), channel_id=1, source_target_pairs={{0,4},{4,0},{8,12},{12,8},{16,20},{20,16},{24,28},{28,24},{1,5},{5... | collective-permute-start | bytes 147464 | tf_op jit(solution)/shard_map/ppermute | solution.py:360
  22.1 1.2 %collective-permute-start.8 = (bf16[8,3072]{1,0:T(8,128)(2,1)S(1)}, bf16[8,3072]{1,0:T(8,128)(2,1)S(1)}, u32[]{:S(2)}, u32[]{:S(2)}) collective-permute-start(bf16[8,3072]{1,0:T(8,128)(2,1)S(1)} %collective-permute-done.7.refs_6_), channel_id=1, source_target_pairs={{0,4},{4,0},{8,12},{12,8},{16,20},{20,16},{24,28},{28,24},{1,5},{5... | collective-permute-start | bytes 147464 | tf_op jit(solution)/shard_map/ppermute | solution.py:360
  22.6 1.2 %collective-permute-start.6 = (bf16[8,3072]{1,0:T(8,128)(2,1)S(1)}, bf16[8,3072]{1,0:T(8,128)(2,1)S(1)}, u32[]{:S(2)}, u32[]{:S(2)}) collective-permute-start(bf16[8,3072]{1,0:T(8,128)(2,1)S(1)} %collective-permute-done.5.refs_4_), channel_id=1, source_target_pairs={{0,4},{4,0},{8,12},{12,8},{16,20},{20,16},{24,28},{28,24},{1,5},{5... | collective-permute-start | bytes 147464 | tf_op jit(solution)/shard_map/ppermute | solution.py:360
  24.7 5.6 %collective-permute-start.11 = (bf16[16,1536]{1,0:T(8,128)(2,1)S(1)}, bf16[16,1536]{1,0:T(8,128)(2,1)S(1)}, u32[]{:S(2)}, u32[]{:S(2)}) collective-permute-start(bf16[16,1536]{1,0:T(8,128)(2,1)S(1)} %get-tuple-element.47), channel_id=1, source_target_pairs={{0,1},{1,0},{2,3},{3,2},{4,5},{5,4},{6,7},{7,6},{8,9},{9,8},{10,11... | collective-permute-start | bytes 147464 | tf_op jit(solution)/shard_map/ppermute | solution.py:360
  24.8 8.8 %collective-permute-start.12 = (bf16[16,1536]{1,0:T(8,128)(2,1)S(1)}, bf16[16,1536]{1,0:T(8,128)(2,1)S(1)}, u32[]{:S(2)}, u32[]{:S(2)}) collective-permute-start(bf16[16,1536]{1,0:T(8,128)(2,1)S(1)} %get-tuple-element.48), channel_id=1, source_target_pairs={{0,2},{1,3},{2,0},{3,1},{4,6},{5,7},{6,4},{7,5},{8,10},{9,11},{10,... | collective-permute-start | bytes 147464 | tf_op jit(solution)/shard_map/ppermute | solution.py:360
  26.0 7.6 %collective-permute-start.13 = (bf16[16,1536]{1,0:T(8,128)(2,1)S(1)}, bf16[16,1536]{1,0:T(8,128)(2,1)S(1)}, u32[]{:S(2)}, u32[]{:S(2)}) collective-permute-start(bf16[16,1536]{1,0:T(8,128)(2,1)S(1)} %get-tuple-element.49), channel_id=1, source_target_pairs={{0,3},{1,2},{2,1},{3,0},{4,7},{5,6},{6,5},{7,4},{8,11},{9,10},{10,... | collective-permute-start | bytes 147464 | tf_op jit(solution)/shard_map/ppermute | solution.py:360
  29.2 5.6 %collective-permute-start.14 = (bf16[16,1536]{1,0:T(8,128)(2,1)S(1)}, bf16[16,1536]{1,0:T(8,128)(2,1)S(1)}, u32[]{:S(2)}, u32[]{:S(2)}) collective-permute-start(bf16[16,1536]{1,0:T(8,128)(2,1)S(1)} %get-tuple-element.55), channel_id=1, source_target_pairs={{0,1},{1,0},{2,3},{3,2},{4,5},{5,4},{6,7},{7,6},{8,9},{9,8},{10,11... | collective-permute-start | bytes 147464 | tf_op jit(solution)/shard_map/ppermute | solution.py:360
  29.2 7.2 %collective-permute-start.15 = (bf16[16,1536]{1,0:T(8,128)(2,1)S(1)}, bf16[16,1536]{1,0:T(8,128)(2,1)S(1)}, u32[]{:S(2)}, u32[]{:S(2)}) collective-permute-start(bf16[16,1536]{1,0:T(8,128)(2,1)S(1)} %get-tuple-element.56), channel_id=1, source_target_pairs={{0,2},{1,3},{2,0},{3,1},{4,6},{5,7},{6,4},{7,5},{8,10},{9,11},{10,... | collective-permute-start | bytes 147464 | tf_op jit(solution)/shard_map/ppermute | solution.py:360
  30.4 6.0 %collective-permute-start.16 = (bf16[16,1536]{1,0:T(8,128)(2,1)S(1)}, bf16[16,1536]{1,0:T(8,128)(2,1)S(1)}, u32[]{:S(2)}, u32[]{:S(2)}) collective-permute-start(bf16[16,1536]{1,0:T(8,128)(2,1)S(1)} %get-tuple-element.57), channel_id=1, source_target_pairs={{0,3},{1,2},{2,1},{3,0},{4,7},{5,6},{6,5},{7,4},{8,11},{9,10},{10,... | collective-permute-start | bytes 147464 | tf_op jit(solution)/shard_map/ppermute | solution.py:360
  37.0 16.1 %collective-permute-start.17 = (bf16[64,1536]{1,0:T(8,128)(2,1)S(1)}, bf16[64,1536]{1,0:T(8,128)(2,1)S(1)}, u32[]{:S(2)}, u32[]{:S(2)}) collective-permute-start(bf16[64,1536]{1,0:T(8,128)(2,1)S(1)} %get-tuple-element.62), channel_id=1, source_target_pairs={{0,2},{1,3},{2,0},{3,1},{4,6},{5,7},{6,4},{7,5},{8,10},{9,11},{10,... | collective-permute-start | bytes 589832 | tf_op jit(solution)/shard_map/ppermute | solution.py:360
  37.6 17.7 %collective-permute-start.21 = (bf16[64,1536]{1,0:T(8,128)(2,1)S(1)}, bf16[64,1536]{1,0:T(8,128)(2,1)S(1)}, u32[]{:S(2)}, u32[]{:S(2)}) collective-permute-start(bf16[64,1536]{1,0:T(8,128)(2,1)S(1)} %get-tuple-element.71), channel_id=1, source_target_pairs={{0,2},{1,3},{2,0},{3,1},{4,6},{5,7},{6,4},{7,5},{8,10},{9,11},{10,... | collective-permute-start | bytes 589832 | tf_op jit(solution)/shard_map/ppermute | solution.py:360
  40.0 23.9 %collective-permute-start.18 = (bf16[64,3072]{1,0:T(8,128)(2,1)S(1)}, bf16[64,3072]{1,0:T(8,128)(2,1)S(1)}, u32[]{:S(2)}, u32[]{:S(2)}) collective-permute-start(bf16[64,3072]{1,0:T(8,128)(2,1)S(1)} %get-tuple-element.70.refs_1_), channel_id=1, source_target_pairs={{0,1},{1,0},{2,3},{3,2},{4,5},{5,4},{6,7},{7,6},{8,9},{9,8},{10,11... | collective-permute-start | bytes 1179656 | tf_op jit(solution)/shard_map/ppermute | solution.py:399
  53.1 10.8 %collective-permute-start.19 = (bf16[64,3072]{1,0:T(8,128)(2,1)S(1)}, bf16[64,3072]{1,0:T(8,128)(2,1)S(1)}, u32[]{:S(2)}, u32[]{:S(2)}) collective-permute-start(bf16[64,3072]{1,0:T(8,128)(2,1)S(1)} %get-tuple-element.70.refs_1_), channel_id=1, source_target_pairs={{1,2},{2,1},{5,6},{6,5},{9,10},{10,9},{13,14},{14,13},{17,18},{18,... | collective-permute-start | bytes 1179656 | tf_op jit(solution)/shard_map/ppermute | solution.py:403
  55.3 8.5 %collective-permute-start.22 = (bf16[64,1536]{1,0:T(8,128)(2,1)S(1)}, bf16[64,1536]{1,0:T(8,128)(2,1)S(1)}, u32[]{:S(2)}, u32[]{:S(2)}) collective-permute-start(bf16[64,1536]{1,0:T(8,128)(2,1)S(1)} %collective-permute-done.21.refs_4_), channel_id=1, source_target_pairs={{1,0},{2,3},{5,4},{6,7},{9,8},{10,11},{13,12},{14,15},{17,16},{18,... | collective-permute-start | bytes 589832 | tf_op jit(solution)/shard_map/ppermute | solution.py:401
  56.6 9.4 %collective-permute-start.20 = (bf16[64,1536]{1,0:T(8,128)(2,1)S(1)}, bf16[64,1536]{1,0:T(8,128)(2,1)S(1)}, u32[]{:S(2)}, u32[]{:S(2)}) collective-permute-start(bf16[64,1536]{1,0:T(8,128)(2,1)S(1)} %collective-permute-done.17.refs_4_), channel_id=1, source_target_pairs={{1,0},{2,3},{5,4},{6,7},{9,8},{10,11},{13,12},{14,15},{17,16},{18,... | collective-permute-start | bytes 589832 | tf_op jit(solution)/shard_map/ppermute | solution.py:401

commit v8 on v7

--- a/solution.py
+++ b/solution.py
@@ -397,9 +397,9 @@
     outward = [(1, 0), (2, 3)]
     second = [swap(part, "fsdp", 2) for part in parts]
     near = lax.ppermute(both, "fsdp", near_pairs)
-    second[1], beside = lax.optimization_barrier((second[1], beside))
+    second[0], beside = lax.optimization_barrier((second[0], beside))
     outer = [lax.ppermute(piece, "fsdp", outward) for piece in second]
-    late, _ = lax.optimization_barrier((both, second[1]))
+    late, _ = lax.optimization_barrier((both, second[0]))
     inner = lax.ppermute(late, "fsdp", middle_pairs)
     return near, inner, second, outer, beside
 
@@ -441,8 +441,8 @@
         operands = [[lax.all_gather(grad_both, "fsdp", axis=0, tiled=True)]] * 2
     chosen_text, grad_query = slot_texts(members, groups, each, depth, paired, dp_paired, table, text, score_grads, keys)
     cut = parts[0].shape[1]
-    grad_weight = weight_grad(line, chosen_text, operands[0], 0, cut)
-    grad_weight = weight_grad(line, chosen_text, operands[1], cut, 2 * width - cut, grad_weight)
+    grad_weight = weight_grad(line, chosen_text, operands[1], cut, 2 * width - cut)
+    grad_weight = weight_grad(line, chosen_text, operands[0], 0, cut, grad_weight)
     return grad_query, grad_weight[None]
 
 

time: 68.2 us -> 68.2 us (level)
  no operation moved by 1% of the time
where the time goes in v8:
time: 68.2 us; the launch traced here: 68 us
  starting transfers between devices  25.4 us (37%)
  waiting for transfers between devices  19.5 us (29%)
  Pallas kernels  11.5 us (17%)
  blocking collectives  10.7 us (16%)
  between operations  0.85 us (1%)
    ppermute x19, starting transfers between devices, swap(): lax.ppermute(x, axis, [(i, i ^ k) for i in range(lax.axis_size(axis))])  21.1 us
    ppermute x19, waiting for transfers between devices, swap(): lax.ppermute(x, axis, [(i, i ^ k) for i in range(lax.axis_size(axis))])  15.1 us
    all_gather x1, blocking collectives, gather_chips(): return lax.all_gather(x, 'dp', axis=0, tiled=True, axis_index_groups=cores)  10.7 us
    ppermute x2, waiting for transfers between devices, gather_line(): outer = [lax.ppermute(piece, 'fsdp', outward) for piece in second]  4.38 us
    pallas_call x2, Pallas kernels, weight_grad(): pl.pallas_call(functools.partial(weight_kernel, line, start, blocks), in_...  4.04 us
    pallas_call x1, Pallas kernels, project(): pl.pallas_call(functools.partial(project_kernel, groups, paired, chunks),...  3.21 us
    ppermute x2, starting transfers between devices, gather_line(): outer = [lax.ppermute(piece, 'fsdp', outward) for piece in second]  2.57 us
    pallas_call x1, Pallas kernels, slot_texts(): pl.pallas_call(functools.partial(text_kernel, members, groups, each, dept...  1.64 us
  transfers between devices with their start and end apart: 23, of which 13 were waited for; matrix products, arithmetic and copies ran while one was open for 0% of the time, Pallas kernels for 7%

profile of v8, /device:TPU:0, one launch (start us, length us, event | category | flops | bytes accessed | tf_op | source)
XLA Modules:
  0.0 68.0 jit_solution(14065715946124479048)
XLA Ops:
  0.6 0.0 copy-start.2
  0.6 0.0 copy-start.3
  0.7 0.0 copy-start.4
  0.7 0.0 copy-start.5
  0.7 0.0 copy-start.6
  0.7 0.0 copy-start.1
  0.7 0.0 copy-start
  0.7 3.2 %project.1 = (bf16[8,3072]{1,0:T(8,128)(2,1)S(1)}, bf16[8,3072]{1,0:T(8,128)(2,1)S(1)}, bf16[8,3072]{1,0:T(8,128)(2,1)S(1)}, bf16[8,3072]{1,0:T(8,128)(2,1)S(1)}) custom-call(bf16[32,1024]{1,0:T(8,128)(2,1)} %refs_0_, bf16[1024,3072]{1,0:T(8,128)(2,1)} %weight.1), custom_call_target="tpu_custom_call" | custom-call | tf_op jit(solution)/shard_map/project/pallas_call | solution.py:97
  3.9 4.1 %collective-permute-start.1 = (bf16[8,3072]{1,0:T(8,128)(2,1)S(1)}, bf16[8,3072]{1,0:T(8,128)(2,1)S(1)}, u32[]{:S(2)}, u32[]{:S(2)}) collective-permute-start(bf16[8,3072]{1,0:T(8,128)(2,1)S(1)} %get-tuple-element.43), channel_id=1, source_target_pairs={{0,2},{1,3},{2,0},{3,1},{4,6},{5,7},{6,4},{7,5},{8,10},{9,11},{10,... | collective-permute-start | bytes 147464 | tf_op jit(solution)/shard_map/ppermute | solution.py:360
  8.0 1.6 %collective-permute-start.2 = (bf16[8,3072]{1,0:T(8,128)(2,1)S(1)}, bf16[8,3072]{1,0:T(8,128)(2,1)S(1)}, u32[]{:S(2)}, u32[]{:S(2)}) collective-permute-start(bf16[8,3072]{1,0:T(8,128)(2,1)S(1)} %get-tuple-element.44), channel_id=1, source_target_pairs={{0,1},{1,0},{2,3},{3,2},{4,5},{5,4},{6,7},{7,6},{8,9},{9,8},{10,11... | collective-permute-start | bytes 147464 | tf_op jit(solution)/shard_map/ppermute | solution.py:360
  9.6 0.0 collective-permute-start.3
  9.6 0.0 copy-done.2
  9.6 0.0 collective-permute-start
  9.6 0.0 copy-done.3
  9.6 0.1 pad_add_fusion.1
  9.7 1.0 %collective-permute-done.1 = bf16[8,3072]{1,0:T(8,128)(2,1)S(1)} collective-permute-done((bf16[8,3072]{1,0:T(8,128)(2,1)S(1)}, bf16[8,3072]{1,0:T(8,128)(2,1)S(1)}, u32[]{:S(2)}, u32[]{:S(2)}) %collective-permute-start.1) | collective-permute-done | bytes 49184 | tf_op jit(solution)/shard_map/ppermute | solution.py:360
  10.7 1.4 %collective-permute-done.2 = bf16[8,3072]{1,0:T(8,128)(2,1)S(1)} collective-permute-done((bf16[8,3072]{1,0:T(8,128)(2,1)S(1)}, bf16[8,3072]{1,0:T(8,128)(2,1)S(1)}, u32[]{:S(2)}, u32[]{:S(2)}) %collective-permute-start.2) | collective-permute-done | bytes 49184 | tf_op jit(solution)/shard_map/ppermute | solution.py:360
  12.1 3.4 %collective-permute-done.3 = bf16[8,3072]{1,0:T(8,128)(2,1)S(1)} collective-permute-done((bf16[8,3072]{1,0:T(8,128)(2,1)S(1)}, bf16[8,3072]{1,0:T(8,128)(2,1)S(1)}, u32[]{:S(2)}, u32[]{:S(2)}) %collective-permute-start.3) | collective-permute-done | bytes 49184 | tf_op jit(solution)/shard_map/ppermute | solution.py:360
  15.5 2.5 %collective-permute-start.9 = (bf16[8,3072]{1,0:T(8,128)(2,1)S(1)}, bf16[8,3072]{1,0:T(8,128)(2,1)S(1)}, u32[]{:S(2)}, u32[]{:S(2)}) collective-permute-start(bf16[8,3072]{1,0:T(8,128)(2,1)S(1)} %add_convert_fusion.refs_2_), channel_id=1, source_target_pairs={{0,24},{4,28},{8,16},{12,20},{16,8},{20,12},{24,0},{28,4},{1,25},{... | collective-permute-start | bytes 147464 | tf_op jit(solution)/shard_map/ppermute | solution.py:360
  18.0 0.5 collective-permute-start.7
  18.5 0.5 collective-permute-start.5
  19.1 0.0 collective-permute-start.4
  19.1 1.7 %collective-permute-done.9.refs_8_ = bf16[8,3072]{1,0:T(8,128)(2,1)S(1)} collective-permute-done((bf16[8,3072]{1,0:T(8,128)(2,1)S(1)}, bf16[8,3072]{1,0:T(8,128)(2,1)S(1)}, u32[]{:S(2)}, u32[]{:S(2)}) %collective-permute-start.9) | collective-permute-done | bytes 49184 | tf_op jit(solution)/shard_map/ppermute | solution.py:360
  20.8 0.0 collective-permute-start.10
  20.8 1.3 %collective-permute-done.7.refs_6_ = bf16[8,3072]{1,0:T(8,128)(2,1)S(1)} collective-permute-done((bf16[8,3072]{1,0:T(8,128)(2,1)S(1)}, bf16[8,3072]{1,0:T(8,128)(2,1)S(1)}, u32[]{:S(2)}, u32[]{:S(2)}) %collective-permute-start.7) | collective-permute-done | bytes 49184 | tf_op jit(solution)/shard_map/ppermute | solution.py:360
  22.1 0.0 collective-permute-start.8
  22.1 0.5 collective-permute-done.5.refs_4_
  22.6 0.0 collective-permute-start.6
  22.7 0.0 collective-permute-done.refs_1_
  22.7 0.0 collective-permute-done.4.refs_3_
  22.7 0.0 collective-permute-done.10.refs_9_
  22.7 0.7 collective-permute-done.8.refs_7_
  23.4 0.5 collective-permute-done.6.refs_5_
  23.9 0.8 %select_rows.1 = (bf16[16,1536]{1,0:T(8,128)(2,1)S(1)}, bf16[16,1536]{1,0:T(8,128)(2,1)S(1)}, bf16[16,1536]{1,0:T(8,128)(2,1)S(1)}, bf16[16,1536]{1,0:T(8,128)(2...) custom-call(s32[4,8]{1,0:T(4,128)S(1)} %pad_add_fusion.table, ...), custom_call_target="tpu_custom_call" | custom-call | tf_op jit(solution)/shard_map/select_rows/pallas_call | solution.py:144
  24.7 0.1 collective-permute-start.11
  24.8 1.2 %collective-permute-start.12 = (bf16[16,1536]{1,0:T(8,128)(2,1)S(1)}, bf16[16,1536]{1,0:T(8,128)(2,1)S(1)}, u32[]{:S(2)}, u32[]{:S(2)}) collective-permute-start(bf16[16,1536]{1,0:T(8,128)(2,1)S(1)} %get-tuple-element.48), channel_id=1, source_target_pairs={{0,2},{1,3},{2,0},{3,1},{4,6},{5,7},{6,4},{7,5},{8,10},{9,11},{10,... | collective-permute-start | bytes 147464 | tf_op jit(solution)/shard_map/ppermute | solution.py:360
  26.0 3.2 %collective-permute-start.13 = (bf16[16,1536]{1,0:T(8,128)(2,1)S(1)}, bf16[16,1536]{1,0:T(8,128)(2,1)S(1)}, u32[]{:S(2)}, u32[]{:S(2)}) collective-permute-start(bf16[16,1536]{1,0:T(8,128)(2,1)S(1)} %get-tuple-element.49), channel_id=1, source_target_pairs={{0,3},{1,2},{2,1},{3,0},{4,7},{5,6},{6,5},{7,4},{8,11},{9,10},{10,... | collective-permute-start | bytes 147464 | tf_op jit(solution)/shard_map/ppermute | solution.py:360
  29.2 0.0 collective-permute-start.14
  29.2 1.2 %collective-permute-start.15 = (bf16[16,1536]{1,0:T(8,128)(2,1)S(1)}, bf16[16,1536]{1,0:T(8,128)(2,1)S(1)}, u32[]{:S(2)}, u32[]{:S(2)}) collective-permute-start(bf16[16,1536]{1,0:T(8,128)(2,1)S(1)} %get-tuple-element.56), channel_id=1, source_target_pairs={{0,2},{1,3},{2,0},{3,1},{4,6},{5,7},{6,4},{7,5},{8,10},{9,11},{10,... | collective-permute-start | bytes 147464 | tf_op jit(solution)/shard_map/ppermute | solution.py:360
  30.4 0.0 collective-permute-done.11.refs_1_
  30.4 3.2 %collective-permute-start.16 = (bf16[16,1536]{1,0:T(8,128)(2,1)S(1)}, bf16[16,1536]{1,0:T(8,128)(2,1)S(1)}, u32[]{:S(2)}, u32[]{:S(2)}) collective-permute-start(bf16[16,1536]{1,0:T(8,128)(2,1)S(1)} %get-tuple-element.57), channel_id=1, source_target_pairs={{0,3},{1,2},{2,1},{3,0},{4,7},{5,6},{6,5},{7,4},{8,11},{9,10},{10,... | collective-permute-start | bytes 147464 | tf_op jit(solution)/shard_map/ppermute | solution.py:360
  33.6 0.0 collective-permute-done.12.refs_2_
  33.6 0.0 collective-permute-done.13.refs_3_
  33.6 1.2 %value_gradients.1 = (f32[12,64,128]{2,1,0:T(8,128)S(1)}, bf16[64,1536]{1,0:T(8,128)(2,1)S(1)}) custom-call(s32[4,8]{1,0:T(4,128)S(1)} %pad_add_fusion.table, bf16[128,1536]{1,0:T(8,128)(2,1)S(1)} %copy-done, bf16[128,1536]{1,0:T(8,128)(2,1)S(1)} %copy-done.1, bf16[16,1536]{1,0:T(8,128)(2,1)S(1)} %get-tuple-element.46.refs_0_, ...), custom_call_target="tpu_custom_call" | custom-call | tf_op jit(solution)/shard_map/value_gradients/pallas_call | solution.py:202
  34.7 0.0 collective-permute-done.14.refs_1_
  34.8 1.6 %collective-permute-done.15.refs_2_ = bf16[16,1536]{1,0:T(8,128)(2,1)S(1)} collective-permute-done((bf16[16,1536]{1,0:T(8,128)(2,1)S(1)}, bf16[16,1536]{1,0:T(8,128)(2,1)S(1)}, u32[]{:S(2)}, u32[]{:S(2)}) %collective-permute-start.15) | collective-permute-done | bytes 49184 | tf_op jit(solution)/shard_map/ppermute | solution.py:360
  36.4 0.0 collective-permute-done.16.refs_3_
  36.4 0.6 key_gradients.1
  37.0 0.7 collective-permute-start.17
  37.6 2.3 %collective-permute-start.21 = (bf16[64,1536]{1,0:T(8,128)(2,1)S(1)}, bf16[64,1536]{1,0:T(8,128)(2,1)S(1)}, u32[]{:S(2)}, u32[]{:S(2)}) collective-permute-start(bf16[64,1536]{1,0:T(8,128)(2,1)S(1)} %get-tuple-element.71), channel_id=1, source_target_pairs={{0,2},{1,3},{2,0},{3,1},{4,6},{5,7},{6,4},{7,5},{8,10},{9,11},{10,... | collective-permute-start | bytes 589832 | tf_op jit(solution)/shard_map/ppermute | solution.py:360
  40.0 1.1 %collective-permute-start.18 = (bf16[64,3072]{1,0:T(8,128)(2,1)S(1)}, bf16[64,3072]{1,0:T(8,128)(2,1)S(1)}, u32[]{:S(2)}, u32[]{:S(2)}) collective-permute-start(bf16[64,3072]{1,0:T(8,128)(2,1)S(1)} %get-tuple-element.70.refs_1_), channel_id=1, source_target_pairs={{0,1},{1,0},{2,3},{3,2},{4,5},{5,4},{6,7},{7,6},{8,9},{9,8},{10,11... | collective-permute-start | bytes 1179656 | tf_op jit(solution)/shard_map/ppermute | solution.py:399
  41.1 10.7 %all_gather.3.text = bf16[256,1024]{1,0:T(8,128)(2,1)S(1)} all-gather(bf16[64,1024]{1,0:T(8,128)(2,1)S(1)} %get-tuple-element.63), channel_id=1, replica_groups={{0,8,16,24},{4,12,20,28},{1,9,17,25},{5,13,21,29},{2,10,18,26},{6,14,22..., dimensions={0}, use_global_device_ids=true | all-gather | bytes 655360 | tf_op jit(solution)/shard_map/all_gather | solution.py:377
  51.7 1.4 %collective-permute-done.17.refs_4_ = bf16[64,1536]{1,0:T(8,128)(2,1)S(1)} collective-permute-done((bf16[64,1536]{1,0:T(8,128)(2,1)S(1)}, bf16[64,1536]{1,0:T(8,128)(2,1)S(1)}, u32[]{:S(2)}, u32[]{:S(2)}) %collective-permute-start.17) | collective-permute-done | bytes 196640 | tf_op jit(solution)/shard_map/ppermute | solution.py:360
  53.1 0.7 collective-permute-start.19
  53.8 1.6 %collective-permute-done.21.refs_4_ = bf16[64,1536]{1,0:T(8,128)(2,1)S(1)} collective-permute-done((bf16[64,1536]{1,0:T(8,128)(2,1)S(1)}, bf16[64,1536]{1,0:T(8,128)(2,1)S(1)}, u32[]{:S(2)}, u32[]{:S(2)}) %collective-permute-start.21) | collective-permute-done | bytes 196640 | tf_op jit(solution)/shard_map/ppermute | solution.py:360
  55.3 1.3 %collective-permute-start.22 = (bf16[64,1536]{1,0:T(8,128)(2,1)S(1)}, bf16[64,1536]{1,0:T(8,128)(2,1)S(1)}, u32[]{:S(2)}, u32[]{:S(2)}) collective-permute-start(bf16[64,1536]{1,0:T(8,128)(2,1)S(1)} %collective-permute-done.21.refs_4_), channel_id=1, source_target_pairs={{1,0},{2,3},{5,4},{6,7},{9,8},{10,11},{13,12},{14,15},{17,16},{18,... | collective-permute-start | bytes 589832 | tf_op jit(solution)/shard_map/ppermute | solution.py:401
  56.6 1.3 %collective-permute-start.20 = (bf16[64,1536]{1,0:T(8,128)(2,1)S(1)}, bf16[64,1536]{1,0:T(8,128)(2,1)S(1)}, u32[]{:S(2)}, u32[]{:S(2)}) collective-permute-start(bf16[64,1536]{1,0:T(8,128)(2,1)S(1)} %collective-permute-done.17.refs_4_), channel_id=1, source_target_pairs={{1,0},{2,3},{5,4},{6,7},{9,8},{10,11},{13,12},{14,15},{17,16},{18,... | collective-permute-start | bytes 589832 | tf_op jit(solution)/shard_map/ppermute | solution.py:401
  57.9 1.6 %slot_texts.1 = (bf16[1024,256]{1,0:T(8,128)(2,1)S(1)}, bf16[128,1536]{1,0:T(8,128)(2,1)}) custom-call(s32[4,8]{1,0:T(4,128)S(1)} %pad_add_fusion.table, bf16[256,1024]{1,0:T(8,128)(2,1)S(1)} %all_gather.3.text, bf16[12,64,128]{2,1,0:T(8,128)(2,1)S(1)} %get-tuple-element.65.score_grads, bf16[16,1536]{1,0:T(8,128)(2,1)S(1)} %get-tuple-element.46.refs_0_, ...), custom_call_target="tpu_custom_call" | custom-call | tf_op jit(solution)/shard_map/slot_texts/pallas_call | solution.py:294
  59.6 4.3 %collective-permute-done.22.refs_5_ = bf16[64,1536]{1,0:T(8,128)(2,1)S(1)} collective-permute-done((bf16[64,1536]{1,0:T(8,128)(2,1)S(1)}, bf16[64,1536]{1,0:T(8,128)(2,1)S(1)}, u32[]{:S(2)}, u32[]{:S(2)}) %collective-permute-start.22) | collective-permute-done | bytes 196640 | tf_op jit(solution)/shard_map/ppermute | solution.py:401
  63.9 0.0 collective-permute-done.18.refs_2_
  63.9 0.0 collective-permute-done.19.refs_3_
  63.9 2.0 %weight_gradient.2.refs_6_ = bf16[1024,3072]{1,0:T(8,128)(2,1)} custom-call(bf16[1024,256]{1,0:T(8,128)(2,1)S(1)} %get-tuple-element.67.refs_0_, bf16[64,3072]{1,0:T(8,128)(2,1)S(1)} %get-tuple-element.70.refs_1_, bf16[64,3072]{1,0:T(8,128)(2,1)S(1)} %collective-permute-done.18.refs_2_, bf16[64,3072]{1,0:T(8,128)(2,1)S(1)} %collective-permute-done.19.refs_3_, ...), custom_call_target="tpu_custom_call" | custom-call | tf_op jit(solution)/shard_map/weight_gradient/pallas_call | solution.py:343
  65.9 0.1 collective-permute-done.20.refs_5_
  66.0 2.0 %weight_gradient.3 = bf16[1024,3072]{1,0:T(8,128)(2,1)} custom-call(bf16[1024,256]{1,0:T(8,128)(2,1)S(1)} %get-tuple-element.67.refs_0_, bf16[64,3072]{1,0:T(8,128)(2,1)S(1)} %get-tuple-element.70.refs_1_, bf16[64,3072]{1,0:T(8,128)(2,1)S(1)} %collective-permute-done.18.refs_2_, ...), custom_call_target="tpu_custom_call", output_to_operand_aliasing={{}: (6, {})} | custom-call | tf_op jit(solution)/shard_map/weight_gradient/pallas_call | solution.py:343
  (8 shorter events, 0.1 us)
Async XLA Ops:
  0.6 9.0 %copy-start.2 = (bf16[32,1024]{1,0:T(8,128)(2,1)S(1)}, bf16[32,1024]{1,0:T(8,128)(2,1)}, u32[]{:S(2)}) copy-start(bf16[32,1024]{1,0:T(8,128)(2,1)} %refs_0_) | copy-start | bytes 196612
  0.6 9.0 %copy-start.3 = (s32[1,2]{1,0:T(1,128)S(1)}, s32[1,2]{1,0:T(1,128)}, u32[]{:S(2)}) copy-start(s32[1,2]{1,0:T(1,128)} %param.12) | copy-start | bytes 28
  0.7 22.0 %copy-start.4 = (s32[1,8]{1,0:T(1,128)S(1)}, s32[1,8]{1,0:T(1,128)}, u32[]{:S(2)}) copy-start(s32[1,8]{1,0:T(1,128)} %param.15) | copy-start | bytes 100
  0.7 22.0 %copy-start.5 = (s32[1,8]{1,0:T(1,128)S(1)}, s32[1,8]{1,0:T(1,128)}, u32[]{:S(2)}) copy-start(s32[1,8]{1,0:T(1,128)} %param.14) | copy-start | bytes 100
  0.7 22.0 %copy-start.6 = (s32[1,8]{1,0:T(1,128)S(1)}, s32[1,8]{1,0:T(1,128)}, u32[]{:S(2)}) copy-start(s32[1,8]{1,0:T(1,128)} %param.13) | copy-start | bytes 100
  0.7 32.9 %copy-start.1 = (bf16[128,1536]{1,0:T(8,128)(2,1)S(1)}, bf16[128,1536]{1,0:T(8,128)(2,1)}, u32[]{:S(2)}) copy-start(bf16[128,1536]{1,0:T(8,128)(2,1)} %cotangent.3) | copy-start | bytes 1179652
  0.7 32.9 %copy-start = (bf16[128,1536]{1,0:T(8,128)(2,1)S(1)}, bf16[128,1536]{1,0:T(8,128)(2,1)}, u32[]{:S(2)}) copy-start(bf16[128,1536]{1,0:T(8,128)(2,1)} %queries.3) | copy-start | bytes 1179652
  3.9 6.8 %collective-permute-start.1 = (bf16[8,3072]{1,0:T(8,128)(2,1)S(1)}, bf16[8,3072]{1,0:T(8,128)(2,1)S(1)}, u32[]{:S(2)}, u32[]{:S(2)}) collective-permute-start(bf16[8,3072]{1,0:T(8,128)(2,1)S(1)} %get-tuple-element.43), channel_id=1, source_target_pairs={{0,2},{1,3},{2,0},{3,1},{4,6},{5,7},{6,4},{7,5},{8,10},{9,11},{10,... | collective-permute-start | bytes 147464 | tf_op jit(solution)/shard_map/ppermute | solution.py:360
  8.0 4.1 %collective-permute-start.2 = (bf16[8,3072]{1,0:T(8,128)(2,1)S(1)}, bf16[8,3072]{1,0:T(8,128)(2,1)S(1)}, u32[]{:S(2)}, u32[]{:S(2)}) collective-permute-start(bf16[8,3072]{1,0:T(8,128)(2,1)S(1)} %get-tuple-element.44), channel_id=1, source_target_pairs={{0,1},{1,0},{2,3},{3,2},{4,5},{5,4},{6,7},{7,6},{8,9},{9,8},{10,11... | collective-permute-start | bytes 147464 | tf_op jit(solution)/shard_map/ppermute | solution.py:360
  9.6 5.9 %collective-permute-start.3 = (bf16[8,3072]{1,0:T(8,128)(2,1)S(1)}, bf16[8,3072]{1,0:T(8,128)(2,1)S(1)}, u32[]{:S(2)}, u32[]{:S(2)}) collective-permute-start(bf16[8,3072]{1,0:T(8,128)(2,1)S(1)} %get-tuple-element.45), channel_id=1, source_target_pairs={{0,3},{1,2},{2,1},{3,0},{4,7},{5,6},{6,5},{7,4},{8,11},{9,10},{10,... | collective-permute-start | bytes 147464 | tf_op jit(solution)/shard_map/ppermute | solution.py:360
  9.6 13.1 %collective-permute-start = (bf16[32,1024]{1,0:T(8,128)(2,1)S(1)}, bf16[32,1024]{1,0:T(8,128)(2,1)S(1)}, u32[]{:S(2)}, u32[]{:S(2)}) collective-permute-start(bf16[32,1024]{1,0:T(8,128)(2,1)S(1)} %copy-done.2), channel_id=1, source_target_pairs={{0,4},{4,0},{8,12},{12,8},{16,20},{20,16},{24,28},{28,24},{1,5},{5... | collective-permute-start | bytes 196616 | tf_op jit(solution)/shard_map/ppermute | solution.py:360
  15.5 5.3 %collective-permute-start.9 = (bf16[8,3072]{1,0:T(8,128)(2,1)S(1)}, bf16[8,3072]{1,0:T(8,128)(2,1)S(1)}, u32[]{:S(2)}, u32[]{:S(2)}) collective-permute-start(bf16[8,3072]{1,0:T(8,128)(2,1)S(1)} %add_convert_fusion.refs_2_), channel_id=1, source_target_pairs={{0,24},{4,28},{8,16},{12,20},{16,8},{20,12},{24,0},{28,4},{1,25},{... | collective-permute-start | bytes 147464 | tf_op jit(solution)/shard_map/ppermute | solution.py:360
  18.0 4.1 %collective-permute-start.7 = (bf16[8,3072]{1,0:T(8,128)(2,1)S(1)}, bf16[8,3072]{1,0:T(8,128)(2,1)S(1)}, u32[]{:S(2)}, u32[]{:S(2)}) collective-permute-start(bf16[8,3072]{1,0:T(8,128)(2,1)S(1)} %add_convert_fusion.refs_2_), channel_id=1, source_target_pairs={{0,16},{4,20},{8,24},{12,28},{16,0},{20,4},{24,8},{28,12},{1,17},{... | collective-permute-start | bytes 147464 | tf_op jit(solution)/shard_map/ppermute | solution.py:360
  18.5 4.1 %collective-permute-start.5 = (bf16[8,3072]{1,0:T(8,128)(2,1)S(1)}, bf16[8,3072]{1,0:T(8,128)(2,1)S(1)}, u32[]{:S(2)}, u32[]{:S(2)}) collective-permute-start(bf16[8,3072]{1,0:T(8,128)(2,1)S(1)} %add_convert_fusion.refs_2_), channel_id=1, source_target_pairs={{0,8},{4,12},{8,0},{12,4},{16,24},{20,28},{24,16},{28,20},{1,9},{5... | collective-permute-start | bytes 147464 | tf_op jit(solution)/shard_map/ppermute | solution.py:360
  19.1 3.6 %collective-permute-start.4 = (bf16[8,3072]{1,0:T(8,128)(2,1)S(1)}, bf16[8,3072]{1,0:T(8,128)(2,1)S(1)}, u32[]{:S(2)}, u32[]{:S(2)}) collective-permute-start(bf16[8,3072]{1,0:T(8,128)(2,1)S(1)} %add_convert_fusion.refs_2_), channel_id=1, source_target_pairs={{0,4},{4,0},{8,12},{12,8},{16,20},{20,16},{24,28},{28,24},{1,5},{5... | collective-permute-start | bytes 147464 | tf_op jit(solution)/shard_map/ppermute | solution.py:360
  20.8 1.9 %collective-permute-start.10 = (bf16[8,3072]{1,0:T(8,128)(2,1)S(1)}, bf16[8,3072]{1,0:T(8,128)(2,1)S(1)}, u32[]{:S(2)}, u32[]{:S(2)}) collective-permute-start(bf16[8,3072]{1,0:T(8,128)(2,1)S(1)} %collective-permute-done.9.refs_8_), channel_id=1, source_target_pairs={{0,4},{4,0},{8,12},{12,8},{16,20},{20,16},{24,28},{28,24},{1,5},{5... | collective-permute-start | bytes 147464 | tf_op jit(solution)/shard_map/ppermute | solution.py:360
  22.1 1.2 %collective-permute-start.8 = (bf16[8,3072]{1,0:T(8,128)(2,1)S(1)}, bf16[8,3072]{1,0:T(8,128)(2,1)S(1)}, u32[]{:S(2)}, u32[]{:S(2)}) collective-permute-start(bf16[8,3072]{1,0:T(8,128)(2,1)S(1)} %collective-permute-done.7.refs_6_), channel_id=1, source_target_pairs={{0,4},{4,0},{8,12},{12,8},{16,20},{20,16},{24,28},{28,24},{1,5},{5... | collective-permute-start | bytes 147464 | tf_op jit(solution)/shard_map/ppermute | solution.py:360
  22.6 1.2 %collective-permute-start.6 = (bf16[8,3072]{1,0:T(8,128)(2,1)S(1)}, bf16[8,3072]{1,0:T(8,128)(2,1)S(1)}, u32[]{:S(2)}, u32[]{:S(2)}) collective-permute-start(bf16[8,3072]{1,0:T(8,128)(2,1)S(1)} %collective-permute-done.5.refs_4_), channel_id=1, source_target_pairs={{0,4},{4,0},{8,12},{12,8},{16,20},{20,16},{24,28},{28,24},{1,5},{5... | collective-permute-start | bytes 147464 | tf_op jit(solution)/shard_map/ppermute | solution.py:360
  24.7 5.6 %collective-permute-start.11 = (bf16[16,1536]{1,0:T(8,128)(2,1)S(1)}, bf16[16,1536]{1,0:T(8,128)(2,1)S(1)}, u32[]{:S(2)}, u32[]{:S(2)}) collective-permute-start(bf16[16,1536]{1,0:T(8,128)(2,1)S(1)} %get-tuple-element.47), channel_id=1, source_target_pairs={{0,1},{1,0},{2,3},{3,2},{4,5},{5,4},{6,7},{7,6},{8,9},{9,8},{10,11... | collective-permute-start | bytes 147464 | tf_op jit(solution)/shard_map/ppermute | solution.py:360
  24.8 8.8 %collective-permute-start.12 = (bf16[16,1536]{1,0:T(8,128)(2,1)S(1)}, bf16[16,1536]{1,0:T(8,128)(2,1)S(1)}, u32[]{:S(2)}, u32[]{:S(2)}) collective-permute-start(bf16[16,1536]{1,0:T(8,128)(2,1)S(1)} %get-tuple-element.48), channel_id=1, source_target_pairs={{0,2},{1,3},{2,0},{3,1},{4,6},{5,7},{6,4},{7,5},{8,10},{9,11},{10,... | collective-permute-start | bytes 147464 | tf_op jit(solution)/shard_map/ppermute | solution.py:360
  26.0 7.6 %collective-permute-start.13 = (bf16[16,1536]{1,0:T(8,128)(2,1)S(1)}, bf16[16,1536]{1,0:T(8,128)(2,1)S(1)}, u32[]{:S(2)}, u32[]{:S(2)}) collective-permute-start(bf16[16,1536]{1,0:T(8,128)(2,1)S(1)} %get-tuple-element.49), channel_id=1, source_target_pairs={{0,3},{1,2},{2,1},{3,0},{4,7},{5,6},{6,5},{7,4},{8,11},{9,10},{10,... | collective-permute-start | bytes 147464 | tf_op jit(solution)/shard_map/ppermute | solution.py:360
  29.2 5.6 %collective-permute-start.14 = (bf16[16,1536]{1,0:T(8,128)(2,1)S(1)}, bf16[16,1536]{1,0:T(8,128)(2,1)S(1)}, u32[]{:S(2)}, u32[]{:S(2)}) collective-permute-start(bf16[16,1536]{1,0:T(8,128)(2,1)S(1)} %get-tuple-element.55), channel_id=1, source_target_pairs={{0,1},{1,0},{2,3},{3,2},{4,5},{5,4},{6,7},{7,6},{8,9},{9,8},{10,11... | collective-permute-start | bytes 147464 | tf_op jit(solution)/shard_map/ppermute | solution.py:360
  29.2 7.2 %collective-permute-start.15 = (bf16[16,1536]{1,0:T(8,128)(2,1)S(1)}, bf16[16,1536]{1,0:T(8,128)(2,1)S(1)}, u32[]{:S(2)}, u32[]{:S(2)}) collective-permute-start(bf16[16,1536]{1,0:T(8,128)(2,1)S(1)} %get-tuple-element.56), channel_id=1, source_target_pairs={{0,2},{1,3},{2,0},{3,1},{4,6},{5,7},{6,4},{7,5},{8,10},{9,11},{10,... | collective-permute-start | bytes 147464 | tf_op jit(solution)/shard_map/ppermute | solution.py:360
  30.4 6.0 %collective-permute-start.16 = (bf16[16,1536]{1,0:T(8,128)(2,1)S(1)}, bf16[16,1536]{1,0:T(8,128)(2,1)S(1)}, u32[]{:S(2)}, u32[]{:S(2)}) collective-permute-start(bf16[16,1536]{1,0:T(8,128)(2,1)S(1)} %get-tuple-element.57), channel_id=1, source_target_pairs={{0,3},{1,2},{2,1},{3,0},{4,7},{5,6},{6,5},{7,4},{8,11},{9,10},{10,... | collective-permute-start | bytes 147464 | tf_op jit(solution)/shard_map/ppermute | solution.py:360
  37.0 16.1 %collective-permute-start.17 = (bf16[64,1536]{1,0:T(8,128)(2,1)S(1)}, bf16[64,1536]{1,0:T(8,128)(2,1)S(1)}, u32[]{:S(2)}, u32[]{:S(2)}) collective-permute-start(bf16[64,1536]{1,0:T(8,128)(2,1)S(1)} %get-tuple-element.62), channel_id=1, source_target_pairs={{0,2},{1,3},{2,0},{3,1},{4,6},{5,7},{6,4},{7,5},{8,10},{9,11},{10,... | collective-permute-start | bytes 589832 | tf_op jit(solution)/shard_map/ppermute | solution.py:360
  37.6 17.7 %collective-permute-start.21 = (bf16[64,1536]{1,0:T(8,128)(2,1)S(1)}, bf16[64,1536]{1,0:T(8,128)(2,1)S(1)}, u32[]{:S(2)}, u32[]{:S(2)}) collective-permute-start(bf16[64,1536]{1,0:T(8,128)(2,1)S(1)} %get-tuple-element.71), channel_id=1, source_target_pairs={{0,2},{1,3},{2,0},{3,1},{4,6},{5,7},{6,4},{7,5},{8,10},{9,11},{10,... | collective-permute-start | bytes 589832 | tf_op jit(solution)/shard_map/ppermute | solution.py:360
  40.0 23.9 %collective-permute-start.18 = (bf16[64,3072]{1,0:T(8,128)(2,1)S(1)}, bf16[64,3072]{1,0:T(8,128)(2,1)S(1)}, u32[]{:S(2)}, u32[]{:S(2)}) collective-permute-start(bf16[64,3072]{1,0:T(8,128)(2,1)S(1)} %get-tuple-element.70.refs_1_), channel_id=1, source_target_pairs={{0,1},{1,0},{2,3},{3,2},{4,5},{5,4},{6,7},{7,6},{8,9},{9,8},{10,11... | collective-permute-start | bytes 1179656 | tf_op jit(solution)/shard_map/ppermute | solution.py:399
  53.1 10.8 %collective-permute-start.19 = (bf16[64,3072]{1,0:T(8,128)(2,1)S(1)}, bf16[64,3072]{1,0:T(8,128)(2,1)S(1)}, u32[]{:S(2)}, u32[]{:S(2)}) collective-permute-start(bf16[64,3072]{1,0:T(8,128)(2,1)S(1)} %get-tuple-element.70.refs_1_), channel_id=1, source_target_pairs={{1,2},{2,1},{5,6},{6,5},{9,10},{10,9},{13,14},{14,13},{17,18},{18,... | collective-permute-start | bytes 1179656 | tf_op jit(solution)/shard_map/ppermute | solution.py:403
  55.3 8.5 %collective-permute-start.22 = (bf16[64,1536]{1,0:T(8,128)(2,1)S(1)}, bf16[64,1536]{1,0:T(8,128)(2,1)S(1)}, u32[]{:S(2)}, u32[]{:S(2)}) collective-permute-start(bf16[64,1536]{1,0:T(8,128)(2,1)S(1)} %collective-permute-done.21.refs_4_), channel_id=1, source_target_pairs={{1,0},{2,3},{5,4},{6,7},{9,8},{10,11},{13,12},{14,15},{17,16},{18,... | collective-permute-start | bytes 589832 | tf_op jit(solution)/shard_map/ppermute | solution.py:401
  56.6 9.4 %collective-permute-start.20 = (bf16[64,1536]{1,0:T(8,128)(2,1)S(1)}, bf16[64,1536]{1,0:T(8,128)(2,1)S(1)}, u32[]{:S(2)}, u32[]{:S(2)}) collective-permute-start(bf16[64,1536]{1,0:T(8,128)(2,1)S(1)} %collective-permute-done.17.refs_4_), channel_id=1, source_target_pairs={{1,0},{2,3},{5,4},{6,7},{9,8},{10,11},{13,12},{14,15},{17,16},{18,... | collective-permute-start | bytes 589832 | tf_op jit(solution)/shard_map/ppermute | solution.py:401

commit v9 on v7

--- a/solution.py
+++ b/solution.py
@@ -304,7 +304,7 @@
     )(table, text, score_grads, *keys)
 
 
-def weight_kernel(line, start, blocks, *refs):
+def weight_kernel(line, start, *refs):
     chosen_text, *grads = refs[:6] if line else refs[:2]
     out, every, built, sems = refs[-4:]
     at = slice(start, start + every.shape[1])
@@ -319,14 +319,16 @@
         every[3 * each :] = jnp.where(is_inner, inner[:, at], outer[...])
     else:
         every[...] = grads[0][:, at]
-    rows = built.shape[0] // blocks
+    features = built.shape[0]
+    sizes = [features // 16, 3 * features // 16] + [features // 4] * 3
     copies = []
-    for i in range(blocks):
-        block = slice(i * rows, (i + 1) * rows)
+    for i, rows in enumerate(sizes):
+        begin = sum(sizes[:i])
+        block = slice(begin, begin + rows)
         built[block] = jnp.dot(chosen_text[block], every[...], preferred_element_type=F32).astype(BF16)
         copy = pltpu.make_async_copy(
-            built.at[pl.ds(i * rows, rows)],
-            out.at[pl.ds(i * rows, rows), pl.ds(start, every.shape[1])],
+            built.at[pl.ds(begin, rows)],
+            out.at[pl.ds(begin, rows), pl.ds(start, every.shape[1])],
             sems.at[i],
         )
         copy.start()
@@ -338,17 +340,16 @@
 def weight_grad(line, chosen_text, grads, start, size, before=None):
     features, slots = chosen_text.shape
     width = grads[0].shape[1]
-    blocks = 8
     earlier = [] if before is None else [before]
     return pl.pallas_call(
-        functools.partial(weight_kernel, line, start, blocks),
+        functools.partial(weight_kernel, line, start),
         in_specs=[VMEM_SPEC] * (1 + len(grads)) + [ANY_SPEC] * len(earlier),
         out_specs=ANY_SPEC,
         out_shape=jax.ShapeDtypeStruct((features, width), BF16),
         scratch_shapes=[
             pltpu.VMEM((slots, size), BF16),
             pltpu.VMEM((features, size), BF16),
-            pltpu.SemaphoreType.DMA((blocks,)),
+            pltpu.SemaphoreType.DMA((5,)),
         ],
         input_output_aliases={1 + len(grads): 0} if earlier else {},
         compiler_params=kernel_params(),

time: 68.2 us -> 68.3 us (level)
  transfers between devices with their start and end apart: 23 -> 23, of which waited for: 13 -> 12; matrix products, arithmetic and copies ran while one was open for 0% -> 0% of each run, Pallas kernels for 7% -> 7%
where the time goes in v9:
time: 68.3 us; the launch traced here: 68.1 us
  starting transfers between devices  25.4 us (37%)
  waiting for transfers between devices  19.4 us (28%)
  Pallas kernels  11.6 us (17%)
  blocking collectives  10.7 us (16%)
  between operations  0.86 us (1%)
    ppermute x19, starting transfers between devices, swap(): lax.ppermute(x, axis, [(i, i ^ k) for i in range(lax.axis_size(axis))])  21.1 us
    ppermute x19, waiting for transfers between devices, swap(): lax.ppermute(x, axis, [(i, i ^ k) for i in range(lax.axis_size(axis))])  15.1 us
    all_gather x1, blocking collectives, gather_chips(): return lax.all_gather(x, 'dp', axis=0, tiled=True, axis_index_groups=cores)  10.7 us
    ppermute x2, waiting for transfers between devices, gather_line(): outer = [lax.ppermute(piece, 'fsdp', outward) for piece in second]  4.31 us
    pallas_call x2, Pallas kernels, weight_grad(): pl.pallas_call(functools.partial(weight_kernel, line, start), in_specs=[V...  4.21 us
    pallas_call x1, Pallas kernels, project(): pl.pallas_call(functools.partial(project_kernel, groups, paired, chunks),...  3.21 us
    ppermute x2, starting transfers between devices, gather_line(): outer = [lax.ppermute(piece, 'fsdp', outward) for piece in second]  2.57 us
    pallas_call x1, Pallas kernels, slot_texts(): pl.pallas_call(functools.partial(text_kernel, members, groups, each, dept...  1.64 us
  transfers between devices with their start and end apart: 23, of which 12 were waited for; matrix products, arithmetic and copies ran while one was open for 0% of the time, Pallas kernels for 7%

profile of v9, /device:TPU:0, one launch (start us, length us, event | category | flops | bytes accessed | tf_op | source)
XLA Modules:
  0.0 68.1 jit_solution(2331348478083040660)
XLA Ops:
  0.6 0.0 copy-start.2
  0.6 0.0 copy-start.3
  0.7 0.0 copy-start.4
  0.7 0.0 copy-start.5
  0.7 0.0 copy-start.6
  0.7 3.2 %project.1 = (bf16[8,3072]{1,0:T(8,128)(2,1)S(1)}, bf16[8,3072]{1,0:T(8,128)(2,1)S(1)}, bf16[8,3072]{1,0:T(8,128)(2,1)S(1)}, bf16[8,3072]{1,0:T(8,128)(2,1)S(1)}) custom-call(bf16[32,1024]{1,0:T(8,128)(2,1)} %refs_0_, bf16[1024,3072]{1,0:T(8,128)(2,1)} %weight.1), custom_call_target="tpu_custom_call" | custom-call | tf_op jit(solution)/shard_map/project/pallas_call | solution.py:97
  3.9 4.1 %collective-permute-start.1 = (bf16[8,3072]{1,0:T(8,128)(2,1)S(1)}, bf16[8,3072]{1,0:T(8,128)(2,1)S(1)}, u32[]{:S(2)}, u32[]{:S(2)}) collective-permute-start(bf16[8,3072]{1,0:T(8,128)(2,1)S(1)} %get-tuple-element.43), channel_id=1, source_target_pairs={{0,2},{1,3},{2,0},{3,1},{4,6},{5,7},{6,4},{7,5},{8,10},{9,11},{10,... | collective-permute-start | bytes 147464 | tf_op jit(solution)/shard_map/ppermute | solution.py:361
  8.0 1.6 %collective-permute-start.2 = (bf16[8,3072]{1,0:T(8,128)(2,1)S(1)}, bf16[8,3072]{1,0:T(8,128)(2,1)S(1)}, u32[]{:S(2)}, u32[]{:S(2)}) collective-permute-start(bf16[8,3072]{1,0:T(8,128)(2,1)S(1)} %get-tuple-element.44), channel_id=1, source_target_pairs={{0,1},{1,0},{2,3},{3,2},{4,5},{5,4},{6,7},{7,6},{8,9},{9,8},{10,11... | collective-permute-start | bytes 147464 | tf_op jit(solution)/shard_map/ppermute | solution.py:361
  9.6 0.0 collective-permute-start.3
  9.6 0.0 copy-done.2
  9.6 0.0 collective-permute-start
  9.6 0.0 copy-done.3
  9.6 0.1 pad_add_fusion.1
  9.7 1.0 %collective-permute-done.1 = bf16[8,3072]{1,0:T(8,128)(2,1)S(1)} collective-permute-done((bf16[8,3072]{1,0:T(8,128)(2,1)S(1)}, bf16[8,3072]{1,0:T(8,128)(2,1)S(1)}, u32[]{:S(2)}, u32[]{:S(2)}) %collective-permute-start.1) | collective-permute-done | bytes 49184 | tf_op jit(solution)/shard_map/ppermute | solution.py:361
  10.7 1.4 %collective-permute-done.2 = bf16[8,3072]{1,0:T(8,128)(2,1)S(1)} collective-permute-done((bf16[8,3072]{1,0:T(8,128)(2,1)S(1)}, bf16[8,3072]{1,0:T(8,128)(2,1)S(1)}, u32[]{:S(2)}, u32[]{:S(2)}) %collective-permute-start.2) | collective-permute-done | bytes 49184 | tf_op jit(solution)/shard_map/ppermute | solution.py:361
  12.1 3.4 %collective-permute-done.3 = bf16[8,3072]{1,0:T(8,128)(2,1)S(1)} collective-permute-done((bf16[8,3072]{1,0:T(8,128)(2,1)S(1)}, bf16[8,3072]{1,0:T(8,128)(2,1)S(1)}, u32[]{:S(2)}, u32[]{:S(2)}) %collective-permute-start.3) | collective-permute-done | bytes 49184 | tf_op jit(solution)/shard_map/ppermute | solution.py:361
  15.5 2.5 %collective-permute-start.9 = (bf16[8,3072]{1,0:T(8,128)(2,1)S(1)}, bf16[8,3072]{1,0:T(8,128)(2,1)S(1)}, u32[]{:S(2)}, u32[]{:S(2)}) collective-permute-start(bf16[8,3072]{1,0:T(8,128)(2,1)S(1)} %add_convert_fusion.refs_2_), channel_id=1, source_target_pairs={{0,24},{4,28},{8,16},{12,20},{16,8},{20,12},{24,0},{28,4},{1,25},{... | collective-permute-start | bytes 147464 | tf_op jit(solution)/shard_map/ppermute | solution.py:361
  18.0 0.5 collective-permute-start.7
  18.5 0.5 collective-permute-start.5
  19.1 0.0 collective-permute-start.4
  19.1 1.7 %collective-permute-done.9.refs_8_ = bf16[8,3072]{1,0:T(8,128)(2,1)S(1)} collective-permute-done((bf16[8,3072]{1,0:T(8,128)(2,1)S(1)}, bf16[8,3072]{1,0:T(8,128)(2,1)S(1)}, u32[]{:S(2)}, u32[]{:S(2)}) %collective-permute-start.9) | collective-permute-done | bytes 49184 | tf_op jit(solution)/shard_map/ppermute | solution.py:361
  20.8 0.0 collective-permute-start.10
  20.8 1.3 %collective-permute-done.7.refs_6_ = bf16[8,3072]{1,0:T(8,128)(2,1)S(1)} collective-permute-done((bf16[8,3072]{1,0:T(8,128)(2,1)S(1)}, bf16[8,3072]{1,0:T(8,128)(2,1)S(1)}, u32[]{:S(2)}, u32[]{:S(2)}) %collective-permute-start.7) | collective-permute-done | bytes 49184 | tf_op jit(solution)/shard_map/ppermute | solution.py:361
  22.1 0.0 collective-permute-start.8
  22.1 0.5 collective-permute-done.5.refs_4_
  22.6 0.0 collective-permute-start.6
  22.6 0.0 copy-done.5
  22.7 0.0 collective-permute-done.refs_1_
  22.7 0.0 collective-permute-done.4.refs_3_
  22.7 0.0 collective-permute-done.10.refs_9_
  22.7 0.7 collective-permute-done.8.refs_7_
  23.4 0.5 collective-permute-done.6.refs_5_
  23.9 0.8 %select_rows.1 = (bf16[16,1536]{1,0:T(8,128)(2,1)S(1)}, bf16[16,1536]{1,0:T(8,128)(2,1)S(1)}, bf16[16,1536]{1,0:T(8,128)(2,1)S(1)}, bf16[16,1536]{1,0:T(8,128)(2...) custom-call(s32[4,8]{1,0:T(4,128)S(1)} %pad_add_fusion.table, ...), custom_call_target="tpu_custom_call" | custom-call | tf_op jit(solution)/shard_map/select_rows/pallas_call | solution.py:144
  24.7 0.1 collective-permute-start.11
  24.8 1.2 %collective-permute-start.12 = (bf16[16,1536]{1,0:T(8,128)(2,1)S(1)}, bf16[16,1536]{1,0:T(8,128)(2,1)S(1)}, u32[]{:S(2)}, u32[]{:S(2)}) collective-permute-start(bf16[16,1536]{1,0:T(8,128)(2,1)S(1)} %get-tuple-element.48), channel_id=1, source_target_pairs={{0,2},{1,3},{2,0},{3,1},{4,6},{5,7},{6,4},{7,5},{8,10},{9,11},{10,... | collective-permute-start | bytes 147464 | tf_op jit(solution)/shard_map/ppermute | solution.py:361
  26.0 3.2 %collective-permute-start.13 = (bf16[16,1536]{1,0:T(8,128)(2,1)S(1)}, bf16[16,1536]{1,0:T(8,128)(2,1)S(1)}, u32[]{:S(2)}, u32[]{:S(2)}) collective-permute-start(bf16[16,1536]{1,0:T(8,128)(2,1)S(1)} %get-tuple-element.49), channel_id=1, source_target_pairs={{0,3},{1,2},{2,1},{3,0},{4,7},{5,6},{6,5},{7,4},{8,11},{9,10},{10,... | collective-permute-start | bytes 147464 | tf_op jit(solution)/shard_map/ppermute | solution.py:361
  29.2 0.0 collective-permute-start.14
  29.2 1.2 %collective-permute-start.15 = (bf16[16,1536]{1,0:T(8,128)(2,1)S(1)}, bf16[16,1536]{1,0:T(8,128)(2,1)S(1)}, u32[]{:S(2)}, u32[]{:S(2)}) collective-permute-start(bf16[16,1536]{1,0:T(8,128)(2,1)S(1)} %get-tuple-element.56), channel_id=1, source_target_pairs={{0,2},{1,3},{2,0},{3,1},{4,6},{5,7},{6,4},{7,5},{8,10},{9,11},{10,... | collective-permute-start | bytes 147464 | tf_op jit(solution)/shard_map/ppermute | solution.py:361
  30.4 0.0 collective-permute-done.11.refs_1_
  30.4 3.2 %collective-permute-start.16 = (bf16[16,1536]{1,0:T(8,128)(2,1)S(1)}, bf16[16,1536]{1,0:T(8,128)(2,1)S(1)}, u32[]{:S(2)}, u32[]{:S(2)}) collective-permute-start(bf16[16,1536]{1,0:T(8,128)(2,1)S(1)} %get-tuple-element.57), channel_id=1, source_target_pairs={{0,3},{1,2},{2,1},{3,0},{4,7},{5,6},{6,5},{7,4},{8,11},{9,10},{10,... | collective-permute-start | bytes 147464 | tf_op jit(solution)/shard_map/ppermute | solution.py:361
  33.6 0.0 collective-permute-done.12.refs_2_
  33.6 0.0 collective-permute-done.13.refs_3_
  33.6 0.0 copy-done.1
  33.6 1.2 %value_gradients.1 = (f32[12,64,128]{2,1,0:T(8,128)S(1)}, bf16[64,1536]{1,0:T(8,128)(2,1)S(1)}) custom-call(s32[4,8]{1,0:T(4,128)S(1)} %pad_add_fusion.table, bf16[128,1536]{1,0:T(8,128)(2,1)S(1)} %copy-done, bf16[128,1536]{1,0:T(8,128)(2,1)S(1)} %copy-done.1, bf16[16,1536]{1,0:T(8,128)(2,1)S(1)} %get-tuple-element.46.refs_0_, ...), custom_call_target="tpu_custom_call" | custom-call | tf_op jit(solution)/shard_map/value_gradients/pallas_call | solution.py:202
  34.7 0.0 collective-permute-done.14.refs_1_
  34.8 1.6 %collective-permute-done.15.refs_2_ = bf16[16,1536]{1,0:T(8,128)(2,1)S(1)} collective-permute-done((bf16[16,1536]{1,0:T(8,128)(2,1)S(1)}, bf16[16,1536]{1,0:T(8,128)(2,1)S(1)}, u32[]{:S(2)}, u32[]{:S(2)}) %collective-permute-start.15) | collective-permute-done | bytes 49184 | tf_op jit(solution)/shard_map/ppermute | solution.py:361
  36.4 0.0 collective-permute-done.16.refs_3_
  36.4 0.6 key_gradients.1
  37.0 0.7 collective-permute-start.17
  37.6 2.3 %collective-permute-start.21 = (bf16[64,1536]{1,0:T(8,128)(2,1)S(1)}, bf16[64,1536]{1,0:T(8,128)(2,1)S(1)}, u32[]{:S(2)}, u32[]{:S(2)}) collective-permute-start(bf16[64,1536]{1,0:T(8,128)(2,1)S(1)} %get-tuple-element.71), channel_id=1, source_target_pairs={{0,2},{1,3},{2,0},{3,1},{4,6},{5,7},{6,4},{7,5},{8,10},{9,11},{10,... | collective-permute-start | bytes 589832 | tf_op jit(solution)/shard_map/ppermute | solution.py:361
  40.0 1.1 %collective-permute-start.18 = (bf16[64,3072]{1,0:T(8,128)(2,1)S(1)}, bf16[64,3072]{1,0:T(8,128)(2,1)S(1)}, u32[]{:S(2)}, u32[]{:S(2)}) collective-permute-start(bf16[64,3072]{1,0:T(8,128)(2,1)S(1)} %get-tuple-element.70.refs_1_), channel_id=1, source_target_pairs={{0,1},{1,0},{2,3},{3,2},{4,5},{5,4},{6,7},{7,6},{8,9},{9,8},{10,11... | collective-permute-start | bytes 1179656 | tf_op jit(solution)/shard_map/ppermute | solution.py:400
  41.1 10.7 %all_gather.3.text = bf16[256,1024]{1,0:T(8,128)(2,1)S(1)} all-gather(bf16[64,1024]{1,0:T(8,128)(2,1)S(1)} %get-tuple-element.63), channel_id=1, replica_groups={{0,8,16,24},{4,12,20,28},{1,9,17,25},{5,13,21,29},{2,10,18,26},{6,14,22..., dimensions={0}, use_global_device_ids=true | all-gather | bytes 655360 | tf_op jit(solution)/shard_map/all_gather | solution.py:378
  51.7 1.4 %collective-permute-done.17.refs_4_ = bf16[64,1536]{1,0:T(8,128)(2,1)S(1)} collective-permute-done((bf16[64,1536]{1,0:T(8,128)(2,1)S(1)}, bf16[64,1536]{1,0:T(8,128)(2,1)S(1)}, u32[]{:S(2)}, u32[]{:S(2)}) %collective-permute-start.17) | collective-permute-done | bytes 196640 | tf_op jit(solution)/shard_map/ppermute | solution.py:361
  53.1 0.7 collective-permute-start.19
  53.8 1.6 %collective-permute-done.21.refs_4_ = bf16[64,1536]{1,0:T(8,128)(2,1)S(1)} collective-permute-done((bf16[64,1536]{1,0:T(8,128)(2,1)S(1)}, bf16[64,1536]{1,0:T(8,128)(2,1)S(1)}, u32[]{:S(2)}, u32[]{:S(2)}) %collective-permute-start.21) | collective-permute-done | bytes 196640 | tf_op jit(solution)/shard_map/ppermute | solution.py:361
  55.3 1.3 %collective-permute-start.22 = (bf16[64,1536]{1,0:T(8,128)(2,1)S(1)}, bf16[64,1536]{1,0:T(8,128)(2,1)S(1)}, u32[]{:S(2)}, u32[]{:S(2)}) collective-permute-start(bf16[64,1536]{1,0:T(8,128)(2,1)S(1)} %collective-permute-done.21.refs_4_), channel_id=1, source_target_pairs={{1,0},{2,3},{5,4},{6,7},{9,8},{10,11},{13,12},{14,15},{17,16},{18,... | collective-permute-start | bytes 589832 | tf_op jit(solution)/shard_map/ppermute | solution.py:402
  56.6 1.3 %collective-permute-start.20 = (bf16[64,1536]{1,0:T(8,128)(2,1)S(1)}, bf16[64,1536]{1,0:T(8,128)(2,1)S(1)}, u32[]{:S(2)}, u32[]{:S(2)}) collective-permute-start(bf16[64,1536]{1,0:T(8,128)(2,1)S(1)} %collective-permute-done.17.refs_4_), channel_id=1, source_target_pairs={{1,0},{2,3},{5,4},{6,7},{9,8},{10,11},{13,12},{14,15},{17,16},{18,... | collective-permute-start | bytes 589832 | tf_op jit(solution)/shard_map/ppermute | solution.py:402
  57.9 1.6 %slot_texts.1 = (bf16[1024,256]{1,0:T(8,128)(2,1)S(1)}, bf16[128,1536]{1,0:T(8,128)(2,1)}) custom-call(s32[4,8]{1,0:T(4,128)S(1)} %pad_add_fusion.table, bf16[256,1024]{1,0:T(8,128)(2,1)S(1)} %all_gather.3.text, bf16[12,64,128]{2,1,0:T(8,128)(2,1)S(1)} %get-tuple-element.65.score_grads, bf16[16,1536]{1,0:T(8,128)(2,1)S(1)} %get-tuple-element.46.refs_0_, ...), custom_call_target="tpu_custom_call" | custom-call | tf_op jit(solution)/shard_map/slot_texts/pallas_call | solution.py:294
  59.6 4.3 %collective-permute-done.22.refs_5_ = bf16[64,1536]{1,0:T(8,128)(2,1)S(1)} collective-permute-done((bf16[64,1536]{1,0:T(8,128)(2,1)S(1)}, bf16[64,1536]{1,0:T(8,128)(2,1)S(1)}, u32[]{:S(2)}, u32[]{:S(2)}) %collective-permute-start.22) | collective-permute-done | bytes 196640 | tf_op jit(solution)/shard_map/ppermute | solution.py:402
  63.9 0.0 collective-permute-done.18.refs_2_
  63.9 0.0 collective-permute-done.19.refs_3_
  63.9 2.1 %weight_gradient.2.refs_6_ = bf16[1024,3072]{1,0:T(8,128)(2,1)} custom-call(bf16[1024,256]{1,0:T(8,128)(2,1)S(1)} %get-tuple-element.67.refs_0_, bf16[64,3072]{1,0:T(8,128)(2,1)S(1)} %get-tuple-element.70.refs_1_, bf16[64,3072]{1,0:T(8,128)(2,1)S(1)} %collective-permute-done.18.refs_2_, bf16[64,3072]{1,0:T(8,128)(2,1)S(1)} %collective-permute-done.19.refs_3_, ...), custom_call_target="tpu_custom_call" | custom-call | tf_op jit(solution)/shard_map/weight_gradient/pallas_call | solution.py:344
  66.0 0.0 collective-permute-done.20.refs_5_
  66.0 2.1 %weight_gradient.3 = bf16[1024,3072]{1,0:T(8,128)(2,1)} custom-call(bf16[1024,256]{1,0:T(8,128)(2,1)S(1)} %get-tuple-element.67.refs_0_, bf16[64,3072]{1,0:T(8,128)(2,1)S(1)} %get-tuple-element.70.refs_1_, bf16[64,3072]{1,0:T(8,128)(2,1)S(1)} %collective-permute-done.18.refs_2_, ...), custom_call_target="tpu_custom_call", output_to_operand_aliasing={{}: (6, {})} | custom-call | tf_op jit(solution)/shard_map/weight_gradient/pallas_call | solution.py:344
  (8 shorter events, 0.1 us)
Async XLA Ops:
  0.6 9.0 %copy-start.2 = (bf16[32,1024]{1,0:T(8,128)(2,1)S(1)}, bf16[32,1024]{1,0:T(8,128)(2,1)}, u32[]{:S(2)}) copy-start(bf16[32,1024]{1,0:T(8,128)(2,1)} %refs_0_) | copy-start | bytes 196612
  0.6 9.0 %copy-start.3 = (s32[1,2]{1,0:T(1,128)S(1)}, s32[1,2]{1,0:T(1,128)}, u32[]{:S(2)}) copy-start(s32[1,2]{1,0:T(1,128)} %param.12) | copy-start | bytes 28
  0.7 22.0 %copy-start.4 = (s32[1,8]{1,0:T(1,128)S(1)}, s32[1,8]{1,0:T(1,128)}, u32[]{:S(2)}) copy-start(s32[1,8]{1,0:T(1,128)} %param.15) | copy-start | bytes 100
  0.7 22.0 %copy-start.5 = (s32[1,8]{1,0:T(1,128)S(1)}, s32[1,8]{1,0:T(1,128)}, u32[]{:S(2)}) copy-start(s32[1,8]{1,0:T(1,128)} %param.14) | copy-start | bytes 100
  0.7 22.0 %copy-start.6 = (s32[1,8]{1,0:T(1,128)S(1)}, s32[1,8]{1,0:T(1,128)}, u32[]{:S(2)}) copy-start(s32[1,8]{1,0:T(1,128)} %param.13) | copy-start | bytes 100
  0.7 32.9 %copy-start.1 = (bf16[128,1536]{1,0:T(8,128)(2,1)S(1)}, bf16[128,1536]{1,0:T(8,128)(2,1)}, u32[]{:S(2)}) copy-start(bf16[128,1536]{1,0:T(8,128)(2,1)} %cotangent.3) | copy-start | bytes 1179652
  0.7 32.9 %copy-start = (bf16[128,1536]{1,0:T(8,128)(2,1)S(1)}, bf16[128,1536]{1,0:T(8,128)(2,1)}, u32[]{:S(2)}) copy-start(bf16[128,1536]{1,0:T(8,128)(2,1)} %queries.3) | copy-start | bytes 1179652
  3.9 6.8 %collective-permute-start.1 = (bf16[8,3072]{1,0:T(8,128)(2,1)S(1)}, bf16[8,3072]{1,0:T(8,128)(2,1)S(1)}, u32[]{:S(2)}, u32[]{:S(2)}) collective-permute-start(bf16[8,3072]{1,0:T(8,128)(2,1)S(1)} %get-tuple-element.43), channel_id=1, source_target_pairs={{0,2},{1,3},{2,0},{3,1},{4,6},{5,7},{6,4},{7,5},{8,10},{9,11},{10,... | collective-permute-start | bytes 147464 | tf_op jit(solution)/shard_map/ppermute | solution.py:361
  8.0 4.1 %collective-permute-start.2 = (bf16[8,3072]{1,0:T(8,128)(2,1)S(1)}, bf16[8,3072]{1,0:T(8,128)(2,1)S(1)}, u32[]{:S(2)}, u32[]{:S(2)}) collective-permute-start(bf16[8,3072]{1,0:T(8,128)(2,1)S(1)} %get-tuple-element.44), channel_id=1, source_target_pairs={{0,1},{1,0},{2,3},{3,2},{4,5},{5,4},{6,7},{7,6},{8,9},{9,8},{10,11... | collective-permute-start | bytes 147464 | tf_op jit(solution)/shard_map/ppermute | solution.py:361
  9.6 5.9 %collective-permute-start.3 = (bf16[8,3072]{1,0:T(8,128)(2,1)S(1)}, bf16[8,3072]{1,0:T(8,128)(2,1)S(1)}, u32[]{:S(2)}, u32[]{:S(2)}) collective-permute-start(bf16[8,3072]{1,0:T(8,128)(2,1)S(1)} %get-tuple-element.45), channel_id=1, source_target_pairs={{0,3},{1,2},{2,1},{3,0},{4,7},{5,6},{6,5},{7,4},{8,11},{9,10},{10,... | collective-permute-start | bytes 147464 | tf_op jit(solution)/shard_map/ppermute | solution.py:361
  9.6 13.1 %collective-permute-start = (bf16[32,1024]{1,0:T(8,128)(2,1)S(1)}, bf16[32,1024]{1,0:T(8,128)(2,1)S(1)}, u32[]{:S(2)}, u32[]{:S(2)}) collective-permute-start(bf16[32,1024]{1,0:T(8,128)(2,1)S(1)} %copy-done.2), channel_id=1, source_target_pairs={{0,4},{4,0},{8,12},{12,8},{16,20},{20,16},{24,28},{28,24},{1,5},{5... | collective-permute-start | bytes 196616 | tf_op jit(solution)/shard_map/ppermute | solution.py:361
  15.5 5.3 %collective-permute-start.9 = (bf16[8,3072]{1,0:T(8,128)(2,1)S(1)}, bf16[8,3072]{1,0:T(8,128)(2,1)S(1)}, u32[]{:S(2)}, u32[]{:S(2)}) collective-permute-start(bf16[8,3072]{1,0:T(8,128)(2,1)S(1)} %add_convert_fusion.refs_2_), channel_id=1, source_target_pairs={{0,24},{4,28},{8,16},{12,20},{16,8},{20,12},{24,0},{28,4},{1,25},{... | collective-permute-start | bytes 147464 | tf_op jit(solution)/shard_map/ppermute | solution.py:361
  18.0 4.1 %collective-permute-start.7 = (bf16[8,3072]{1,0:T(8,128)(2,1)S(1)}, bf16[8,3072]{1,0:T(8,128)(2,1)S(1)}, u32[]{:S(2)}, u32[]{:S(2)}) collective-permute-start(bf16[8,3072]{1,0:T(8,128)(2,1)S(1)} %add_convert_fusion.refs_2_), channel_id=1, source_target_pairs={{0,16},{4,20},{8,24},{12,28},{16,0},{20,4},{24,8},{28,12},{1,17},{... | collective-permute-start | bytes 147464 | tf_op jit(solution)/shard_map/ppermute | solution.py:361
  18.5 4.1 %collective-permute-start.5 = (bf16[8,3072]{1,0:T(8,128)(2,1)S(1)}, bf16[8,3072]{1,0:T(8,128)(2,1)S(1)}, u32[]{:S(2)}, u32[]{:S(2)}) collective-permute-start(bf16[8,3072]{1,0:T(8,128)(2,1)S(1)} %add_convert_fusion.refs_2_), channel_id=1, source_target_pairs={{0,8},{4,12},{8,0},{12,4},{16,24},{20,28},{24,16},{28,20},{1,9},{5... | collective-permute-start | bytes 147464 | tf_op jit(solution)/shard_map/ppermute | solution.py:361
  19.1 3.6 %collective-permute-start.4 = (bf16[8,3072]{1,0:T(8,128)(2,1)S(1)}, bf16[8,3072]{1,0:T(8,128)(2,1)S(1)}, u32[]{:S(2)}, u32[]{:S(2)}) collective-permute-start(bf16[8,3072]{1,0:T(8,128)(2,1)S(1)} %add_convert_fusion.refs_2_), channel_id=1, source_target_pairs={{0,4},{4,0},{8,12},{12,8},{16,20},{20,16},{24,28},{28,24},{1,5},{5... | collective-permute-start | bytes 147464 | tf_op jit(solution)/shard_map/ppermute | solution.py:361
  20.8 1.9 %collective-permute-start.10 = (bf16[8,3072]{1,0:T(8,128)(2,1)S(1)}, bf16[8,3072]{1,0:T(8,128)(2,1)S(1)}, u32[]{:S(2)}, u32[]{:S(2)}) collective-permute-start(bf16[8,3072]{1,0:T(8,128)(2,1)S(1)} %collective-permute-done.9.refs_8_), channel_id=1, source_target_pairs={{0,4},{4,0},{8,12},{12,8},{16,20},{20,16},{24,28},{28,24},{1,5},{5... | collective-permute-start | bytes 147464 | tf_op jit(solution)/shard_map/ppermute | solution.py:361
  22.1 1.2 %collective-permute-start.8 = (bf16[8,3072]{1,0:T(8,128)(2,1)S(1)}, bf16[8,3072]{1,0:T(8,128)(2,1)S(1)}, u32[]{:S(2)}, u32[]{:S(2)}) collective-permute-start(bf16[8,3072]{1,0:T(8,128)(2,1)S(1)} %collective-permute-done.7.refs_6_), channel_id=1, source_target_pairs={{0,4},{4,0},{8,12},{12,8},{16,20},{20,16},{24,28},{28,24},{1,5},{5... | collective-permute-start | bytes 147464 | tf_op jit(solution)/shard_map/ppermute | solution.py:361
  22.6 1.2 %collective-permute-start.6 = (bf16[8,3072]{1,0:T(8,128)(2,1)S(1)}, bf16[8,3072]{1,0:T(8,128)(2,1)S(1)}, u32[]{:S(2)}, u32[]{:S(2)}) collective-permute-start(bf16[8,3072]{1,0:T(8,128)(2,1)S(1)} %collective-permute-done.5.refs_4_), channel_id=1, source_target_pairs={{0,4},{4,0},{8,12},{12,8},{16,20},{20,16},{24,28},{28,24},{1,5},{5... | collective-permute-start | bytes 147464 | tf_op jit(solution)/shard_map/ppermute | solution.py:361
  24.7 5.6 %collective-permute-start.11 = (bf16[16,1536]{1,0:T(8,128)(2,1)S(1)}, bf16[16,1536]{1,0:T(8,128)(2,1)S(1)}, u32[]{:S(2)}, u32[]{:S(2)}) collective-permute-start(bf16[16,1536]{1,0:T(8,128)(2,1)S(1)} %get-tuple-element.47), channel_id=1, source_target_pairs={{0,1},{1,0},{2,3},{3,2},{4,5},{5,4},{6,7},{7,6},{8,9},{9,8},{10,11... | collective-permute-start | bytes 147464 | tf_op jit(solution)/shard_map/ppermute | solution.py:361
  24.8 8.8 %collective-permute-start.12 = (bf16[16,1536]{1,0:T(8,128)(2,1)S(1)}, bf16[16,1536]{1,0:T(8,128)(2,1)S(1)}, u32[]{:S(2)}, u32[]{:S(2)}) collective-permute-start(bf16[16,1536]{1,0:T(8,128)(2,1)S(1)} %get-tuple-element.48), channel_id=1, source_target_pairs={{0,2},{1,3},{2,0},{3,1},{4,6},{5,7},{6,4},{7,5},{8,10},{9,11},{10,... | collective-permute-start | bytes 147464 | tf_op jit(solution)/shard_map/ppermute | solution.py:361
  26.0 7.6 %collective-permute-start.13 = (bf16[16,1536]{1,0:T(8,128)(2,1)S(1)}, bf16[16,1536]{1,0:T(8,128)(2,1)S(1)}, u32[]{:S(2)}, u32[]{:S(2)}) collective-permute-start(bf16[16,1536]{1,0:T(8,128)(2,1)S(1)} %get-tuple-element.49), channel_id=1, source_target_pairs={{0,3},{1,2},{2,1},{3,0},{4,7},{5,6},{6,5},{7,4},{8,11},{9,10},{10,... | collective-permute-start | bytes 147464 | tf_op jit(solution)/shard_map/ppermute | solution.py:361
  29.2 5.6 %collective-permute-start.14 = (bf16[16,1536]{1,0:T(8,128)(2,1)S(1)}, bf16[16,1536]{1,0:T(8,128)(2,1)S(1)}, u32[]{:S(2)}, u32[]{:S(2)}) collective-permute-start(bf16[16,1536]{1,0:T(8,128)(2,1)S(1)} %get-tuple-element.55), channel_id=1, source_target_pairs={{0,1},{1,0},{2,3},{3,2},{4,5},{5,4},{6,7},{7,6},{8,9},{9,8},{10,11... | collective-permute-start | bytes 147464 | tf_op jit(solution)/shard_map/ppermute | solution.py:361
  29.2 7.2 %collective-permute-start.15 = (bf16[16,1536]{1,0:T(8,128)(2,1)S(1)}, bf16[16,1536]{1,0:T(8,128)(2,1)S(1)}, u32[]{:S(2)}, u32[]{:S(2)}) collective-permute-start(bf16[16,1536]{1,0:T(8,128)(2,1)S(1)} %get-tuple-element.56), channel_id=1, source_target_pairs={{0,2},{1,3},{2,0},{3,1},{4,6},{5,7},{6,4},{7,5},{8,10},{9,11},{10,... | collective-permute-start | bytes 147464 | tf_op jit(solution)/shard_map/ppermute | solution.py:361
  30.4 6.0 %collective-permute-start.16 = (bf16[16,1536]{1,0:T(8,128)(2,1)S(1)}, bf16[16,1536]{1,0:T(8,128)(2,1)S(1)}, u32[]{:S(2)}, u32[]{:S(2)}) collective-permute-start(bf16[16,1536]{1,0:T(8,128)(2,1)S(1)} %get-tuple-element.57), channel_id=1, source_target_pairs={{0,3},{1,2},{2,1},{3,0},{4,7},{5,6},{6,5},{7,4},{8,11},{9,10},{10,... | collective-permute-start | bytes 147464 | tf_op jit(solution)/shard_map/ppermute | solution.py:361
  37.0 16.1 %collective-permute-start.17 = (bf16[64,1536]{1,0:T(8,128)(2,1)S(1)}, bf16[64,1536]{1,0:T(8,128)(2,1)S(1)}, u32[]{:S(2)}, u32[]{:S(2)}) collective-permute-start(bf16[64,1536]{1,0:T(8,128)(2,1)S(1)} %get-tuple-element.62), channel_id=1, source_target_pairs={{0,2},{1,3},{2,0},{3,1},{4,6},{5,7},{6,4},{7,5},{8,10},{9,11},{10,... | collective-permute-start | bytes 589832 | tf_op jit(solution)/shard_map/ppermute | solution.py:361
  37.6 17.7 %collective-permute-start.21 = (bf16[64,1536]{1,0:T(8,128)(2,1)S(1)}, bf16[64,1536]{1,0:T(8,128)(2,1)S(1)}, u32[]{:S(2)}, u32[]{:S(2)}) collective-permute-start(bf16[64,1536]{1,0:T(8,128)(2,1)S(1)} %get-tuple-element.71), channel_id=1, source_target_pairs={{0,2},{1,3},{2,0},{3,1},{4,6},{5,7},{6,4},{7,5},{8,10},{9,11},{10,... | collective-permute-start | bytes 589832 | tf_op jit(solution)/shard_map/ppermute | solution.py:361
  40.0 23.9 %collective-permute-start.18 = (bf16[64,3072]{1,0:T(8,128)(2,1)S(1)}, bf16[64,3072]{1,0:T(8,128)(2,1)S(1)}, u32[]{:S(2)}, u32[]{:S(2)}) collective-permute-start(bf16[64,3072]{1,0:T(8,128)(2,1)S(1)} %get-tuple-element.70.refs_1_), channel_id=1, source_target_pairs={{0,1},{1,0},{2,3},{3,2},{4,5},{5,4},{6,7},{7,6},{8,9},{9,8},{10,11... | collective-permute-start | bytes 1179656 | tf_op jit(solution)/shard_map/ppermute | solution.py:400
  53.1 10.8 %collective-permute-start.19 = (bf16[64,3072]{1,0:T(8,128)(2,1)S(1)}, bf16[64,3072]{1,0:T(8,128)(2,1)S(1)}, u32[]{:S(2)}, u32[]{:S(2)}) collective-permute-start(bf16[64,3072]{1,0:T(8,128)(2,1)S(1)} %get-tuple-element.70.refs_1_), channel_id=1, source_target_pairs={{1,2},{2,1},{5,6},{6,5},{9,10},{10,9},{13,14},{14,13},{17,18},{18,... | collective-permute-start | bytes 1179656 | tf_op jit(solution)/shard_map/ppermute | solution.py:404
  55.3 8.5 %collective-permute-start.22 = (bf16[64,1536]{1,0:T(8,128)(2,1)S(1)}, bf16[64,1536]{1,0:T(8,128)(2,1)S(1)}, u32[]{:S(2)}, u32[]{:S(2)}) collective-permute-start(bf16[64,1536]{1,0:T(8,128)(2,1)S(1)} %collective-permute-done.21.refs_4_), channel_id=1, source_target_pairs={{1,0},{2,3},{5,4},{6,7},{9,8},{10,11},{13,12},{14,15},{17,16},{18,... | collective-permute-start | bytes 589832 | tf_op jit(solution)/shard_map/ppermute | solution.py:402
  56.6 9.4 %collective-permute-start.20 = (bf16[64,1536]{1,0:T(8,128)(2,1)S(1)}, bf16[64,1536]{1,0:T(8,128)(2,1)S(1)}, u32[]{:S(2)}, u32[]{:S(2)}) collective-permute-start(bf16[64,1536]{1,0:T(8,128)(2,1)S(1)} %collective-permute-done.17.refs_4_), channel_id=1, source_target_pairs={{1,0},{2,3},{5,4},{6,7},{9,8},{10,11},{13,12},{14,15},{17,16},{18,... | collective-permute-start | bytes 589832 | tf_op jit(solution)/shard_map/ppermute | solution.py:402
